TPU v7x, 32 devices: a whole 2x2x4 slice. The times are simulated.
32 devices in a mesh: dp: 16 (over z, y, core), expert: 2 (over x).
Axes of the slice: x: 2, y: 2, z: 4, core: 2. Of those that a mesh axis runs over, the one named last changes fastest.
Arguments:
- tokens: bfloat16 [8192, 1536], P(('dp', 'expert')), may hold values from -6 to 6
- norm1_gain: bfloat16 [1536], P('dp'), may hold values from 0.5 to 1.5
- w_query: bfloat16 [1536, 1536], P('dp'), may hold values from -0.15625 to 0.15625
- w_key: bfloat16 [1536, 256], P('dp'), may hold values from -0.15625 to 0.15625
- w_value: bfloat16 [1536, 256], P('dp'), may hold values from -0.15625 to 0.15625
- w_out: bfloat16 [1536, 1536], P('dp'), may hold values from -0.625 to 0.625
- norm2_gain: bfloat16 [1536], P('dp'), may hold values from 0.5 to 1.5
- w_router: bfloat16 [1536, 8], P('dp'), may hold values from -0.06982422 to 0.06982422
- w_gate: bfloat16 [8, 1536, 768], P('expert'), may hold values from -0.15625 to 0.15625
- w_up: bfloat16 [8, 1536, 768], P('expert'), may hold values from -0.15625 to 0.15625
- w_down: bfloat16 [8, 768, 1536], P('expert'), may hold values from -0.44921875 to 0.44921875
- expert_ids: int32 [8192, 4], P(('dp', 'expert')), may hold values from 0 to 7, all different within a row; in each aligned block of 128 rows (0 to 127, 128 to 255, ...) at most 96 rows name the same one
- prefix_len: int32 [32], P(('dp', 'expert')), may hold values from 25 to 128
- out_grad: bfloat16 [8192, 1536], P(('dp', 'expert')), may hold values from -6 to 6
Outputs:
- block_out: bfloat16 [8192, 1536], P(('dp', 'expert'))
- tokens_grad: bfloat16 [8192, 1536], P(('dp', 'expert'))
- norm1_grad: float32 [1536], P('dp')
- query_grad: float32 [1536, 1536], P('dp')
- key_grad: float32 [1536, 256], P('dp')
- value_grad: float32 [1536, 256], P('dp')
- outproj_grad: float32 [1536, 1536], P('dp')
- norm2_grad: float32 [1536], P('dp')
- router_grad: float32 [1536, 8], P('dp')
- gate_grad: float32 [8, 1536, 768], P('expert', 'dp')
- up_grad: float32 [8, 1536, 768], P('expert', 'dp')
- down_grad: float32 [8, 768, 1536], P('expert', None, 'dp')
Inputs may be any that keep to these rules, and one draw needn't show every extreme that they name: `expert_ids`: each row names 4 different experts. Within the rows of one device's micro-batch (aligned blocks of 128 rows) no expert is named by more than 96 rows, and some block reaches 96.
All inputs are finite; a program needn't handle non-finite values.
Results may differ from a plain program's by a relative error of at most 0.024.
Values may be sent and summed in bfloat16 or wider, within the bound.
No kernel may reach another device: no remote copies, remote signals or barrier semaphores. Data moves between devices by JAX's collectives and lax.ppermute only.
A program may use at most 192 MiB of HBM per device.

v0:
```python
import functools
import math

import jax
import jax.numpy as jnp
from jax import lax
from jax.experimental import pallas as pl
from jax.experimental.pallas import tpu as pltpu
from jax.sharding import PartitionSpec as P

HQ = 12
HK = 2
HD = 128
MICRO = 2
PLANE = ("y", "c", "x")
GROUP = ("z", "y", "c")


def rms_scale(values, gain_vec):
    inverse = lax.rsqrt(jnp.mean(values * values, axis=-1, keepdims=True) + 1e-06)
    return values * inverse * gain_vec


def angles(length, head_size):
    positions = jnp.arange(length).astype(jnp.float32)
    freq_rates = jnp.exp(
        -(2.0 * jnp.arange(head_size // 2).astype(jnp.float32) / head_size) * math.log(1000000.0)
    )
    angle_tab = positions[:, None] * freq_rates[None, :]
    return (jnp.cos(angle_tab)[:, None, :], jnp.sin(angle_tab)[:, None, :])


def rotary(values, cosine_tab, sine_tab):
    half_dim = values.shape[-1] // 2
    first_half = values[..., :half_dim]
    second_half = values[..., half_dim:]
    return jnp.concatenate(
        [
            first_half * cosine_tab - second_half * sine_tab,
            second_half * cosine_tab + first_half * sine_tab,
        ],
        axis=-1,
    )


def expert_act(gate_pre, up_pre):
    return jax.nn.gelu(gate_pre, approximate=True) * up_pre


def left_product(left_mat, right_mat):
    return lax.dot_general(
        left_mat, right_mat, (((0,), (0,)), ((), ())), preferred_element_type=jnp.float32
    )


def gather(block, axes):
    return lax.all_gather(block, axes, axis=0, tiled=True)


def exchange(block, axes):
    return lax.all_to_all(block, axes, split_axis=0, concat_axis=0, tiled=True)


def scatter_sum(block, axes):
    return lax.psum_scatter(block, axes, scatter_dimension=0, tiled=True)


def by_owner(cols, parts):
    rows, total = cols.shape
    return jnp.moveaxis(cols.reshape(rows, parts, total // parts), 1, 0).reshape(
        parts * rows, total // parts
    )


def local_wide(
    tokens,
    norm1_gain,
    w_query,
    w_key,
    w_value,
    w_out,
    norm2_gain,
    w_router,
    w_gate,
    w_up,
    w_down,
    expert_ids,
    prefix_len,
    out_grad,
):
    bf16, f32 = jnp.bfloat16, jnp.float32
    length, model_width = tokens.shape
    shard_rows = w_query.shape[0]
    local_count, _, hidden_width = w_gate.shape
    owners = lax.axis_size("x")
    depth = lax.axis_size("z")
    plane = lax.axis_size(PLANE)
    experts_all = w_router.shape[1]
    top_count = expert_ids.shape[1]
    block_rows = length // MICRO
    capacity = 3 * block_rows * top_count // (2 * experts_all)
    plane_rows = plane * length
    blocks = plane_rows // block_rows
    group_size = HQ // HK
    score_scale = HD ** (-0.5)
    q_cols, kv_cols = w_query.shape[1], w_key.shape[1]
    own_local = lax.axis_index(("y", "c"))
    own_expert = lax.axis_index("x") * local_count + own_local
    own_place = lax.axis_index(PLANE)

    narrow = jnp.concatenate([w_router, norm1_gain[:, None], norm2_gain[:, None]], axis=1)
    narrow = jnp.pad(narrow, ((0, 0), (0, -narrow.shape[1] % 128)))
    packed = gather(jnp.concatenate([w_query, w_key, w_value, narrow], axis=1), GROUP)
    qkv_cols = q_cols + 2 * kv_cols
    qkv_w = packed[:, :qkv_cols]
    router_w = packed[:, qkv_cols : qkv_cols + experts_all]
    gains = packed[:, qkv_cols + experts_all : qkv_cols + experts_all + 2].T.astype(f32)
    gain_one, gain_two = gains[0], gains[1]
    output_w = gather(w_out, GROUP)

    ids_all = gather(expert_ids, PLANE)
    cot_all = gather(out_grad, PLANE)
    chosen_mask = jnp.any(
        ids_all[:, :, None] == jnp.arange(experts_all, dtype=jnp.int32)[None, None, :], axis=1
    )
    own_mask = jnp.any(ids_all == own_expert, axis=1).reshape(blocks, block_rows)
    place = jnp.cumsum(own_mask.astype(jnp.int32), axis=1) - 1
    dispatch = (
        own_mask[:, None, :]
        & (place[:, None, :] == jnp.arange(capacity, dtype=jnp.int32)[None, :, None])
    ).astype(bf16)

    cosine_tab, sine_tab = angles(length, HD)
    inputs_f = tokens.astype(f32)
    first_in = rms_scale(inputs_f, gain_one).astype(bf16)
    qkv = jnp.dot(first_in, qkv_w, preferred_element_type=f32)
    queries = (
        rotary(qkv[:, :q_cols].reshape(length, HQ, HD), cosine_tab, sine_tab)
        .astype(bf16)
        .reshape(length, HK, group_size, HD)
    )
    keys_rot = rotary(
        qkv[:, q_cols : q_cols + kv_cols].reshape(length, HK, HD), cosine_tab, sine_tab
    ).astype(bf16)
    values_b = qkv[:, q_cols + kv_cols :].astype(bf16).reshape(length, HK, HD)
    positions = jnp.arange(length)
    allowed = (positions[None, :] <= positions[:, None]) | (positions[None, :] < prefix_len[0])

    def masked_scores():
        scores = jnp.einsum("ihrd,jhd->hrij", queries, keys_rot, preferred_element_type=f32)
        return jnp.where(allowed, scores * score_scale, -1e30)

    masked = masked_scores()
    row_peak = jnp.max(masked, axis=-1, keepdims=True)
    log_total = row_peak + jnp.log(jnp.sum(jnp.exp(masked - row_peak), axis=-1, keepdims=True))
    prob_bf = jnp.exp(masked - log_total).astype(bf16)
    attended = jnp.einsum("hrij,jhd->ihrd", prob_bf, values_b, preferred_element_type=f32)
    attended = attended.reshape(length, HQ * HD).astype(bf16)
    resid = inputs_f + jnp.dot(attended, output_w, preferred_element_type=f32)
    second_in = rms_scale(resid, gain_two).astype(bf16)

    second_all = gather(second_in, PLANE)
    logits = jnp.dot(second_all, router_w, preferred_element_type=f32)
    gates_all = jax.nn.softmax(jnp.where(chosen_mask, logits, -jnp.inf), axis=-1)
    own_gates = lax.dynamic_index_in_dim(gates_all, own_expert, 1, keepdims=False)
    own_gates = own_gates.reshape(blocks, block_rows)
    gate_rows = jnp.einsum(
        "bct,bt->bc", dispatch.astype(f32), own_gates, precision=lax.Precision.HIGHEST
    )[:, :, None]
    gate_w = lax.dynamic_index_in_dim(w_gate, own_local, 0, keepdims=False)
    up_w = lax.dynamic_index_in_dim(w_up, own_local, 0, keepdims=False)
    down_w = lax.dynamic_index_in_dim(w_down, own_local, 0, keepdims=False)

    def to_rows(array):
        return jnp.einsum(
            "bct,btd->bcd",
            dispatch,
            array.reshape(blocks, block_rows, model_width),
            preferred_element_type=f32,
        ).astype(bf16)

    def to_tokens(rows):
        return (
            jnp.einsum("bct,bcd->btd", dispatch, rows.astype(bf16), preferred_element_type=f32)
            .astype(bf16)
            .reshape(plane_rows, model_width)
        )

    rows_in = to_rows(second_all)
    rows_cot = to_rows(cot_all)
    gate_pre = jnp.einsum("bcd,df->bcf", rows_in, gate_w, preferred_element_type=f32)
    up_pre = jnp.einsum("bcd,df->bcf", rows_in, up_w, preferred_element_type=f32)
    hidden, act_pull = jax.vjp(expert_act, gate_pre, up_pre)
    gated = (gate_rows * hidden).astype(bf16)
    down_part = jnp.einsum("bcd,bcf->df", rows_cot, gated, preferred_element_type=f32)
    down_sum = scatter_sum(down_part.astype(bf16), "z")
    cot_hidden = jnp.einsum("bcd,fd->bcf", rows_cot, down_w, preferred_element_type=f32)
    gate_signal_rows = jnp.sum(hidden * cot_hidden, axis=-1)
    gate_pgrad, up_pgrad = act_pull(gate_rows * cot_hidden)
    gate_pgrad = gate_pgrad.astype(bf16)
    up_pgrad = up_pgrad.astype(bf16)
    gate_part = jnp.einsum("bcd,bcf->df", rows_in, gate_pgrad, preferred_element_type=f32)
    gate_sum = scatter_sum(gate_part.astype(bf16), "z")
    up_part = jnp.einsum("bcd,bcf->df", rows_in, up_pgrad, preferred_element_type=f32)
    up_sum = scatter_sum(up_part.astype(bf16), "z")
    rows_grad = jnp.einsum("bcf,df->bcd", gate_pgrad, gate_w, preferred_element_type=f32)
    rows_grad = rows_grad + jnp.einsum("bcf,df->bcd", up_pgrad, up_w, preferred_element_type=f32)
    second_back = scatter_sum(to_tokens(rows_grad), PLANE).astype(f32)
    gate_signal = jnp.einsum(
        "bct,bc->bt", dispatch.astype(f32), gate_signal_rows, precision=lax.Precision.HIGHEST
    )
    gate_signal = exchange(gate_signal.reshape(plane, length), PLANE)
    gate_signal = jnp.transpose(
        gate_signal.reshape(local_count, owners, length), (2, 1, 0)
    ).reshape(length, experts_all)
    expert_rows = jnp.einsum("bcf,fd->bcd", gated, down_w, preferred_element_type=f32)
    mixture = scatter_sum(to_tokens(expert_rows), PLANE).astype(f32)
    block_out = (resid + mixture).astype(bf16)

    cotangent = out_grad.astype(f32)
    gate_probs = lax.dynamic_slice_in_dim(gates_all, own_place * length, length, 0)
    logit_grad = (
        gate_probs
        * (gate_signal - jnp.sum(gate_probs * gate_signal, axis=-1, keepdims=True))
    ).astype(bf16)
    router_acc = left_product(second_in, logit_grad)
    second_grad = second_back + jnp.dot(logit_grad, router_w.T, preferred_element_type=f32)
    _, norm_two_pull = jax.vjp(rms_scale, resid, gain_two)
    resid_norm_grad, gain_two_grad = norm_two_pull(second_grad)
    resid_grad = cotangent + resid_norm_grad
    branch_grad = resid_grad.astype(bf16)

    attended_all = gather(attended, PLANE)
    branch_cols = exchange(by_owner(branch_grad, plane), PLANE)
    output_part = left_product(attended_all, branch_cols)
    attended_grad = jnp.dot(branch_grad, output_w.T, preferred_element_type=f32).astype(bf16)
    attended_grad = attended_grad.reshape(length, HK, group_size, HD)
    masked = masked_scores()
    prob_full = jnp.exp(masked - log_total)
    prob_bf = prob_full.astype(bf16)
    prob_grad = jnp.einsum("ihrd,jhd->hrij", attended_grad, values_b, preferred_element_type=f32)
    row_inner = jnp.sum(prob_full * prob_grad, axis=-1, keepdims=True)
    score_grad = (prob_full * (prob_grad - row_inner)).astype(bf16)
    query_rot_grad = (
        jnp.einsum("hrij,jhd->ihrd", score_grad, keys_rot, preferred_element_type=f32)
        * score_scale
    )
    query_back = rotary(query_rot_grad.reshape(length, HQ, HD), cosine_tab, -sine_tab)
    query_back = query_back.astype(bf16).reshape(length, HQ * HD)
    key_rot_grad = (
        jnp.einsum("hrij,ihrd->jhd", score_grad, queries, preferred_element_type=f32)
        * score_scale
    )
    key_back = rotary(key_rot_grad, cosine_tab, -sine_tab).astype(bf16).reshape(length, HK * HD)
    value_back = jnp.einsum("hrij,ihrd->jhd", prob_bf, attended_grad, preferred_element_type=f32)
    value_back = value_back.astype(bf16).reshape(length, HK * HD)
    qkv_back = jnp.concatenate([query_back, key_back, value_back], axis=1)
    first_all = gather(first_in, PLANE)
    qkv_part = left_product(first_all, exchange(by_owner(qkv_back, plane), PLANE))
    first_grad = lax.dot_general(
        qkv_back, qkv_w, (((1,), (1,)), ((), ())), preferred_element_type=f32
    )
    _, norm_one_pull = jax.vjp(rms_scale, inputs_f, gain_one)
    input_norm_grad, gain_one_grad = norm_one_pull(first_grad)
    tokens_grad = (resid_grad + input_norm_grad).astype(bf16)

    narrow_part = jnp.concatenate(
        [router_acc, gain_one_grad[:, None], gain_two_grad[:, None]], axis=1
    ).astype(bf16)
    narrow_cols = narrow_part.shape[1]
    narrow_sum = lax.psum(scatter_sum(narrow_part, GROUP), "x").astype(f32)
    dense_part = jnp.concatenate([qkv_part, output_part], axis=1).astype(bf16)
    dense_sum = scatter_sum(dense_part, "z")
    dense_cols = dense_sum.shape[1]
    dense_sum = gather(dense_sum, PLANE).reshape(plane, local_count, shard_rows, dense_cols)
    dense_sum = lax.dynamic_index_in_dim(dense_sum, own_local, 1, keepdims=False).astype(f32)
    dense_sum = jnp.moveaxis(dense_sum, 0, 1)
    qkv_width = qkv_cols // plane
    qkv_sum = dense_sum[:, :, :qkv_width].reshape(shard_rows, qkv_cols)
    output_sum = dense_sum[:, :, qkv_width:].reshape(shard_rows, model_width)

    def placed(total):
        total = exchange(total, ("y", "c"))
        return total.reshape(local_count, shard_rows, hidden_width).astype(f32)

    return (
        block_out,
        tokens_grad,
        narrow_sum[:, experts_all],
        qkv_sum[:, :q_cols],
        qkv_sum[:, q_cols : q_cols + kv_cols],
        qkv_sum[:, q_cols + kv_cols :],
        output_sum,
        narrow_sum[:, experts_all + 1],
        narrow_sum[:, :experts_all],
        placed(gate_sum),
        placed(up_sum),
        jnp.swapaxes(placed(down_sum), 1, 2),
    )


def rounded(values):
    return lax.reduce_precision(values, 8, 7).astype(jnp.bfloat16)


def after(block, *others):
    return lax.optimization_barrier((block,) + others)[0]


def swap(block, axis):
    return lax.ppermute(block, axis, [(0, 1), (1, 0)])


def shifts(block):
    depth = lax.axis_size("z")
    return [
        lax.ppermute(block, "z", [(i, (i + k) % depth) for i in range(depth)])
        for k in range(1, depth)
    ]


def plane_sides(block):
    return swap(block, "x"), swap(block, "y")


def plane_corner(sides, before=(), later=()):
    over_x, over_y = sides
    half = over_x.shape[0] // 2
    over_y, over_x = lax.optimization_barrier((over_y[:half], over_x[half:]) + before)[:2]
    parts = (swap(over_y, "x"), swap(over_x, "y"))
    return jnp.concatenate(lax.optimization_barrier(parts + later)[:2], axis=0)


def plane_pieces(block, sides=None, corner=None):
    sides = plane_sides(block) if sides is None else sides
    corner = plane_corner(sides) if corner is None else corner
    pieces = [block, *sides, corner]
    return pieces + [swap(piece, "c") for piece in pieces]


def small_gather(block):
    for axis in ("x", "y", "c"):
        block = jnp.concatenate([block, swap(block, axis)], axis=1)
    return block


def small_group_gather(block):
    depth = lax.axis_size("z")
    order = jnp.stack(([block] + shifts(block))[::-1] * 2)
    start = (depth - 1 - lax.axis_index("z")) % depth
    total = lax.dynamic_slice_in_dim(order, start, depth, 0)[:, None, None]
    for dim, axis in ((1, "y"), (2, "c")):
        other = swap(total, axis)
        last = lax.axis_index(axis) == 1
        pair = [jnp.where(last, other, total), jnp.where(last, total, other)]
        total = jnp.concatenate(pair, axis=dim)
    return total.reshape(-1, block.shape[1])


def add(left, right):
    return rounded(left.astype(jnp.float32) + right.astype(jnp.float32))


def over_core(near, far):
    return add(near, swap(far, "c"))


def early_sums(over_x, over_y):
    half = over_x.shape[0] // 2
    return swap(over_x[:half], "x"), swap(over_y[half:], "y")


def corner_first(corner):
    half = corner.shape[0] // 2
    return swap(corner[:half], "x"), swap(corner[half:], "y")


def corner_last(over_x, over_y, first):
    half = over_x.shape[0] // 2
    over_y, over_x = add(over_y[:half], first[0]), add(over_x[half:], first[1])
    return swap(over_y, "y"), swap(over_x, "x"), over_y, over_x


def cost(micros):
    return pl.CostEstimate(flops=micros * 10**9, bytes_accessed=micros * 10**6, transcendentals=0)


def dot(left, right, dims=((1,), (0,)), precision=None):
    return lax.dot_general(
        left, right, (dims, ((), ())), precision=precision, preferred_element_type=jnp.float32
    )


WHOLE = pl.BlockSpec(memory_space=pltpu.VMEM)
IN_HBM = pl.BlockSpec(memory_space=pltpu.HBM)
SCALARS = pl.BlockSpec(memory_space=pltpu.SMEM)


def run_kernel(kernel, micros, at, operands, outs, megabytes=16, scratch=(), hbm_in=0, hbm_out=0):
    return pl.pallas_call(
        kernel,
        out_shape=[jax.ShapeDtypeStruct(shape, dtype) for shape, dtype in outs],
        in_specs=[SCALARS] + [WHOLE] * (len(operands) - hbm_in) + [IN_HBM] * hbm_in,
        out_specs=[WHOLE] * (len(outs) - hbm_out) + [IN_HBM] * hbm_out,
        scratch_shapes=scratch,
        cost_estimate=cost(micros),
        compiler_params=pltpu.CompilerParams(vmem_limit_bytes=megabytes * 2**20),
    )(at, *operands)


def place_pieces(at, refs, weight):
    depth = weight.shape[1]
    for n, ref in enumerate(refs):
        dc, dy, dx = n // 4, n // 2 % 2, n % 2
        for k in range(depth):
            z = lax.rem(at[3] + depth - k, depth)
            weight[at[2] ^ dx, z, at[0] ^ dy, at[1] ^ dc] = ref[k]


def rms_kernel(values, gain):
    inverse = lax.rsqrt(jnp.mean(values * values, axis=-1, keepdims=True) + 1e-06)
    return (values * inverse * gain).astype(jnp.bfloat16)


def rms_back(values, gain, grad):
    inverse = lax.rsqrt(jnp.mean(values * values, axis=-1, keepdims=True) + 1e-06)
    normed = values * inverse
    gain_grad = jnp.sum(grad * normed, axis=0, keepdims=True)
    grad = grad * gain
    along = jnp.mean(grad * normed, axis=-1, keepdims=True)
    return inverse * (grad - normed * along), gain_grad


def turned(values, cosine_tab, sine_tab):
    return values * cosine_tab + pltpu.roll(values, HD // 2, 1) * sine_tab


def attend_kernel(at, tokens, gain, cosine, sine, *refs):
    first_ref, query_ref, key_ref, value_ref, out_ref = refs[8:13]
    prob_out, weight_out, prob_ref, weight, sems = refs[13:]
    place_pieces(at, refs[:8], weight)
    copies = [pltpu.make_async_copy(weight, weight_out, sems.at[HK])]
    copies[0].start()
    length = tokens.shape[0]
    first_in = rms_kernel(tokens[...].astype(jnp.float32), gain[...])
    first_ref[...] = first_in
    rows = lax.broadcasted_iota(jnp.int32, (length, length), 0)
    cols = lax.broadcasted_iota(jnp.int32, (length, length), 1)
    allowed = (cols <= rows) | (cols < at[4])
    cosine_tab, sine_tab = cosine[...], sine[...]
    group_size = HQ // HK
    for group in range(HK):
        matrix = weight[group].reshape(first_in.shape[1], -1)
        qkv = dot(first_in, matrix)
        at_key = group_size * HD
        key = turned(qkv[:, at_key : at_key + HD], cosine_tab, sine_tab).astype(jnp.bfloat16)
        value = qkv[:, at_key + HD :].astype(jnp.bfloat16)
        key_ref[:, group * HD : (group + 1) * HD] = key
        value_ref[:, group * HD : (group + 1) * HD] = value
        for member in range(group_size):
            head = group * group_size + member
            here = slice(head * HD, (head + 1) * HD)
            query = turned(qkv[:, member * HD : (member + 1) * HD], cosine_tab, sine_tab)
            query = query.astype(jnp.bfloat16)
            query_ref[:, here] = query
            scores = dot(query, key, ((1,), (1,)))
            scores = jnp.where(allowed, scores * HD ** (-0.5), -1e30)
            weights = jnp.exp(scores - jnp.max(scores, axis=-1, keepdims=True))
            prob = weights * (1.0 / jnp.sum(weights, axis=-1, keepdims=True))
            prob = prob.astype(jnp.bfloat16)
            prob_ref[head] = prob
            out_ref[:, here] = dot(prob, value).astype(jnp.bfloat16)
        here = pl.ds(group * group_size, group_size)
        copies.append(
            pltpu.make_async_copy(prob_ref.at[here], prob_out.at[here], sems.at[group])
        )
        copies[-1].start()
    for copy in copies:
        copy.wait()


def project_kernel(at, tokens, gain, attended, *refs):
    resid_ref, second_ref, weight_out, weight, sem = refs[8:]
    place_pieces(at, refs[:8], weight)
    copy = pltpu.make_async_copy(weight, weight_out, sem)
    copy.start()
    heads = attended[...]
    halves = [dot(heads, weight[half].reshape(heads.shape[1], -1)) for half in range(2)]
    resid = tokens[...].astype(jnp.float32) + jnp.concatenate(halves, axis=1)
    resid_ref[...] = resid
    second_ref[...] = rms_kernel(resid, gain[...])
    copy.wait()


def one_hot(slots, capacity, dtype):
    shape = (capacity, slots.shape[1])
    return (slots == lax.broadcasted_iota(jnp.int32, shape, 0)).astype(jnp.float32).astype(dtype)


def slots_of(ids, expert, start, rows):
    named = jnp.any(ids[:, start : start + rows] == expert, axis=0, keepdims=True)
    named = named.astype(jnp.float32)
    before = lax.broadcasted_iota(jnp.int32, (rows, rows), 0)
    upto = lax.broadcasted_iota(jnp.int32, (rows, rows), 1)
    counts = dot(named.astype(jnp.bfloat16), (before <= upto).astype(jnp.float32).astype(jnp.bfloat16))
    return jnp.where(named > 0.0, counts - 1.0, -1.0).astype(jnp.int32)


def spread(picks, capacity, rows, outs):
    rows = rows.astype(jnp.bfloat16)
    block = picks[0].shape[1]
    for n in range(len(picks) // 2):
        for part in range(2):
            pick = picks[2 * n + part]
            at_row = (2 * n + part) * capacity
            tokens = dot(pick, rows[at_row : at_row + capacity], ((0,), (0,)))
            outs[n][part * block : (part + 1) * block] = tokens.astype(jnp.bfloat16)


def expert_kernel(capacity, pieces, at, ids, router, *refs):
    count = len(pieces)
    second, cot = refs[:count], refs[count : 2 * count]
    gate_w, up_w, down_w = refs[2 * count : 2 * count + 3]
    rows_in, rows_cot, gated_ref, gate_back, up_back, gates_ref = refs[2 * count + 3 : 2 * count + 9]
    backs, gate_rows = refs[2 * count + 9 : -1], refs[-1]
    f32, bf16 = jnp.float32, jnp.bfloat16
    length, width = second[0].shape
    wide = router.shape[1]
    half = length // 2
    picks = []
    experts = lax.broadcasted_iota(jnp.int32, (wide, length), 0)
    for n, piece in enumerate(pieces):
        tokens = second[n][...]
        named = ids[:, piece * length : (piece + 1) * length]
        chosen = functools.reduce(
            jnp.logical_or, [named[k : k + 1] == experts for k in range(named.shape[0])]
        )
        logits = jnp.where(chosen, dot(router[...], tokens, ((0,), (1,))), -1e30)
        weights = jnp.exp(logits - jnp.max(logits, axis=0, keepdims=True))
        gates = weights * (1.0 / jnp.sum(weights, axis=0, keepdims=True))
        if n == 0:
            gates_ref[...] = gates
        own = jnp.sum(jnp.where(experts == at[5], gates, 0.0), axis=0, keepdims=True)
        for part in range(2):
            here = slice(part * half, (part + 1) * half)
            place = slice((2 * n + part) * capacity, (2 * n + part + 1) * capacity)
            slots = slots_of(ids, at[5], piece * length + part * half, half)
            pick = one_hot(slots, capacity, f32)
            picks.append(pick.astype(bf16))
            rows_in[place] = dot(picks[-1], tokens[here]).astype(bf16)
            rows_cot[place] = dot(picks[-1], cot[n][here]).astype(bf16)
            gate_rows[place] = jnp.sum(pick * own[:, here], axis=1, keepdims=True)
    gate = gate_rows[...]
    gate_pre = dot(rows_in[...], gate_w[...])
    up_pre = dot(rows_in[...], up_w[...])
    cot_hidden = dot(rows_cot[...], down_w[...], ((1,), (1,)))
    scale = math.sqrt(2.0 / math.pi)
    square = gate_pre * gate_pre
    bent = jnp.tanh(scale * gate_pre * (1.0 + 0.044715 * square))
    open_part = 0.5 * (1.0 + bent)
    active = gate_pre * open_part
    slope = open_part + 0.5 * gate_pre * (1.0 - bent * bent) * scale * (
        1.0 + 3 * 0.044715 * square
    )
    hidden = active * up_pre
    gated_ref[...] = (gate * hidden).astype(bf16)
    signal = jnp.sum(hidden * cot_hidden, axis=1, keepdims=True)
    back = gate * cot_hidden
    gate_back[...] = (back * up_pre * slope).astype(bf16)
    up_back[...] = (back * active).astype(bf16)
    high = signal.astype(bf16)
    low = (signal - high.astype(f32)).astype(bf16)
    lanes = lax.broadcasted_iota(jnp.int32, (signal.shape[0], wide), 1)
    signal = jnp.where(lanes == at[5], high.astype(f32), 0.0)
    signal = jnp.where(lanes == at[5] + wide // 2, low.astype(f32), signal)
    by_rows = ((1,), (1,))
    rows = dot(gate_back[...], gate_w[...], by_rows) + dot(up_back[...], up_w[...], by_rows)
    spread(picks, capacity, jnp.concatenate([rows, signal], axis=1), backs)


def run_expert(pieces, at, ids, router, weights, second, cot, capacity):
    count = len(pieces)
    rows, wide = 2 * count * capacity, router.shape[1]
    (length, width), hidden = second[0].shape, weights[0].shape[1]
    bf16, f32 = jnp.bfloat16, jnp.float32
    outs = [(rows, width)] * 2 + [(rows, hidden)] * 3
    outs = [(shape, bf16) for shape in outs] + [((wide, length), f32)]
    outs = outs + [((length, width + wide), bf16)] * count
    return run_kernel(
        functools.partial(expert_kernel, capacity, pieces),
        4 * count,
        at,
        (ids, router, *second, *cot, *weights),
        outs,
        6 + 4 * count,
        [pltpu.VMEM((rows, 1), f32)],
    )


def mixture_kernel(capacity, groups, at, ids, *refs):
    gated, down_w, outs = refs[: len(groups)], refs[len(groups)], refs[len(groups) + 1 :]
    length = outs[0].shape[0]
    for pieces, rows in zip(groups, gated):
        picks = []
        for piece in pieces:
            for part in range(2):
                start = piece * length + part * length // 2
                slots = slots_of(ids, at[5], start, length // 2)
                picks.append(one_hot(slots, capacity, jnp.bfloat16))
        spread(picks, capacity, dot(rows[...], down_w[...]), [outs[piece] for piece in pieces])


def row_sum_kernel(parts, at, *refs):
    arrays = [
        jnp.concatenate([ref[...] for ref in refs[n : n + parts]], axis=0)
        for n in range(0, len(refs) - len(refs) // (parts + 1), parts)
    ]
    outs = refs[len(arrays) * parts :]
    for out, right in zip(outs, arrays[1:]):
        out[...] = dot(arrays[0], right, ((0,), (0,))).astype(jnp.bfloat16)


def row_sums(at, left, *rights):
    operands = [part for parts in (left, *rights) for part in parts]
    outs = [((left[0].shape[1], right[0].shape[1]), jnp.bfloat16) for right in rights]
    kernel = functools.partial(row_sum_kernel, len(left))
    return run_kernel(kernel, 4 * len(rights), at, operands, outs, 24 if len(rights) == 1 else 56)


def branch_back_kernel(
    at, near, far, first_x, first_y, last_y, last_x, resid, gain, second, gates, router, cot, weight, *outs
):
    resid_grad_ref, branch_ref, attended_ref, router_ref, gain_ref = outs
    f32, bf16 = jnp.float32, jnp.bfloat16
    halves = [first_x[...].astype(f32) + last_y[...], first_y[...].astype(f32) + last_x[...]]
    total = near[...].astype(f32) + far[...] + jnp.concatenate(halves, axis=0)
    width = resid.shape[1]
    signal = total[:, width:]
    signal = signal + pltpu.roll(signal, signal.shape[1] // 2, 1)
    chosen = gates[...].T
    logit_grad = chosen * (signal - jnp.sum(chosen * signal, axis=-1, keepdims=True))
    logit_grad = logit_grad.astype(bf16)
    second_grad = total[:, :width] + dot(logit_grad, router[...], ((1,), (1,)))
    norm_grad, gain_grad = rms_back(resid[...], gain[...], second_grad)
    gain_ref[...] = gain_grad
    resid_grad = cot[...].astype(f32) + norm_grad
    resid_grad_ref[...] = resid_grad
    branch = resid_grad.astype(bf16)
    branch_ref[...] = branch
    wide = weight.shape[2]
    attended_ref[...] = (
        dot(branch[:, :wide], weight[0], ((1,), (1,)))
        + dot(branch[:, wide:], weight[1], ((1,), (1,)))
    ).astype(bf16)
    router_ref[...] = dot(second[...], logit_grad, ((0,), (0,)))


def attend_back_kernel(
    at, attended, probs, queries, keys, values, cosine, sine, branch, back_ref
):
    f32, bf16 = jnp.float32, jnp.bfloat16
    cosine_tab, sine_tab = cosine[...], -sine[...]
    group_size = HQ // HK
    places, length = back_ref.shape[0], branch.shape[0]
    branch_width = branch.shape[1] // places
    width = back_ref.shape[2] - branch_width
    for place in range(places):
        here = slice(place * branch_width, (place + 1) * branch_width)
        back_ref[place, :length, width:] = branch[:, here]
        back_ref[place, length:] = jnp.zeros((back_ref.shape[1] - length, back_ref.shape[2]), bf16)
    scale = HD ** (-0.5)

    def put(position, block):
        back_ref[position // width, :length, position % width : position % width + HD] = block

    for group in range(HK):
        own = slice(group * HD, (group + 1) * HD)
        key, value = keys[:, own], values[:, own]
        key_grad = value_grad = 0.0
        start = group * (group_size + 2) * HD
        for member in range(group_size):
            head = group * group_size + member
            here = slice(head * HD, (head + 1) * HD)
            out_grad, query, prob = attended[:, here], queries[:, here], probs[head]
            prob_grad = dot(out_grad, value, ((1,), (1,)))
            prob_f = prob.astype(f32)
            inner = jnp.sum(prob_f * prob_grad, axis=-1, keepdims=True)
            score_grad = (prob_f * (prob_grad - inner)).astype(bf16)
            query_grad = turned(dot(score_grad, key) * scale, cosine_tab, sine_tab)
            put(start + member * HD, query_grad.astype(bf16))
            key_grad = key_grad + dot(score_grad, query, ((0,), (0,)))
            value_grad = value_grad + dot(prob, out_grad, ((0,), (0,)))
        key_grad = turned(key_grad * scale, cosine_tab, sine_tab)
        put(start + group_size * HD, key_grad.astype(bf16))
        put(start + (group_size + 1) * HD, value_grad.astype(bf16))


def first_back_kernel(at, back, weight, tokens, gain, resid_grad, tokens_ref, gain_ref):
    f32 = jnp.float32
    parts = back.shape[0]
    cols = weight.shape[0] * weight.shape[2] // parts
    first_grad = 0.0
    for part in range(parts):
        group, place = divmod(part * cols, weight.shape[2])
        first_grad = first_grad + dot(
            back[part, : tokens.shape[0], :cols], weight[group, :, place : place + cols], ((1,), (1,))
        )
    norm_grad, gain_grad = rms_back(tokens[...].astype(f32), gain[...], first_grad)
    gain_ref[...] = gain_grad
    tokens_ref[...] = (resid_grad[...] + norm_grad).astype(jnp.bfloat16)


def dense_grad_kernel(at, narrow, back, *refs):
    pieces, out_ref, held, sems = refs[:8], refs[8], refs[9], refs[10]
    copies = [
        pltpu.make_async_copy(piece, held.at[n], sems.at[n]) for n, piece in enumerate(pieces)
    ]
    for copy in copies:
        copy.start()
    depth, rows, cols = out_ref.shape
    length = held.shape[1] // 2
    qkv_width = cols - held.shape[2] // back.shape[0]
    narrow = sum(narrow[place].astype(jnp.float32) for place in range(narrow.shape[0]))
    sums = [0.0, 0.0]
    for n, copy in enumerate(copies):
        copy.wait()
        dc, dy, dx = n // 4, n // 2 % 2, n % 2
        place = 4 * (at[0] ^ dy) + 2 * (at[1] ^ dc) + (at[2] ^ dx)
        own = back[place, :length]
        sums[0] = sums[0] + dot(held[n, length:], own[:, :qkv_width], ((0,), (0,)))
        sums[1] = sums[1] + dot(held[n, :length], own[:, qkv_width:], ((0,), (0,)))
    wide = held.shape[2] // depth
    each = narrow.shape[0] // depth
    for z in range(depth):
        here = slice(z * wide, (z + 1) * wide)
        both = jnp.concatenate([part[here] for part in sums], axis=1)
        out_ref[z, :wide] = both.astype(jnp.bfloat16)
        kept = [narrow[z * each : (z + 1) * each], jnp.zeros((rows - wide - each, cols), jnp.float32)]
        out_ref[z, wide:] = jnp.concatenate(kept, axis=0).astype(jnp.bfloat16)


def finish_kernel(at, sums, query_ref, key_ref, value_ref, output_ref):
    places, _, cols = sums.shape
    rows, out_width = query_ref.shape[0], output_ref.shape[1] // places
    width = cols - out_width
    for place in range(places):
        block = sums[place, :rows].astype(jnp.float32)
        output_ref[:, place * out_width : (place + 1) * out_width] = block[:, width:]
        for at_col in range(0, width, HD):
            group, head = divmod((place * width + at_col) // HD, HQ // HK + 2)
            part = block[:, at_col : at_col + HD]
            if head < HQ // HK:
                start = (group * (HQ // HK) + head) * HD
                query_ref[:, start : start + HD] = part
            elif head == HQ // HK:
                key_ref[:, group * HD : (group + 1) * HD] = part
            else:
                value_ref[:, group * HD : (group + 1) * HD] = part


def local_pairs(
    tokens,
    norm1_gain,
    w_query,
    w_key,
    w_value,
    w_out,
    norm2_gain,
    w_router,
    w_gate,
    w_up,
    w_down,
    expert_ids,
    prefix_len,
    out_grad,
):
    bf16, f32 = jnp.bfloat16, jnp.float32
    length, model_width = tokens.shape
    shard_rows = w_query.shape[0]
    local_count, _, hidden_width = w_gate.shape
    owners = lax.axis_size("x")
    depth = lax.axis_size("z")
    plane = lax.axis_size(PLANE)
    experts_all = w_router.shape[1]
    block_rows = length // MICRO
    capacity = 3 * block_rows * expert_ids.shape[1] // (2 * experts_all)
    plane_rows = plane * length
    blocks = plane_rows // block_rows
    q_cols, kv_cols = w_query.shape[1], w_key.shape[1]
    qkv_cols = q_cols + 2 * kv_cols
    q_group, out_half = q_cols // HK, model_width // 2
    y, c, x, z = (lax.axis_index(axis) for axis in ("y", "c", "x", "z"))
    own_local = 2 * y + c
    own_expert = x * local_count + own_local
    at = jnp.stack([y, c, x, z, prefix_len[0], own_expert, own_local])

    own_half = jnp.concatenate(
        [
            lax.dynamic_slice_in_dim(part, x * (part.shape[1] // 2), part.shape[1] // 2, 1)
            for part in (w_query, w_key, w_value, w_out)
        ],
        axis=1,
    )
    narrow = jnp.concatenate([w_router, norm1_gain[:, None], norm2_gain[:, None]], axis=1)
    narrow = jnp.pad(narrow, ((0, 0), (0, 128 - narrow.shape[1])))
    router_w = small_group_gather(narrow)
    ids_all = small_gather(expert_ids.T)
    column = [own_half] + shifts(own_half)
    cot_sides = plane_sides(after(out_grad, router_w, ids_all))
    qkv_half = qkv_cols // 2
    qkv_column = jnp.stack([part[:, :qkv_half] for part in column])
    out_column = jnp.stack([part[:, qkv_half:] for part in column])
    qkv_column, out_column = lax.optimization_barrier((qkv_column, out_column, *cot_sides))[:2]
    sliced = after(own_local, column[-1])
    gate_w, up_w, down_w = (
        lax.dynamic_index_in_dim(weight, sliced, 0, keepdims=False)
        for weight in (w_gate, w_up, w_down)
    )
    qkv_sides = plane_sides(qkv_column)
    gains = router_w[:, experts_all : experts_all + 2].T.astype(f32)
    gain_one, gain_two = gains[:1], gains[1:]
    qkv_corner = plane_corner(qkv_sides, (gate_w, up_w, down_w, gain_one, gain_two))
    out_sides = plane_sides(after(out_column, *qkv_sides))
    qkv_pieces = plane_pieces(qkv_column, qkv_sides, qkv_corner)
    cosine_tab, sine_tab = angles(length, HD)
    cosine_all = jnp.concatenate([cosine_tab, cosine_tab], axis=2)[:, 0]
    sine_all = jnp.concatenate([-sine_tab, sine_tab], axis=2)[:, 0]
    weight_lead = (2, depth, 2, 2, shard_rows)
    first_in, queries, keys_rot, values_b, attended, probs, qkv_w = run_kernel(
        attend_kernel,
        11,
        at,
        (tokens, gain_one, cosine_all, sine_all, *qkv_pieces),
        [
            ((length, model_width), bf16),
            ((length, q_cols), bf16),
            ((length, kv_cols), bf16),
            ((length, kv_cols), bf16),
            ((length, q_cols), bf16),
            ((HQ, length, length), bf16),
            (weight_lead + (qkv_half,), bf16),
        ],
        28,
        [
            pltpu.VMEM((HQ, length, length), bf16),
            pltpu.VMEM(weight_lead + (qkv_half,), bf16),
            pltpu.SemaphoreType.DMA((HK + 1,)),
        ],
        hbm_out=2,
    )
    out_sides = lax.optimization_barrier((*out_sides, attended))[:2]
    out_corner = plane_corner(out_sides)
    cot_corner = plane_corner(cot_sides)
    out_pieces = plane_pieces(out_column, out_sides, out_corner)
    cot_pieces = plane_pieces(out_grad, cot_sides, cot_corner)
    resid, second_in, output_w = run_kernel(
        project_kernel,
        4,
        at,
        (tokens, after(gain_two, cot_corner), attended, *out_pieces),
        [
            ((length, model_width), f32),
            ((length, model_width), bf16),
            (weight_lead + (out_half,), bf16),
        ],
        44,
        [pltpu.VMEM(weight_lead + (out_half,), bf16), pltpu.SemaphoreType.DMA],
        hbm_out=1,
    )
    qkv_w = qkv_w.reshape(HK, model_width, qkv_half)
    output_w = output_w.reshape(2, q_cols, out_half)

    expert = functools.partial(
        run_expert,
        at=at,
        ids=ids_all,
        router=router_w,
        weights=(gate_w, up_w, down_w),
        capacity=capacity,
    )
    second_sides = plane_sides(second_in)
    groups = ((0, 4), (1, 5, 2, 6), (3, 7))
    second_pieces = {0: second_in, 4: swap(second_in, "c")}

    def run_group(pieces):
        return expert(
            pieces,
            second=[second_pieces[piece] for piece in pieces],
            cot=[cot_pieces[piece] for piece in pieces],
        )

    stage_own = run_group(groups[0])
    second_sides = lax.optimization_barrier((*second_sides, stage_own[0]))[:2]
    for piece, block in zip((1, 2), second_sides):
        second_pieces[piece], second_pieces[piece + 4] = block, swap(block, "c")
    stage_sides = run_group(groups[1])
    second_corner = plane_corner(second_sides, later=(stage_sides[0],))
    second_pieces[3], second_pieces[7] = second_corner, swap(second_corner, "c")
    own_near, own_far = stage_own[6:]
    own_far = swap(own_far, "c")
    x_near, x_far, y_near, y_far = stage_sides[6:]
    back_x, back_y = over_core(x_near, x_far), over_core(y_near, y_far)
    first_x, first_y = early_sums(back_x, back_y)
    stage_corner = run_group(groups[2])
    corner = over_core(*stage_corner[6:])
    passed = corner_first(corner)
    stages = (stage_own, stage_sides, stage_corner)
    rows_in, rows_cot, gated, gate_back, up_back = ([stage[n] for stage in stages] for n in range(5))
    gates = stage_own[5]
    (down_part,) = row_sums(at, [after(rows_cot[0], corner)] + rows_cot[1:], gated)
    down_sum = scatter_sum(down_part, "z")
    passed = lax.optimization_barrier((*passed, down_part))[:2]
    last_y, last_x, *sent = corner_last(back_x, back_y, passed)
    gate_part, up_part = row_sums(
        at, [after(rows_in[0], *sent, first_x, first_y, own_far)] + rows_in[1:], gate_back, up_back
    )
    gate_sum, up_sum = scatter_sum(gate_part, "z"), scatter_sum(up_part, "z")
    own_near = after(own_near, gate_part)

    resid_grad, branch_grad, attended_grad, router_acc, gain_two_grad = run_kernel(
        branch_back_kernel,
        6,
        at,
        (
            own_near,
            own_far,
            first_x,
            first_y,
            last_y,
            last_x,
            resid,
            gain_two,
            second_in,
            gates,
            router_w,
            out_grad,
            output_w,
        ),
        [
            ((length, model_width), f32),
            ((length, model_width), bf16),
            ((length, q_cols), bf16),
            ((model_width, 128), f32),
            ((1, model_width), f32),
        ],
        56,
    )
    qkv_width, branch_width = qkv_cols // plane, model_width // plane
    dense_cols = qkv_width + branch_width
    (back_cols,) = run_kernel(
        attend_back_kernel,
        6,
        at,
        (
            attended_grad,
            probs,
            queries,
            keys_rot,
            values_b,
            cosine_all,
            sine_all,
            branch_grad,
        ),
        [((plane, length + 16, dense_cols), bf16)],
        56,
    )
    tokens_grad, gain_one_grad = run_kernel(
        first_back_kernel,
        5,
        at,
        (back_cols, qkv_w, tokens, gain_one, resid_grad),
        [((length, model_width), bf16), ((1, model_width), f32)],
        24,
    )

    both = jnp.concatenate(
        lax.optimization_barrier((attended, first_in, last_y, last_x))[:2], axis=0
    )
    both_sides = plane_sides(both)
    narrow_part = jnp.concatenate(
        [router_acc[:, :experts_all], gain_one_grad.T, gain_two_grad.T], axis=1
    )
    narrow_cols = -(-narrow_part.shape[1] // owners) * owners
    narrow_part = jnp.pad(narrow_part, ((0, 0), (0, narrow_cols - narrow_part.shape[1])))
    narrow_part = jnp.transpose(
        narrow_part.reshape(depth, 2, 2, shard_rows, owners, narrow_cols // owners),
        (1, 2, 4, 0, 3, 5),
    ).reshape(plane, depth, shard_rows * narrow_cols // owners)
    narrow_len = narrow_part.shape[2]
    narrow_rows = -(-narrow_len // dense_cols)
    each_rows = -(-narrow_rows // 4) * 4
    narrow_part = jnp.pad(
        narrow_part, ((0, 0), (0, 0), (0, each_rows * dense_cols - narrow_len))
    ).reshape(plane, depth * each_rows, dense_cols)
    back_cols = exchange(after(back_cols, down_sum, *both_sides), PLANE)
    narrow_part = exchange(narrow_part.astype(bf16), PLANE)
    both_corner = plane_corner(both_sides, (back_cols, gain_one_grad))
    both_pieces = plane_pieces(both, both_sides, both_corner)
    def placed(total):
        total = exchange(total, ("y", "c"))
        return total.reshape(local_count, shard_rows, hidden_width).astype(f32)

    down_grad = placed(down_sum)
    kept_rows = -(-narrow_rows // 16) * 16
    wide_rows = local_count * shard_rows
    dense_shape = (depth, wide_rows + kept_rows, dense_cols)
    dense_part = pl.pallas_call(
        dense_grad_kernel,
        out_shape=jax.ShapeDtypeStruct(dense_shape, bf16),
        in_specs=[SCALARS, WHOLE, WHOLE] + [IN_HBM] * 8,
        out_specs=WHOLE,
        scratch_shapes=[
            pltpu.VMEM((plane, 2 * length, model_width), bf16),
            pltpu.SemaphoreType.DMA((plane,)),
        ],
        cost_estimate=cost(8),
        compiler_params=pltpu.CompilerParams(vmem_limit_bytes=32 * 2**20),
    )(at, narrow_part, after(back_cols, up_sum, down_grad), *both_pieces)
    dense_sum = scatter_sum(dense_part.reshape(-1, dense_cols), "z")
    wide_sum = dense_sum[: local_count * shard_rows].reshape(2, 2, 1, shard_rows, dense_cols)
    wide_sum = jnp.broadcast_to(wide_sum, (2, 2, owners, shard_rows, dense_cols)).reshape(
        plane, shard_rows, dense_cols
    )
    narrow_sum = dense_sum[local_count * shard_rows :][:narrow_rows]
    narrow_sum = jnp.broadcast_to(narrow_sum[None], (plane, narrow_rows, dense_cols))
    pad_rows = -(shard_rows + narrow_rows) % 16
    padding = jnp.zeros((plane, pad_rows, dense_cols), bf16)
    dense_sum = exchange(jnp.concatenate([wide_sum, narrow_sum, padding], axis=1), PLANE)
    query_grad, key_grad, value_grad, output_grad = run_kernel(
        finish_kernel,
        2,
        at,
        (dense_sum,),
        [
            ((shard_rows, q_cols), f32),
            ((shard_rows, kv_cols), f32),
            ((shard_rows, kv_cols), f32),
            ((shard_rows, model_width), f32),
        ],
    )
    narrow_sum = dense_sum[:, shard_rows : shard_rows + narrow_rows].reshape(
        2, 2, owners, narrow_rows * dense_cols
    )
    narrow_sum = narrow_sum[y, c, :, :narrow_len].reshape(owners, shard_rows, -1)
    narrow_sum = jnp.moveaxis(narrow_sum, 0, 1).reshape(shard_rows, narrow_cols).astype(f32)

    shares = run_kernel(
        functools.partial(mixture_kernel, capacity, groups),
        10,
        at,
        (ids_all, after(gated[0], both_corner), *gated[1:], down_w),
        [((length, model_width), bf16)] * plane,
        56,
    )
    mixed = [over_core(near, far) for near, far in zip(shares[:4], shares[4:])]
    early = early_sums(mixed[1], mixed[2])
    last = corner_last(mixed[1], mixed[2], corner_first(mixed[3]))[:2]
    mixture = jnp.concatenate(
        [left.astype(f32) + right.astype(f32) for left, right in zip(early, last)], axis=0
    )
    block_out = (resid + (mixture + mixed[0].astype(f32))).astype(bf16)

    return (
        block_out,
        tokens_grad,
        narrow_sum[:, experts_all],
        query_grad,
        key_grad,
        value_grad,
        output_grad,
        narrow_sum[:, experts_all + 1],
        narrow_sum[:, :experts_all],
        placed(after(gate_sum, dense_part)),
        placed(after(up_sum, dense_part)),
        jnp.swapaxes(down_grad, 1, 2),
    )


def solution(mesh):
    groups, owners = mesh.shape["dp"], mesh.shape["expert"]
    grid = jax.sharding.Mesh(
        mesh.devices.reshape(groups // 4, 2, 2, owners), ("z", "y", "c", "x")
    )
    rows = P(("z", "y", "c", "x"), None)
    shard, shard_rows = P(GROUP), P(GROUP, None)
    expert = P("x", None, None)
    return jax.shard_map(
        local_pairs if owners == 2 else local_wide,
        mesh=grid,
        in_specs=(
            rows,
            shard,
            shard_rows,
            shard_rows,
            shard_rows,
            shard_rows,
            shard,
            shard_rows,
            expert,
            expert,
            expert,
            rows,
            P(("z", "y", "c", "x")),
            rows,
        ),
        out_specs=(
            rows,
            rows,
            shard,
            shard_rows,
            shard_rows,
            shard_rows,
            shard_rows,
            shard,
            shard_rows,
            P("x", GROUP, None),
            P("x", GROUP, None),
            P("x", None, GROUP),
        ),
        check_vma=False,
    )
```

profile of v0, /device:TPU:0, one launch (start us, length us, event | category | flops | bytes accessed | tf_op | source)
XLA Modules:
  0.0 463.2 jit_solution(10077391275691633814)
XLA Ops:
  8.1 5.1 %collective-permute-start = (bf16[96,128]{1,0:T(8,128)(2,1)S(1)}, bf16[96,128]{1,0:T(8,128)(2,1)S(1)}, u32[]{:S(2)}, u32[]{:S(2)}) collective-permute-start(bf16[96,128]{1,0:T(8,128)(2,1)S(1)} %pad.9), channel_id=1, source_target_pairs={{0,24},{8,0},{16,8},{24,16},{1,25},{9,1},{17,9},{25,17},{2,26},{10... | collective-permute-start | bytes 73736 | tf_op jit(solution)/shard_map/ppermute | solution.py:317
  18.2 2.8 collective-permute-start.14
  26.1 2.7 collective-permute-done.3
  33.0 18.3 %collective-permute-done.13 = bf16[96,1792]{1,0:T(8,128)(2,1)} collective-permute-done((bf16[96,1792]{1,0:T(8,128)(2,1)}, bf16[96,1792]{1,0:T(8,128)(2,1)}, u32[]{:S(2)}, u32[]{:S(2)}) %collective-permute-start.13) | collective-permute-done | bytes 344096 | tf_op jit(solution)/shard_map/ppermute | solution.py:317
  61.7 4.1 dynamic-slice_bitcast_fusion.1.refs_5_.refs_9_
  65.8 3.2 dynamic-slice_bitcast_fusion.2.refs_4_.refs_8_
  69.0 6.7 %collective-permute-done.16.refs_2_ = bf16[4,96,1024]{2,1,0:T(8,128)(2,1)} collective-permute-done((bf16[4,96,1024]{2,1,0:T(8,128)(2,1)S(1)}, bf16[4,96,1024]{2,1,0:T(8,128)(2,1)}, u32[]{:S(2)}, u32[]{:S(2)}) %collective-permute-start.16) | collective-permute-done | bytes 786464 | tf_op jit(solution)/shard_map/ppermute | solution.py:311
  80.4 5.3 %collective-permute-done.17 = bf16[2,96,1024]{2,1,0:T(8,128)(2,1)S(1)} collective-permute-done((bf16[2,96,1024]{2,1,0:T(8,128)(2,1)S(1)}, bf16[2,96,1024]{2,1,0:T(8,128)(2,1)S(1)}, u32[]{:S(2)}, u32[]{:S(2)}) %collective-permute-start.17) | collective-permute-done | bytes 393248 | tf_op jit(solution)/shard_map/ppermute | solution.py:311
  95.7 9.0 %shard_map.229 = (bf16[256,1536]{1,0:T(8,128)(2,1)S(1)}, bf16[256,1536]{1,0:T(8,128)(2,1)S(1)}, bf16[256,256]{1,0:T(8,128)(2,1)S(1)}, bf16[256,256]{1,0:T(8,128)...) custom-call(s32[7]{0:T(128)S(1)} %copy-done.39, ...), custom_call_target="tpu_custom_call" | custom-call | flops 11000000512 | bytes 11000000 | tf_op jit(solution)/shard_map/pallas_call | solution.py:400
  104.7 2.7 copy-done.51
  113.0 5.7 %collective-permute-done.25 = bf16[2,96,768]{2,1,0:T(8,128)(2,1)S(1)} collective-permute-done((bf16[2,96,768]{2,1,0:T(8,128)(2,1)S(1)}, bf16[2,96,768]{2,1,0:T(8,128)(2,1)S(1)}, u32[]{:S(2)}, u32[]{:S(2)}) %collective-permute-start.25) | collective-permute-done | bytes 294944 | tf_op jit(solution)/shard_map/ppermute | solution.py:311
  119.3 6.7 %collective-permute-done.10 = bf16[128,1536]{1,0:T(8,128)(2,1)S(1)} collective-permute-done((bf16[128,1536]{1,0:T(8,128)(2,1)S(1)}, bf16[128,1536]{1,0:T(8,128)(2,1)S(1)}, u32[]{:S(2)}, u32[]{:S(2)}) %collective-permute-start.10) | collective-permute-done | bytes 393248 | tf_op jit(solution)/shard_map/ppermute | solution.py:311
  128.2 4.1 shard_map.230
  136.3 9.5 %shard_map.231 = (bf16[384,1536]{1,0:T(8,128)(2,1)S(1)}, bf16[384,1536]{1,0:T(8,128)(2,1)S(1)}, bf16[384,768]{1,0:T(8,128)(2,1)S(1)}, bf16[384,768]{1,0:T(8,128)...) custom-call(s32[7]{0:T(128)S(1)} %copy-done.40, ...), custom_call_target="tpu_custom_call" | custom-call | flops 8000000000 | bytes 8000000 | tf_op jit(solution)/shard_map/pallas_call | solution.py:400
  149.2 4.4 collective-permute-done.33.refs_0_
  156.9 2.2 collective-permute-done.36.refs_3_
  159.2 16.2 %shard_map.232 = (bf16[768,1536]{1,0:T(8,128)(2,1)S(1)}, bf16[768,1536]{1,0:T(8,128)(2,1)S(1)}, bf16[768,768]{1,0:T(8,128)(2,1)S(1)}, bf16[768,768]{1,0:T(8,128)...) custom-call(s32[7]{0:T(128)S(1)} %copy-done.40, ...), custom_call_target="tpu_custom_call" | custom-call | flops 16000000000 | bytes 16000000 | tf_op jit(solution)/shard_map/pallas_call | solution.py:400
  181.0 2.2 collective-permute-done.42.refs_1_
  183.2 9.8 %shard_map.233 = (bf16[384,1536]{1,0:T(8,128)(2,1)S(1)}, bf16[384,1536]{1,0:T(8,128)(2,1)S(1)}, bf16[384,768]{1,0:T(8,128)(2,1)S(1)}, bf16[384,768]{1,0:T(8,128)...) custom-call(s32[7]{0:T(128)S(1)} %copy-done.40, ...), custom_call_target="tpu_custom_call" | custom-call | flops 8000000000 | bytes 8000000 | tf_op jit(solution)/shard_map/pallas_call | solution.py:400
  193.9 2.2 collective-permute-done.44
  197.3 5.9 %shard_map.234 = bf16[1536,768]{1,0:T(8,128)(2,1)} custom-call(s32[7]{0:T(128)S(1)} %copy-done.40, bf16[384,1536]{1,0:T(8,128)(2,1)S(1)} %get-tuple-element.147.refs_0_, bf16[768,1536]{1,0:T(8,128)(2,1)S(1)} %get-tuple-element.148.refs_1_, bf16[384,1536]{1,0:T(8,128)(2,1)S(1)} %get-tuple-element.149.refs_2_, ...), custom_call_target="tpu_custom_call" | custom-call | flops 4000000000 | bytes 4000000 | tf_op jit(solution)/shard_map/pallas_call | solution.py:400
  211.0 16.5 %collective-permute-done.45 = bf16[128,1664]{1,0:T(8,128)(2,1)S(1)} collective-permute-done((bf16[128,1664]{1,0:T(8,128)(2,1)S(1)}, bf16[128,1664]{1,0:T(8,128)(2,1)S(1)}, u32[]{:S(2)}, u32[]{:S(2)}) %collective-permute-start.45) | collective-permute-done | bytes 426016 | tf_op jit(solution)/shard_map/ppermute | solution.py:311
  229.8 12.7 %shard_map.235 = (bf16[1536,768]{1,0:T(8,128)(2,1)}, bf16[1536,768]{1,0:T(8,128)(2,1)}) custom-call(s32[7]{0:T(128)} %stack.76.at, bf16[384,1536]{1,0:T(8,128)(2,1)} %copy-done.60, bf16[768,1536]{1,0:T(8,128)(2,1)} %copy-done.59, bf16[384,1536]{1,0:T(8,128)(2,1)} %copy-done.61, bf16[384,768]{1,0:T(8,128)(2,1)} %copy-done.65, bf16[768,768]{1,0:T(8,128)(2,1)} %copy-done.63, ...), custom_call_target="tpu_custom_call" | custom-call | flops 8000000000 | bytes 8000000 | tf_op jit(solution)/shard_map/pallas_call | solution.py:400
  244.2 9.1 %collective-permute-done.49.last_x = bf16[128,1664]{1,0:T(8,128)(2,1)S(1)} collective-permute-done((bf16[128,1664]{1,0:T(8,128)(2,1)S(1)}, bf16[128,1664]{1,0:T(8,128)(2,1)S(1)}, u32[]{:S(2)}, u32[]{:S(2)}) %collective-permute-start.49) | collective-permute-done | bytes 426016 | tf_op jit(solution)/shard_map/ppermute | solution.py:311
  257.5 8.8 %shard_map.236 = (f32[256,1536]{1,0:T(8,128)}, bf16[256,1536]{1,0:T(8,128)(2,1)}, bf16[256,1536]{1,0:T(8,128)(2,1)}, f32[1536,128]{1,0:T(8,128)}, f32[1,1536]{1,0:T(1,128)}) custom-call(s32[7]{0:T(128)} %stack.76.at, bf16[256,1664]{1,0:T(8,128)(2,1)} %copy-done.57, bf16[256,1664]{1,0:T(8,128)(2,1)} %copy-done.84, bf16[128,1664]{1,0:T(8,128)(2,1)} %copy-done.85, ...), custom_call_target="tpu_custom_call" | custom-call | flops 6000000000 | bytes 6000000 | tf_op jit(solution)/shard_map/pallas_call | solution.py:400
  266.3 8.4 %shard_map.237.back = bf16[8,272,448]{2,1,0:T(8,128)(2,1)} custom-call(s32[7]{0:T(128)} %stack.76.at, bf16[256,1536]{1,0:T(8,128)(2,1)} %get-tuple-element.172.attended, bf16[12,256,256]{2,1,0:T(8,128)(2,1)} %copy-done.58, bf16[256,1536]{1,0:T(8,128)(2,1)} %copy-done.62, bf16[256,256]{1,0:T(8,128)(2,1)} %copy-done.70, bf16[256,256]{1,0:T(8,128)(2,1)} %copy-done.71, ...), custom_call_target="tpu_custom_call" | custom-call | flops 6000000000 | bytes 6000000 | tf_op jit(solution)/shard_map/pallas_call | solution.py:400
  274.7 15.9 %collective-permute-done.50.refs_2_ = bf16[512,1536]{1,0:T(8,128)(2,1)S(1)} collective-permute-done((bf16[512,1536]{1,0:T(8,128)(2,1)}, bf16[512,1536]{1,0:T(8,128)(2,1)S(1)}, u32[]{:S(2)}, u32[]{:S(2)}) %collective-permute-start.50) | collective-permute-done | bytes 1572896 | tf_op jit(solution)/shard_map/ppermute | solution.py:311
  292.3 3.6 all-to-all-start
  298.7 2.8 copy-done.52
  303.0 3.7 shard_map.238
  308.4 15.0 %all-to-all-done.back = bf16[8,272,448]{2,1,0:T(8,128)(2,1)S(1)} async-done(((bf16[8,272,448]{2,1,0:T(8,128)(2,1)}), bf16[8,272,448]{2,1,0:T(8,128)(2,1)S(1)}, u32[]{:S(2)}, u32[]{:S(2)}) %all-to-all-start) | async-done | bytes 1949728 | tf_op jit(solution)/shard_map/all_to_all | solution.py:61
  325.7 4.2 all-to-all-start.2
  329.8 13.1 %collective-permute-done.55 = bf16[256,1536]{1,0:T(8,128)(2,1)} collective-permute-done((bf16[256,1536]{1,0:T(8,128)(2,1)}, bf16[256,1536]{1,0:T(8,128)(2,1)}, u32[]{:S(2)}, u32[]{:S(2)}) %collective-permute-start.55) | collective-permute-done | bytes 786464 | tf_op jit(solution)/shard_map/ppermute | solution.py:311
  345.0 2.1 constant_dynamic-update-slice_fusion.19
  347.1 2.2 constant_dynamic-update-slice_fusion.18.refs_3_
  349.3 9.4 %shard_map.239 = (bf16[256,1536]{1,0:T(8,128)(2,1)}, bf16[256,1536]{1,0:T(8,128)(2,1)}, bf16[256,1536]{1,0:T(8,128)(2,1)}, bf16[256,1536]{1,0:T(8,128)(2,1)}, bf...) custom-call(s32[7]{0:T(128)} %stack.76.at, ...), custom_call_target="tpu_custom_call" | custom-call | flops 10000000000 | bytes 10000000 | tf_op jit(solution)/shard_map/pallas_call | solution.py:400
  361.8 3.4 all-to-all-start.1
  365.5 2.2 convert_bitcast_fusion
  373.1 6.9 %shard_map.240 = bf16[4,400,448]{2,1,0:T(8,128)(2,1)S(1)} custom-call(s32[7]{0:T(128)S(1)} %copy-done.42, bf16[8,16,448]{2,1,0:T(8,128)(2,1)S(1)} %all-to-all-done.1.narrow, bf16[8,272,448]{2,1,0:T(8,128)(2,1)S(1)} %all-to-all-done.back, bf16[512,1536]{1,0:T(8,128)(2,1)} %constant_dynamic-update-slice_fusion.16.refs_0_, bf16[512,1536]{1,0:T(8,128)(2,1)S(1)} %copy-done.22, ...), custom_call_target="tpu_custom_call" | custom-call | flops 8000000000 | bytes 8000000 | tf_op jit(solution)/shard_map/pallas_call | solution.py:1007
  389.8 4.2 collective-permute-done.61
  395.9 3.5 all-to-all-start.5
  399.3 9.1 %collective-permute-done.64 = bf16[128,1536]{1,0:T(8,128)(2,1)} collective-permute-done((bf16[128,1536]{1,0:T(8,128)(2,1)}, bf16[128,1536]{1,0:T(8,128)(2,1)}, u32[]{:S(2)}, u32[]{:S(2)}) %collective-permute-start.64) | collective-permute-done | bytes 393248 | tf_op jit(solution)/shard_map/ppermute | solution.py:311
  411.9 10.3 %all-to-all-done.5 = bf16[4,96,768]{2,1,0:T(8,128)(2,1)S(1)} async-done(((bf16[4,96,768]{2,1,0:T(8,128)(2,1)}), bf16[4,96,768]{2,1,0:T(8,128)(2,1)S(1)}, u32[]{:S(2)}, u32[]{:S(2)}) %all-to-all-start.5) | async-done | bytes 589856 | tf_op jit(solution)/shard_map/all_to_all | solution.py:61
  422.2 3.5 all-to-all-start.4
  430.0 5.2 %all-to-all-done.4 = bf16[4,96,768]{2,1,0:T(8,128)(2,1)S(1)} async-done(((bf16[4,96,768]{2,1,0:T(8,128)(2,1)}), bf16[4,96,768]{2,1,0:T(8,128)(2,1)S(1)}, u32[]{:S(2)}, u32[]{:S(2)}) %all-to-all-start.4) | async-done | bytes 589856 | tf_op jit(solution)/shard_map/all_to_all | solution.py:61
  436.1 3.6 all-to-all-start.3
  441.0 2.6 fusion.1
  445.9 7.2 %all-to-all-done.3.sums = bf16[8,112,448]{2,1,0:T(8,128)(2,1)S(1)} async-done(((bf16[8,112,448]{2,1,0:T(8,128)(2,1)}), bf16[8,112,448]{2,1,0:T(8,128)(2,1)S(1)}, u32[]{:S(2)}, u32[]{:S(2)}) %all-to-all-start.3) | async-done | bytes 802848 | tf_op jit(solution)/shard_map/all_to_all | solution.py:61
  (422 shorter events, 129.2 us)
Async XLA Ops:
  7.2 283.6 %reduce-scatter.5.cloned.1.call-start = ((), (), s32[]{:S(2)}) async-start(), calls=%async_computation.10 | async-start | bytes 2949120 | tf_op jit(solution)/shard_map/reduce_scatter | solution.py:65
  8.1 14.2 %collective-permute-start = (bf16[96,128]{1,0:T(8,128)(2,1)S(1)}, bf16[96,128]{1,0:T(8,128)(2,1)S(1)}, u32[]{:S(2)}, u32[]{:S(2)}) collective-permute-start(bf16[96,128]{1,0:T(8,128)(2,1)S(1)} %pad.9), channel_id=1, source_target_pairs={{0,24},{8,0},{16,8},{24,16},{1,25},{9,1},{17,9},{25,17},{2,26},{10... | collective-permute-start | bytes 73736 | tf_op jit(solution)/shard_map/ppermute | solution.py:317
  21.1 30.2 %collective-permute-start.13 = (bf16[96,1792]{1,0:T(8,128)(2,1)}, bf16[96,1792]{1,0:T(8,128)(2,1)}, u32[]{:S(2)}, u32[]{:S(2)}) collective-permute-start(bf16[96,1792]{1,0:T(8,128)(2,1)} %pad_maximum_fusion.3), channel_id=1, source_target_pairs={{0,16},{8,24},{16,0},{24,8},{1,17},{9,25},{17,1},{25,9},{2,18},{10... | collective-permute-start | bytes 1032200 | tf_op jit(solution)/shard_map/ppermute | solution.py:317
  22.3 29.9 %collective-permute-start.12 = (bf16[96,1792]{1,0:T(8,128)(2,1)}, bf16[96,1792]{1,0:T(8,128)(2,1)}, u32[]{:S(2)}, u32[]{:S(2)}) collective-permute-start(bf16[96,1792]{1,0:T(8,128)(2,1)} %pad_maximum_fusion.3), channel_id=1, source_target_pairs={{0,8},{8,16},{16,24},{24,0},{1,9},{9,17},{17,25},{25,1},{2,10},{10... | collective-permute-start | bytes 1032200 | tf_op jit(solution)/shard_map/ppermute | solution.py:317
  30.5 26.5 %collective-permute-start.8 = (bf16[256,1536]{1,0:T(8,128)(2,1)}, bf16[256,1536]{1,0:T(8,128)(2,1)S(1)}, u32[]{:S(2)}, u32[]{:S(2)}) collective-permute-start(bf16[256,1536]{1,0:T(8,128)(2,1)} %cot.1), channel_id=1, source_target_pairs={{0,4},{4,0},{1,5},{5,1},{2,6},{6,2},{3,7},{7,3},{8,12},{12,8},{9,1... | collective-permute-start | bytes 2359304 | tf_op jit(solution)/shard_map/ppermute | solution.py:311
  31.1 25.9 %collective-permute-start.9 = (bf16[256,1536]{1,0:T(8,128)(2,1)}, bf16[256,1536]{1,0:T(8,128)(2,1)S(1)}, u32[]{:S(2)}, u32[]{:S(2)}) collective-permute-start(bf16[256,1536]{1,0:T(8,128)(2,1)} %cot.1), channel_id=1, source_target_pairs={{0,1},{1,0},{2,3},{3,2},{4,5},{5,4},{6,7},{7,6},{8,9},{9,8},{10,11... | collective-permute-start | bytes 2359304 | tf_op jit(solution)/shard_map/ppermute | solution.py:311
  57.0 19.7 %collective-permute-start.15 = (bf16[4,96,1024]{2,1,0:T(8,128)(2,1)S(1)}, bf16[4,96,1024]{2,1,0:T(8,128)(2,1)}, u32[]{:S(2)}, u32[]{:S(2)}) collective-permute-start(bf16[4,96,1024]{2,1,0:T(8,128)(2,1)S(1)} %pad_maximum_fusion.refs_0_), channel_id=1, source_target_pairs={{0,1},{1,0},{2,3},{3,2},{4,5},{5,4},{6,7},{7,6},{8,9},{9,8},{10,11... | collective-permute-start | bytes 2359304 | tf_op jit(solution)/shard_map/ppermute | solution.py:311
  58.4 17.3 %collective-permute-start.16 = (bf16[4,96,1024]{2,1,0:T(8,128)(2,1)S(1)}, bf16[4,96,1024]{2,1,0:T(8,128)(2,1)}, u32[]{:S(2)}, u32[]{:S(2)}) collective-permute-start(bf16[4,96,1024]{2,1,0:T(8,128)(2,1)S(1)} %pad_maximum_fusion.refs_0_), channel_id=1, source_target_pairs={{0,4},{4,0},{1,5},{5,1},{2,6},{6,2},{3,7},{7,3},{8,12},{12,8},{9,1... | collective-permute-start | bytes 2359304 | tf_op jit(solution)/shard_map/ppermute | solution.py:311
  89.7 18.9 %collective-permute-start.23 = (bf16[4,96,768]{2,1,0:T(8,128)(2,1)}, bf16[4,96,768]{2,1,0:T(8,128)(2,1)S(1)}, u32[]{:S(2)}, u32[]{:S(2)}) collective-permute-start(bf16[4,96,768]{2,1,0:T(8,128)(2,1)} %pad_maximum_fusion.1.refs_0_), channel_id=1, source_target_pairs={{0,1},{1,0},{2,3},{3,2},{4,5},{5,4},{6,7},{7,6},{8,9},{9,8},{10,11... | collective-permute-start | bytes 1769480 | tf_op jit(solution)/shard_map/ppermute | solution.py:311
  91.2 17.4 %collective-permute-start.24 = (bf16[4,96,768]{2,1,0:T(8,128)(2,1)}, bf16[4,96,768]{2,1,0:T(8,128)(2,1)S(1)}, u32[]{:S(2)}, u32[]{:S(2)}) collective-permute-start(bf16[4,96,768]{2,1,0:T(8,128)(2,1)} %pad_maximum_fusion.1.refs_0_), channel_id=1, source_target_pairs={{0,4},{4,0},{1,5},{5,1},{2,6},{6,2},{3,7},{7,3},{8,12},{12,8},{9,1... | collective-permute-start | bytes 1769480 | tf_op jit(solution)/shard_map/ppermute | solution.py:311
  110.3 15.7 %collective-permute-start.10 = (bf16[128,1536]{1,0:T(8,128)(2,1)S(1)}, bf16[128,1536]{1,0:T(8,128)(2,1)S(1)}, u32[]{:S(2)}, u32[]{:S(2)}) collective-permute-start(bf16[128,1536]{1,0:T(8,128)(2,1)S(1)} %slice.159), channel_id=1, source_target_pairs={{0,1},{1,0},{2,3},{3,2},{4,5},{5,4},{6,7},{7,6},{8,9},{9,8},{10,11... | collective-permute-start | bytes 1179656 | tf_op jit(solution)/shard_map/ppermute | solution.py:311
  111.4 14.9 %collective-permute-start.11 = (bf16[128,1536]{1,0:T(8,128)(2,1)S(1)}, bf16[128,1536]{1,0:T(8,128)(2,1)S(1)}, u32[]{:S(2)}, u32[]{:S(2)}) collective-permute-start(bf16[128,1536]{1,0:T(8,128)(2,1)S(1)} %slice.160), channel_id=1, source_target_pairs={{0,4},{4,0},{1,5},{5,1},{2,6},{6,2},{3,7},{7,3},{8,12},{12,8},{9,1... | collective-permute-start | bytes 1179656 | tf_op jit(solution)/shard_map/ppermute | solution.py:311
  113.0 15.2 %collective-permute-start.27 = (bf16[4,96,768]{2,1,0:T(8,128)(2,1)S(1)}, bf16[4,96,768]{2,1,0:T(8,128)(2,1)S(1)}, u32[]{:S(2)}, u32[]{:S(2)}) collective-permute-start(bf16[4,96,768]{2,1,0:T(8,128)(2,1)S(1)} %copy-done.16), channel_id=1, source_target_pairs={{0,2},{2,0},{1,3},{3,1},{4,6},{6,4},{5,7},{7,5},{8,10},{10,8},{9,1... | collective-permute-start | bytes 1769480 | tf_op jit(solution)/shard_map/ppermute | solution.py:311
  133.8 19.9 %collective-permute-start.33 = (bf16[256,1536]{1,0:T(8,128)(2,1)}, bf16[256,1536]{1,0:T(8,128)(2,1)S(1)}, u32[]{:S(2)}, u32[]{:S(2)}) collective-permute-start(bf16[256,1536]{1,0:T(8,128)(2,1)} %get-tuple-element.131.refs_0_.second), channel_id=1, source_target_pairs={{0,1},{1,0},{2,3},{3,2},{4,5},{5,4},{6,7},{7,6},{8,9},{9,8},{10,11... | collective-permute-start | bytes 2359304 | tf_op jit(solution)/shard_map/ppermute | solution.py:311
  135.3 19.4 %collective-permute-start.34 = (bf16[256,1536]{1,0:T(8,128)(2,1)}, bf16[256,1536]{1,0:T(8,128)(2,1)S(1)}, u32[]{:S(2)}, u32[]{:S(2)}) collective-permute-start(bf16[256,1536]{1,0:T(8,128)(2,1)} %get-tuple-element.131.refs_0_.second), channel_id=1, source_target_pairs={{0,4},{4,0},{1,5},{5,1},{2,6},{6,2},{3,7},{7,3},{8,12},{12,8},{9,1... | collective-permute-start | bytes 2359304 | tf_op jit(solution)/shard_map/ppermute | solution.py:311
  135.8 19.5 %collective-permute-start.37 = (bf16[256,1536]{1,0:T(8,128)(2,1)S(1)}, bf16[256,1536]{1,0:T(8,128)(2,1)S(1)}, u32[]{:S(2)}, u32[]{:S(2)}) collective-permute-start(bf16[256,1536]{1,0:T(8,128)(2,1)S(1)} %copy-done.28), channel_id=1, source_target_pairs={{0,2},{2,0},{1,3},{3,1},{4,6},{6,4},{5,7},{7,5},{8,10},{10,8},{9,1... | collective-permute-start | bytes 2359304 | tf_op jit(solution)/shard_map/ppermute | solution.py:311
  135.8 20.3 %collective-permute-start.38 = (bf16[256,1536]{1,0:T(8,128)(2,1)S(1)}, bf16[256,1536]{1,0:T(8,128)(2,1)S(1)}, u32[]{:S(2)}, u32[]{:S(2)}) collective-permute-start(bf16[256,1536]{1,0:T(8,128)(2,1)S(1)} %copy-done.25), channel_id=1, source_target_pairs={{0,2},{2,0},{1,3},{3,1},{4,6},{6,4},{5,7},{7,5},{8,10},{10,8},{9,1... | collective-permute-start | bytes 2359304 | tf_op jit(solution)/shard_map/ppermute | solution.py:311
  155.1 25.8 %collective-permute-start.43 = (bf16[256,1536]{1,0:T(8,128)(2,1)}, bf16[256,1536]{1,0:T(8,128)(2,1)S(1)}, u32[]{:S(2)}, u32[]{:S(2)}) collective-permute-start(bf16[256,1536]{1,0:T(8,128)(2,1)} %constant_dynamic-update-slice_fusion.8.refs_2_), channel_id=1, source_target_pairs={{0,2},{2,0},{1,3},{3,1},{4,6},{6,4},{5,7},{7,5},{8,10},{10,8},{9,1... | collective-permute-start | bytes 2359304 | tf_op jit(solution)/shard_map/ppermute | solution.py:311
  155.2 25.5 %collective-permute-start.40 = (bf16[128,1536]{1,0:T(8,128)(2,1)S(1)}, bf16[128,1536]{1,0:T(8,128)(2,1)S(1)}, u32[]{:S(2)}, u32[]{:S(2)}) collective-permute-start(bf16[128,1536]{1,0:T(8,128)(2,1)S(1)} %slice.135), channel_id=1, source_target_pairs={{0,1},{1,0},{2,3},{3,2},{4,5},{5,4},{6,7},{7,6},{8,9},{9,8},{10,11... | collective-permute-start | bytes 1179656 | tf_op jit(solution)/shard_map/ppermute | solution.py:311
  156.1 24.6 %collective-permute-start.41 = (bf16[128,1536]{1,0:T(8,128)(2,1)S(1)}, bf16[128,1536]{1,0:T(8,128)(2,1)S(1)}, u32[]{:S(2)}, u32[]{:S(2)}) collective-permute-start(bf16[128,1536]{1,0:T(8,128)(2,1)S(1)} %slice.136), channel_id=1, source_target_pairs={{0,4},{4,0},{1,5},{5,1},{2,6},{6,2},{3,7},{7,3},{8,12},{12,8},{9,1... | collective-permute-start | bytes 1179656 | tf_op jit(solution)/shard_map/ppermute | solution.py:311
  203.2 164.5 %reduce-scatter.7.cloned.1.call-start = ((), (), s32[]{:S(2)}) async-start(), calls=%async_computation.11 | async-start | bytes 2949120 | tf_op jit(solution)/shard_map/reduce_scatter | solution.py:65
  204.4 23.3 %collective-permute-start.54 = (bf16[256,1664]{1,0:T(8,128)(2,1)S(1)}, bf16[256,1664]{1,0:T(8,128)(2,1)S(1)}, u32[]{:S(2)}, u32[]{:S(2)}) collective-permute-start(bf16[256,1664]{1,0:T(8,128)(2,1)S(1)} %copy-done.44), channel_id=1, source_target_pairs={{0,2},{2,0},{1,3},{3,1},{4,6},{6,4},{5,7},{7,5},{8,10},{10,8},{9,1... | collective-permute-start | bytes 2555912 | tf_op jit(solution)/shard_map/ppermute | solution.py:311
  206.4 21.3 %collective-permute-start.52 = (bf16[128,1664]{1,0:T(8,128)(2,1)S(1)}, bf16[128,1664]{1,0:T(8,128)(2,1)S(1)}, u32[]{:S(2)}, u32[]{:S(2)}) collective-permute-start(bf16[128,1664]{1,0:T(8,128)(2,1)S(1)} %slice.176), channel_id=1, source_target_pairs={{0,1},{1,0},{2,3},{3,2},{4,5},{5,4},{6,7},{7,6},{8,9},{9,8},{10,11... | collective-permute-start | bytes 1277960 | tf_op jit(solution)/shard_map/ppermute | solution.py:311
  207.3 20.1 %collective-permute-start.45 = (bf16[128,1664]{1,0:T(8,128)(2,1)S(1)}, bf16[128,1664]{1,0:T(8,128)(2,1)S(1)}, u32[]{:S(2)}, u32[]{:S(2)}) collective-permute-start(bf16[128,1664]{1,0:T(8,128)(2,1)S(1)} %get-tuple-element.207), channel_id=1, source_target_pairs={{0,1},{1,0},{2,3},{3,2},{4,5},{5,4},{6,7},{7,6},{8,9},{9,8},{10,11... | collective-permute-start | bytes 1277960 | tf_op jit(solution)/shard_map/ppermute | solution.py:311
  208.6 18.8 %collective-permute-start.46 = (bf16[128,1664]{1,0:T(8,128)(2,1)S(1)}, bf16[128,1664]{1,0:T(8,128)(2,1)S(1)}, u32[]{:S(2)}, u32[]{:S(2)}) collective-permute-start(bf16[128,1664]{1,0:T(8,128)(2,1)S(1)} %get-tuple-element.206), channel_id=1, source_target_pairs={{0,4},{4,0},{1,5},{5,1},{2,6},{6,2},{3,7},{7,3},{8,12},{12,8},{9,1... | collective-permute-start | bytes 1277960 | tf_op jit(solution)/shard_map/ppermute | solution.py:311
  209.4 19.7 %collective-permute-start.53 = (bf16[128,1664]{1,0:T(8,128)(2,1)S(1)}, bf16[128,1664]{1,0:T(8,128)(2,1)S(1)}, u32[]{:S(2)}, u32[]{:S(2)}) collective-permute-start(bf16[128,1664]{1,0:T(8,128)(2,1)S(1)} %slice.177), channel_id=1, source_target_pairs={{0,4},{4,0},{1,5},{5,1},{2,6},{6,2},{3,7},{7,3},{8,12},{12,8},{9,1... | collective-permute-start | bytes 1277960 | tf_op jit(solution)/shard_map/ppermute | solution.py:311
  256.2 34.4 %collective-permute-start.50 = (bf16[512,1536]{1,0:T(8,128)(2,1)}, bf16[512,1536]{1,0:T(8,128)(2,1)S(1)}, u32[]{:S(2)}, u32[]{:S(2)}) collective-permute-start(bf16[512,1536]{1,0:T(8,128)(2,1)} %constant_dynamic-update-slice_fusion.16.refs_0_), channel_id=1, source_target_pairs={{0,4},{4,0},{1,5},{5,1},{2,6},{6,2},{3,7},{7,3},{8,12},{12,8},{9,1... | collective-permute-start | bytes 4718600 | tf_op jit(solution)/shard_map/ppermute | solution.py:311
  256.7 34.1 %collective-permute-start.51 = (bf16[512,1536]{1,0:T(8,128)(2,1)}, bf16[512,1536]{1,0:T(8,128)(2,1)S(1)}, u32[]{:S(2)}, u32[]{:S(2)}) collective-permute-start(bf16[512,1536]{1,0:T(8,128)(2,1)} %constant_dynamic-update-slice_fusion.16.refs_0_), channel_id=1, source_target_pairs={{0,1},{1,0},{2,3},{3,2},{4,5},{5,4},{6,7},{7,6},{8,9},{9,8},{10,11... | collective-permute-start | bytes 4718600 | tf_op jit(solution)/shard_map/ppermute | solution.py:311
  292.3 31.1 %all-to-all-start = ((bf16[8,272,448]{2,1,0:T(8,128)(2,1)}), bf16[8,272,448]{2,1,0:T(8,128)(2,1)S(1)}, u32[]{:S(2)}, u32[]{:S(2)}) async-start(bf16[8,272,448]{2,1,0:T(8,128)(2,1)} %shard_map.237.back), calls=%async_computation.1 | async-start | bytes 4456448 | tf_op jit(solution)/shard_map/all_to_all | solution.py:61
  295.9 116.0 %reduce-scatter.11.cloned.1.call-start = ((), (), s32[]{:S(2)}) async-start(), calls=%async_computation.13 | async-start | bytes 2949120 | tf_op jit(solution)/shard_map/reduce_scatter | solution.py:65
  323.4 19.5 %collective-permute-start.55 = (bf16[256,1536]{1,0:T(8,128)(2,1)}, bf16[256,1536]{1,0:T(8,128)(2,1)}, u32[]{:S(2)}, u32[]{:S(2)}) collective-permute-start(bf16[256,1536]{1,0:T(8,128)(2,1)} %slice.174), channel_id=1, source_target_pairs={{0,1},{1,0},{2,3},{3,2},{4,5},{5,4},{6,7},{7,6},{8,9},{9,8},{10,11... | collective-permute-start | bytes 2359304 | tf_op jit(solution)/shard_map/ppermute | solution.py:311
  324.4 20.6 %collective-permute-start.56 = (bf16[256,1536]{1,0:T(8,128)(2,1)S(1)}, bf16[256,1536]{1,0:T(8,128)(2,1)}, u32[]{:S(2)}, u32[]{:S(2)}) collective-permute-start(bf16[256,1536]{1,0:T(8,128)(2,1)S(1)} %slice.175), channel_id=1, source_target_pairs={{0,4},{4,0},{1,5},{5,1},{2,6},{6,2},{3,7},{7,3},{8,12},{12,8},{9,1... | collective-permute-start | bytes 2359304 | tf_op jit(solution)/shard_map/ppermute | solution.py:311
  325.0 44.6 %collective-permute-start.67 = (bf16[512,1536]{1,0:T(8,128)(2,1)}, bf16[512,1536]{1,0:T(8,128)(2,1)}, u32[]{:S(2)}, u32[]{:S(2)}) collective-permute-start(bf16[512,1536]{1,0:T(8,128)(2,1)} %constant_dynamic-update-slice_fusion.16.refs_0_), channel_id=1, source_target_pairs={{0,2},{2,0},{1,3},{3,1},{4,6},{6,4},{5,7},{7,5},{8,10},{10,8},{9,1... | collective-permute-start | bytes 4718600 | tf_op jit(solution)/shard_map/ppermute | solution.py:311
  325.1 44.8 %collective-permute-start.68 = (bf16[512,1536]{1,0:T(8,128)(2,1)}, bf16[512,1536]{1,0:T(8,128)(2,1)}, u32[]{:S(2)}, u32[]{:S(2)}) collective-permute-start(bf16[512,1536]{1,0:T(8,128)(2,1)} %copy-done.20), channel_id=1, source_target_pairs={{0,2},{2,0},{1,3},{3,1},{4,6},{6,4},{5,7},{7,5},{8,10},{10,8},{9,1... | collective-permute-start | bytes 4718600 | tf_op jit(solution)/shard_map/ppermute | solution.py:311
  325.6 44.8 %collective-permute-start.69 = (bf16[512,1536]{1,0:T(8,128)(2,1)}, bf16[512,1536]{1,0:T(8,128)(2,1)}, u32[]{:S(2)}, u32[]{:S(2)}) collective-permute-start(bf16[512,1536]{1,0:T(8,128)(2,1)} %copy-done.17), channel_id=1, source_target_pairs={{0,2},{2,0},{1,3},{3,1},{4,6},{6,4},{5,7},{7,5},{8,10},{10,8},{9,1... | collective-permute-start | bytes 4718600 | tf_op jit(solution)/shard_map/ppermute | solution.py:311
  325.7 36.2 %all-to-all-start.2 = ((bf16[4,96,768]{2,1,0:T(8,128)(2,1)}), bf16[4,96,768]{2,1,0:T(8,128)(2,1)}, u32[]{:S(2)}, u32[]{:S(2)}) async-start(bf16[4,96,768]{2,1,0:T(8,128)(2,1)} %bitcast.88), calls=%async_computation.4 | async-start | bytes 1179648 | tf_op jit(solution)/shard_map/all_to_all | solution.py:61
  349.3 21.0 %collective-permute-start.70 = (bf16[512,1536]{1,0:T(8,128)(2,1)}, bf16[512,1536]{1,0:T(8,128)(2,1)}, u32[]{:S(2)}, u32[]{:S(2)}) collective-permute-start(bf16[512,1536]{1,0:T(8,128)(2,1)} %constant_dynamic-update-slice_fusion.18.refs_3_), channel_id=1, source_target_pairs={{0,2},{2,0},{1,3},{3,1},{4,6},{6,4},{5,7},{7,5},{8,10},{10,8},{9,1... | collective-permute-start | bytes 4718600 | tf_op jit(solution)/shard_map/ppermute | solution.py:311
  365.2 62.4 %reduce-scatter.9.cloned.1.call-start = ((), (), s32[]{:S(2)}) async-start(), calls=%async_computation.12 | async-start | bytes 2048000 | tf_op jit(solution)/shard_map/reduce_scatter | solution.py:65
  367.7 18.0 %collective-permute-start.59 = (bf16[256,1536]{1,0:T(8,128)(2,1)}, bf16[256,1536]{1,0:T(8,128)(2,1)}, u32[]{:S(2)}, u32[]{:S(2)}) collective-permute-start(bf16[256,1536]{1,0:T(8,128)(2,1)} %get-tuple-element.190), channel_id=1, source_target_pairs={{0,2},{2,0},{1,3},{3,1},{4,6},{6,4},{5,7},{7,5},{8,10},{10,8},{9,1... | collective-permute-start | bytes 2359304 | tf_op jit(solution)/shard_map/ppermute | solution.py:311
  369.7 14.0 %collective-permute-start.57 = (bf16[256,1536]{1,0:T(8,128)(2,1)}, bf16[256,1536]{1,0:T(8,128)(2,1)}, u32[]{:S(2)}, u32[]{:S(2)}) collective-permute-start(bf16[256,1536]{1,0:T(8,128)(2,1)} %get-tuple-element.188), channel_id=1, source_target_pairs={{0,2},{2,0},{1,3},{3,1},{4,6},{6,4},{5,7},{7,5},{8,10},{10,8},{9,1... | collective-permute-start | bytes 2359304 | tf_op jit(solution)/shard_map/ppermute | solution.py:311
  369.9 71.0 %collective-permute-start.66 = (bf16[256,1536]{1,0:T(8,128)(2,1)}, bf16[256,1536]{1,0:T(8,128)(2,1)}, u32[]{:S(2)}, u32[]{:S(2)}) collective-permute-start(bf16[256,1536]{1,0:T(8,128)(2,1)} %get-tuple-element.194), channel_id=1, source_target_pairs={{0,2},{2,0},{1,3},{3,1},{4,6},{6,4},{5,7},{7,5},{8,10},{10,8},{9,1... | collective-permute-start | bytes 2359304 | tf_op jit(solution)/shard_map/ppermute | solution.py:311
  385.2 40.6 %collective-permute-start.58 = (bf16[128,1536]{1,0:T(8,128)(2,1)S(1)}, bf16[128,1536]{1,0:T(8,128)(2,1)S(1)}, u32[]{:S(2)}, u32[]{:S(2)}) collective-permute-start(bf16[128,1536]{1,0:T(8,128)(2,1)S(1)} %slice.178), channel_id=1, source_target_pairs={{0,1},{1,0},{2,3},{3,2},{4,5},{5,4},{6,7},{7,6},{8,9},{9,8},{10,11... | collective-permute-start | bytes 1179656 | tf_op jit(solution)/shard_map/ppermute | solution.py:311
  387.8 51.9 %collective-permute-start.63 = (bf16[128,1536]{1,0:T(8,128)(2,1)}, bf16[128,1536]{1,0:T(8,128)(2,1)}, u32[]{:S(2)}, u32[]{:S(2)}) collective-permute-start(bf16[128,1536]{1,0:T(8,128)(2,1)} %slice.181), channel_id=1, source_target_pairs={{0,4},{4,0},{1,5},{5,1},{2,6},{6,2},{3,7},{7,3},{8,12},{12,8},{9,1... | collective-permute-start | bytes 1179656 | tf_op jit(solution)/shard_map/ppermute | solution.py:311
  389.4 19.1 %collective-permute-start.64 = (bf16[128,1536]{1,0:T(8,128)(2,1)}, bf16[128,1536]{1,0:T(8,128)(2,1)}, u32[]{:S(2)}, u32[]{:S(2)}) collective-permute-start(bf16[128,1536]{1,0:T(8,128)(2,1)} %get-tuple-element.209), channel_id=1, source_target_pairs={{0,4},{4,0},{1,5},{5,1},{2,6},{6,2},{3,7},{7,3},{8,12},{12,8},{9,1... | collective-permute-start | bytes 1179656 | tf_op jit(solution)/shard_map/ppermute | solution.py:311
  394.1 32.4 %collective-permute-start.62 = (bf16[128,1536]{1,0:T(8,128)(2,1)S(1)}, bf16[128,1536]{1,0:T(8,128)(2,1)S(1)}, u32[]{:S(2)}, u32[]{:S(2)}) collective-permute-start(bf16[128,1536]{1,0:T(8,128)(2,1)S(1)} %reduce-precision_convert_fusion.10), channel_id=1, source_target_pairs={{0,4},{4,0},{1,5},{5,1},{2,6},{6,2},{3,7},{7,3},{8,12},{12,8},{9,1... | collective-permute-start | bytes 1179656 | tf_op jit(solution)/shard_map/ppermute | solution.py:311
  395.9 26.4 %all-to-all-start.5 = ((bf16[4,96,768]{2,1,0:T(8,128)(2,1)}), bf16[4,96,768]{2,1,0:T(8,128)(2,1)S(1)}, u32[]{:S(2)}, u32[]{:S(2)}) async-start(bf16[4,96,768]{2,1,0:T(8,128)(2,1)} %bitcast.42), calls=%async_computation.9 | async-start | bytes 1179648 | tf_op jit(solution)/shard_map/all_to_all | solution.py:61
  410.3 29.3 %collective-permute-start.65 = (bf16[128,1536]{1,0:T(8,128)(2,1)}, bf16[128,1536]{1,0:T(8,128)(2,1)}, u32[]{:S(2)}, u32[]{:S(2)}) collective-permute-start(bf16[128,1536]{1,0:T(8,128)(2,1)} %reduce-precision_convert_fusion.9), channel_id=1, source_target_pairs={{0,1},{1,0},{2,3},{3,2},{4,5},{5,4},{6,7},{7,6},{8,9},{9,8},{10,11... | collective-permute-start | bytes 1179656 | tf_op jit(solution)/shard_map/ppermute | solution.py:311
  436.1 17.0 %all-to-all-start.3 = ((bf16[8,112,448]{2,1,0:T(8,128)(2,1)}), bf16[8,112,448]{2,1,0:T(8,128)(2,1)S(1)}, u32[]{:S(2)}, u32[]{:S(2)}) async-start(bf16[8,112,448]{2,1,0:T(8,128)(2,1)} %maximum_maximum_fusion), calls=%async_computation.6 | async-start | bytes 1835008 | tf_op jit(solution)/shard_map/all_to_all | solution.py:61
  (123 other events, 1157.1 us)
Sparse Core Ops, SparseCore 0:
  203.4 47.9 reduce-scatter.4
  253.6 47.5 reduce-scatter.6
  303.5 47.5 reduce-scatter.10
  381.4 37.8 reduce-scatter.8
where the time goes:
time: 472 us; the launch traced here: 463 us
  waiting for transfers between devices  173 us (37%)
  Pallas kernels  106 us (22%)
  starting transfers between devices  73.2 us (16%)
  local copies, waits for them, and re-layouts  71.7 us (15%)
  other arithmetic  22.7 us (5%)
  between operations  16.2 us (3%)
    ppermute x65, waiting for transfers between devices, swap(): return lax.ppermute(block, axis, [(0, 1), (1, 0)])  117 us
    pallas_call x12, Pallas kernels, run_kernel(): pl.pallas_call(kernel, out_shape=[jax.ShapeDtypeStruct(shape, dtype) for...  99.1 us
    unnamed x194, local copies, waits for them, and re-layouts  41 us
    ppermute x65, starting transfers between devices, swap(): return lax.ppermute(block, axis, [(0, 1), (1, 0)])  40.7 us
    all_to_all x6, waiting for transfers between devices, exchange(): return lax.all_to_all(block, axes, split_axis=0, concat_axis=0, tiled=True)  37.7 us
    all_to_all x6, starting transfers between devices, exchange(): return lax.all_to_all(block, axes, split_axis=0, concat_axis=0, tiled=True)  21.7 us
    ppermute x6, waiting for transfers between devices, shifts(): lax.ppermute(block, 'z', [(i, (i + k) % depth) for i in range(depth)])  18.3 us
    ppermute x6, starting transfers between devices, shifts(): lax.ppermute(block, 'z', [(i, (i + k) % depth) for i in range(depth)])  10.2 us
  transfers between devices with their start and end apart: 81, of which 32 were waited for; matrix products, arithmetic and copies ran while one was open for 12% of the time, Pallas kernels for 19%

commit v1 on v0

--- a/solution.py
+++ b/solution.py
@@ -710,7 +710,7 @@
     tokens_ref[...] = (resid_grad[...] + norm_grad).astype(jnp.bfloat16)
 
 
-def dense_grad_kernel(at, narrow, back, *refs):
+def dense_grad_kernel(at, back, *refs):
     pieces, out_ref, held, sems = refs[:8], refs[8], refs[9], refs[10]
     copies = [
         pltpu.make_async_copy(piece, held.at[n], sems.at[n]) for n, piece in enumerate(pieces)
@@ -720,7 +720,7 @@
     depth, rows, cols = out_ref.shape
     length = held.shape[1] // 2
     qkv_width = cols - held.shape[2] // back.shape[0]
-    narrow = sum(narrow[place].astype(jnp.float32) for place in range(narrow.shape[0]))
+    narrow = sum(back[place, length:].astype(jnp.float32) for place in range(back.shape[0]))
     sums = [0.0, 0.0]
     for n, copy in enumerate(copies):
         copy.wait()
@@ -730,7 +730,7 @@
         sums[0] = sums[0] + dot(held[n, length:], own[:, :qkv_width], ((0,), (0,)))
         sums[1] = sums[1] + dot(held[n, :length], own[:, qkv_width:], ((0,), (0,)))
     wide = held.shape[2] // depth
-    each = narrow.shape[0] // depth
+    each = 4
     for z in range(depth):
         here = slice(z * wide, (z + 1) * wide)
         both = jnp.concatenate([part[here] for part in sums], axis=1)
@@ -907,14 +907,15 @@
     stages = (stage_own, stage_sides, stage_corner)
     rows_in, rows_cot, gated, gate_back, up_back = ([stage[n] for stage in stages] for n in range(5))
     gates = stage_own[5]
-    (down_part,) = row_sums(at, [after(rows_cot[0], corner)] + rows_cot[1:], gated)
+    last_y, last_x, *sent = corner_last(back_x, back_y, passed)
+    (down_part,) = row_sums(
+        at, [after(rows_cot[0], *sent, first_x, first_y)] + rows_cot[1:], gated
+    )
     down_sum = scatter_sum(down_part, "z")
-    passed = lax.optimization_barrier((*passed, down_part))[:2]
-    last_y, last_x, *sent = corner_last(back_x, back_y, passed)
     gate_part, up_part = row_sums(
-        at, [after(rows_in[0], *sent, first_x, first_y, own_far)] + rows_in[1:], gate_back, up_back
-    )
-    gate_sum, up_sum = scatter_sum(gate_part, "z"), scatter_sum(up_part, "z")
+        at, [after(rows_in[0], down_part, own_far)] + rows_in[1:], gate_back, up_back
+    )
+    gate_sum = scatter_sum(gate_part, "z")
     own_near = after(own_near, gate_part)
 
     resid_grad, branch_grad, attended_grad, router_acc, gain_two_grad = run_kernel(
@@ -992,22 +993,25 @@
     narrow_part = jnp.pad(
         narrow_part, ((0, 0), (0, 0), (0, each_rows * dense_cols - narrow_len))
     ).reshape(plane, depth * each_rows, dense_cols)
+    narrow_part = jnp.pad(
+        narrow_part.astype(bf16), ((0, 0), (0, 16 - depth * each_rows), (0, 0))
+    )
+    back_cols = lax.dynamic_update_slice(back_cols, narrow_part, (0, length, 0))
     back_cols = exchange(after(back_cols, down_sum, *both_sides), PLANE)
-    narrow_part = exchange(narrow_part.astype(bf16), PLANE)
-    both_corner = plane_corner(both_sides, (back_cols, gain_one_grad))
+    both_corner = plane_corner(both_sides, (back_cols,))
     both_pieces = plane_pieces(both, both_sides, both_corner)
     def placed(total):
         total = exchange(total, ("y", "c"))
         return total.reshape(local_count, shard_rows, hidden_width).astype(f32)
 
-    down_grad = placed(down_sum)
+    down_grad, gate_grad = placed(down_sum), placed(gate_sum)
     kept_rows = -(-narrow_rows // 16) * 16
     wide_rows = local_count * shard_rows
     dense_shape = (depth, wide_rows + kept_rows, dense_cols)
     dense_part = pl.pallas_call(
         dense_grad_kernel,
         out_shape=jax.ShapeDtypeStruct(dense_shape, bf16),
-        in_specs=[SCALARS, WHOLE, WHOLE] + [IN_HBM] * 8,
+        in_specs=[SCALARS, WHOLE] + [IN_HBM] * 8,
         out_specs=WHOLE,
         scratch_shapes=[
             pltpu.VMEM((plane, 2 * length, model_width), bf16),
@@ -1015,7 +1019,8 @@
         ],
         cost_estimate=cost(8),
         compiler_params=pltpu.CompilerParams(vmem_limit_bytes=32 * 2**20),
-    )(at, narrow_part, after(back_cols, up_sum, down_grad), *both_pieces)
+    )(at, after(back_cols, down_grad), *both_pieces)
+    dense_part = after(dense_part, gate_sum)
     dense_sum = scatter_sum(dense_part.reshape(-1, dense_cols), "z")
     wide_sum = dense_sum[: local_count * shard_rows].reshape(2, 2, 1, shard_rows, dense_cols)
     wide_sum = jnp.broadcast_to(wide_sum, (2, 2, owners, shard_rows, dense_cols)).reshape(
@@ -1044,11 +1049,13 @@
     narrow_sum = narrow_sum[y, c, :, :narrow_len].reshape(owners, shard_rows, -1)
     narrow_sum = jnp.moveaxis(narrow_sum, 0, 1).reshape(shard_rows, narrow_cols).astype(f32)
 
+    up_sum = scatter_sum(after(up_part, dense_sum), "z")
+
     shares = run_kernel(
         functools.partial(mixture_kernel, capacity, groups),
         10,
         at,
-        (ids_all, after(gated[0], both_corner), *gated[1:], down_w),
+        (ids_all, after(gated[0], *both_sides), *gated[1:], down_w),
         [((length, model_width), bf16)] * plane,
         56,
     )
@@ -1070,8 +1077,8 @@
         output_grad,
         narrow_sum[:, experts_all + 1],
         narrow_sum[:, :experts_all],
-        placed(after(gate_sum, dense_part)),
-        placed(after(up_sum, dense_part)),
+        gate_grad,
+        placed(up_sum),
         jnp.swapaxes(down_grad, 1, 2),
     )
 

time: 472 us -> 486 us (1.030)
  waiting for transfers between devices: 173 us -> 207 us
  local copies, waits for them, and re-layouts: 71.7 us -> 59.9 us
  starting transfers between devices: 73.2 us -> 67.9 us
    reduce_scatter x4, waiting for transfers between devices: 0.03 us -> 28 us  [scatter_sum(): return lax.psum_scatter(block, axes, scatter_dimension=0, tiled=True)]
    all_to_all x6 -> x5, waiting for transfers between devices: 37.7 us -> 55.2 us  [exchange(): return lax.all_to_all(block, axes, split_axis=0, concat_axis=0, tiled=True)]
    unnamed x194 -> x158, local copies, waits for them, and re-layouts: 41 us -> 28.9 us
    ppermute x65, waiting for transfers between devices: 117 us -> 105 us  [swap(): return lax.ppermute(block, axis, [(0, 1), (1, 0)])]
    all_to_all x6 -> x5, starting transfers between devices: 21.7 us -> 19.1 us  [exchange(): return lax.all_to_all(block, axes, split_axis=0, concat_axis=0, tiled=True)]
  transfers between devices with their start and end apart: 81 -> 80, of which waited for: 32 -> 35; matrix products, arithmetic and copies ran while one was open for 12% -> 11% of each run, Pallas kernels for 19% -> 22%
where the time goes in v1:
time: 486 us; the launch traced here: 477 us
  waiting for transfers between devices  207 us (43%)
  Pallas kernels  107 us (22%)
  starting transfers between devices  67.9 us (14%)
  local copies, waits for them, and re-layouts  59.9 us (12%)
  other arithmetic  19.5 us (4%)
  between operations  15.9 us (3%)
    ppermute x65, waiting for transfers between devices, swap(): return lax.ppermute(block, axis, [(0, 1), (1, 0)])  105 us
    pallas_call x12, Pallas kernels, run_kernel(): pl.pallas_call(kernel, out_shape=[jax.ShapeDtypeStruct(shape, dtype) for...  99.9 us
    all_to_all x5, waiting for transfers between devices, exchange(): return lax.all_to_all(block, axes, split_axis=0, concat_axis=0, tiled=True)  55.2 us
    ppermute x65, starting transfers between devices, swap(): return lax.ppermute(block, axis, [(0, 1), (1, 0)])  38.5 us
    unnamed x158, local copies, waits for them, and re-layouts  28.9 us
    reduce_scatter x4, waiting for transfers between devices, scatter_sum(): return lax.psum_scatter(block, axes, scatter_dimension=0, tiled=True)  28 us
    all_to_all x5, starting transfers between devices, exchange(): return lax.all_to_all(block, axes, split_axis=0, concat_axis=0, tiled=True)  19.1 us
    ppermute x6, waiting for transfers between devices, shifts(): lax.ppermute(block, 'z', [(i, (i + k) % depth) for i in range(depth)])  18.3 us
  transfers between devices with their start and end apart: 80, of which 35 were waited for; matrix products, arithmetic and copies ran while one was open for 11% of the time, Pallas kernels for 22%

profile of v1, /device:TPU:0, one launch (start us, length us, event | category | flops | bytes accessed | tf_op | source)
XLA Modules:
  0.0 477.5 jit_solution(10472717108371785410)
XLA Ops:
  8.1 5.1 %collective-permute-start = (bf16[96,128]{1,0:T(8,128)(2,1)S(1)}, bf16[96,128]{1,0:T(8,128)(2,1)S(1)}, u32[]{:S(2)}, u32[]{:S(2)}) collective-permute-start(bf16[96,128]{1,0:T(8,128)(2,1)S(1)} %pad.9), channel_id=1, source_target_pairs={{0,24},{8,0},{16,8},{24,16},{1,25},{9,1},{17,9},{25,17},{2,26},{10... | collective-permute-start | bytes 73736 | tf_op jit(solution)/shard_map/ppermute | solution.py:317
  18.2 2.8 collective-permute-start.14
  26.1 2.7 collective-permute-done.3
  33.0 18.3 %collective-permute-done.13 = bf16[96,1792]{1,0:T(8,128)(2,1)} collective-permute-done((bf16[96,1792]{1,0:T(8,128)(2,1)}, bf16[96,1792]{1,0:T(8,128)(2,1)}, u32[]{:S(2)}, u32[]{:S(2)}) %collective-permute-start.13) | collective-permute-done | bytes 344096 | tf_op jit(solution)/shard_map/ppermute | solution.py:317
  61.7 4.0 dynamic-slice_bitcast_fusion.1.refs_5_.refs_9_
  65.8 3.2 dynamic-slice_bitcast_fusion.2.refs_4_.refs_8_
  69.0 6.7 %collective-permute-done.16.refs_2_ = bf16[4,96,1024]{2,1,0:T(8,128)(2,1)} collective-permute-done((bf16[4,96,1024]{2,1,0:T(8,128)(2,1)S(1)}, bf16[4,96,1024]{2,1,0:T(8,128)(2,1)}, u32[]{:S(2)}, u32[]{:S(2)}) %collective-permute-start.16) | collective-permute-done | bytes 786464 | tf_op jit(solution)/shard_map/ppermute | solution.py:311
  80.4 5.3 %collective-permute-done.17 = bf16[2,96,1024]{2,1,0:T(8,128)(2,1)S(1)} collective-permute-done((bf16[2,96,1024]{2,1,0:T(8,128)(2,1)S(1)}, bf16[2,96,1024]{2,1,0:T(8,128)(2,1)S(1)}, u32[]{:S(2)}, u32[]{:S(2)}) %collective-permute-start.17) | collective-permute-done | bytes 393248 | tf_op jit(solution)/shard_map/ppermute | solution.py:311
  95.8 9.1 %shard_map.229 = (bf16[256,1536]{1,0:T(8,128)(2,1)S(1)}, bf16[256,1536]{1,0:T(8,128)(2,1)S(1)}, bf16[256,256]{1,0:T(8,128)(2,1)S(1)}, bf16[256,256]{1,0:T(8,128)...) custom-call(s32[7]{0:T(128)S(1)} %copy-done.34, ...), custom_call_target="tpu_custom_call" | custom-call | flops 11000000512 | bytes 11000000 | tf_op jit(solution)/shard_map/pallas_call | solution.py:400
  104.9 2.7 copy-done.41
  113.1 5.7 %collective-permute-done.25 = bf16[2,96,768]{2,1,0:T(8,128)(2,1)S(1)} collective-permute-done((bf16[2,96,768]{2,1,0:T(8,128)(2,1)S(1)}, bf16[2,96,768]{2,1,0:T(8,128)(2,1)S(1)}, u32[]{:S(2)}, u32[]{:S(2)}) %collective-permute-start.25) | collective-permute-done | bytes 294944 | tf_op jit(solution)/shard_map/ppermute | solution.py:311
  119.5 6.7 %collective-permute-done.10 = bf16[128,1536]{1,0:T(8,128)(2,1)S(1)} collective-permute-done((bf16[128,1536]{1,0:T(8,128)(2,1)S(1)}, bf16[128,1536]{1,0:T(8,128)(2,1)S(1)}, u32[]{:S(2)}, u32[]{:S(2)}) %collective-permute-start.10) | collective-permute-done | bytes 393248 | tf_op jit(solution)/shard_map/ppermute | solution.py:311
  128.3 4.1 shard_map.230
  136.5 10.4 %shard_map.231 = (bf16[384,1536]{1,0:T(8,128)(2,1)S(1)}, bf16[384,1536]{1,0:T(8,128)(2,1)S(1)}, bf16[384,768]{1,0:T(8,128)(2,1)S(1)}, bf16[384,768]{1,0:T(8,128)...) custom-call(s32[7]{0:T(128)S(1)} %copy-done.35, ...), custom_call_target="tpu_custom_call" | custom-call | flops 8000000000 | bytes 8000000 | tf_op jit(solution)/shard_map/pallas_call | solution.py:400
  149.6 4.3 collective-permute-done.33.refs_0_
  157.1 2.2 collective-permute-done.36.refs_3_
  159.3 16.4 %shard_map.232 = (bf16[768,1536]{1,0:T(8,128)(2,1)S(1)}, bf16[768,1536]{1,0:T(8,128)(2,1)S(1)}, bf16[768,768]{1,0:T(8,128)(2,1)S(1)}, bf16[768,768]{1,0:T(8,128)...) custom-call(s32[7]{0:T(128)S(1)} %copy-done.35, ...), custom_call_target="tpu_custom_call" | custom-call | flops 16000000000 | bytes 16000000 | tf_op jit(solution)/shard_map/pallas_call | solution.py:400
  180.7 9.5 %shard_map.233 = (bf16[384,1536]{1,0:T(8,128)(2,1)S(1)}, bf16[384,1536]{1,0:T(8,128)(2,1)S(1)}, bf16[384,768]{1,0:T(8,128)(2,1)S(1)}, bf16[384,768]{1,0:T(8,128)...) custom-call(s32[7]{0:T(128)S(1)} %copy-done.35, ...), custom_call_target="tpu_custom_call" | custom-call | flops 8000000000 | bytes 8000000 | tf_op jit(solution)/shard_map/pallas_call | solution.py:400
  196.8 8.9 %collective-permute-done.48 = bf16[128,1664]{1,0:T(8,128)(2,1)S(1)} collective-permute-done((bf16[128,1664]{1,0:T(8,128)(2,1)S(1)}, bf16[128,1664]{1,0:T(8,128)(2,1)S(1)}, u32[]{:S(2)}, u32[]{:S(2)}) %collective-permute-start.48) | collective-permute-done | bytes 426016 | tf_op jit(solution)/shard_map/ppermute | solution.py:311
  205.8 6.8 %collective-permute-done.45 = bf16[128,1664]{1,0:T(8,128)(2,1)S(1)} collective-permute-done((bf16[128,1664]{1,0:T(8,128)(2,1)S(1)}, bf16[128,1664]{1,0:T(8,128)(2,1)S(1)}, u32[]{:S(2)}, u32[]{:S(2)}) %collective-permute-start.45) | collective-permute-done | bytes 426016 | tf_op jit(solution)/shard_map/ppermute | solution.py:311
  214.8 5.9 %shard_map.235 = bf16[1536,768]{1,0:T(8,128)(2,1)} custom-call(s32[7]{0:T(128)S(1)} %copy-done.35, bf16[384,1536]{1,0:T(8,128)(2,1)S(1)} %get-tuple-element.161.refs_0_, bf16[768,1536]{1,0:T(8,128)(2,1)S(1)} %get-tuple-element.162.refs_1_, bf16[384,1536]{1,0:T(8,128)(2,1)S(1)} %get-tuple-element.163.refs_2_, ...), custom_call_target="tpu_custom_call" | custom-call | flops 4000000000 | bytes 4000000 | tf_op jit(solution)/shard_map/pallas_call | solution.py:400
  222.1 13.2 %shard_map.236 = (bf16[1536,768]{1,0:T(8,128)(2,1)}, bf16[1536,768]{1,0:T(8,128)(2,1)}) custom-call(s32[7]{0:T(128)} %stack.76.at, bf16[384,1536]{1,0:T(8,128)(2,1)} %copy-done.50, bf16[768,1536]{1,0:T(8,128)(2,1)} %copy-done.49, bf16[384,1536]{1,0:T(8,128)(2,1)} %copy-done.51, bf16[384,768]{1,0:T(8,128)(2,1)} %copy-done.55, bf16[768,768]{1,0:T(8,128)(2,1)} %copy-done.53, ...), custom_call_target="tpu_custom_call" | custom-call | flops 8000000000 | bytes 8000000 | tf_op jit(solution)/shard_map/pallas_call | solution.py:400
  240.1 8.3 %shard_map.237 = (f32[256,1536]{1,0:T(8,128)}, bf16[256,1536]{1,0:T(8,128)(2,1)}, bf16[256,1536]{1,0:T(8,128)(2,1)}, f32[1536,128]{1,0:T(8,128)}, f32[1,1536]{1,0:T(1,128)}) custom-call(s32[7]{0:T(128)} %stack.76.at, bf16[256,1664]{1,0:T(8,128)(2,1)} %copy-done.47, bf16[256,1664]{1,0:T(8,128)(2,1)} %collective-permute-done.64.far, ...), custom_call_target="tpu_custom_call" | custom-call | flops 6000000000 | bytes 6000000 | tf_op jit(solution)/shard_map/pallas_call | solution.py:400
  250.4 8.3 %shard_map.238.back = bf16[8,272,448]{2,1,0:T(8,128)(2,1)} custom-call(s32[7]{0:T(128)} %stack.76.at, bf16[256,1536]{1,0:T(8,128)(2,1)} %get-tuple-element.177.attended, bf16[12,256,256]{2,1,0:T(8,128)(2,1)} %copy-done.48, bf16[256,1536]{1,0:T(8,128)(2,1)} %copy-done.52, bf16[256,256]{1,0:T(8,128)(2,1)} %copy-done.60, bf16[256,256]{1,0:T(8,128)(2,1)} %copy-done.61, ...), custom_call_target="tpu_custom_call" | custom-call | flops 6000000000 | bytes 6000000 | tf_op jit(solution)/shard_map/pallas_call | solution.py:400
  260.4 2.8 copy-done.42
  263.2 3.7 shard_map.239
  274.7 3.6 all-to-all-start
  279.2 2.2 slice.183
  281.4 24.4 %all-to-all-done.back = bf16[8,272,448]{2,1,0:T(8,128)(2,1)S(1)} async-done(((bf16[8,272,448]{2,1,0:T(8,128)(2,1)}), bf16[8,272,448]{2,1,0:T(8,128)(2,1)S(1)}, u32[]{:S(2)}, u32[]{:S(2)}) %all-to-all-start) | async-done | bytes 1949728 | tf_op jit(solution)/shard_map/all_to_all | solution.py:61
  307.9 17.4 %collective-permute-done.65 = bf16[256,1536]{1,0:T(8,128)(2,1)S(1)} collective-permute-done((bf16[256,1536]{1,0:T(8,128)(2,1)}, bf16[256,1536]{1,0:T(8,128)(2,1)S(1)}, u32[]{:S(2)}, u32[]{:S(2)}) %collective-permute-start.65) | collective-permute-done | bytes 786464 | tf_op jit(solution)/shard_map/ppermute | solution.py:311
  326.0 3.4 collective-permute-done.70.refs_7_
  329.4 6.9 %shard_map.240 = bf16[4,400,448]{2,1,0:T(8,128)(2,1)S(1)} custom-call(s32[7]{0:T(128)S(1)} %copy-done.36, bf16[8,272,448]{2,1,0:T(8,128)(2,1)S(1)} %all-to-all-done.back, bf16[512,1536]{1,0:T(8,128)(2,1)} %constant_dynamic-update-slice_fusion.16.refs_0_, bf16[512,1536]{1,0:T(8,128)(2,1)S(1)} %copy-done.15, bf16[512,1536]{1,0:T(8,128)(2,1)S(1)} %copy-done.17, ...), custom_call_target="tpu_custom_call" | custom-call | flops 8000000000 | bytes 8000000 | tf_op jit(solution)/shard_map/pallas_call | solution.py:1011
  337.6 9.3 %shard_map.234 = (bf16[256,1536]{1,0:T(8,128)(2,1)}, bf16[256,1536]{1,0:T(8,128)(2,1)}, bf16[256,1536]{1,0:T(8,128)(2,1)}, bf16[256,1536]{1,0:T(8,128)(2,1)}, bf...) custom-call(s32[7]{0:T(128)} %stack.76.at, ...), custom_call_target="tpu_custom_call" | custom-call | flops 10000000000 | bytes 10000000 | tf_op jit(solution)/shard_map/pallas_call | solution.py:400
  347.1 27.9 %reduce-scatter.9.cloned.1.call-done = bf16[400,448]{1,0:T(8,128)(2,1)} async-done(((bf16[1600,448]{1,0:T(8,128)(2,1)}), bf16[400,448]{1,0:T(8,128)(2,1)}) %reduce-scatter.9.cloned.1.call-update) | async-done | bytes 358416 | tf_op jit(solution)/shard_map/reduce_scatter | solution.py:65
  377.4 3.7 all-to-all-start.2
  382.1 12.4 %all-to-all-done.2.sums = bf16[8,112,448]{2,1,0:T(8,128)(2,1)S(1)} async-done(((bf16[8,112,448]{2,1,0:T(8,128)(2,1)}), bf16[8,112,448]{2,1,0:T(8,128)(2,1)S(1)}, u32[]{:S(2)}, u32[]{:S(2)}) %all-to-all-start.2) | async-done | bytes 802848 | tf_op jit(solution)/shard_map/all_to_all | solution.py:61
  401.5 5.5 %collective-permute-done.56 = bf16[128,1536]{1,0:T(8,128)(2,1)S(1)} collective-permute-done((bf16[128,1536]{1,0:T(8,128)(2,1)S(1)}, bf16[128,1536]{1,0:T(8,128)(2,1)S(1)}, u32[]{:S(2)}, u32[]{:S(2)}) %collective-permute-start.56) | collective-permute-done | bytes 393248 | tf_op jit(solution)/shard_map/ppermute | solution.py:311
  407.6 12.5 %collective-permute-done.59 = bf16[128,1536]{1,0:T(8,128)(2,1)S(1)} collective-permute-done((bf16[128,1536]{1,0:T(8,128)(2,1)S(1)}, bf16[128,1536]{1,0:T(8,128)(2,1)S(1)}, u32[]{:S(2)}, u32[]{:S(2)}) %collective-permute-start.59) | collective-permute-done | bytes 393248 | tf_op jit(solution)/shard_map/ppermute | solution.py:311
  422.0 4.7 collective-permute-done.57
  426.8 4.2 all-to-all-start.3
  431.0 2.2 convert_add_fusion
  433.2 7.4 %all-to-all-done.3 = bf16[4,96,768]{2,1,0:T(8,128)(2,1)} async-done(((bf16[4,96,768]{2,1,0:T(8,128)(2,1)}), bf16[4,96,768]{2,1,0:T(8,128)(2,1)}, u32[]{:S(2)}, u32[]{:S(2)}) %all-to-all-start.3) | async-done | bytes 589856 | tf_op jit(solution)/shard_map/all_to_all | solution.py:61
  440.5 4.2 all-to-all-start.1
  444.7 2.9 fusion.1
  449.8 4.5 all-to-all-done.1
  454.3 2.2 convert_bitcast_fusion
  456.6 3.5 all-to-all-start.4
  463.2 6.4 %all-to-all-done.4 = bf16[4,96,768]{2,1,0:T(8,128)(2,1)S(1)} async-done(((bf16[4,96,768]{2,1,0:T(8,128)(2,1)}), bf16[4,96,768]{2,1,0:T(8,128)(2,1)S(1)}, u32[]{:S(2)}, u32[]{:S(2)}) %all-to-all-start.4) | async-done | bytes 589856 | tf_op jit(solution)/shard_map/all_to_all | solution.py:61
  (385 shorter events, 113.0 us)
Async XLA Ops:
  7.2 266.4 %reduce-scatter.5.cloned.1.call-start = ((), (), s32[]{:S(2)}) async-start(), calls=%async_computation.9 | async-start | bytes 2949120 | tf_op jit(solution)/shard_map/reduce_scatter | solution.py:65
  8.1 14.2 %collective-permute-start = (bf16[96,128]{1,0:T(8,128)(2,1)S(1)}, bf16[96,128]{1,0:T(8,128)(2,1)S(1)}, u32[]{:S(2)}, u32[]{:S(2)}) collective-permute-start(bf16[96,128]{1,0:T(8,128)(2,1)S(1)} %pad.9), channel_id=1, source_target_pairs={{0,24},{8,0},{16,8},{24,16},{1,25},{9,1},{17,9},{25,17},{2,26},{10... | collective-permute-start | bytes 73736 | tf_op jit(solution)/shard_map/ppermute | solution.py:317
  18.2 13.8 %collective-permute-start.14 = (bf16[96,1792]{1,0:T(8,128)(2,1)}, bf16[96,1792]{1,0:T(8,128)(2,1)}, u32[]{:S(2)}, u32[]{:S(2)}) collective-permute-start(bf16[96,1792]{1,0:T(8,128)(2,1)} %pad_maximum_fusion.3), channel_id=1, source_target_pairs={{0,24},{8,0},{16,8},{24,16},{1,25},{9,1},{17,9},{25,17},{2,26},{10... | collective-permute-start | bytes 1032200 | tf_op jit(solution)/shard_map/ppermute | solution.py:317
  21.1 30.2 %collective-permute-start.13 = (bf16[96,1792]{1,0:T(8,128)(2,1)}, bf16[96,1792]{1,0:T(8,128)(2,1)}, u32[]{:S(2)}, u32[]{:S(2)}) collective-permute-start(bf16[96,1792]{1,0:T(8,128)(2,1)} %pad_maximum_fusion.3), channel_id=1, source_target_pairs={{0,16},{8,24},{16,0},{24,8},{1,17},{9,25},{17,1},{25,9},{2,18},{10... | collective-permute-start | bytes 1032200 | tf_op jit(solution)/shard_map/ppermute | solution.py:317
  22.3 29.9 %collective-permute-start.12 = (bf16[96,1792]{1,0:T(8,128)(2,1)}, bf16[96,1792]{1,0:T(8,128)(2,1)}, u32[]{:S(2)}, u32[]{:S(2)}) collective-permute-start(bf16[96,1792]{1,0:T(8,128)(2,1)} %pad_maximum_fusion.3), channel_id=1, source_target_pairs={{0,8},{8,16},{16,24},{24,0},{1,9},{9,17},{17,25},{25,1},{2,10},{10... | collective-permute-start | bytes 1032200 | tf_op jit(solution)/shard_map/ppermute | solution.py:317
  30.5 26.5 %collective-permute-start.8 = (bf16[256,1536]{1,0:T(8,128)(2,1)}, bf16[256,1536]{1,0:T(8,128)(2,1)S(1)}, u32[]{:S(2)}, u32[]{:S(2)}) collective-permute-start(bf16[256,1536]{1,0:T(8,128)(2,1)} %cot.1), channel_id=1, source_target_pairs={{0,4},{4,0},{1,5},{5,1},{2,6},{6,2},{3,7},{7,3},{8,12},{12,8},{9,1... | collective-permute-start | bytes 2359304 | tf_op jit(solution)/shard_map/ppermute | solution.py:311
  31.1 25.9 %collective-permute-start.9 = (bf16[256,1536]{1,0:T(8,128)(2,1)}, bf16[256,1536]{1,0:T(8,128)(2,1)S(1)}, u32[]{:S(2)}, u32[]{:S(2)}) collective-permute-start(bf16[256,1536]{1,0:T(8,128)(2,1)} %cot.1), channel_id=1, source_target_pairs={{0,1},{1,0},{2,3},{3,2},{4,5},{5,4},{6,7},{7,6},{8,9},{9,8},{10,11... | collective-permute-start | bytes 2359304 | tf_op jit(solution)/shard_map/ppermute | solution.py:311
  57.0 19.7 %collective-permute-start.15 = (bf16[4,96,1024]{2,1,0:T(8,128)(2,1)S(1)}, bf16[4,96,1024]{2,1,0:T(8,128)(2,1)}, u32[]{:S(2)}, u32[]{:S(2)}) collective-permute-start(bf16[4,96,1024]{2,1,0:T(8,128)(2,1)S(1)} %pad_maximum_fusion.refs_0_), channel_id=1, source_target_pairs={{0,1},{1,0},{2,3},{3,2},{4,5},{5,4},{6,7},{7,6},{8,9},{9,8},{10,11... | collective-permute-start | bytes 2359304 | tf_op jit(solution)/shard_map/ppermute | solution.py:311
  58.4 17.3 %collective-permute-start.16 = (bf16[4,96,1024]{2,1,0:T(8,128)(2,1)S(1)}, bf16[4,96,1024]{2,1,0:T(8,128)(2,1)}, u32[]{:S(2)}, u32[]{:S(2)}) collective-permute-start(bf16[4,96,1024]{2,1,0:T(8,128)(2,1)S(1)} %pad_maximum_fusion.refs_0_), channel_id=1, source_target_pairs={{0,4},{4,0},{1,5},{5,1},{2,6},{6,2},{3,7},{7,3},{8,12},{12,8},{9,1... | collective-permute-start | bytes 2359304 | tf_op jit(solution)/shard_map/ppermute | solution.py:311
  89.7 19.0 %collective-permute-start.23 = (bf16[4,96,768]{2,1,0:T(8,128)(2,1)}, bf16[4,96,768]{2,1,0:T(8,128)(2,1)S(1)}, u32[]{:S(2)}, u32[]{:S(2)}) collective-permute-start(bf16[4,96,768]{2,1,0:T(8,128)(2,1)} %pad_maximum_fusion.1.refs_0_), channel_id=1, source_target_pairs={{0,1},{1,0},{2,3},{3,2},{4,5},{5,4},{6,7},{7,6},{8,9},{9,8},{10,11... | collective-permute-start | bytes 1769480 | tf_op jit(solution)/shard_map/ppermute | solution.py:311
  91.3 17.4 %collective-permute-start.24 = (bf16[4,96,768]{2,1,0:T(8,128)(2,1)}, bf16[4,96,768]{2,1,0:T(8,128)(2,1)S(1)}, u32[]{:S(2)}, u32[]{:S(2)}) collective-permute-start(bf16[4,96,768]{2,1,0:T(8,128)(2,1)} %pad_maximum_fusion.1.refs_0_), channel_id=1, source_target_pairs={{0,4},{4,0},{1,5},{5,1},{2,6},{6,2},{3,7},{7,3},{8,12},{12,8},{9,1... | collective-permute-start | bytes 1769480 | tf_op jit(solution)/shard_map/ppermute | solution.py:311
  110.4 15.7 %collective-permute-start.10 = (bf16[128,1536]{1,0:T(8,128)(2,1)S(1)}, bf16[128,1536]{1,0:T(8,128)(2,1)S(1)}, u32[]{:S(2)}, u32[]{:S(2)}) collective-permute-start(bf16[128,1536]{1,0:T(8,128)(2,1)S(1)} %slice.159), channel_id=1, source_target_pairs={{0,1},{1,0},{2,3},{3,2},{4,5},{5,4},{6,7},{7,6},{8,9},{9,8},{10,11... | collective-permute-start | bytes 1179656 | tf_op jit(solution)/shard_map/ppermute | solution.py:311
  111.6 14.9 %collective-permute-start.11 = (bf16[128,1536]{1,0:T(8,128)(2,1)S(1)}, bf16[128,1536]{1,0:T(8,128)(2,1)S(1)}, u32[]{:S(2)}, u32[]{:S(2)}) collective-permute-start(bf16[128,1536]{1,0:T(8,128)(2,1)S(1)} %slice.160), channel_id=1, source_target_pairs={{0,4},{4,0},{1,5},{5,1},{2,6},{6,2},{3,7},{7,3},{8,12},{12,8},{9,1... | collective-permute-start | bytes 1179656 | tf_op jit(solution)/shard_map/ppermute | solution.py:311
  113.1 15.2 %collective-permute-start.27 = (bf16[4,96,768]{2,1,0:T(8,128)(2,1)S(1)}, bf16[4,96,768]{2,1,0:T(8,128)(2,1)S(1)}, u32[]{:S(2)}, u32[]{:S(2)}) collective-permute-start(bf16[4,96,768]{2,1,0:T(8,128)(2,1)S(1)} %copy-done.12), channel_id=1, source_target_pairs={{0,2},{2,0},{1,3},{3,1},{4,6},{6,4},{5,7},{7,5},{8,10},{10,8},{9,1... | collective-permute-start | bytes 1769480 | tf_op jit(solution)/shard_map/ppermute | solution.py:311
  133.9 19.9 %collective-permute-start.33 = (bf16[256,1536]{1,0:T(8,128)(2,1)}, bf16[256,1536]{1,0:T(8,128)(2,1)S(1)}, u32[]{:S(2)}, u32[]{:S(2)}) collective-permute-start(bf16[256,1536]{1,0:T(8,128)(2,1)} %get-tuple-element.129.refs_0_.second), channel_id=1, source_target_pairs={{0,1},{1,0},{2,3},{3,2},{4,5},{5,4},{6,7},{7,6},{8,9},{9,8},{10,11... | collective-permute-start | bytes 2359304 | tf_op jit(solution)/shard_map/ppermute | solution.py:311
  135.4 19.4 %collective-permute-start.34 = (bf16[256,1536]{1,0:T(8,128)(2,1)}, bf16[256,1536]{1,0:T(8,128)(2,1)S(1)}, u32[]{:S(2)}, u32[]{:S(2)}) collective-permute-start(bf16[256,1536]{1,0:T(8,128)(2,1)} %get-tuple-element.129.refs_0_.second), channel_id=1, source_target_pairs={{0,4},{4,0},{1,5},{5,1},{2,6},{6,2},{3,7},{7,3},{8,12},{12,8},{9,1... | collective-permute-start | bytes 2359304 | tf_op jit(solution)/shard_map/ppermute | solution.py:311
  135.9 19.5 %collective-permute-start.37 = (bf16[256,1536]{1,0:T(8,128)(2,1)S(1)}, bf16[256,1536]{1,0:T(8,128)(2,1)S(1)}, u32[]{:S(2)}, u32[]{:S(2)}) collective-permute-start(bf16[256,1536]{1,0:T(8,128)(2,1)S(1)} %copy-done.23), channel_id=1, source_target_pairs={{0,2},{2,0},{1,3},{3,1},{4,6},{6,4},{5,7},{7,5},{8,10},{10,8},{9,1... | collective-permute-start | bytes 2359304 | tf_op jit(solution)/shard_map/ppermute | solution.py:311
  135.9 20.3 %collective-permute-start.38 = (bf16[256,1536]{1,0:T(8,128)(2,1)S(1)}, bf16[256,1536]{1,0:T(8,128)(2,1)S(1)}, u32[]{:S(2)}, u32[]{:S(2)}) collective-permute-start(bf16[256,1536]{1,0:T(8,128)(2,1)S(1)} %copy-done.20), channel_id=1, source_target_pairs={{0,2},{2,0},{1,3},{3,1},{4,6},{6,4},{5,7},{7,5},{8,10},{10,8},{9,1... | collective-permute-start | bytes 2359304 | tf_op jit(solution)/shard_map/ppermute | solution.py:311
  155.3 23.6 %collective-permute-start.43 = (bf16[256,1536]{1,0:T(8,128)(2,1)}, bf16[256,1536]{1,0:T(8,128)(2,1)S(1)}, u32[]{:S(2)}, u32[]{:S(2)}) collective-permute-start(bf16[256,1536]{1,0:T(8,128)(2,1)} %constant_dynamic-update-slice_fusion.8.refs_2_), channel_id=1, source_target_pairs={{0,2},{2,0},{1,3},{3,1},{4,6},{6,4},{5,7},{7,5},{8,10},{10,8},{9,1... | collective-permute-start | bytes 2359304 | tf_op jit(solution)/shard_map/ppermute | solution.py:311
  155.4 22.9 %collective-permute-start.40 = (bf16[128,1536]{1,0:T(8,128)(2,1)S(1)}, bf16[128,1536]{1,0:T(8,128)(2,1)S(1)}, u32[]{:S(2)}, u32[]{:S(2)}) collective-permute-start(bf16[128,1536]{1,0:T(8,128)(2,1)S(1)} %slice.135), channel_id=1, source_target_pairs={{0,1},{1,0},{2,3},{3,2},{4,5},{5,4},{6,7},{7,6},{8,9},{9,8},{10,11... | collective-permute-start | bytes 1179656 | tf_op jit(solution)/shard_map/ppermute | solution.py:311
  156.3 22.0 %collective-permute-start.41 = (bf16[128,1536]{1,0:T(8,128)(2,1)S(1)}, bf16[128,1536]{1,0:T(8,128)(2,1)S(1)}, u32[]{:S(2)}, u32[]{:S(2)}) collective-permute-start(bf16[128,1536]{1,0:T(8,128)(2,1)S(1)} %slice.136), channel_id=1, source_target_pairs={{0,4},{4,0},{1,5},{5,1},{2,6},{6,2},{3,7},{7,3},{8,12},{12,8},{9,1... | collective-permute-start | bytes 1179656 | tf_op jit(solution)/shard_map/ppermute | solution.py:311
  190.5 31.6 %collective-permute-start.64 = (bf16[256,1664]{1,0:T(8,128)(2,1)}, bf16[256,1664]{1,0:T(8,128)(2,1)}, u32[]{:S(2)}, u32[]{:S(2)}) collective-permute-start(bf16[256,1664]{1,0:T(8,128)(2,1)} %get-tuple-element.164), channel_id=1, source_target_pairs={{0,2},{2,0},{1,3},{3,1},{4,6},{6,4},{5,7},{7,5},{8,10},{10,8},{9,1... | collective-permute-start | bytes 2555912 | tf_op jit(solution)/shard_map/ppermute | solution.py:311
  191.6 21.1 %collective-permute-start.62 = (bf16[128,1664]{1,0:T(8,128)(2,1)S(1)}, bf16[128,1664]{1,0:T(8,128)(2,1)S(1)}, u32[]{:S(2)}, u32[]{:S(2)}) collective-permute-start(bf16[128,1664]{1,0:T(8,128)(2,1)S(1)} %slice.180), channel_id=1, source_target_pairs={{0,1},{1,0},{2,3},{3,2},{4,5},{5,4},{6,7},{7,6},{8,9},{9,8},{10,11... | collective-permute-start | bytes 1277960 | tf_op jit(solution)/shard_map/ppermute | solution.py:311
  195.4 18.6 %collective-permute-start.63 = (bf16[128,1664]{1,0:T(8,128)(2,1)S(1)}, bf16[128,1664]{1,0:T(8,128)(2,1)S(1)}, u32[]{:S(2)}, u32[]{:S(2)}) collective-permute-start(bf16[128,1664]{1,0:T(8,128)(2,1)S(1)} %slice.181), channel_id=1, source_target_pairs={{0,4},{4,0},{1,5},{5,1},{2,6},{6,2},{3,7},{7,3},{8,12},{12,8},{9,1... | collective-permute-start | bytes 1277960 | tf_op jit(solution)/shard_map/ppermute | solution.py:311
  196.0 16.7 %collective-permute-start.45 = (bf16[128,1664]{1,0:T(8,128)(2,1)S(1)}, bf16[128,1664]{1,0:T(8,128)(2,1)S(1)}, u32[]{:S(2)}, u32[]{:S(2)}) collective-permute-start(bf16[128,1664]{1,0:T(8,128)(2,1)S(1)} %get-tuple-element.203), channel_id=1, source_target_pairs={{0,1},{1,0},{2,3},{3,2},{4,5},{5,4},{6,7},{7,6},{8,9},{9,8},{10,11... | collective-permute-start | bytes 1277960 | tf_op jit(solution)/shard_map/ppermute | solution.py:311
  220.7 14.5 %collective-permute-start.49 = (bf16[128,1664]{1,0:T(8,128)(2,1)S(1)}, bf16[128,1664]{1,0:T(8,128)(2,1)S(1)}, u32[]{:S(2)}, u32[]{:S(2)}) collective-permute-start(bf16[128,1664]{1,0:T(8,128)(2,1)S(1)} %reduce-precision_convert_fusion.7), channel_id=1, source_target_pairs={{0,1},{1,0},{2,3},{3,2},{4,5},{5,4},{6,7},{7,6},{8,9},{9,8},{10,11... | collective-permute-start | bytes 1277960 | tf_op jit(solution)/shard_map/ppermute | solution.py:311
  237.4 35.1 %collective-permute-start.50 = (bf16[512,1536]{1,0:T(8,128)(2,1)}, bf16[512,1536]{1,0:T(8,128)(2,1)S(1)}, u32[]{:S(2)}, u32[]{:S(2)}) collective-permute-start(bf16[512,1536]{1,0:T(8,128)(2,1)} %constant_dynamic-update-slice_fusion.16.refs_0_), channel_id=1, source_target_pairs={{0,1},{1,0},{2,3},{3,2},{4,5},{5,4},{6,7},{7,6},{8,9},{9,8},{10,11... | collective-permute-start | bytes 4718600 | tf_op jit(solution)/shard_map/ppermute | solution.py:311
  238.6 35.0 %collective-permute-start.51 = (bf16[512,1536]{1,0:T(8,128)(2,1)}, bf16[512,1536]{1,0:T(8,128)(2,1)S(1)}, u32[]{:S(2)}, u32[]{:S(2)}) collective-permute-start(bf16[512,1536]{1,0:T(8,128)(2,1)} %constant_dynamic-update-slice_fusion.16.refs_0_), channel_id=1, source_target_pairs={{0,4},{4,0},{1,5},{5,1},{2,6},{6,2},{3,7},{7,3},{8,12},{12,8},{9,1... | collective-permute-start | bytes 4718600 | tf_op jit(solution)/shard_map/ppermute | solution.py:311
  274.7 31.1 %all-to-all-start = ((bf16[8,272,448]{2,1,0:T(8,128)(2,1)}), bf16[8,272,448]{2,1,0:T(8,128)(2,1)S(1)}, u32[]{:S(2)}, u32[]{:S(2)}) async-start(bf16[8,272,448]{2,1,0:T(8,128)(2,1)} %constant_dynamic-update-slice_fusion.20), calls=%async_computation.1 | async-start | bytes 4456448 | tf_op jit(solution)/shard_map/all_to_all | solution.py:61
  278.4 59.1 %reduce-scatter.7.cloned.1.call-start = ((), (), s32[]{:S(2)}) async-start(), calls=%async_computation.10 | async-start | bytes 2949120 | tf_op jit(solution)/shard_map/reduce_scatter | solution.py:65
  279.1 95.9 %reduce-scatter.9.cloned.1.call-start = ((), (), s32[]{:S(2)}) async-start(), calls=%async_computation.11 | async-start | bytes 2048000 | tf_op jit(solution)/shard_map/reduce_scatter | solution.py:65
  305.8 19.4 %collective-permute-start.65 = (bf16[256,1536]{1,0:T(8,128)(2,1)}, bf16[256,1536]{1,0:T(8,128)(2,1)S(1)}, u32[]{:S(2)}, u32[]{:S(2)}) collective-permute-start(bf16[256,1536]{1,0:T(8,128)(2,1)} %slice.183), channel_id=1, source_target_pairs={{0,1},{1,0},{2,3},{3,2},{4,5},{5,4},{6,7},{7,6},{8,9},{9,8},{10,11... | collective-permute-start | bytes 2359304 | tf_op jit(solution)/shard_map/ppermute | solution.py:311
  306.8 18.9 %collective-permute-start.66 = (bf16[256,1536]{1,0:T(8,128)(2,1)S(1)}, bf16[256,1536]{1,0:T(8,128)(2,1)S(1)}, u32[]{:S(2)}, u32[]{:S(2)}) collective-permute-start(bf16[256,1536]{1,0:T(8,128)(2,1)S(1)} %slice.184), channel_id=1, source_target_pairs={{0,4},{4,0},{1,5},{5,1},{2,6},{6,2},{3,7},{7,3},{8,12},{12,8},{9,1... | collective-permute-start | bytes 2359304 | tf_op jit(solution)/shard_map/ppermute | solution.py:311
  307.4 18.6 %collective-permute-start.67 = (bf16[512,1536]{1,0:T(8,128)(2,1)}, bf16[512,1536]{1,0:T(8,128)(2,1)S(1)}, u32[]{:S(2)}, u32[]{:S(2)}) collective-permute-start(bf16[512,1536]{1,0:T(8,128)(2,1)} %constant_dynamic-update-slice_fusion.16.refs_0_), channel_id=1, source_target_pairs={{0,2},{2,0},{1,3},{3,1},{4,6},{6,4},{5,7},{7,5},{8,10},{10,8},{9,1... | collective-permute-start | bytes 4718600 | tf_op jit(solution)/shard_map/ppermute | solution.py:311
  307.4 18.6 %collective-permute-start.68 = (bf16[512,1536]{1,0:T(8,128)(2,1)}, bf16[512,1536]{1,0:T(8,128)(2,1)S(1)}, u32[]{:S(2)}, u32[]{:S(2)}) collective-permute-start(bf16[512,1536]{1,0:T(8,128)(2,1)} %copy-done.13), channel_id=1, source_target_pairs={{0,2},{2,0},{1,3},{3,1},{4,6},{6,4},{5,7},{7,5},{8,10},{10,8},{9,1... | collective-permute-start | bytes 4718600 | tf_op jit(solution)/shard_map/ppermute | solution.py:311
  307.9 18.1 %collective-permute-start.69 = (bf16[512,1536]{1,0:T(8,128)(2,1)}, bf16[512,1536]{1,0:T(8,128)(2,1)S(1)}, u32[]{:S(2)}, u32[]{:S(2)}) collective-permute-start(bf16[512,1536]{1,0:T(8,128)(2,1)} %copy-done.16), channel_id=1, source_target_pairs={{0,2},{2,0},{1,3},{3,1},{4,6},{6,4},{5,7},{7,5},{8,10},{10,8},{9,1... | collective-permute-start | bytes 4718600 | tf_op jit(solution)/shard_map/ppermute | solution.py:311
  346.9 47.7 %collective-permute-start.55 = (bf16[256,1536]{1,0:T(8,128)(2,1)}, bf16[256,1536]{1,0:T(8,128)(2,1)S(1)}, u32[]{:S(2)}, u32[]{:S(2)}) collective-permute-start(bf16[256,1536]{1,0:T(8,128)(2,1)} %get-tuple-element.156), channel_id=1, source_target_pairs={{0,2},{2,0},{1,3},{3,1},{4,6},{6,4},{5,7},{7,5},{8,10},{10,8},{9,1... | collective-permute-start | bytes 2359304 | tf_op jit(solution)/shard_map/ppermute | solution.py:311
  377.4 17.2 %all-to-all-start.2 = ((bf16[8,112,448]{2,1,0:T(8,128)(2,1)}), bf16[8,112,448]{2,1,0:T(8,128)(2,1)S(1)}, u32[]{:S(2)}, u32[]{:S(2)}) async-start(bf16[8,112,448]{2,1,0:T(8,128)(2,1)} %maximum_maximum_fusion), calls=%async_computation.5 | async-start | bytes 1835008 | tf_op jit(solution)/shard_map/all_to_all | solution.py:61
  381.0 75.6 %reduce-scatter.11.cloned.1.call-start = ((), (), s32[]{:S(2)}) async-start(), calls=%async_computation.12 | async-start | bytes 2949120 | tf_op jit(solution)/shard_map/reduce_scatter | solution.py:65
  381.1 17.4 %collective-permute-start.54 = (bf16[256,1536]{1,0:T(8,128)(2,1)}, bf16[256,1536]{1,0:T(8,128)(2,1)S(1)}, u32[]{:S(2)}, u32[]{:S(2)}) collective-permute-start(bf16[256,1536]{1,0:T(8,128)(2,1)} %get-tuple-element.154), channel_id=1, source_target_pairs={{0,2},{2,0},{1,3},{3,1},{4,6},{6,4},{5,7},{7,5},{8,10},{10,8},{9,1... | collective-permute-start | bytes 2359304 | tf_op jit(solution)/shard_map/ppermute | solution.py:311
  381.6 14.3 %collective-permute-start.52 = (bf16[256,1536]{1,0:T(8,128)(2,1)}, bf16[256,1536]{1,0:T(8,128)(2,1)}, u32[]{:S(2)}, u32[]{:S(2)}) collective-permute-start(bf16[256,1536]{1,0:T(8,128)(2,1)} %get-tuple-element.152), channel_id=1, source_target_pairs={{0,2},{2,0},{1,3},{3,1},{4,6},{6,4},{5,7},{7,5},{8,10},{10,8},{9,1... | collective-permute-start | bytes 2359304 | tf_op jit(solution)/shard_map/ppermute | solution.py:311
  381.7 63.0 %collective-permute-start.61 = (bf16[256,1536]{1,0:T(8,128)(2,1)}, bf16[256,1536]{1,0:T(8,128)(2,1)}, u32[]{:S(2)}, u32[]{:S(2)}) collective-permute-start(bf16[256,1536]{1,0:T(8,128)(2,1)} %get-tuple-element.158), channel_id=1, source_target_pairs={{0,2},{2,0},{1,3},{3,1},{4,6},{6,4},{5,7},{7,5},{8,10},{10,8},{9,1... | collective-permute-start | bytes 2359304 | tf_op jit(solution)/shard_map/ppermute | solution.py:311
  397.4 24.6 %collective-permute-start.53 = (bf16[128,1536]{1,0:T(8,128)(2,1)S(1)}, bf16[128,1536]{1,0:T(8,128)(2,1)S(1)}, u32[]{:S(2)}, u32[]{:S(2)}) collective-permute-start(bf16[128,1536]{1,0:T(8,128)(2,1)S(1)} %slice.174), channel_id=1, source_target_pairs={{0,1},{1,0},{2,3},{3,2},{4,5},{5,4},{6,7},{7,6},{8,9},{9,8},{10,11... | collective-permute-start | bytes 1179656 | tf_op jit(solution)/shard_map/ppermute | solution.py:311
  399.4 31.5 %collective-permute-start.58 = (bf16[128,1536]{1,0:T(8,128)(2,1)}, bf16[128,1536]{1,0:T(8,128)(2,1)}, u32[]{:S(2)}, u32[]{:S(2)}) collective-permute-start(bf16[128,1536]{1,0:T(8,128)(2,1)} %slice.177), channel_id=1, source_target_pairs={{0,4},{4,0},{1,5},{5,1},{2,6},{6,2},{3,7},{7,3},{8,12},{12,8},{9,1... | collective-permute-start | bytes 1179656 | tf_op jit(solution)/shard_map/ppermute | solution.py:311
  400.0 20.1 %collective-permute-start.59 = (bf16[128,1536]{1,0:T(8,128)(2,1)S(1)}, bf16[128,1536]{1,0:T(8,128)(2,1)S(1)}, u32[]{:S(2)}, u32[]{:S(2)}) collective-permute-start(bf16[128,1536]{1,0:T(8,128)(2,1)S(1)} %get-tuple-element.205), channel_id=1, source_target_pairs={{0,4},{4,0},{1,5},{5,1},{2,6},{6,2},{3,7},{7,3},{8,12},{12,8},{9,1... | collective-permute-start | bytes 1179656 | tf_op jit(solution)/shard_map/ppermute | solution.py:311
  407.1 19.6 %collective-permute-start.57 = (bf16[128,1536]{1,0:T(8,128)(2,1)S(1)}, bf16[128,1536]{1,0:T(8,128)(2,1)S(1)}, u32[]{:S(2)}, u32[]{:S(2)}) collective-permute-start(bf16[128,1536]{1,0:T(8,128)(2,1)S(1)} %reduce-precision_convert_fusion.10), channel_id=1, source_target_pairs={{0,4},{4,0},{1,5},{5,1},{2,6},{6,2},{3,7},{7,3},{8,12},{12,8},{9,1... | collective-permute-start | bytes 1179656 | tf_op jit(solution)/shard_map/ppermute | solution.py:311
  426.8 13.8 %all-to-all-start.3 = ((bf16[4,96,768]{2,1,0:T(8,128)(2,1)}), bf16[4,96,768]{2,1,0:T(8,128)(2,1)}, u32[]{:S(2)}, u32[]{:S(2)}) async-start(bf16[4,96,768]{2,1,0:T(8,128)(2,1)} %bitcast.41), calls=%async_computation.6 | async-start | bytes 1179648 | tf_op jit(solution)/shard_map/all_to_all | solution.py:61
  440.5 13.8 %all-to-all-start.1 = ((bf16[4,96,768]{2,1,0:T(8,128)(2,1)}), bf16[4,96,768]{2,1,0:T(8,128)(2,1)}, u32[]{:S(2)}, u32[]{:S(2)}) async-start(bf16[4,96,768]{2,1,0:T(8,128)(2,1)} %bitcast.88), calls=%async_computation.2 | async-start | bytes 1179648 | tf_op jit(solution)/shard_map/all_to_all | solution.py:61
  (104 other events, 1212.3 us)
Sparse Core Ops, SparseCore 0:
  220.9 47.9 reduce-scatter.4
  281.5 49.9 reduce-scatter.6
  337.6 37.3 reduce-scatter.8
  394.7 45.6 reduce-scatter.10

commit v2 on v1

--- a/solution.py
+++ b/solution.py
@@ -517,12 +517,14 @@
             outs[n][part * block : (part + 1) * block] = tokens.astype(jnp.bfloat16)
 
 
-def expert_kernel(capacity, pieces, at, ids, router, *refs):
+def expert_kernel(capacity, pieces, earlier, at, ids, router, *refs):
     count = len(pieces)
     second, cot = refs[:count], refs[count : 2 * count]
     gate_w, up_w, down_w = refs[2 * count : 2 * count + 3]
-    rows_in, rows_cot, gated_ref, gate_back, up_back, gates_ref = refs[2 * count + 3 : 2 * count + 9]
-    backs, gate_rows = refs[2 * count + 9 : -1], refs[-1]
+    before = refs[2 * count + 3 : 2 * count + 3 + 2 * earlier]
+    refs = refs[2 * count + 3 + 2 * earlier :]
+    rows_in, rows_cot, gated_ref, gate_back, up_back, gates_ref = refs[:6]
+    backs, gate_rows = refs[6 : 6 + count], refs[-1]
     f32, bf16 = jnp.float32, jnp.bfloat16
     length, width = second[0].shape
     wide = router.shape[1]
@@ -576,9 +578,14 @@
     by_rows = ((1,), (1,))
     rows = dot(gate_back[...], gate_w[...], by_rows) + dot(up_back[...], up_w[...], by_rows)
     spread(picks, capacity, jnp.concatenate([rows, signal], axis=1), backs)
-
-
-def run_expert(pieces, at, ids, router, weights, second, cot, capacity):
+    if earlier:
+        lefts = [ref[...] for ref in (*before[:earlier], rows_cot)]
+        rights = [ref[...] for ref in (*before[earlier:], gated_ref)]
+        total = dot(jnp.concatenate(lefts, axis=0), jnp.concatenate(rights, axis=0), ((0,), (0,)))
+        refs[6 + count][...] = total.astype(bf16)
+
+
+def run_expert(pieces, at, ids, router, weights, second, cot, capacity, before=()):
     count = len(pieces)
     rows, wide = 2 * count * capacity, router.shape[1]
     (length, width), hidden = second[0].shape, weights[0].shape[1]
@@ -586,13 +593,15 @@
     outs = [(rows, width)] * 2 + [(rows, hidden)] * 3
     outs = [(shape, bf16) for shape in outs] + [((wide, length), f32)]
     outs = outs + [((length, width + wide), bf16)] * count
+    if before:
+        outs = outs + [((width, hidden), bf16)]
     return run_kernel(
-        functools.partial(expert_kernel, capacity, pieces),
+        functools.partial(expert_kernel, capacity, pieces, len(before) // 2),
         4 * count,
         at,
-        (ids, router, *second, *cot, *weights),
+        (ids, router, *second, *cot, *weights, *before),
         outs,
-        6 + 4 * count,
+        6 + 4 * count + 5 * len(before) // 2,
         [pltpu.VMEM((rows, 1), f32)],
     )
 
@@ -882,9 +891,10 @@
     groups = ((0, 4), (1, 5, 2, 6), (3, 7))
     second_pieces = {0: second_in, 4: swap(second_in, "c")}
 
-    def run_group(pieces):
+    def run_group(pieces, before=()):
         return expert(
             pieces,
+            before=before,
             second=[second_pieces[piece] for piece in pieces],
             cot=[cot_pieces[piece] for piece in pieces],
         )
@@ -901,21 +911,20 @@
     x_near, x_far, y_near, y_far = stage_sides[6:]
     back_x, back_y = over_core(x_near, x_far), over_core(y_near, y_far)
     first_x, first_y = early_sums(back_x, back_y)
-    stage_corner = run_group(groups[2])
+    two = (stage_own, stage_sides)
+    stage_corner = run_group(groups[2], [stage[1] for stage in two] + [stage[2] for stage in two])
+    *stage_corner, down_part = stage_corner
     corner = over_core(*stage_corner[6:])
     passed = corner_first(corner)
     stages = (stage_own, stage_sides, stage_corner)
     rows_in, rows_cot, gated, gate_back, up_back = ([stage[n] for stage in stages] for n in range(5))
     gates = stage_own[5]
     last_y, last_x, *sent = corner_last(back_x, back_y, passed)
-    (down_part,) = row_sums(
-        at, [after(rows_cot[0], *sent, first_x, first_y)] + rows_cot[1:], gated
-    )
     down_sum = scatter_sum(down_part, "z")
     gate_part, up_part = row_sums(
-        at, [after(rows_in[0], down_part, own_far)] + rows_in[1:], gate_back, up_back
-    )
-    gate_sum = scatter_sum(gate_part, "z")
+        at, [after(rows_in[0], *sent, own_far)] + rows_in[1:], gate_back, up_back
+    )
+    gate_sum, up_sum = scatter_sum(gate_part, "z"), scatter_sum(up_part, "z")
     own_near = after(own_near, gate_part)
 
     resid_grad, branch_grad, attended_grad, router_acc, gain_two_grad = run_kernel(
@@ -998,13 +1007,23 @@
     )
     back_cols = lax.dynamic_update_slice(back_cols, narrow_part, (0, length, 0))
     back_cols = exchange(after(back_cols, down_sum, *both_sides), PLANE)
-    both_corner = plane_corner(both_sides, (back_cols,))
+    shares = run_kernel(
+        functools.partial(mixture_kernel, capacity, groups),
+        10,
+        at,
+        (ids_all, after(gated[0], *both_sides), *gated[1:], down_w),
+        [((length, model_width), bf16)] * plane,
+        56,
+    )
+    sides, shares = lax.optimization_barrier((both_sides, shares))
+    both_corner = plane_corner(sides, (back_cols,))
     both_pieces = plane_pieces(both, both_sides, both_corner)
     def placed(total):
         total = exchange(total, ("y", "c"))
         return total.reshape(local_count, shard_rows, hidden_width).astype(f32)
 
     down_grad, gate_grad = placed(down_sum), placed(gate_sum)
+    back_cols, down_grad = lax.optimization_barrier((back_cols, down_grad))
     kept_rows = -(-narrow_rows // 16) * 16
     wide_rows = local_count * shard_rows
     dense_shape = (depth, wide_rows + kept_rows, dense_cols)
@@ -1019,9 +1038,20 @@
         ],
         cost_estimate=cost(8),
         compiler_params=pltpu.CompilerParams(vmem_limit_bytes=32 * 2**20),
-    )(at, after(back_cols, down_grad), *both_pieces)
-    dense_part = after(dense_part, gate_sum)
+    )(at, back_cols, *both_pieces)
+    dense_part, gate_grad, up_sum = lax.optimization_barrier((dense_part, gate_grad, up_sum))
     dense_sum = scatter_sum(dense_part.reshape(-1, dense_cols), "z")
+    mixed = [over_core(near, far) for near, far in zip(shares[:4], shares[4:])]
+    early = early_sums(mixed[1], mixed[2])
+    last = corner_last(mixed[1], mixed[2], corner_first(mixed[3]))[:2]
+    mixture = jnp.concatenate(
+        [left.astype(f32) + right.astype(f32) for left, right in zip(early, last)], axis=0
+    )
+    block_out = (resid + (mixture + mixed[0].astype(f32))).astype(bf16)
+
+    dense_sum, up_grad, block_out = lax.optimization_barrier(
+        (dense_sum, placed(up_sum), block_out)
+    )
     wide_sum = dense_sum[: local_count * shard_rows].reshape(2, 2, 1, shard_rows, dense_cols)
     wide_sum = jnp.broadcast_to(wide_sum, (2, 2, owners, shard_rows, dense_cols)).reshape(
         plane, shard_rows, dense_cols
@@ -1049,24 +1079,6 @@
     narrow_sum = narrow_sum[y, c, :, :narrow_len].reshape(owners, shard_rows, -1)
     narrow_sum = jnp.moveaxis(narrow_sum, 0, 1).reshape(shard_rows, narrow_cols).astype(f32)
 
-    up_sum = scatter_sum(after(up_part, dense_sum), "z")
-
-    shares = run_kernel(
-        functools.partial(mixture_kernel, capacity, groups),
-        10,
-        at,
-        (ids_all, after(gated[0], *both_sides), *gated[1:], down_w),
-        [((length, model_width), bf16)] * plane,
-        56,
-    )
-    mixed = [over_core(near, far) for near, far in zip(shares[:4], shares[4:])]
-    early = early_sums(mixed[1], mixed[2])
-    last = corner_last(mixed[1], mixed[2], corner_first(mixed[3]))[:2]
-    mixture = jnp.concatenate(
-        [left.astype(f32) + right.astype(f32) for left, right in zip(early, last)], axis=0
-    )
-    block_out = (resid + (mixture + mixed[0].astype(f32))).astype(bf16)
-
     return (
         block_out,
         tokens_grad,
@@ -1078,7 +1090,7 @@
         narrow_sum[:, experts_all + 1],
         narrow_sum[:, :experts_all],
         gate_grad,
-        placed(up_sum),
+        up_grad,
         jnp.swapaxes(down_grad, 1, 2),
     )
 

time: 486 us -> 473 us (0.973)
  waiting for transfers between devices: 207 us -> 179 us
  local copies, waits for them, and re-layouts: 59.9 us -> 74.7 us
    reduce_scatter x4, waiting for transfers between devices: 28 us -> 0.03 us  [scatter_sum(): return lax.psum_scatter(block, axes, scatter_dimension=0, tiled=True)]
    unnamed x158 -> x192, local copies, waits for them, and re-layouts: 28.9 us -> 43.1 us
    all_to_all x5, waiting for transfers between devices: 55.2 us -> 48 us  [exchange(): return lax.all_to_all(block, axes, split_axis=0, concat_axis=0, tiled=True)]
    ppermute x65, waiting for transfers between devices: 105 us -> 112 us  [swap(): return lax.ppermute(block, axis, [(0, 1), (1, 0)])]
    pallas_call x12 -> x11, Pallas kernels: 99.9 us -> 96.5 us  [run_kernel(): pl.pallas_call(kernel, out_shape=[jax.ShapeDtypeStruct(shape, dtype) for...]
  transfers between devices with their start and end apart: 80 -> 80, of which waited for: 35 -> 35; matrix products, arithmetic and copies ran while one was open for 11% -> 12% of each run, Pallas kernels for 22% -> 19%
where the time goes in v2:
time: 473 us; the launch traced here: 464 us
  waiting for transfers between devices  179 us (38%)
  Pallas kernels  103 us (22%)
  local copies, waits for them, and re-layouts  74.7 us (16%)
  starting transfers between devices  68.7 us (15%)
  other arithmetic  22.8 us (5%)
  between operations  16.1 us (3%)
    ppermute x65, waiting for transfers between devices, swap(): return lax.ppermute(block, axis, [(0, 1), (1, 0)])  112 us
    pallas_call x11, Pallas kernels, run_kernel(): pl.pallas_call(kernel, out_shape=[jax.ShapeDtypeStruct(shape, dtype) for...  96.5 us
    all_to_all x5, waiting for transfers between devices, exchange(): return lax.all_to_all(block, axes, split_axis=0, concat_axis=0, tiled=True)  48 us
    unnamed x192, local copies, waits for them, and re-layouts  43.1 us
    ppermute x65, starting transfers between devices, swap(): return lax.ppermute(block, axis, [(0, 1), (1, 0)])  39 us
    all_to_all x5, starting transfers between devices, exchange(): return lax.all_to_all(block, axes, split_axis=0, concat_axis=0, tiled=True)  18.9 us
    ppermute x6, waiting for transfers between devices, shifts(): lax.ppermute(block, 'z', [(i, (i + k) % depth) for i in range(depth)])  18.3 us
    ppermute x6, starting transfers between devices, shifts(): lax.ppermute(block, 'z', [(i, (i + k) % depth) for i in range(depth)])  10.2 us
  transfers between devices with their start and end apart: 80, of which 35 were waited for; matrix products, arithmetic and copies ran while one was open for 12% of the time, Pallas kernels for 19%

profile of v2, /device:TPU:0, one launch (start us, length us, event | category | flops | bytes accessed | tf_op | source)
XLA Modules:
  0.0 464.5 jit_solution(5189585171904157560)
XLA Ops:
  8.1 5.1 %collective-permute-start.3 = (bf16[96,128]{1,0:T(8,128)(2,1)S(1)}, bf16[96,128]{1,0:T(8,128)(2,1)S(1)}, u32[]{:S(2)}, u32[]{:S(2)}) collective-permute-start(bf16[96,128]{1,0:T(8,128)(2,1)S(1)} %pad.9), channel_id=1, source_target_pairs={{0,24},{8,0},{16,8},{24,16},{1,25},{9,1},{17,9},{25,17},{2,26},{10... | collective-permute-start | bytes 73736 | tf_op jit(solution)/shard_map/ppermute | solution.py:317
  18.2 2.8 collective-permute-start.14
  26.1 2.7 collective-permute-done.6
  33.0 18.3 %collective-permute-done.13 = bf16[96,1792]{1,0:T(8,128)(2,1)} collective-permute-done((bf16[96,1792]{1,0:T(8,128)(2,1)}, bf16[96,1792]{1,0:T(8,128)(2,1)}, u32[]{:S(2)}, u32[]{:S(2)}) %collective-permute-start.13) | collective-permute-done | bytes 344096 | tf_op jit(solution)/shard_map/ppermute | solution.py:317
  61.7 4.1 dynamic-slice_bitcast_fusion.1.refs_5_.refs_9_
  65.8 3.2 dynamic-slice_bitcast_fusion.2.refs_4_.refs_8_
  69.0 6.7 %collective-permute-done.16.refs_2_ = bf16[4,96,1024]{2,1,0:T(8,128)(2,1)} collective-permute-done((bf16[4,96,1024]{2,1,0:T(8,128)(2,1)S(1)}, bf16[4,96,1024]{2,1,0:T(8,128)(2,1)}, u32[]{:S(2)}, u32[]{:S(2)}) %collective-permute-start.16) | collective-permute-done | bytes 786464 | tf_op jit(solution)/shard_map/ppermute | solution.py:311
  80.4 5.3 %collective-permute-done.17 = bf16[2,96,1024]{2,1,0:T(8,128)(2,1)S(1)} collective-permute-done((bf16[2,96,1024]{2,1,0:T(8,128)(2,1)S(1)}, bf16[2,96,1024]{2,1,0:T(8,128)(2,1)S(1)}, u32[]{:S(2)}, u32[]{:S(2)}) %collective-permute-start.17) | collective-permute-done | bytes 393248 | tf_op jit(solution)/shard_map/ppermute | solution.py:311
  95.8 9.0 %shard_map.229 = (bf16[256,1536]{1,0:T(8,128)(2,1)S(1)}, bf16[256,1536]{1,0:T(8,128)(2,1)S(1)}, bf16[256,256]{1,0:T(8,128)(2,1)S(1)}, bf16[256,256]{1,0:T(8,128)...) custom-call(s32[7]{0:T(128)S(1)} %copy-done.42, ...), custom_call_target="tpu_custom_call" | custom-call | flops 11000000512 | bytes 11000000 | tf_op jit(solution)/shard_map/pallas_call | solution.py:400
  104.8 2.7 copy-done.53
  113.1 5.7 %collective-permute-done.25 = bf16[2,96,768]{2,1,0:T(8,128)(2,1)S(1)} collective-permute-done((bf16[2,96,768]{2,1,0:T(8,128)(2,1)S(1)}, bf16[2,96,768]{2,1,0:T(8,128)(2,1)S(1)}, u32[]{:S(2)}, u32[]{:S(2)}) %collective-permute-start.25) | collective-permute-done | bytes 294944 | tf_op jit(solution)/shard_map/ppermute | solution.py:311
  119.4 6.7 %collective-permute-done.10 = bf16[128,1536]{1,0:T(8,128)(2,1)S(1)} collective-permute-done((bf16[128,1536]{1,0:T(8,128)(2,1)S(1)}, bf16[128,1536]{1,0:T(8,128)(2,1)S(1)}, u32[]{:S(2)}, u32[]{:S(2)}) %collective-permute-start.10) | collective-permute-done | bytes 393248 | tf_op jit(solution)/shard_map/ppermute | solution.py:311
  128.3 4.1 shard_map.230
  136.4 9.5 %shard_map.231 = (bf16[384,1536]{1,0:T(8,128)(2,1)S(1)}, bf16[384,1536]{1,0:T(8,128)(2,1)S(1)}, bf16[384,768]{1,0:T(8,128)(2,1)S(1)}, bf16[384,768]{1,0:T(8,128)...) custom-call(s32[7]{0:T(128)S(1)} %copy-done.43, ...), custom_call_target="tpu_custom_call" | custom-call | flops 8000000000 | bytes 8000000 | tf_op jit(solution)/shard_map/pallas_call | solution.py:400
  148.5 5.3 %collective-permute-done.33.refs_0_ = bf16[256,1536]{1,0:T(8,128)(2,1)S(1)} collective-permute-done((bf16[256,1536]{1,0:T(8,128)(2,1)}, bf16[256,1536]{1,0:T(8,128)(2,1)S(1)}, u32[]{:S(2)}, u32[]{:S(2)}) %collective-permute-start.33) | collective-permute-done | bytes 786464 | tf_op jit(solution)/shard_map/ppermute | solution.py:311
  157.0 2.2 collective-permute-done.36.refs_3_
  159.3 16.2 %shard_map.232 = (bf16[768,1536]{1,0:T(8,128)(2,1)S(1)}, bf16[768,1536]{1,0:T(8,128)(2,1)S(1)}, bf16[768,768]{1,0:T(8,128)(2,1)S(1)}, bf16[768,768]{1,0:T(8,128)...) custom-call(s32[7]{0:T(128)S(1)} %copy-done.43, ...), custom_call_target="tpu_custom_call" | custom-call | flops 16000000000 | bytes 16000000 | tf_op jit(solution)/shard_map/pallas_call | solution.py:400
  181.1 2.2 collective-permute-done.42.refs_1_
  183.3 13.3 %shard_map.233 = (bf16[384,1536]{1,0:T(8,128)(2,1)S(1)}, bf16[384,1536]{1,0:T(8,128)(2,1)}, bf16[384,768]{1,0:T(8,128)(2,1)S(1)}, bf16[384,768]{1,0:T(8,128)(2,1...) custom-call(s32[7]{0:T(128)S(1)} %copy-done.43, ...), custom_call_target="tpu_custom_call" | custom-call | flops 8000000000 | bytes 8000000 | tf_op jit(solution)/shard_map/pallas_call | solution.py:400
  206.5 2.2 collective-permute-done.44
  211.0 9.9 %collective-permute-done.47 = bf16[128,1664]{1,0:T(8,128)(2,1)S(1)} collective-permute-done((bf16[128,1664]{1,0:T(8,128)(2,1)S(1)}, bf16[128,1664]{1,0:T(8,128)(2,1)S(1)}, u32[]{:S(2)}, u32[]{:S(2)}) %collective-permute-start.47) | collective-permute-done | bytes 426016 | tf_op jit(solution)/shard_map/ppermute | solution.py:311
  223.1 12.7 %shard_map.234 = (bf16[1536,768]{1,0:T(8,128)(2,1)}, bf16[1536,768]{1,0:T(8,128)(2,1)}) custom-call(s32[7]{0:T(128)} %stack.76.at, bf16[384,1536]{1,0:T(8,128)(2,1)} %copy-done.61, bf16[768,1536]{1,0:T(8,128)(2,1)} %copy-done.60, bf16[384,1536]{1,0:T(8,128)(2,1)} %copy-done.59, bf16[384,768]{1,0:T(8,128)(2,1)} %copy-done.69, bf16[768,768]{1,0:T(8,128)(2,1)} %copy-done.67, ...), custom_call_target="tpu_custom_call" | custom-call | flops 8000000000 | bytes 8000000 | tf_op jit(solution)/shard_map/pallas_call | solution.py:400
  241.1 7.6 %collective-permute-done.52.last_x = bf16[128,1664]{1,0:T(8,128)(2,1)S(1)} collective-permute-done((bf16[128,1664]{1,0:T(8,128)(2,1)S(1)}, bf16[128,1664]{1,0:T(8,128)(2,1)S(1)}, u32[]{:S(2)}, u32[]{:S(2)}) %collective-permute-start.52) | collective-permute-done | bytes 426016 | tf_op jit(solution)/shard_map/ppermute | solution.py:311
  253.6 4.1 collective-permute-done.49.first_x
  259.4 8.3 %shard_map.235 = (f32[256,1536]{1,0:T(8,128)}, bf16[256,1536]{1,0:T(8,128)(2,1)}, bf16[256,1536]{1,0:T(8,128)(2,1)}, f32[1536,128]{1,0:T(8,128)}, f32[1,1536]{1,0:T(1,128)}) custom-call(s32[7]{0:T(128)} %stack.76.at, bf16[256,1664]{1,0:T(8,128)(2,1)} %copy-done.56, bf16[256,1664]{1,0:T(8,128)(2,1)} %collective-permute-done.48.far, ...), custom_call_target="tpu_custom_call" | custom-call | flops 6000000000 | bytes 6000000 | tf_op jit(solution)/shard_map/pallas_call | solution.py:400
  269.6 8.5 %shard_map.236.back = bf16[8,272,448]{2,1,0:T(8,128)(2,1)} custom-call(s32[7]{0:T(128)} %stack.76.at, bf16[256,1536]{1,0:T(8,128)(2,1)} %get-tuple-element.176.attended, bf16[12,256,256]{2,1,0:T(8,128)(2,1)} %copy-done.57, bf16[256,1536]{1,0:T(8,128)(2,1)} %copy-done.62, bf16[256,256]{1,0:T(8,128)(2,1)} %copy-done.72, bf16[256,256]{1,0:T(8,128)(2,1)} %copy-done.73, ...), custom_call_target="tpu_custom_call" | custom-call | flops 6000000000 | bytes 6000000 | tf_op jit(solution)/shard_map/pallas_call | solution.py:400
  279.9 2.8 copy-done.54
  282.7 3.7 shard_map.237
  287.8 2.0 reshape.215
  292.5 3.6 all-to-all-start
  296.9 9.5 %shard_map.238 = (bf16[256,1536]{1,0:T(8,128)(2,1)}, bf16[256,1536]{1,0:T(8,128)(2,1)}, bf16[256,1536]{1,0:T(8,128)(2,1)}, bf16[256,1536]{1,0:T(8,128)(2,1)}, bf...) custom-call(s32[7]{0:T(128)} %stack.76.at, ...), custom_call_target="tpu_custom_call" | custom-call | flops 10000000000 | bytes 10000000 | tf_op jit(solution)/shard_map/pallas_call | solution.py:400
  308.1 15.5 %all-to-all-done.back = bf16[8,272,448]{2,1,0:T(8,128)(2,1)S(1)} async-done(((bf16[8,272,448]{2,1,0:T(8,128)(2,1)}), bf16[8,272,448]{2,1,0:T(8,128)(2,1)S(1)}, u32[]{:S(2)}, u32[]{:S(2)}) %all-to-all-start) | async-done | bytes 1949728 | tf_op jit(solution)/shard_map/all_to_all | solution.py:61
  325.7 17.4 %collective-permute-done.55 = bf16[256,1536]{1,0:T(8,128)(2,1)S(1)} collective-permute-done((bf16[256,1536]{1,0:T(8,128)(2,1)}, bf16[256,1536]{1,0:T(8,128)(2,1)S(1)}, u32[]{:S(2)}, u32[]{:S(2)}) %collective-permute-start.55) | collective-permute-done | bytes 786464 | tf_op jit(solution)/shard_map/ppermute | solution.py:311
  346.2 4.1 all-to-all-start.1
  350.8 2.5 reduce-precision_convert_fusion.6
  353.3 6.7 %all-to-all-done.1 = bf16[4,96,768]{2,1,0:T(8,128)(2,1)} async-done(((bf16[4,96,768]{2,1,0:T(8,128)(2,1)}), bf16[4,96,768]{2,1,0:T(8,128)(2,1)}, u32[]{:S(2)}, u32[]{:S(2)}) %all-to-all-start.1) | async-done | bytes 589856 | tf_op jit(solution)/shard_map/all_to_all | solution.py:61
  360.0 4.2 all-to-all-start.2
  365.7 2.2 convert_element_type.198
  367.9 5.8 %all-to-all-done.2 = bf16[4,96,768]{2,1,0:T(8,128)(2,1)} async-done(((bf16[4,96,768]{2,1,0:T(8,128)(2,1)}), bf16[4,96,768]{2,1,0:T(8,128)(2,1)}, u32[]{:S(2)}, u32[]{:S(2)}) %all-to-all-start.2) | async-done | bytes 589856 | tf_op jit(solution)/shard_map/all_to_all | solution.py:61
  373.7 2.3 convert_element_type.199
  379.5 6.9 %shard_map.239 = bf16[4,400,448]{2,1,0:T(8,128)(2,1)S(1)} custom-call(s32[7]{0:T(128)S(1)} %copy-done.45, bf16[8,272,448]{2,1,0:T(8,128)(2,1)S(1)} %all-to-all-done.back, bf16[512,1536]{1,0:T(8,128)(2,1)} %constant_dynamic-update-slice_fusion.16.refs_0_, bf16[512,1536]{1,0:T(8,128)(2,1)S(1)} %copy-done.22, bf16[512,1536]{1,0:T(8,128)(2,1)S(1)} %copy-done.25, ...), custom_call_target="tpu_custom_call" | custom-call | flops 8000000000 | bytes 8000000 | tf_op jit(solution)/shard_map/pallas_call | solution.py:1030
  393.8 16.9 %collective-permute-done.68 = bf16[128,1536]{1,0:T(8,128)(2,1)S(1)} collective-permute-done((bf16[128,1536]{1,0:T(8,128)(2,1)S(1)}, bf16[128,1536]{1,0:T(8,128)(2,1)S(1)}, u32[]{:S(2)}, u32[]{:S(2)}) %collective-permute-start.68) | collective-permute-done | bytes 393248 | tf_op jit(solution)/shard_map/ppermute | solution.py:311
  411.9 6.1 %collective-permute-done.66 = bf16[128,1536]{1,0:T(8,128)(2,1)S(1)} collective-permute-done((bf16[128,1536]{1,0:T(8,128)(2,1)S(1)}, bf16[128,1536]{1,0:T(8,128)(2,1)S(1)}, u32[]{:S(2)}, u32[]{:S(2)}) %collective-permute-start.66) | collective-permute-done | bytes 393248 | tf_op jit(solution)/shard_map/ppermute | solution.py:311
  420.8 3.5 all-to-all-start.3
  424.3 3.0 fusion.1
  427.3 6.5 %all-to-all-done.3 = bf16[4,96,768]{2,1,0:T(8,128)(2,1)S(1)} async-done(((bf16[4,96,768]{2,1,0:T(8,128)(2,1)}), bf16[4,96,768]{2,1,0:T(8,128)(2,1)S(1)}, u32[]{:S(2)}, u32[]{:S(2)}) %all-to-all-start.3) | async-done | bytes 589856 | tf_op jit(solution)/shard_map/all_to_all | solution.py:61
  437.3 3.6 all-to-all-start.4
  440.9 13.4 %all-to-all-done.4.sums = bf16[8,112,448]{2,1,0:T(8,128)(2,1)S(1)} async-done(((bf16[8,112,448]{2,1,0:T(8,128)(2,1)}), bf16[8,112,448]{2,1,0:T(8,128)(2,1)S(1)}, u32[]{:S(2)}, u32[]{:S(2)}) %all-to-all-start.4) | async-done | bytes 802848 | tf_op jit(solution)/shard_map/all_to_all | solution.py:61
  (418 shorter events, 127.9 us)
Async XLA Ops:
  7.2 283.6 %reduce-scatter.5.cloned.1.call-start = ((), (), s32[]{:S(2)}) async-start(), calls=%async_computation.9 | async-start | bytes 2949120 | tf_op jit(solution)/shard_map/reduce_scatter | solution.py:65
  8.1 14.2 %collective-permute-start.3 = (bf16[96,128]{1,0:T(8,128)(2,1)S(1)}, bf16[96,128]{1,0:T(8,128)(2,1)S(1)}, u32[]{:S(2)}, u32[]{:S(2)}) collective-permute-start(bf16[96,128]{1,0:T(8,128)(2,1)S(1)} %pad.9), channel_id=1, source_target_pairs={{0,24},{8,0},{16,8},{24,16},{1,25},{9,1},{17,9},{25,17},{2,26},{10... | collective-permute-start | bytes 73736 | tf_op jit(solution)/shard_map/ppermute | solution.py:317
  18.2 13.8 %collective-permute-start.14 = (bf16[96,1792]{1,0:T(8,128)(2,1)}, bf16[96,1792]{1,0:T(8,128)(2,1)}, u32[]{:S(2)}, u32[]{:S(2)}) collective-permute-start(bf16[96,1792]{1,0:T(8,128)(2,1)} %pad_maximum_fusion.3), channel_id=1, source_target_pairs={{0,24},{8,0},{16,8},{24,16},{1,25},{9,1},{17,9},{25,17},{2,26},{10... | collective-permute-start | bytes 1032200 | tf_op jit(solution)/shard_map/ppermute | solution.py:317
  21.1 30.2 %collective-permute-start.13 = (bf16[96,1792]{1,0:T(8,128)(2,1)}, bf16[96,1792]{1,0:T(8,128)(2,1)}, u32[]{:S(2)}, u32[]{:S(2)}) collective-permute-start(bf16[96,1792]{1,0:T(8,128)(2,1)} %pad_maximum_fusion.3), channel_id=1, source_target_pairs={{0,16},{8,24},{16,0},{24,8},{1,17},{9,25},{17,1},{25,9},{2,18},{10... | collective-permute-start | bytes 1032200 | tf_op jit(solution)/shard_map/ppermute | solution.py:317
  22.3 29.9 %collective-permute-start.12 = (bf16[96,1792]{1,0:T(8,128)(2,1)}, bf16[96,1792]{1,0:T(8,128)(2,1)}, u32[]{:S(2)}, u32[]{:S(2)}) collective-permute-start(bf16[96,1792]{1,0:T(8,128)(2,1)} %pad_maximum_fusion.3), channel_id=1, source_target_pairs={{0,8},{8,16},{16,24},{24,0},{1,9},{9,17},{17,25},{25,1},{2,10},{10... | collective-permute-start | bytes 1032200 | tf_op jit(solution)/shard_map/ppermute | solution.py:317
  30.5 26.5 %collective-permute-start.8 = (bf16[256,1536]{1,0:T(8,128)(2,1)}, bf16[256,1536]{1,0:T(8,128)(2,1)S(1)}, u32[]{:S(2)}, u32[]{:S(2)}) collective-permute-start(bf16[256,1536]{1,0:T(8,128)(2,1)} %cot.1), channel_id=1, source_target_pairs={{0,4},{4,0},{1,5},{5,1},{2,6},{6,2},{3,7},{7,3},{8,12},{12,8},{9,1... | collective-permute-start | bytes 2359304 | tf_op jit(solution)/shard_map/ppermute | solution.py:311
  31.1 25.9 %collective-permute-start.9 = (bf16[256,1536]{1,0:T(8,128)(2,1)}, bf16[256,1536]{1,0:T(8,128)(2,1)S(1)}, u32[]{:S(2)}, u32[]{:S(2)}) collective-permute-start(bf16[256,1536]{1,0:T(8,128)(2,1)} %cot.1), channel_id=1, source_target_pairs={{0,1},{1,0},{2,3},{3,2},{4,5},{5,4},{6,7},{7,6},{8,9},{9,8},{10,11... | collective-permute-start | bytes 2359304 | tf_op jit(solution)/shard_map/ppermute | solution.py:311
  57.0 19.7 %collective-permute-start.15 = (bf16[4,96,1024]{2,1,0:T(8,128)(2,1)S(1)}, bf16[4,96,1024]{2,1,0:T(8,128)(2,1)}, u32[]{:S(2)}, u32[]{:S(2)}) collective-permute-start(bf16[4,96,1024]{2,1,0:T(8,128)(2,1)S(1)} %pad_maximum_fusion.refs_0_), channel_id=1, source_target_pairs={{0,1},{1,0},{2,3},{3,2},{4,5},{5,4},{6,7},{7,6},{8,9},{9,8},{10,11... | collective-permute-start | bytes 2359304 | tf_op jit(solution)/shard_map/ppermute | solution.py:311
  58.4 17.3 %collective-permute-start.16 = (bf16[4,96,1024]{2,1,0:T(8,128)(2,1)S(1)}, bf16[4,96,1024]{2,1,0:T(8,128)(2,1)}, u32[]{:S(2)}, u32[]{:S(2)}) collective-permute-start(bf16[4,96,1024]{2,1,0:T(8,128)(2,1)S(1)} %pad_maximum_fusion.refs_0_), channel_id=1, source_target_pairs={{0,4},{4,0},{1,5},{5,1},{2,6},{6,2},{3,7},{7,3},{8,12},{12,8},{9,1... | collective-permute-start | bytes 2359304 | tf_op jit(solution)/shard_map/ppermute | solution.py:311
  89.7 19.0 %collective-permute-start.23 = (bf16[4,96,768]{2,1,0:T(8,128)(2,1)}, bf16[4,96,768]{2,1,0:T(8,128)(2,1)S(1)}, u32[]{:S(2)}, u32[]{:S(2)}) collective-permute-start(bf16[4,96,768]{2,1,0:T(8,128)(2,1)} %pad_maximum_fusion.1.refs_0_), channel_id=1, source_target_pairs={{0,1},{1,0},{2,3},{3,2},{4,5},{5,4},{6,7},{7,6},{8,9},{9,8},{10,11... | collective-permute-start | bytes 1769480 | tf_op jit(solution)/shard_map/ppermute | solution.py:311
  91.3 17.4 %collective-permute-start.24 = (bf16[4,96,768]{2,1,0:T(8,128)(2,1)}, bf16[4,96,768]{2,1,0:T(8,128)(2,1)S(1)}, u32[]{:S(2)}, u32[]{:S(2)}) collective-permute-start(bf16[4,96,768]{2,1,0:T(8,128)(2,1)} %pad_maximum_fusion.1.refs_0_), channel_id=1, source_target_pairs={{0,4},{4,0},{1,5},{5,1},{2,6},{6,2},{3,7},{7,3},{8,12},{12,8},{9,1... | collective-permute-start | bytes 1769480 | tf_op jit(solution)/shard_map/ppermute | solution.py:311
  110.4 15.7 %collective-permute-start.10 = (bf16[128,1536]{1,0:T(8,128)(2,1)S(1)}, bf16[128,1536]{1,0:T(8,128)(2,1)S(1)}, u32[]{:S(2)}, u32[]{:S(2)}) collective-permute-start(bf16[128,1536]{1,0:T(8,128)(2,1)S(1)} %slice.159), channel_id=1, source_target_pairs={{0,1},{1,0},{2,3},{3,2},{4,5},{5,4},{6,7},{7,6},{8,9},{9,8},{10,11... | collective-permute-start | bytes 1179656 | tf_op jit(solution)/shard_map/ppermute | solution.py:311
  111.5 14.9 %collective-permute-start.11 = (bf16[128,1536]{1,0:T(8,128)(2,1)S(1)}, bf16[128,1536]{1,0:T(8,128)(2,1)S(1)}, u32[]{:S(2)}, u32[]{:S(2)}) collective-permute-start(bf16[128,1536]{1,0:T(8,128)(2,1)S(1)} %slice.160), channel_id=1, source_target_pairs={{0,4},{4,0},{1,5},{5,1},{2,6},{6,2},{3,7},{7,3},{8,12},{12,8},{9,1... | collective-permute-start | bytes 1179656 | tf_op jit(solution)/shard_map/ppermute | solution.py:311
  113.1 15.2 %collective-permute-start.27 = (bf16[4,96,768]{2,1,0:T(8,128)(2,1)S(1)}, bf16[4,96,768]{2,1,0:T(8,128)(2,1)S(1)}, u32[]{:S(2)}, u32[]{:S(2)}) collective-permute-start(bf16[4,96,768]{2,1,0:T(8,128)(2,1)S(1)} %copy-done.19), channel_id=1, source_target_pairs={{0,2},{2,0},{1,3},{3,1},{4,6},{6,4},{5,7},{7,5},{8,10},{10,8},{9,1... | collective-permute-start | bytes 1769480 | tf_op jit(solution)/shard_map/ppermute | solution.py:311
  133.9 19.9 %collective-permute-start.33 = (bf16[256,1536]{1,0:T(8,128)(2,1)}, bf16[256,1536]{1,0:T(8,128)(2,1)S(1)}, u32[]{:S(2)}, u32[]{:S(2)}) collective-permute-start(bf16[256,1536]{1,0:T(8,128)(2,1)} %get-tuple-element.142.refs_0_.second), channel_id=1, source_target_pairs={{0,1},{1,0},{2,3},{3,2},{4,5},{5,4},{6,7},{7,6},{8,9},{9,8},{10,11... | collective-permute-start | bytes 2359304 | tf_op jit(solution)/shard_map/ppermute | solution.py:311
  135.4 19.4 %collective-permute-start.34 = (bf16[256,1536]{1,0:T(8,128)(2,1)}, bf16[256,1536]{1,0:T(8,128)(2,1)S(1)}, u32[]{:S(2)}, u32[]{:S(2)}) collective-permute-start(bf16[256,1536]{1,0:T(8,128)(2,1)} %get-tuple-element.142.refs_0_.second), channel_id=1, source_target_pairs={{0,4},{4,0},{1,5},{5,1},{2,6},{6,2},{3,7},{7,3},{8,12},{12,8},{9,1... | collective-permute-start | bytes 2359304 | tf_op jit(solution)/shard_map/ppermute | solution.py:311
  135.9 19.5 %collective-permute-start.37 = (bf16[256,1536]{1,0:T(8,128)(2,1)S(1)}, bf16[256,1536]{1,0:T(8,128)(2,1)S(1)}, u32[]{:S(2)}, u32[]{:S(2)}) collective-permute-start(bf16[256,1536]{1,0:T(8,128)(2,1)S(1)} %copy-done.31), channel_id=1, source_target_pairs={{0,2},{2,0},{1,3},{3,1},{4,6},{6,4},{5,7},{7,5},{8,10},{10,8},{9,1... | collective-permute-start | bytes 2359304 | tf_op jit(solution)/shard_map/ppermute | solution.py:311
  135.9 20.3 %collective-permute-start.38 = (bf16[256,1536]{1,0:T(8,128)(2,1)S(1)}, bf16[256,1536]{1,0:T(8,128)(2,1)S(1)}, u32[]{:S(2)}, u32[]{:S(2)}) collective-permute-start(bf16[256,1536]{1,0:T(8,128)(2,1)S(1)} %copy-done.28), channel_id=1, source_target_pairs={{0,2},{2,0},{1,3},{3,1},{4,6},{6,4},{5,7},{7,5},{8,10},{10,8},{9,1... | collective-permute-start | bytes 2359304 | tf_op jit(solution)/shard_map/ppermute | solution.py:311
  155.3 25.8 %collective-permute-start.43 = (bf16[256,1536]{1,0:T(8,128)(2,1)}, bf16[256,1536]{1,0:T(8,128)(2,1)S(1)}, u32[]{:S(2)}, u32[]{:S(2)}) collective-permute-start(bf16[256,1536]{1,0:T(8,128)(2,1)} %constant_dynamic-update-slice_fusion.8.refs_2_), channel_id=1, source_target_pairs={{0,2},{2,0},{1,3},{3,1},{4,6},{6,4},{5,7},{7,5},{8,10},{10,8},{9,1... | collective-permute-start | bytes 2359304 | tf_op jit(solution)/shard_map/ppermute | solution.py:311
  155.3 25.5 %collective-permute-start.40 = (bf16[128,1536]{1,0:T(8,128)(2,1)S(1)}, bf16[128,1536]{1,0:T(8,128)(2,1)S(1)}, u32[]{:S(2)}, u32[]{:S(2)}) collective-permute-start(bf16[128,1536]{1,0:T(8,128)(2,1)S(1)} %slice.135), channel_id=1, source_target_pairs={{0,1},{1,0},{2,3},{3,2},{4,5},{5,4},{6,7},{7,6},{8,9},{9,8},{10,11... | collective-permute-start | bytes 1179656 | tf_op jit(solution)/shard_map/ppermute | solution.py:311
  156.2 24.6 %collective-permute-start.41 = (bf16[128,1536]{1,0:T(8,128)(2,1)S(1)}, bf16[128,1536]{1,0:T(8,128)(2,1)S(1)}, u32[]{:S(2)}, u32[]{:S(2)}) collective-permute-start(bf16[128,1536]{1,0:T(8,128)(2,1)S(1)} %slice.136), channel_id=1, source_target_pairs={{0,4},{4,0},{1,5},{5,1},{2,6},{6,2},{3,7},{7,3},{8,12},{12,8},{9,1... | collective-permute-start | bytes 1179656 | tf_op jit(solution)/shard_map/ppermute | solution.py:311
  203.3 156.6 %reduce-scatter.7.cloned.1.call-start = ((), (), s32[]{:S(2)}) async-start(), calls=%async_computation.10 | async-start | bytes 2949120 | tf_op jit(solution)/shard_map/reduce_scatter | solution.py:65
  204.1 18.9 %collective-permute-start.48 = (bf16[256,1664]{1,0:T(8,128)(2,1)}, bf16[256,1664]{1,0:T(8,128)(2,1)}, u32[]{:S(2)}, u32[]{:S(2)}) collective-permute-start(bf16[256,1664]{1,0:T(8,128)(2,1)} %copy-done.46), channel_id=1, source_target_pairs={{0,2},{2,0},{1,3},{3,1},{4,6},{6,4},{5,7},{7,5},{8,10},{10,8},{9,1... | collective-permute-start | bytes 2555912 | tf_op jit(solution)/shard_map/ppermute | solution.py:311
  238.5 19.2 %collective-permute-start.49 = (bf16[128,1664]{1,0:T(8,128)(2,1)S(1)}, bf16[128,1664]{1,0:T(8,128)(2,1)S(1)}, u32[]{:S(2)}, u32[]{:S(2)}) collective-permute-start(bf16[128,1664]{1,0:T(8,128)(2,1)S(1)} %slice.174), channel_id=1, source_target_pairs={{0,1},{1,0},{2,3},{3,2},{4,5},{5,4},{6,7},{7,6},{8,9},{9,8},{10,11... | collective-permute-start | bytes 1277960 | tf_op jit(solution)/shard_map/ppermute | solution.py:311
  239.8 18.8 %collective-permute-start.50 = (bf16[128,1664]{1,0:T(8,128)(2,1)S(1)}, bf16[128,1664]{1,0:T(8,128)(2,1)S(1)}, u32[]{:S(2)}, u32[]{:S(2)}) collective-permute-start(bf16[128,1664]{1,0:T(8,128)(2,1)S(1)} %slice.175), channel_id=1, source_target_pairs={{0,4},{4,0},{1,5},{5,1},{2,6},{6,2},{3,7},{7,3},{8,12},{12,8},{9,1... | collective-permute-start | bytes 1277960 | tf_op jit(solution)/shard_map/ppermute | solution.py:311
  251.5 39.2 %collective-permute-start.53 = (bf16[512,1536]{1,0:T(8,128)(2,1)}, bf16[512,1536]{1,0:T(8,128)(2,1)S(1)}, u32[]{:S(2)}, u32[]{:S(2)}) collective-permute-start(bf16[512,1536]{1,0:T(8,128)(2,1)} %constant_dynamic-update-slice_fusion.16.refs_0_), channel_id=1, source_target_pairs={{0,1},{1,0},{2,3},{3,2},{4,5},{5,4},{6,7},{7,6},{8,9},{9,8},{10,11... | collective-permute-start | bytes 4718600 | tf_op jit(solution)/shard_map/ppermute | solution.py:311
  252.9 37.9 %collective-permute-start.54 = (bf16[512,1536]{1,0:T(8,128)(2,1)}, bf16[512,1536]{1,0:T(8,128)(2,1)S(1)}, u32[]{:S(2)}, u32[]{:S(2)}) collective-permute-start(bf16[512,1536]{1,0:T(8,128)(2,1)} %constant_dynamic-update-slice_fusion.16.refs_0_), channel_id=1, source_target_pairs={{0,4},{4,0},{1,5},{5,1},{2,6},{6,2},{3,7},{7,3},{8,12},{12,8},{9,1... | collective-permute-start | bytes 4718600 | tf_op jit(solution)/shard_map/ppermute | solution.py:311
  292.5 31.1 %all-to-all-start = ((bf16[8,272,448]{2,1,0:T(8,128)(2,1)}), bf16[8,272,448]{2,1,0:T(8,128)(2,1)S(1)}, u32[]{:S(2)}, u32[]{:S(2)}) async-start(bf16[8,272,448]{2,1,0:T(8,128)(2,1)} %constant_dynamic-update-slice_fusion.20), calls=%async_computation.1 | async-start | bytes 4456448 | tf_op jit(solution)/shard_map/all_to_all | solution.py:61
  296.1 91.5 %reduce-scatter.9.cloned.1.call-start = ((), (), s32[]{:S(2)}) async-start(), calls=%async_computation.11 | async-start | bytes 2949120 | tf_op jit(solution)/shard_map/reduce_scatter | solution.py:65
  323.6 19.4 %collective-permute-start.55 = (bf16[256,1536]{1,0:T(8,128)(2,1)}, bf16[256,1536]{1,0:T(8,128)(2,1)S(1)}, u32[]{:S(2)}, u32[]{:S(2)}) collective-permute-start(bf16[256,1536]{1,0:T(8,128)(2,1)} %slice.143), channel_id=1, source_target_pairs={{0,1},{1,0},{2,3},{3,2},{4,5},{5,4},{6,7},{7,6},{8,9},{9,8},{10,11... | collective-permute-start | bytes 2359304 | tf_op jit(solution)/shard_map/ppermute | solution.py:311
  324.6 18.9 %collective-permute-start.56 = (bf16[256,1536]{1,0:T(8,128)(2,1)S(1)}, bf16[256,1536]{1,0:T(8,128)(2,1)S(1)}, u32[]{:S(2)}, u32[]{:S(2)}) collective-permute-start(bf16[256,1536]{1,0:T(8,128)(2,1)S(1)} %slice.144), channel_id=1, source_target_pairs={{0,4},{4,0},{1,5},{5,1},{2,6},{6,2},{3,7},{7,3},{8,12},{12,8},{9,1... | collective-permute-start | bytes 2359304 | tf_op jit(solution)/shard_map/ppermute | solution.py:311
  325.2 20.3 %collective-permute-start.64 = (bf16[256,1536]{1,0:T(8,128)(2,1)}, bf16[256,1536]{1,0:T(8,128)(2,1)S(1)}, u32[]{:S(2)}, u32[]{:S(2)}) collective-permute-start(bf16[256,1536]{1,0:T(8,128)(2,1)} %get-tuple-element.217), channel_id=1, source_target_pairs={{0,2},{2,0},{1,3},{3,1},{4,6},{6,4},{5,7},{7,5},{8,10},{10,8},{9,1... | collective-permute-start | bytes 2359304 | tf_op jit(solution)/shard_map/ppermute | solution.py:311
  325.2 50.9 %collective-permute-start.57 = (bf16[512,1536]{1,0:T(8,128)(2,1)}, bf16[512,1536]{1,0:T(8,128)(2,1)}, u32[]{:S(2)}, u32[]{:S(2)}) collective-permute-start(bf16[512,1536]{1,0:T(8,128)(2,1)} %constant_dynamic-update-slice_fusion.16.refs_0_), channel_id=1, source_target_pairs={{0,2},{2,0},{1,3},{3,1},{4,6},{6,4},{5,7},{7,5},{8,10},{10,8},{9,1... | collective-permute-start | bytes 4718600 | tf_op jit(solution)/shard_map/ppermute | solution.py:311
  325.7 24.7 %collective-permute-start.61 = (bf16[256,1536]{1,0:T(8,128)(2,1)}, bf16[256,1536]{1,0:T(8,128)(2,1)}, u32[]{:S(2)}, u32[]{:S(2)}) collective-permute-start(bf16[256,1536]{1,0:T(8,128)(2,1)} %get-tuple-element.213), channel_id=1, source_target_pairs={{0,2},{2,0},{1,3},{3,1},{4,6},{6,4},{5,7},{7,5},{8,10},{10,8},{9,1... | collective-permute-start | bytes 2359304 | tf_op jit(solution)/shard_map/ppermute | solution.py:311
  343.0 33.0 %collective-permute-start.58 = (bf16[512,1536]{1,0:T(8,128)(2,1)}, bf16[512,1536]{1,0:T(8,128)(2,1)}, u32[]{:S(2)}, u32[]{:S(2)}) collective-permute-start(bf16[512,1536]{1,0:T(8,128)(2,1)} %copy-done.20), channel_id=1, source_target_pairs={{0,2},{2,0},{1,3},{3,1},{4,6},{6,4},{5,7},{7,5},{8,10},{10,8},{9,1... | collective-permute-start | bytes 4718600 | tf_op jit(solution)/shard_map/ppermute | solution.py:311
  343.5 33.6 %collective-permute-start.59 = (bf16[512,1536]{1,0:T(8,128)(2,1)}, bf16[512,1536]{1,0:T(8,128)(2,1)}, u32[]{:S(2)}, u32[]{:S(2)}) collective-permute-start(bf16[512,1536]{1,0:T(8,128)(2,1)} %copy-done.23), channel_id=1, source_target_pairs={{0,2},{2,0},{1,3},{3,1},{4,6},{6,4},{5,7},{7,5},{8,10},{10,8},{9,1... | collective-permute-start | bytes 4718600 | tf_op jit(solution)/shard_map/ppermute | solution.py:311
  345.4 32.7 %collective-permute-start.60 = (bf16[512,1536]{1,0:T(8,128)(2,1)}, bf16[512,1536]{1,0:T(8,128)(2,1)}, u32[]{:S(2)}, u32[]{:S(2)}) collective-permute-start(bf16[512,1536]{1,0:T(8,128)(2,1)} %constant_dynamic-update-slice_fusion.18.refs_3_), channel_id=1, source_target_pairs={{0,2},{2,0},{1,3},{3,1},{4,6},{6,4},{5,7},{7,5},{8,10},{10,8},{9,1... | collective-permute-start | bytes 4718600 | tf_op jit(solution)/shard_map/ppermute | solution.py:311
  346.2 13.8 %all-to-all-start.1 = ((bf16[4,96,768]{2,1,0:T(8,128)(2,1)}), bf16[4,96,768]{2,1,0:T(8,128)(2,1)}, u32[]{:S(2)}, u32[]{:S(2)}) async-start(bf16[4,96,768]{2,1,0:T(8,128)(2,1)} %bitcast.88), calls=%async_computation.2 | async-start | bytes 1179648 | tf_op jit(solution)/shard_map/all_to_all | solution.py:61
  350.4 37.3 %collective-permute-start.63 = (bf16[256,1536]{1,0:T(8,128)(2,1)}, bf16[256,1536]{1,0:T(8,128)(2,1)}, u32[]{:S(2)}, u32[]{:S(2)}) collective-permute-start(bf16[256,1536]{1,0:T(8,128)(2,1)} %get-tuple-element.215), channel_id=1, source_target_pairs={{0,2},{2,0},{1,3},{3,1},{4,6},{6,4},{5,7},{7,5},{8,10},{10,8},{9,1... | collective-permute-start | bytes 2359304 | tf_op jit(solution)/shard_map/ppermute | solution.py:311
  360.0 13.8 %all-to-all-start.2 = ((bf16[4,96,768]{2,1,0:T(8,128)(2,1)}), bf16[4,96,768]{2,1,0:T(8,128)(2,1)}, u32[]{:S(2)}, u32[]{:S(2)}) async-start(bf16[4,96,768]{2,1,0:T(8,128)(2,1)} %bitcast.89), calls=%async_computation.4 | async-start | bytes 1179648 | tf_op jit(solution)/shard_map/all_to_all | solution.py:61
  364.1 70.8 %reduce-scatter.11.cloned.1.call-start = ((), (), s32[]{:S(2)}) async-start(), calls=%async_computation.12 | async-start | bytes 2048000 | tf_op jit(solution)/shard_map/reduce_scatter | solution.py:65
  376.0 48.3 %collective-permute-start.70 = (bf16[256,1536]{1,0:T(8,128)(2,1)}, bf16[256,1536]{1,0:T(8,128)(2,1)}, u32[]{:S(2)}, u32[]{:S(2)}) collective-permute-start(bf16[256,1536]{1,0:T(8,128)(2,1)} %get-tuple-element.219), channel_id=1, source_target_pairs={{0,2},{2,0},{1,3},{3,1},{4,6},{6,4},{5,7},{7,5},{8,10},{10,8},{9,1... | collective-permute-start | bytes 2359304 | tf_op jit(solution)/shard_map/ppermute | solution.py:311
  376.0 16.2 %collective-permute-start.65 = (bf16[128,1536]{1,0:T(8,128)(2,1)}, bf16[128,1536]{1,0:T(8,128)(2,1)}, u32[]{:S(2)}, u32[]{:S(2)}) collective-permute-start(bf16[128,1536]{1,0:T(8,128)(2,1)} %get-tuple-element.232), channel_id=1, source_target_pairs={{0,1},{1,0},{2,3},{3,2},{4,5},{5,4},{6,7},{7,6},{8,9},{9,8},{10,11... | collective-permute-start | bytes 1179656 | tf_op jit(solution)/shard_map/ppermute | solution.py:311
  377.2 34.7 %collective-permute-start.62 = (bf16[128,1536]{1,0:T(8,128)(2,1)S(1)}, bf16[128,1536]{1,0:T(8,128)(2,1)}, u32[]{:S(2)}, u32[]{:S(2)}) collective-permute-start(bf16[128,1536]{1,0:T(8,128)(2,1)S(1)} %slice.177), channel_id=1, source_target_pairs={{0,1},{1,0},{2,3},{3,2},{4,5},{5,4},{6,7},{7,6},{8,9},{9,8},{10,11... | collective-permute-start | bytes 1179656 | tf_op jit(solution)/shard_map/ppermute | solution.py:311
  390.2 28.9 %collective-permute-start.67 = (bf16[128,1536]{1,0:T(8,128)(2,1)S(1)}, bf16[128,1536]{1,0:T(8,128)(2,1)S(1)}, u32[]{:S(2)}, u32[]{:S(2)}) collective-permute-start(bf16[128,1536]{1,0:T(8,128)(2,1)S(1)} %slice.180), channel_id=1, source_target_pairs={{0,4},{4,0},{1,5},{5,1},{2,6},{6,2},{3,7},{7,3},{8,12},{12,8},{9,1... | collective-permute-start | bytes 1179656 | tf_op jit(solution)/shard_map/ppermute | solution.py:311
  390.6 20.1 %collective-permute-start.68 = (bf16[128,1536]{1,0:T(8,128)(2,1)S(1)}, bf16[128,1536]{1,0:T(8,128)(2,1)S(1)}, u32[]{:S(2)}, u32[]{:S(2)}) collective-permute-start(bf16[128,1536]{1,0:T(8,128)(2,1)S(1)} %get-tuple-element.233), channel_id=1, source_target_pairs={{0,4},{4,0},{1,5},{5,1},{2,6},{6,2},{3,7},{7,3},{8,12},{12,8},{9,1... | collective-permute-start | bytes 1179656 | tf_op jit(solution)/shard_map/ppermute | solution.py:311
  393.4 24.6 %collective-permute-start.66 = (bf16[128,1536]{1,0:T(8,128)(2,1)S(1)}, bf16[128,1536]{1,0:T(8,128)(2,1)S(1)}, u32[]{:S(2)}, u32[]{:S(2)}) collective-permute-start(bf16[128,1536]{1,0:T(8,128)(2,1)S(1)} %reduce-precision_convert_fusion.10), channel_id=1, source_target_pairs={{0,4},{4,0},{1,5},{5,1},{2,6},{6,2},{3,7},{7,3},{8,12},{12,8},{9,1... | collective-permute-start | bytes 1179656 | tf_op jit(solution)/shard_map/ppermute | solution.py:311
  437.3 17.0 %all-to-all-start.4 = ((bf16[8,112,448]{2,1,0:T(8,128)(2,1)}), bf16[8,112,448]{2,1,0:T(8,128)(2,1)S(1)}, u32[]{:S(2)}, u32[]{:S(2)}) async-start(bf16[8,112,448]{2,1,0:T(8,128)(2,1)} %maximum_maximum_fusion), calls=%async_computation.8 | async-start | bytes 1835008 | tf_op jit(solution)/shard_map/all_to_all | solution.py:61
  (121 other events, 1234.4 us)
Sparse Core Ops, SparseCore 0:
  203.5 47.9 reduce-scatter.4
  253.7 47.5 reduce-scatter.6
  303.6 47.5 reduce-scatter.8
  387.8 36.5 reduce-scatter.10

commit v3 on v2

--- a/solution.py
+++ b/solution.py
@@ -601,7 +601,7 @@
         at,
         (ids, router, *second, *cot, *weights, *before),
         outs,
-        6 + 4 * count + 5 * len(before) // 2,
+        4 + 3 * count + 4 * bool(before),
         [pltpu.VMEM((rows, 1), f32)],
     )
 
@@ -1023,7 +1023,6 @@
         return total.reshape(local_count, shard_rows, hidden_width).astype(f32)
 
     down_grad, gate_grad = placed(down_sum), placed(gate_sum)
-    back_cols, down_grad = lax.optimization_barrier((back_cols, down_grad))
     kept_rows = -(-narrow_rows // 16) * 16
     wide_rows = local_count * shard_rows
     dense_shape = (depth, wide_rows + kept_rows, dense_cols)
@@ -1039,7 +1038,7 @@
         cost_estimate=cost(8),
         compiler_params=pltpu.CompilerParams(vmem_limit_bytes=32 * 2**20),
     )(at, back_cols, *both_pieces)
-    dense_part, gate_grad, up_sum = lax.optimization_barrier((dense_part, gate_grad, up_sum))
+    dense_part, up_sum = lax.optimization_barrier((dense_part, up_sum))
     dense_sum = scatter_sum(dense_part.reshape(-1, dense_cols), "z")
     mixed = [over_core(near, far) for near, far in zip(shares[:4], shares[4:])]
     early = early_sums(mixed[1], mixed[2])
@@ -1049,8 +1048,8 @@
     )
     block_out = (resid + (mixture + mixed[0].astype(f32))).astype(bf16)
 
-    dense_sum, up_grad, block_out = lax.optimization_barrier(
-        (dense_sum, placed(up_sum), block_out)
+    dense_sum, down_grad, gate_grad, up_grad, block_out = lax.optimization_barrier(
+        (dense_sum, down_grad, gate_grad, placed(up_sum), block_out)
     )
     wide_sum = dense_sum[: local_count * shard_rows].reshape(2, 2, 1, shard_rows, dense_cols)
     wide_sum = jnp.broadcast_to(wide_sum, (2, 2, owners, shard_rows, dense_cols)).reshape(

time: 473 us -> 469 us (level)
    unnamed x192 -> x190, local copies, waits for them, and re-layouts: 43.1 us -> 40.3 us
  transfers between devices with their start and end apart: 80 -> 80, of which waited for: 35 -> 38; matrix products, arithmetic and copies ran while one was open for 12% -> 12% of each run, Pallas kernels for 19% -> 19%
where the time goes in v3:
time: 469 us; the launch traced here: 461 us
  waiting for transfers between devices  177 us (38%)
  Pallas kernels  103 us (22%)
  local copies, waits for them, and re-layouts  72.4 us (15%)
  starting transfers between devices  68.7 us (15%)
  other arithmetic  23.1 us (5%)
  between operations  15.9 us (3%)
    ppermute x65, waiting for transfers between devices, swap(): return lax.ppermute(block, axis, [(0, 1), (1, 0)])  112 us
    pallas_call x11, Pallas kernels, run_kernel(): pl.pallas_call(kernel, out_shape=[jax.ShapeDtypeStruct(shape, dtype) for...  96.4 us
    all_to_all x5, waiting for transfers between devices, exchange(): return lax.all_to_all(block, axes, split_axis=0, concat_axis=0, tiled=True)  46.1 us
    unnamed x190, local copies, waits for them, and re-layouts  40.3 us
    ppermute x65, starting transfers between devices, swap(): return lax.ppermute(block, axis, [(0, 1), (1, 0)])  39 us
    all_to_all x5, starting transfers between devices, exchange(): return lax.all_to_all(block, axes, split_axis=0, concat_axis=0, tiled=True)  18.9 us
    ppermute x6, waiting for transfers between devices, shifts(): lax.ppermute(block, 'z', [(i, (i + k) % depth) for i in range(depth)])  18.3 us
    ppermute x6, starting transfers between devices, shifts(): lax.ppermute(block, 'z', [(i, (i + k) % depth) for i in range(depth)])  10.2 us
  transfers between devices with their start and end apart: 80, of which 38 were waited for; matrix products, arithmetic and copies ran while one was open for 12% of the time, Pallas kernels for 19%

profile of v3, /device:TPU:0, one launch (start us, length us, event | category | flops | bytes accessed | tf_op | source)
XLA Modules:
  0.0 460.6 jit_solution(5949004271968648205)
XLA Ops:
  8.1 5.1 %collective-permute-start.3 = (bf16[96,128]{1,0:T(8,128)(2,1)S(1)}, bf16[96,128]{1,0:T(8,128)(2,1)S(1)}, u32[]{:S(2)}, u32[]{:S(2)}) collective-permute-start(bf16[96,128]{1,0:T(8,128)(2,1)S(1)} %pad.9), channel_id=1, source_target_pairs={{0,24},{8,0},{16,8},{24,16},{1,25},{9,1},{17,9},{25,17},{2,26},{10... | collective-permute-start | bytes 73736 | tf_op jit(solution)/shard_map/ppermute | solution.py:317
  18.2 2.8 collective-permute-start.14
  26.1 2.7 collective-permute-done.6
  33.0 18.3 %collective-permute-done.13 = bf16[96,1792]{1,0:T(8,128)(2,1)} collective-permute-done((bf16[96,1792]{1,0:T(8,128)(2,1)}, bf16[96,1792]{1,0:T(8,128)(2,1)}, u32[]{:S(2)}, u32[]{:S(2)}) %collective-permute-start.13) | collective-permute-done | bytes 344096 | tf_op jit(solution)/shard_map/ppermute | solution.py:317
  61.7 4.1 dynamic-slice_bitcast_fusion.1.refs_5_.refs_9_
  65.8 3.2 dynamic-slice_bitcast_fusion.2.refs_4_.refs_8_
  69.0 6.7 %collective-permute-done.16.refs_2_ = bf16[4,96,1024]{2,1,0:T(8,128)(2,1)} collective-permute-done((bf16[4,96,1024]{2,1,0:T(8,128)(2,1)S(1)}, bf16[4,96,1024]{2,1,0:T(8,128)(2,1)}, u32[]{:S(2)}, u32[]{:S(2)}) %collective-permute-start.16) | collective-permute-done | bytes 786464 | tf_op jit(solution)/shard_map/ppermute | solution.py:311
  80.4 5.3 %collective-permute-done.17 = bf16[2,96,1024]{2,1,0:T(8,128)(2,1)S(1)} collective-permute-done((bf16[2,96,1024]{2,1,0:T(8,128)(2,1)S(1)}, bf16[2,96,1024]{2,1,0:T(8,128)(2,1)S(1)}, u32[]{:S(2)}, u32[]{:S(2)}) %collective-permute-start.17) | collective-permute-done | bytes 393248 | tf_op jit(solution)/shard_map/ppermute | solution.py:311
  95.6 9.1 %shard_map.229 = (bf16[256,1536]{1,0:T(8,128)(2,1)S(1)}, bf16[256,1536]{1,0:T(8,128)(2,1)S(1)}, bf16[256,256]{1,0:T(8,128)(2,1)S(1)}, bf16[256,256]{1,0:T(8,128)...) custom-call(s32[7]{0:T(128)S(1)} %copy-done.42, ...), custom_call_target="tpu_custom_call" | custom-call | flops 11000000512 | bytes 11000000 | tf_op jit(solution)/shard_map/pallas_call | solution.py:400
  104.8 2.7 copy-done.54
  113.0 5.7 %collective-permute-done.25 = bf16[2,96,768]{2,1,0:T(8,128)(2,1)S(1)} collective-permute-done((bf16[2,96,768]{2,1,0:T(8,128)(2,1)S(1)}, bf16[2,96,768]{2,1,0:T(8,128)(2,1)S(1)}, u32[]{:S(2)}, u32[]{:S(2)}) %collective-permute-start.25) | collective-permute-done | bytes 294944 | tf_op jit(solution)/shard_map/ppermute | solution.py:311
  119.4 6.7 %collective-permute-done.10 = bf16[128,1536]{1,0:T(8,128)(2,1)S(1)} collective-permute-done((bf16[128,1536]{1,0:T(8,128)(2,1)S(1)}, bf16[128,1536]{1,0:T(8,128)(2,1)S(1)}, u32[]{:S(2)}, u32[]{:S(2)}) %collective-permute-start.10) | collective-permute-done | bytes 393248 | tf_op jit(solution)/shard_map/ppermute | solution.py:311
  128.2 4.1 shard_map.230
  136.4 9.5 %shard_map.231 = (bf16[384,1536]{1,0:T(8,128)(2,1)S(1)}, bf16[384,1536]{1,0:T(8,128)(2,1)S(1)}, bf16[384,768]{1,0:T(8,128)(2,1)S(1)}, bf16[384,768]{1,0:T(8,128)...) custom-call(s32[7]{0:T(128)S(1)} %copy-done.43, ...), custom_call_target="tpu_custom_call" | custom-call | flops 8000000000 | bytes 8000000 | tf_op jit(solution)/shard_map/pallas_call | solution.py:400
  148.5 5.3 %collective-permute-done.33.refs_0_ = bf16[256,1536]{1,0:T(8,128)(2,1)S(1)} collective-permute-done((bf16[256,1536]{1,0:T(8,128)(2,1)}, bf16[256,1536]{1,0:T(8,128)(2,1)S(1)}, u32[]{:S(2)}, u32[]{:S(2)}) %collective-permute-start.33) | collective-permute-done | bytes 786464 | tf_op jit(solution)/shard_map/ppermute | solution.py:311
  157.0 2.2 collective-permute-done.36.refs_3_
  159.2 16.4 %shard_map.232 = (bf16[768,1536]{1,0:T(8,128)(2,1)S(1)}, bf16[768,1536]{1,0:T(8,128)(2,1)S(1)}, bf16[768,768]{1,0:T(8,128)(2,1)S(1)}, bf16[768,768]{1,0:T(8,128)...) custom-call(s32[7]{0:T(128)S(1)} %copy-done.43, ...), custom_call_target="tpu_custom_call" | custom-call | flops 16000000000 | bytes 16000000 | tf_op jit(solution)/shard_map/pallas_call | solution.py:400
  181.2 2.2 collective-permute-done.42.refs_1_
  183.4 13.0 %shard_map.233 = (bf16[384,1536]{1,0:T(8,128)(2,1)S(1)}, bf16[384,1536]{1,0:T(8,128)(2,1)}, bf16[384,768]{1,0:T(8,128)(2,1)S(1)}, bf16[384,768]{1,0:T(8,128)(2,1...) custom-call(s32[7]{0:T(128)S(1)} %copy-done.43, ...), custom_call_target="tpu_custom_call" | custom-call | flops 8000000000 | bytes 8000000 | tf_op jit(solution)/shard_map/pallas_call | solution.py:400
  206.6 2.2 collective-permute-done.44
  211.1 9.9 %collective-permute-done.47 = bf16[128,1664]{1,0:T(8,128)(2,1)S(1)} collective-permute-done((bf16[128,1664]{1,0:T(8,128)(2,1)S(1)}, bf16[128,1664]{1,0:T(8,128)(2,1)S(1)}, u32[]{:S(2)}, u32[]{:S(2)}) %collective-permute-start.47) | collective-permute-done | bytes 426016 | tf_op jit(solution)/shard_map/ppermute | solution.py:311
  224.1 12.7 %shard_map.234 = (bf16[1536,768]{1,0:T(8,128)(2,1)}, bf16[1536,768]{1,0:T(8,128)(2,1)}) custom-call(s32[7]{0:T(128)} %stack.76.at, bf16[384,1536]{1,0:T(8,128)(2,1)} %copy-done.62, bf16[768,1536]{1,0:T(8,128)(2,1)} %copy-done.61, bf16[384,1536]{1,0:T(8,128)(2,1)} %copy-done.60, bf16[384,768]{1,0:T(8,128)(2,1)} %copy-done.70, bf16[768,768]{1,0:T(8,128)(2,1)} %copy-done.68, ...), custom_call_target="tpu_custom_call" | custom-call | flops 8000000000 | bytes 8000000 | tf_op jit(solution)/shard_map/pallas_call | solution.py:400
  242.5 7.4 %collective-permute-done.52.last_x = bf16[128,1664]{1,0:T(8,128)(2,1)} collective-permute-done((bf16[128,1664]{1,0:T(8,128)(2,1)}, bf16[128,1664]{1,0:T(8,128)(2,1)}, u32[]{:S(2)}, u32[]{:S(2)}) %collective-permute-start.52) | collective-permute-done | bytes 426016 | tf_op jit(solution)/shard_map/ppermute | solution.py:311
  254.7 4.4 collective-permute-done.49.first_x
  259.7 8.3 %shard_map.235 = (f32[256,1536]{1,0:T(8,128)}, bf16[256,1536]{1,0:T(8,128)(2,1)}, bf16[256,1536]{1,0:T(8,128)(2,1)}, f32[1536,128]{1,0:T(8,128)}, f32[1,1536]{1,0:T(1,128)}) custom-call(s32[7]{0:T(128)} %stack.76.at, bf16[256,1664]{1,0:T(8,128)(2,1)} %copy-done.57, bf16[256,1664]{1,0:T(8,128)(2,1)} %copy-done.86, ...), custom_call_target="tpu_custom_call" | custom-call | flops 6000000000 | bytes 6000000 | tf_op jit(solution)/shard_map/pallas_call | solution.py:400
  269.9 8.5 %shard_map.236.back = bf16[8,272,448]{2,1,0:T(8,128)(2,1)} custom-call(s32[7]{0:T(128)} %stack.76.at, bf16[256,1536]{1,0:T(8,128)(2,1)} %get-tuple-element.175.attended, bf16[12,256,256]{2,1,0:T(8,128)(2,1)} %copy-done.58, bf16[256,1536]{1,0:T(8,128)(2,1)} %copy-done.63, bf16[256,256]{1,0:T(8,128)(2,1)} %copy-done.73, bf16[256,256]{1,0:T(8,128)(2,1)} %copy-done.74, ...), custom_call_target="tpu_custom_call" | custom-call | flops 6000000000 | bytes 6000000 | tf_op jit(solution)/shard_map/pallas_call | solution.py:400
  280.1 2.8 copy-done.55
  282.9 3.7 shard_map.237
  288.0 2.0 reshape.215
  292.8 3.6 all-to-all-start
  297.2 9.5 %shard_map.238 = (bf16[256,1536]{1,0:T(8,128)(2,1)}, bf16[256,1536]{1,0:T(8,128)(2,1)}, bf16[256,1536]{1,0:T(8,128)(2,1)}, bf16[256,1536]{1,0:T(8,128)(2,1)}, bf...) custom-call(s32[7]{0:T(128)} %stack.76.at, ...), custom_call_target="tpu_custom_call" | custom-call | flops 10000000000 | bytes 10000000 | tf_op jit(solution)/shard_map/pallas_call | solution.py:400
  308.4 15.5 %all-to-all-done.back = bf16[8,272,448]{2,1,0:T(8,128)(2,1)S(1)} async-done(((bf16[8,272,448]{2,1,0:T(8,128)(2,1)}), bf16[8,272,448]{2,1,0:T(8,128)(2,1)S(1)}, u32[]{:S(2)}, u32[]{:S(2)}) %all-to-all-start) | async-done | bytes 1949728 | tf_op jit(solution)/shard_map/all_to_all | solution.py:61
  326.0 17.4 %collective-permute-done.55 = bf16[256,1536]{1,0:T(8,128)(2,1)S(1)} collective-permute-done((bf16[256,1536]{1,0:T(8,128)(2,1)}, bf16[256,1536]{1,0:T(8,128)(2,1)S(1)}, u32[]{:S(2)}, u32[]{:S(2)}) %collective-permute-start.55) | collective-permute-done | bytes 786464 | tf_op jit(solution)/shard_map/ppermute | solution.py:311
  347.9 5.8 %collective-permute-done.59.refs_6_ = bf16[512,1536]{1,0:T(8,128)(2,1)S(1)} collective-permute-done((bf16[512,1536]{1,0:T(8,128)(2,1)}, bf16[512,1536]{1,0:T(8,128)(2,1)S(1)}, u32[]{:S(2)}, u32[]{:S(2)}) %collective-permute-start.59) | collective-permute-done | bytes 1572896 | tf_op jit(solution)/shard_map/ppermute | solution.py:311
  354.7 6.9 %shard_map.239 = bf16[4,400,448]{2,1,0:T(8,128)(2,1)S(1)} custom-call(s32[7]{0:T(128)S(1)} %copy-done.45, bf16[8,272,448]{2,1,0:T(8,128)(2,1)S(1)} %all-to-all-done.back, bf16[512,1536]{1,0:T(8,128)(2,1)} %constant_dynamic-update-slice_fusion.16.refs_0_, bf16[512,1536]{1,0:T(8,128)(2,1)S(1)} %copy-done.22, bf16[512,1536]{1,0:T(8,128)(2,1)S(1)} %copy-done.25, ...), custom_call_target="tpu_custom_call" | custom-call | flops 8000000000 | bytes 8000000 | tf_op jit(solution)/shard_map/pallas_call | solution.py:1029
  369.8 17.0 %collective-permute-done.68 = bf16[128,1536]{1,0:T(8,128)(2,1)S(1)} collective-permute-done((bf16[128,1536]{1,0:T(8,128)(2,1)S(1)}, bf16[128,1536]{1,0:T(8,128)(2,1)S(1)}, u32[]{:S(2)}, u32[]{:S(2)}) %collective-permute-start.68) | collective-permute-done | bytes 393248 | tf_op jit(solution)/shard_map/ppermute | solution.py:311
  388.6 3.5 all-to-all-start.1
  395.1 6.5 %all-to-all-done.1 = bf16[4,96,768]{2,1,0:T(8,128)(2,1)S(1)} async-done(((bf16[4,96,768]{2,1,0:T(8,128)(2,1)}), bf16[4,96,768]{2,1,0:T(8,128)(2,1)S(1)}, u32[]{:S(2)}, u32[]{:S(2)}) %all-to-all-start.1) | async-done | bytes 589856 | tf_op jit(solution)/shard_map/all_to_all | solution.py:61
  401.6 4.2 all-to-all-start.2
  405.8 2.2 convert_add_fusion
  408.0 7.4 %all-to-all-done.2 = bf16[4,96,768]{2,1,0:T(8,128)(2,1)} async-done(((bf16[4,96,768]{2,1,0:T(8,128)(2,1)}), bf16[4,96,768]{2,1,0:T(8,128)(2,1)}, u32[]{:S(2)}, u32[]{:S(2)}) %all-to-all-start.2) | async-done | bytes 589856 | tf_op jit(solution)/shard_map/all_to_all | solution.py:61
  415.4 4.2 all-to-all-start.3
  419.6 3.0 fusion.1
  423.6 2.2 convert_element_type.199
  425.8 3.4 all-to-all-done.3
  429.1 2.2 convert_element_type.200
  433.7 3.6 all-to-all-start.4
  437.2 13.4 %all-to-all-done.4.sums = bf16[8,112,448]{2,1,0:T(8,128)(2,1)S(1)} async-done(((bf16[8,112,448]{2,1,0:T(8,128)(2,1)}), bf16[8,112,448]{2,1,0:T(8,128)(2,1)S(1)}, u32[]{:S(2)}, u32[]{:S(2)}) %all-to-all-start.4) | async-done | bytes 802848 | tf_op jit(solution)/shard_map/all_to_all | solution.py:61
  (416 shorter events, 126.7 us)
Async XLA Ops:
  7.2 284.2 %reduce-scatter.5.cloned.1.call-start = ((), (), s32[]{:S(2)}) async-start(), calls=%async_computation.9 | async-start | bytes 2949120 | tf_op jit(solution)/shard_map/reduce_scatter | solution.py:65
  8.1 14.2 %collective-permute-start.3 = (bf16[96,128]{1,0:T(8,128)(2,1)S(1)}, bf16[96,128]{1,0:T(8,128)(2,1)S(1)}, u32[]{:S(2)}, u32[]{:S(2)}) collective-permute-start(bf16[96,128]{1,0:T(8,128)(2,1)S(1)} %pad.9), channel_id=1, source_target_pairs={{0,24},{8,0},{16,8},{24,16},{1,25},{9,1},{17,9},{25,17},{2,26},{10... | collective-permute-start | bytes 73736 | tf_op jit(solution)/shard_map/ppermute | solution.py:317
  18.2 13.8 %collective-permute-start.14 = (bf16[96,1792]{1,0:T(8,128)(2,1)}, bf16[96,1792]{1,0:T(8,128)(2,1)}, u32[]{:S(2)}, u32[]{:S(2)}) collective-permute-start(bf16[96,1792]{1,0:T(8,128)(2,1)} %pad_maximum_fusion.3), channel_id=1, source_target_pairs={{0,24},{8,0},{16,8},{24,16},{1,25},{9,1},{17,9},{25,17},{2,26},{10... | collective-permute-start | bytes 1032200 | tf_op jit(solution)/shard_map/ppermute | solution.py:317
  21.1 30.2 %collective-permute-start.13 = (bf16[96,1792]{1,0:T(8,128)(2,1)}, bf16[96,1792]{1,0:T(8,128)(2,1)}, u32[]{:S(2)}, u32[]{:S(2)}) collective-permute-start(bf16[96,1792]{1,0:T(8,128)(2,1)} %pad_maximum_fusion.3), channel_id=1, source_target_pairs={{0,16},{8,24},{16,0},{24,8},{1,17},{9,25},{17,1},{25,9},{2,18},{10... | collective-permute-start | bytes 1032200 | tf_op jit(solution)/shard_map/ppermute | solution.py:317
  22.3 29.9 %collective-permute-start.12 = (bf16[96,1792]{1,0:T(8,128)(2,1)}, bf16[96,1792]{1,0:T(8,128)(2,1)}, u32[]{:S(2)}, u32[]{:S(2)}) collective-permute-start(bf16[96,1792]{1,0:T(8,128)(2,1)} %pad_maximum_fusion.3), channel_id=1, source_target_pairs={{0,8},{8,16},{16,24},{24,0},{1,9},{9,17},{17,25},{25,1},{2,10},{10... | collective-permute-start | bytes 1032200 | tf_op jit(solution)/shard_map/ppermute | solution.py:317
  30.5 26.5 %collective-permute-start.8 = (bf16[256,1536]{1,0:T(8,128)(2,1)}, bf16[256,1536]{1,0:T(8,128)(2,1)S(1)}, u32[]{:S(2)}, u32[]{:S(2)}) collective-permute-start(bf16[256,1536]{1,0:T(8,128)(2,1)} %cot.1), channel_id=1, source_target_pairs={{0,4},{4,0},{1,5},{5,1},{2,6},{6,2},{3,7},{7,3},{8,12},{12,8},{9,1... | collective-permute-start | bytes 2359304 | tf_op jit(solution)/shard_map/ppermute | solution.py:311
  31.1 25.9 %collective-permute-start.9 = (bf16[256,1536]{1,0:T(8,128)(2,1)}, bf16[256,1536]{1,0:T(8,128)(2,1)S(1)}, u32[]{:S(2)}, u32[]{:S(2)}) collective-permute-start(bf16[256,1536]{1,0:T(8,128)(2,1)} %cot.1), channel_id=1, source_target_pairs={{0,1},{1,0},{2,3},{3,2},{4,5},{5,4},{6,7},{7,6},{8,9},{9,8},{10,11... | collective-permute-start | bytes 2359304 | tf_op jit(solution)/shard_map/ppermute | solution.py:311
  57.0 19.7 %collective-permute-start.15 = (bf16[4,96,1024]{2,1,0:T(8,128)(2,1)S(1)}, bf16[4,96,1024]{2,1,0:T(8,128)(2,1)}, u32[]{:S(2)}, u32[]{:S(2)}) collective-permute-start(bf16[4,96,1024]{2,1,0:T(8,128)(2,1)S(1)} %pad_maximum_fusion.refs_0_), channel_id=1, source_target_pairs={{0,1},{1,0},{2,3},{3,2},{4,5},{5,4},{6,7},{7,6},{8,9},{9,8},{10,11... | collective-permute-start | bytes 2359304 | tf_op jit(solution)/shard_map/ppermute | solution.py:311
  58.4 17.3 %collective-permute-start.16 = (bf16[4,96,1024]{2,1,0:T(8,128)(2,1)S(1)}, bf16[4,96,1024]{2,1,0:T(8,128)(2,1)}, u32[]{:S(2)}, u32[]{:S(2)}) collective-permute-start(bf16[4,96,1024]{2,1,0:T(8,128)(2,1)S(1)} %pad_maximum_fusion.refs_0_), channel_id=1, source_target_pairs={{0,4},{4,0},{1,5},{5,1},{2,6},{6,2},{3,7},{7,3},{8,12},{12,8},{9,1... | collective-permute-start | bytes 2359304 | tf_op jit(solution)/shard_map/ppermute | solution.py:311
  89.7 19.0 %collective-permute-start.23 = (bf16[4,96,768]{2,1,0:T(8,128)(2,1)}, bf16[4,96,768]{2,1,0:T(8,128)(2,1)S(1)}, u32[]{:S(2)}, u32[]{:S(2)}) collective-permute-start(bf16[4,96,768]{2,1,0:T(8,128)(2,1)} %pad_maximum_fusion.1.refs_0_), channel_id=1, source_target_pairs={{0,1},{1,0},{2,3},{3,2},{4,5},{5,4},{6,7},{7,6},{8,9},{9,8},{10,11... | collective-permute-start | bytes 1769480 | tf_op jit(solution)/shard_map/ppermute | solution.py:311
  91.2 17.4 %collective-permute-start.24 = (bf16[4,96,768]{2,1,0:T(8,128)(2,1)}, bf16[4,96,768]{2,1,0:T(8,128)(2,1)S(1)}, u32[]{:S(2)}, u32[]{:S(2)}) collective-permute-start(bf16[4,96,768]{2,1,0:T(8,128)(2,1)} %pad_maximum_fusion.1.refs_0_), channel_id=1, source_target_pairs={{0,4},{4,0},{1,5},{5,1},{2,6},{6,2},{3,7},{7,3},{8,12},{12,8},{9,1... | collective-permute-start | bytes 1769480 | tf_op jit(solution)/shard_map/ppermute | solution.py:311
  110.4 15.7 %collective-permute-start.10 = (bf16[128,1536]{1,0:T(8,128)(2,1)S(1)}, bf16[128,1536]{1,0:T(8,128)(2,1)S(1)}, u32[]{:S(2)}, u32[]{:S(2)}) collective-permute-start(bf16[128,1536]{1,0:T(8,128)(2,1)S(1)} %slice.159), channel_id=1, source_target_pairs={{0,1},{1,0},{2,3},{3,2},{4,5},{5,4},{6,7},{7,6},{8,9},{9,8},{10,11... | collective-permute-start | bytes 1179656 | tf_op jit(solution)/shard_map/ppermute | solution.py:311
  111.5 14.9 %collective-permute-start.11 = (bf16[128,1536]{1,0:T(8,128)(2,1)S(1)}, bf16[128,1536]{1,0:T(8,128)(2,1)S(1)}, u32[]{:S(2)}, u32[]{:S(2)}) collective-permute-start(bf16[128,1536]{1,0:T(8,128)(2,1)S(1)} %slice.160), channel_id=1, source_target_pairs={{0,4},{4,0},{1,5},{5,1},{2,6},{6,2},{3,7},{7,3},{8,12},{12,8},{9,1... | collective-permute-start | bytes 1179656 | tf_op jit(solution)/shard_map/ppermute | solution.py:311
  113.0 15.2 %collective-permute-start.27 = (bf16[4,96,768]{2,1,0:T(8,128)(2,1)S(1)}, bf16[4,96,768]{2,1,0:T(8,128)(2,1)S(1)}, u32[]{:S(2)}, u32[]{:S(2)}) collective-permute-start(bf16[4,96,768]{2,1,0:T(8,128)(2,1)S(1)} %copy-done.19), channel_id=1, source_target_pairs={{0,2},{2,0},{1,3},{3,1},{4,6},{6,4},{5,7},{7,5},{8,10},{10,8},{9,1... | collective-permute-start | bytes 1769480 | tf_op jit(solution)/shard_map/ppermute | solution.py:311
  133.8 19.9 %collective-permute-start.33 = (bf16[256,1536]{1,0:T(8,128)(2,1)}, bf16[256,1536]{1,0:T(8,128)(2,1)S(1)}, u32[]{:S(2)}, u32[]{:S(2)}) collective-permute-start(bf16[256,1536]{1,0:T(8,128)(2,1)} %get-tuple-element.141.refs_0_.second), channel_id=1, source_target_pairs={{0,1},{1,0},{2,3},{3,2},{4,5},{5,4},{6,7},{7,6},{8,9},{9,8},{10,11... | collective-permute-start | bytes 2359304 | tf_op jit(solution)/shard_map/ppermute | solution.py:311
  135.3 19.4 %collective-permute-start.34 = (bf16[256,1536]{1,0:T(8,128)(2,1)}, bf16[256,1536]{1,0:T(8,128)(2,1)S(1)}, u32[]{:S(2)}, u32[]{:S(2)}) collective-permute-start(bf16[256,1536]{1,0:T(8,128)(2,1)} %get-tuple-element.141.refs_0_.second), channel_id=1, source_target_pairs={{0,4},{4,0},{1,5},{5,1},{2,6},{6,2},{3,7},{7,3},{8,12},{12,8},{9,1... | collective-permute-start | bytes 2359304 | tf_op jit(solution)/shard_map/ppermute | solution.py:311
  135.8 19.5 %collective-permute-start.37 = (bf16[256,1536]{1,0:T(8,128)(2,1)S(1)}, bf16[256,1536]{1,0:T(8,128)(2,1)S(1)}, u32[]{:S(2)}, u32[]{:S(2)}) collective-permute-start(bf16[256,1536]{1,0:T(8,128)(2,1)S(1)} %copy-done.31), channel_id=1, source_target_pairs={{0,2},{2,0},{1,3},{3,1},{4,6},{6,4},{5,7},{7,5},{8,10},{10,8},{9,1... | collective-permute-start | bytes 2359304 | tf_op jit(solution)/shard_map/ppermute | solution.py:311
  135.8 20.3 %collective-permute-start.38 = (bf16[256,1536]{1,0:T(8,128)(2,1)S(1)}, bf16[256,1536]{1,0:T(8,128)(2,1)S(1)}, u32[]{:S(2)}, u32[]{:S(2)}) collective-permute-start(bf16[256,1536]{1,0:T(8,128)(2,1)S(1)} %copy-done.28), channel_id=1, source_target_pairs={{0,2},{2,0},{1,3},{3,1},{4,6},{6,4},{5,7},{7,5},{8,10},{10,8},{9,1... | collective-permute-start | bytes 2359304 | tf_op jit(solution)/shard_map/ppermute | solution.py:311
  155.2 26.0 %collective-permute-start.43 = (bf16[256,1536]{1,0:T(8,128)(2,1)}, bf16[256,1536]{1,0:T(8,128)(2,1)S(1)}, u32[]{:S(2)}, u32[]{:S(2)}) collective-permute-start(bf16[256,1536]{1,0:T(8,128)(2,1)} %constant_dynamic-update-slice_fusion.8.refs_2_), channel_id=1, source_target_pairs={{0,2},{2,0},{1,3},{3,1},{4,6},{6,4},{5,7},{7,5},{8,10},{10,8},{9,1... | collective-permute-start | bytes 2359304 | tf_op jit(solution)/shard_map/ppermute | solution.py:311
  155.3 25.7 %collective-permute-start.40 = (bf16[128,1536]{1,0:T(8,128)(2,1)S(1)}, bf16[128,1536]{1,0:T(8,128)(2,1)S(1)}, u32[]{:S(2)}, u32[]{:S(2)}) collective-permute-start(bf16[128,1536]{1,0:T(8,128)(2,1)S(1)} %slice.135), channel_id=1, source_target_pairs={{0,1},{1,0},{2,3},{3,2},{4,5},{5,4},{6,7},{7,6},{8,9},{9,8},{10,11... | collective-permute-start | bytes 1179656 | tf_op jit(solution)/shard_map/ppermute | solution.py:311
  156.1 24.8 %collective-permute-start.41 = (bf16[128,1536]{1,0:T(8,128)(2,1)S(1)}, bf16[128,1536]{1,0:T(8,128)(2,1)S(1)}, u32[]{:S(2)}, u32[]{:S(2)}) collective-permute-start(bf16[128,1536]{1,0:T(8,128)(2,1)S(1)} %slice.136), channel_id=1, source_target_pairs={{0,4},{4,0},{1,5},{5,1},{2,6},{6,2},{3,7},{7,3},{8,12},{12,8},{9,1... | collective-permute-start | bytes 1179656 | tf_op jit(solution)/shard_map/ppermute | solution.py:311
  203.2 159.6 %reduce-scatter.7.cloned.1.call-start = ((), (), s32[]{:S(2)}) async-start(), calls=%async_computation.10 | async-start | bytes 2949120 | tf_op jit(solution)/shard_map/reduce_scatter | solution.py:65
  204.3 18.8 %collective-permute-start.48 = (bf16[256,1664]{1,0:T(8,128)(2,1)S(1)}, bf16[256,1664]{1,0:T(8,128)(2,1)S(1)}, u32[]{:S(2)}, u32[]{:S(2)}) collective-permute-start(bf16[256,1664]{1,0:T(8,128)(2,1)S(1)} %copy-done.47), channel_id=1, source_target_pairs={{0,2},{2,0},{1,3},{3,1},{4,6},{6,4},{5,7},{7,5},{8,10},{10,8},{9,1... | collective-permute-start | bytes 2555912 | tf_op jit(solution)/shard_map/ppermute | solution.py:311
  236.8 13.1 %collective-permute-start.52 = (bf16[128,1664]{1,0:T(8,128)(2,1)}, bf16[128,1664]{1,0:T(8,128)(2,1)}, u32[]{:S(2)}, u32[]{:S(2)}) collective-permute-start(bf16[128,1664]{1,0:T(8,128)(2,1)} %reduce-precision_convert_fusion.7), channel_id=1, source_target_pairs={{0,1},{1,0},{2,3},{3,2},{4,5},{5,4},{6,7},{7,6},{8,9},{9,8},{10,11... | collective-permute-start | bytes 1277960 | tf_op jit(solution)/shard_map/ppermute | solution.py:311
  237.5 13.1 %collective-permute-start.51 = (bf16[128,1664]{1,0:T(8,128)(2,1)}, bf16[128,1664]{1,0:T(8,128)(2,1)}, u32[]{:S(2)}, u32[]{:S(2)}) collective-permute-start(bf16[128,1664]{1,0:T(8,128)(2,1)} %reduce-precision_convert_fusion.8), channel_id=1, source_target_pairs={{0,4},{4,0},{1,5},{5,1},{2,6},{6,2},{3,7},{7,3},{8,12},{12,8},{9,1... | collective-permute-start | bytes 1277960 | tf_op jit(solution)/shard_map/ppermute | solution.py:311
  239.9 19.1 %collective-permute-start.49 = (bf16[128,1664]{1,0:T(8,128)(2,1)}, bf16[128,1664]{1,0:T(8,128)(2,1)}, u32[]{:S(2)}, u32[]{:S(2)}) collective-permute-start(bf16[128,1664]{1,0:T(8,128)(2,1)} %slice.174), channel_id=1, source_target_pairs={{0,1},{1,0},{2,3},{3,2},{4,5},{5,4},{6,7},{7,6},{8,9},{9,8},{10,11... | collective-permute-start | bytes 1277960 | tf_op jit(solution)/shard_map/ppermute | solution.py:311
  241.2 18.5 %collective-permute-start.50 = (bf16[128,1664]{1,0:T(8,128)(2,1)}, bf16[128,1664]{1,0:T(8,128)(2,1)}, u32[]{:S(2)}, u32[]{:S(2)}) collective-permute-start(bf16[128,1664]{1,0:T(8,128)(2,1)} %slice.175), channel_id=1, source_target_pairs={{0,4},{4,0},{1,5},{5,1},{2,6},{6,2},{3,7},{7,3},{8,12},{12,8},{9,1... | collective-permute-start | bytes 1277960 | tf_op jit(solution)/shard_map/ppermute | solution.py:311
  252.5 38.5 %collective-permute-start.53 = (bf16[512,1536]{1,0:T(8,128)(2,1)}, bf16[512,1536]{1,0:T(8,128)(2,1)S(1)}, u32[]{:S(2)}, u32[]{:S(2)}) collective-permute-start(bf16[512,1536]{1,0:T(8,128)(2,1)} %constant_dynamic-update-slice_fusion.16.refs_0_), channel_id=1, source_target_pairs={{0,1},{1,0},{2,3},{3,2},{4,5},{5,4},{6,7},{7,6},{8,9},{9,8},{10,11... | collective-permute-start | bytes 4718600 | tf_op jit(solution)/shard_map/ppermute | solution.py:311
  253.9 37.5 %collective-permute-start.54 = (bf16[512,1536]{1,0:T(8,128)(2,1)}, bf16[512,1536]{1,0:T(8,128)(2,1)S(1)}, u32[]{:S(2)}, u32[]{:S(2)}) collective-permute-start(bf16[512,1536]{1,0:T(8,128)(2,1)} %constant_dynamic-update-slice_fusion.16.refs_0_), channel_id=1, source_target_pairs={{0,4},{4,0},{1,5},{5,1},{2,6},{6,2},{3,7},{7,3},{8,12},{12,8},{9,1... | collective-permute-start | bytes 4718600 | tf_op jit(solution)/shard_map/ppermute | solution.py:311
  292.8 31.1 %all-to-all-start = ((bf16[8,272,448]{2,1,0:T(8,128)(2,1)}), bf16[8,272,448]{2,1,0:T(8,128)(2,1)S(1)}, u32[]{:S(2)}, u32[]{:S(2)}) async-start(bf16[8,272,448]{2,1,0:T(8,128)(2,1)} %constant_dynamic-update-slice_fusion.20), calls=%async_computation.1 | async-start | bytes 4456448 | tf_op jit(solution)/shard_map/all_to_all | solution.py:61
  296.4 105.2 %reduce-scatter.11.cloned.1.call-start = ((), (), s32[]{:S(2)}) async-start(), calls=%async_computation.12 | async-start | bytes 2949120 | tf_op jit(solution)/shard_map/reduce_scatter | solution.py:65
  297.2 134.2 %reduce-scatter.9.cloned.1.call-start = ((), (), s32[]{:S(2)}) async-start(), calls=%async_computation.11 | async-start | bytes 2048000 | tf_op jit(solution)/shard_map/reduce_scatter | solution.py:65
  323.9 19.4 %collective-permute-start.55 = (bf16[256,1536]{1,0:T(8,128)(2,1)}, bf16[256,1536]{1,0:T(8,128)(2,1)S(1)}, u32[]{:S(2)}, u32[]{:S(2)}) collective-permute-start(bf16[256,1536]{1,0:T(8,128)(2,1)} %slice.143), channel_id=1, source_target_pairs={{0,1},{1,0},{2,3},{3,2},{4,5},{5,4},{6,7},{7,6},{8,9},{9,8},{10,11... | collective-permute-start | bytes 2359304 | tf_op jit(solution)/shard_map/ppermute | solution.py:311
  324.9 18.9 %collective-permute-start.56 = (bf16[256,1536]{1,0:T(8,128)(2,1)S(1)}, bf16[256,1536]{1,0:T(8,128)(2,1)S(1)}, u32[]{:S(2)}, u32[]{:S(2)}) collective-permute-start(bf16[256,1536]{1,0:T(8,128)(2,1)S(1)} %slice.144), channel_id=1, source_target_pairs={{0,4},{4,0},{1,5},{5,1},{2,6},{6,2},{3,7},{7,3},{8,12},{12,8},{9,1... | collective-permute-start | bytes 2359304 | tf_op jit(solution)/shard_map/ppermute | solution.py:311
  325.5 18.5 %collective-permute-start.64 = (bf16[256,1536]{1,0:T(8,128)(2,1)}, bf16[256,1536]{1,0:T(8,128)(2,1)S(1)}, u32[]{:S(2)}, u32[]{:S(2)}) collective-permute-start(bf16[256,1536]{1,0:T(8,128)(2,1)} %get-tuple-element.215), channel_id=1, source_target_pairs={{0,2},{2,0},{1,3},{3,1},{4,6},{6,4},{5,7},{7,5},{8,10},{10,8},{9,1... | collective-permute-start | bytes 2359304 | tf_op jit(solution)/shard_map/ppermute | solution.py:311
  325.5 20.8 %collective-permute-start.57 = (bf16[512,1536]{1,0:T(8,128)(2,1)}, bf16[512,1536]{1,0:T(8,128)(2,1)S(1)}, u32[]{:S(2)}, u32[]{:S(2)}) collective-permute-start(bf16[512,1536]{1,0:T(8,128)(2,1)} %constant_dynamic-update-slice_fusion.16.refs_0_), channel_id=1, source_target_pairs={{0,2},{2,0},{1,3},{3,1},{4,6},{6,4},{5,7},{7,5},{8,10},{10,8},{9,1... | collective-permute-start | bytes 4718600 | tf_op jit(solution)/shard_map/ppermute | solution.py:311
  326.0 18.8 %collective-permute-start.61 = (bf16[256,1536]{1,0:T(8,128)(2,1)}, bf16[256,1536]{1,0:T(8,128)(2,1)S(1)}, u32[]{:S(2)}, u32[]{:S(2)}) collective-permute-start(bf16[256,1536]{1,0:T(8,128)(2,1)} %get-tuple-element.211), channel_id=1, source_target_pairs={{0,2},{2,0},{1,3},{3,1},{4,6},{6,4},{5,7},{7,5},{8,10},{10,8},{9,1... | collective-permute-start | bytes 2359304 | tf_op jit(solution)/shard_map/ppermute | solution.py:311
  344.8 18.1 %collective-permute-start.63 = (bf16[256,1536]{1,0:T(8,128)(2,1)}, bf16[256,1536]{1,0:T(8,128)(2,1)}, u32[]{:S(2)}, u32[]{:S(2)}) collective-permute-start(bf16[256,1536]{1,0:T(8,128)(2,1)} %get-tuple-element.213), channel_id=1, source_target_pairs={{0,2},{2,0},{1,3},{3,1},{4,6},{6,4},{5,7},{7,5},{8,10},{10,8},{9,1... | collective-permute-start | bytes 2359304 | tf_op jit(solution)/shard_map/ppermute | solution.py:311
  346.3 73.2 %collective-permute-start.70 = (bf16[256,1536]{1,0:T(8,128)(2,1)}, bf16[256,1536]{1,0:T(8,128)(2,1)}, u32[]{:S(2)}, u32[]{:S(2)}) collective-permute-start(bf16[256,1536]{1,0:T(8,128)(2,1)} %get-tuple-element.217), channel_id=1, source_target_pairs={{0,2},{2,0},{1,3},{3,1},{4,6},{6,4},{5,7},{7,5},{8,10},{10,8},{9,1... | collective-permute-start | bytes 2359304 | tf_op jit(solution)/shard_map/ppermute | solution.py:311
  347.0 21.2 %collective-permute-start.65 = (bf16[128,1536]{1,0:T(8,128)(2,1)}, bf16[128,1536]{1,0:T(8,128)(2,1)}, u32[]{:S(2)}, u32[]{:S(2)}) collective-permute-start(bf16[128,1536]{1,0:T(8,128)(2,1)} %get-tuple-element.230), channel_id=1, source_target_pairs={{0,1},{1,0},{2,3},{3,2},{4,5},{5,4},{6,7},{7,6},{8,9},{9,8},{10,11... | collective-permute-start | bytes 1179656 | tf_op jit(solution)/shard_map/ppermute | solution.py:311
  353.7 38.4 %collective-permute-start.62 = (bf16[128,1536]{1,0:T(8,128)(2,1)S(1)}, bf16[128,1536]{1,0:T(8,128)(2,1)}, u32[]{:S(2)}, u32[]{:S(2)}) collective-permute-start(bf16[128,1536]{1,0:T(8,128)(2,1)S(1)} %slice.177), channel_id=1, source_target_pairs={{0,1},{1,0},{2,3},{3,2},{4,5},{5,4},{6,7},{7,6},{8,9},{9,8},{10,11... | collective-permute-start | bytes 1179656 | tf_op jit(solution)/shard_map/ppermute | solution.py:311
  366.1 39.7 %collective-permute-start.67 = (bf16[128,1536]{1,0:T(8,128)(2,1)}, bf16[128,1536]{1,0:T(8,128)(2,1)}, u32[]{:S(2)}, u32[]{:S(2)}) collective-permute-start(bf16[128,1536]{1,0:T(8,128)(2,1)} %slice.180), channel_id=1, source_target_pairs={{0,4},{4,0},{1,5},{5,1},{2,6},{6,2},{3,7},{7,3},{8,12},{12,8},{9,1... | collective-permute-start | bytes 1179656 | tf_op jit(solution)/shard_map/ppermute | solution.py:311
  366.6 20.1 %collective-permute-start.68 = (bf16[128,1536]{1,0:T(8,128)(2,1)S(1)}, bf16[128,1536]{1,0:T(8,128)(2,1)S(1)}, u32[]{:S(2)}, u32[]{:S(2)}) collective-permute-start(bf16[128,1536]{1,0:T(8,128)(2,1)S(1)} %copy-done.82), channel_id=1, source_target_pairs={{0,4},{4,0},{1,5},{5,1},{2,6},{6,2},{3,7},{7,3},{8,12},{12,8},{9,1... | collective-permute-start | bytes 1179656 | tf_op jit(solution)/shard_map/ppermute | solution.py:311
  369.2 24.8 %collective-permute-start.66 = (bf16[128,1536]{1,0:T(8,128)(2,1)S(1)}, bf16[128,1536]{1,0:T(8,128)(2,1)S(1)}, u32[]{:S(2)}, u32[]{:S(2)}) collective-permute-start(bf16[128,1536]{1,0:T(8,128)(2,1)S(1)} %reduce-precision_convert_fusion.10), channel_id=1, source_target_pairs={{0,4},{4,0},{1,5},{5,1},{2,6},{6,2},{3,7},{7,3},{8,12},{12,8},{9,1... | collective-permute-start | bytes 1179656 | tf_op jit(solution)/shard_map/ppermute | solution.py:311
  387.6 18.2 %collective-permute-start.69 = (bf16[128,1536]{1,0:T(8,128)(2,1)}, bf16[128,1536]{1,0:T(8,128)(2,1)}, u32[]{:S(2)}, u32[]{:S(2)}) collective-permute-start(bf16[128,1536]{1,0:T(8,128)(2,1)} %reduce-precision_convert_fusion.9), channel_id=1, source_target_pairs={{0,1},{1,0},{2,3},{3,2},{4,5},{5,4},{6,7},{7,6},{8,9},{9,8},{10,11... | collective-permute-start | bytes 1179656 | tf_op jit(solution)/shard_map/ppermute | solution.py:311
  401.6 13.8 %all-to-all-start.2 = ((bf16[4,96,768]{2,1,0:T(8,128)(2,1)}), bf16[4,96,768]{2,1,0:T(8,128)(2,1)}, u32[]{:S(2)}, u32[]{:S(2)}) async-start(bf16[4,96,768]{2,1,0:T(8,128)(2,1)} %bitcast.89), calls=%async_computation.6 | async-start | bytes 1179648 | tf_op jit(solution)/shard_map/all_to_all | solution.py:61
  415.4 13.8 %all-to-all-start.3 = ((bf16[4,96,768]{2,1,0:T(8,128)(2,1)}), bf16[4,96,768]{2,1,0:T(8,128)(2,1)}, u32[]{:S(2)}, u32[]{:S(2)}) async-start(bf16[4,96,768]{2,1,0:T(8,128)(2,1)} %bitcast.88), calls=%async_computation.7 | async-start | bytes 1179648 | tf_op jit(solution)/shard_map/all_to_all | solution.py:61
  433.7 17.0 %all-to-all-start.4 = ((bf16[8,112,448]{2,1,0:T(8,128)(2,1)}), bf16[8,112,448]{2,1,0:T(8,128)(2,1)S(1)}, u32[]{:S(2)}, u32[]{:S(2)}) async-start(bf16[8,112,448]{2,1,0:T(8,128)(2,1)} %maximum_maximum_fusion), calls=%async_computation.8 | async-start | bytes 1835008 | tf_op jit(solution)/shard_map/all_to_all | solution.py:61
  (120 other events, 1222.7 us)
Sparse Core Ops, SparseCore 0:
  203.3 47.9 reduce-scatter.4
  253.6 47.5 reduce-scatter.6
  303.5 47.5 reduce-scatter.10
  363.0 37.3 reduce-scatter.8

commit v4 on v3

--- a/solution.py
+++ b/solution.py
@@ -919,13 +919,8 @@
     stages = (stage_own, stage_sides, stage_corner)
     rows_in, rows_cot, gated, gate_back, up_back = ([stage[n] for stage in stages] for n in range(5))
     gates = stage_own[5]
-    last_y, last_x, *sent = corner_last(back_x, back_y, passed)
+    last_y, last_x = corner_last(back_x, back_y, passed)[:2]
     down_sum = scatter_sum(down_part, "z")
-    gate_part, up_part = row_sums(
-        at, [after(rows_in[0], *sent, own_far)] + rows_in[1:], gate_back, up_back
-    )
-    gate_sum, up_sum = scatter_sum(gate_part, "z"), scatter_sum(up_part, "z")
-    own_near = after(own_near, gate_part)
 
     resid_grad, branch_grad, attended_grad, router_acc, gain_two_grad = run_kernel(
         branch_back_kernel,
@@ -955,6 +950,11 @@
         ],
         56,
     )
+    gate_part, up_part = row_sums(
+        at, [after(rows_in[0], resid_grad)] + rows_in[1:], gate_back, up_back
+    )
+    gate_sum, up_sum = scatter_sum(gate_part, "z"), scatter_sum(up_part, "z")
+    attended_grad = after(attended_grad, gate_part)
     qkv_width, branch_width = qkv_cols // plane, model_width // plane
     dense_cols = qkv_width + branch_width
     (back_cols,) = run_kernel(
@@ -1042,15 +1042,17 @@
     dense_sum = scatter_sum(dense_part.reshape(-1, dense_cols), "z")
     mixed = [over_core(near, far) for near, far in zip(shares[:4], shares[4:])]
     early = early_sums(mixed[1], mixed[2])
-    last = corner_last(mixed[1], mixed[2], corner_first(mixed[3]))[:2]
+    first, down_grad, gate_grad = lax.optimization_barrier(
+        (corner_first(mixed[3]), down_grad, gate_grad)
+    )
+    last, up_grad = lax.optimization_barrier(
+        (corner_last(mixed[1], mixed[2], first)[:2], placed(up_sum))
+    )
     mixture = jnp.concatenate(
         [left.astype(f32) + right.astype(f32) for left, right in zip(early, last)], axis=0
     )
     block_out = (resid + (mixture + mixed[0].astype(f32))).astype(bf16)
 
-    dense_sum, down_grad, gate_grad, up_grad, block_out = lax.optimization_barrier(
-        (dense_sum, down_grad, gate_grad, placed(up_sum), block_out)
-    )
     wide_sum = dense_sum[: local_count * shard_rows].reshape(2, 2, 1, shard_rows, dense_cols)
     wide_sum = jnp.broadcast_to(wide_sum, (2, 2, owners, shard_rows, dense_cols)).reshape(
         plane, shard_rows, dense_cols

time: 469 us -> 451 us (0.962)
  waiting for transfers between devices: 177 us -> 157 us
    all_to_all x5, waiting for transfers between devices: 46.1 us -> 35.3 us  [exchange(): return lax.all_to_all(block, axes, split_axis=0, concat_axis=0, tiled=True)]
    ppermute x65, waiting for transfers between devices: 112 us -> 102 us  [swap(): return lax.ppermute(block, axis, [(0, 1), (1, 0)])]
    unnamed x190 -> x178, local copies, waits for them, and re-layouts: 40.3 us -> 40.9 us
  transfers between devices with their start and end apart: 80 -> 80, of which waited for: 38 -> 31; matrix products, arithmetic and copies ran while one was open for 12% -> 13% of each run, Pallas kernels for 19% -> 23%
where the time goes in v4:
time: 451 us; the launch traced here: 442 us
  waiting for transfers between devices  157 us (35%)
  Pallas kernels  105 us (23%)
  local copies, waits for them, and re-layouts  72.2 us (16%)
  starting transfers between devices  68.7 us (15%)
  other arithmetic  23.6 us (5%)
  between operations  16.1 us (4%)
    ppermute x65, waiting for transfers between devices, swap(): return lax.ppermute(block, axis, [(0, 1), (1, 0)])  102 us
    pallas_call x11, Pallas kernels, run_kernel(): pl.pallas_call(kernel, out_shape=[jax.ShapeDtypeStruct(shape, dtype) for...  98.4 us
    unnamed x178, local copies, waits for them, and re-layouts  40.9 us
    ppermute x65, starting transfers between devices, swap(): return lax.ppermute(block, axis, [(0, 1), (1, 0)])  40.2 us
    all_to_all x5, waiting for transfers between devices, exchange(): return lax.all_to_all(block, axes, split_axis=0, concat_axis=0, tiled=True)  35.3 us
    ppermute x6, waiting for transfers between devices, shifts(): lax.ppermute(block, 'z', [(i, (i + k) % depth) for i in range(depth)])  18.3 us
    all_to_all x5, starting transfers between devices, exchange(): return lax.all_to_all(block, axes, split_axis=0, concat_axis=0, tiled=True)  17.7 us
    ppermute x6, starting transfers between devices, shifts(): lax.ppermute(block, 'z', [(i, (i + k) % depth) for i in range(depth)])  10.2 us
  transfers between devices with their start and end apart: 80, of which 31 were waited for; matrix products, arithmetic and copies ran while one was open for 13% of the time, Pallas kernels for 23%

profile of v4, /device:TPU:0, one launch (start us, length us, event | category | flops | bytes accessed | tf_op | source)
XLA Modules:
  0.0 442.5 jit_solution(549115764983745424)
XLA Ops:
  8.1 5.1 %collective-permute-start = (bf16[96,128]{1,0:T(8,128)(2,1)S(1)}, bf16[96,128]{1,0:T(8,128)(2,1)S(1)}, u32[]{:S(2)}, u32[]{:S(2)}) collective-permute-start(bf16[96,128]{1,0:T(8,128)(2,1)S(1)} %pad.9), channel_id=1, source_target_pairs={{0,24},{8,0},{16,8},{24,16},{1,25},{9,1},{17,9},{25,17},{2,26},{10... | collective-permute-start | bytes 73736 | tf_op jit(solution)/shard_map/ppermute | solution.py:317
  18.2 2.8 collective-permute-start.14
  26.1 2.7 collective-permute-done.3
  33.0 18.3 %collective-permute-done.13 = bf16[96,1792]{1,0:T(8,128)(2,1)} collective-permute-done((bf16[96,1792]{1,0:T(8,128)(2,1)}, bf16[96,1792]{1,0:T(8,128)(2,1)}, u32[]{:S(2)}, u32[]{:S(2)}) %collective-permute-start.13) | collective-permute-done | bytes 344096 | tf_op jit(solution)/shard_map/ppermute | solution.py:317
  59.9 1.8 dynamic-slice_bitcast_fusion.refs_6_.refs_10_.refs_3_
  61.7 4.1 dynamic-slice_bitcast_fusion.1.refs_5_.refs_9_
  65.8 3.2 dynamic-slice_bitcast_fusion.2.refs_4_.refs_8_
  69.1 6.6 %collective-permute-done.16.refs_2_ = bf16[4,96,1024]{2,1,0:T(8,128)(2,1)} collective-permute-done((bf16[4,96,1024]{2,1,0:T(8,128)(2,1)S(1)}, bf16[4,96,1024]{2,1,0:T(8,128)(2,1)}, u32[]{:S(2)}, u32[]{:S(2)}) %collective-permute-start.16) | collective-permute-done | bytes 786464 | tf_op jit(solution)/shard_map/ppermute | solution.py:311
  80.4 5.3 %collective-permute-done.17 = bf16[2,96,1024]{2,1,0:T(8,128)(2,1)S(1)} collective-permute-done((bf16[2,96,1024]{2,1,0:T(8,128)(2,1)S(1)}, bf16[2,96,1024]{2,1,0:T(8,128)(2,1)S(1)}, u32[]{:S(2)}, u32[]{:S(2)}) %collective-permute-start.17) | collective-permute-done | bytes 393248 | tf_op jit(solution)/shard_map/ppermute | solution.py:311
  95.8 9.0 %shard_map.229 = (bf16[256,1536]{1,0:T(8,128)(2,1)S(1)}, bf16[256,1536]{1,0:T(8,128)(2,1)S(1)}, bf16[256,256]{1,0:T(8,128)(2,1)S(1)}, bf16[256,256]{1,0:T(8,128)...) custom-call(s32[7]{0:T(128)S(1)} %copy-done.42, ...), custom_call_target="tpu_custom_call" | custom-call | flops 11000000512 | bytes 11000000 | tf_op jit(solution)/shard_map/pallas_call | solution.py:400
  104.8 2.7 copy-done.49
  113.1 5.7 %collective-permute-done.25 = bf16[2,96,768]{2,1,0:T(8,128)(2,1)S(1)} collective-permute-done((bf16[2,96,768]{2,1,0:T(8,128)(2,1)S(1)}, bf16[2,96,768]{2,1,0:T(8,128)(2,1)S(1)}, u32[]{:S(2)}, u32[]{:S(2)}) %collective-permute-start.25) | collective-permute-done | bytes 294944 | tf_op jit(solution)/shard_map/ppermute | solution.py:311
  119.5 6.7 %collective-permute-done.10 = bf16[128,1536]{1,0:T(8,128)(2,1)S(1)} collective-permute-done((bf16[128,1536]{1,0:T(8,128)(2,1)S(1)}, bf16[128,1536]{1,0:T(8,128)(2,1)S(1)}, u32[]{:S(2)}, u32[]{:S(2)}) %collective-permute-start.10) | collective-permute-done | bytes 393248 | tf_op jit(solution)/shard_map/ppermute | solution.py:311
  128.3 4.1 shard_map.230
  136.4 10.4 %shard_map.231 = (bf16[384,1536]{1,0:T(8,128)(2,1)S(1)}, bf16[384,1536]{1,0:T(8,128)(2,1)S(1)}, bf16[384,768]{1,0:T(8,128)(2,1)S(1)}, bf16[384,768]{1,0:T(8,128)...) custom-call(s32[7]{0:T(128)S(1)} %copy-done.43, ...), custom_call_target="tpu_custom_call" | custom-call | flops 8000000000 | bytes 8000000 | tf_op jit(solution)/shard_map/pallas_call | solution.py:400
  148.5 5.3 %collective-permute-done.31.refs_0_ = bf16[256,1536]{1,0:T(8,128)(2,1)S(1)} collective-permute-done((bf16[256,1536]{1,0:T(8,128)(2,1)}, bf16[256,1536]{1,0:T(8,128)(2,1)S(1)}, u32[]{:S(2)}, u32[]{:S(2)}) %collective-permute-start.31) | collective-permute-done | bytes 786464 | tf_op jit(solution)/shard_map/ppermute | solution.py:311
  157.0 2.2 collective-permute-done.36.refs_3_
  159.3 17.2 %shard_map.232 = (bf16[768,1536]{1,0:T(8,128)(2,1)S(1)}, bf16[768,1536]{1,0:T(8,128)(2,1)S(1)}, bf16[768,768]{1,0:T(8,128)(2,1)S(1)}, bf16[768,768]{1,0:T(8,128)...) custom-call(s32[7]{0:T(128)S(1)} %copy-done.43, ...), custom_call_target="tpu_custom_call" | custom-call | flops 16000000000 | bytes 16000000 | tf_op jit(solution)/shard_map/pallas_call | solution.py:400
  180.5 1.8 collective-permute-done.42.refs_1_
  182.3 13.1 %shard_map.233 = (bf16[384,1536]{1,0:T(8,128)(2,1)S(1)}, bf16[384,1536]{1,0:T(8,128)(2,1)}, bf16[384,768]{1,0:T(8,128)(2,1)S(1)}, bf16[384,768]{1,0:T(8,128)(2,1...) custom-call(s32[7]{0:T(128)S(1)} %copy-done.43, ...), custom_call_target="tpu_custom_call" | custom-call | flops 8000000000 | bytes 8000000 | tf_op jit(solution)/shard_map/pallas_call | solution.py:400
  209.9 9.1 %collective-permute-done.48 = bf16[128,1664]{1,0:T(8,128)(2,1)S(1)} collective-permute-done((bf16[128,1664]{1,0:T(8,128)(2,1)S(1)}, bf16[128,1664]{1,0:T(8,128)(2,1)S(1)}, u32[]{:S(2)}, u32[]{:S(2)}) %collective-permute-start.48) | collective-permute-done | bytes 426016 | tf_op jit(solution)/shard_map/ppermute | solution.py:311
  220.5 5.3 %collective-permute-done.45 = bf16[128,1664]{1,0:T(8,128)(2,1)S(1)} collective-permute-done((bf16[128,1664]{1,0:T(8,128)(2,1)S(1)}, bf16[128,1664]{1,0:T(8,128)(2,1)S(1)}, u32[]{:S(2)}, u32[]{:S(2)}) %collective-permute-start.45) | collective-permute-done | bytes 426016 | tf_op jit(solution)/shard_map/ppermute | solution.py:311
  227.1 7.0 %collective-permute-done.49.last_x = bf16[128,1664]{1,0:T(8,128)(2,1)S(1)} collective-permute-done((bf16[128,1664]{1,0:T(8,128)(2,1)S(1)}, bf16[128,1664]{1,0:T(8,128)(2,1)S(1)}, u32[]{:S(2)}, u32[]{:S(2)}) %collective-permute-start.49) | collective-permute-done | bytes 426016 | tf_op jit(solution)/shard_map/ppermute | solution.py:311
  234.1 2.2 collective-permute-done.46.last_y
  237.0 8.3 %shard_map.235 = (f32[256,1536]{1,0:T(8,128)}, bf16[256,1536]{1,0:T(8,128)(2,1)}, bf16[256,1536]{1,0:T(8,128)(2,1)}, f32[1536,128]{1,0:T(8,128)}, f32[1,1536]{1,0:T(1,128)}) custom-call(s32[7]{0:T(128)} %stack.76.at, bf16[256,1664]{1,0:T(8,128)(2,1)} %copy-done.52, bf16[256,1664]{1,0:T(8,128)(2,1)} %collective-permute-done.58.far, ...), custom_call_target="tpu_custom_call" | custom-call | flops 6000000000 | bytes 6000000 | tf_op jit(solution)/shard_map/pallas_call | solution.py:400
  245.3 12.7 %shard_map.236 = (bf16[1536,768]{1,0:T(8,128)(2,1)}, bf16[1536,768]{1,0:T(8,128)(2,1)}) custom-call(s32[7]{0:T(128)} %stack.76.at, bf16[384,1536]{1,0:T(8,128)(2,1)} %copy-done.57, bf16[768,1536]{1,0:T(8,128)(2,1)} %copy-done.56, bf16[384,1536]{1,0:T(8,128)(2,1)} %copy-done.55, bf16[384,768]{1,0:T(8,128)(2,1)} %copy-done.65, bf16[768,768]{1,0:T(8,128)(2,1)} %copy-done.63, ...), custom_call_target="tpu_custom_call" | custom-call | flops 8000000000 | bytes 8000000 | tf_op jit(solution)/shard_map/pallas_call | solution.py:400
  264.7 8.6 %shard_map.237.back = bf16[8,272,448]{2,1,0:T(8,128)(2,1)} custom-call(s32[7]{0:T(128)} %stack.76.at, bf16[256,1536]{1,0:T(8,128)(2,1)} %get-tuple-element.200.attended, bf16[12,256,256]{2,1,0:T(8,128)(2,1)} %copy-done.53, bf16[256,1536]{1,0:T(8,128)(2,1)} %copy-done.58, bf16[256,256]{1,0:T(8,128)(2,1)} %copy-done.68, bf16[256,256]{1,0:T(8,128)(2,1)} %copy-done.69, ...), custom_call_target="tpu_custom_call" | custom-call | flops 6000000000 | bytes 6000000 | tf_op jit(solution)/shard_map/pallas_call | solution.py:400
  274.9 2.8 copy-done.50
  277.7 3.7 shard_map.238
  282.8 2.0 reshape.215
  285.7 9.6 %collective-permute-done.50.refs_1_ = bf16[512,1536]{1,0:T(8,128)(2,1)S(1)} collective-permute-done((bf16[512,1536]{1,0:T(8,128)(2,1)}, bf16[512,1536]{1,0:T(8,128)(2,1)S(1)}, u32[]{:S(2)}, u32[]{:S(2)}) %collective-permute-start.50) | collective-permute-done | bytes 1572896 | tf_op jit(solution)/shard_map/ppermute | solution.py:311
  297.8 3.6 all-to-all-start.2
  302.1 9.5 %shard_map.234 = (bf16[256,1536]{1,0:T(8,128)(2,1)}, bf16[256,1536]{1,0:T(8,128)(2,1)}, bf16[256,1536]{1,0:T(8,128)(2,1)}, bf16[256,1536]{1,0:T(8,128)(2,1)}, bf...) custom-call(s32[7]{0:T(128)} %stack.76.at, ...), custom_call_target="tpu_custom_call" | custom-call | flops 10000000000 | bytes 10000000 | tf_op jit(solution)/shard_map/pallas_call | solution.py:400
  313.4 15.5 %all-to-all-done.2.back = bf16[8,272,448]{2,1,0:T(8,128)(2,1)S(1)} async-done(((bf16[8,272,448]{2,1,0:T(8,128)(2,1)}), bf16[8,272,448]{2,1,0:T(8,128)(2,1)S(1)}, u32[]{:S(2)}, u32[]{:S(2)}) %all-to-all-start.2) | async-done | bytes 1949728 | tf_op jit(solution)/shard_map/all_to_all | solution.py:61
  331.0 17.4 %collective-permute-done.63 = bf16[256,1536]{1,0:T(8,128)(2,1)S(1)} collective-permute-done((bf16[256,1536]{1,0:T(8,128)(2,1)}, bf16[256,1536]{1,0:T(8,128)(2,1)S(1)}, u32[]{:S(2)}, u32[]{:S(2)}) %collective-permute-start.63) | collective-permute-done | bytes 786464 | tf_op jit(solution)/shard_map/ppermute | solution.py:311
  352.2 3.5 all-to-all-start
  362.1 6.9 %shard_map.239 = bf16[4,400,448]{2,1,0:T(8,128)(2,1)S(1)} custom-call(s32[7]{0:T(128)S(1)} %copy-done.45, bf16[8,272,448]{2,1,0:T(8,128)(2,1)S(1)} %all-to-all-done.2.back, bf16[512,1536]{1,0:T(8,128)(2,1)} %constant_dynamic-update-slice_fusion.16.refs_0_, bf16[512,1536]{1,0:T(8,128)(2,1)S(1)} %copy-done.22, bf16[512,1536]{1,0:T(8,128)(2,1)S(1)} %copy-done.25, ...), custom_call_target="tpu_custom_call" | custom-call | flops 8000000000 | bytes 8000000 | tf_op jit(solution)/shard_map/pallas_call | solution.py:1029
  372.7 3.5 all-to-all-start.1
  379.0 6.8 %all-to-all-done.1 = bf16[4,96,768]{2,1,0:T(8,128)(2,1)S(1)} async-done(((bf16[4,96,768]{2,1,0:T(8,128)(2,1)}), bf16[4,96,768]{2,1,0:T(8,128)(2,1)S(1)}, u32[]{:S(2)}, u32[]{:S(2)}) %all-to-all-start.1) | async-done | bytes 589856 | tf_op jit(solution)/shard_map/all_to_all | solution.py:61
  386.9 1.8 reduce-precision_convert_fusion.9
  389.7 3.5 all-to-all-start.3
  393.2 1.8 reduce-precision_convert_fusion.10
  395.0 2.0 collective-permute-start.61
  399.0 4.1 all-to-all-done.3
  404.3 7.4 %collective-permute-done.61 = bf16[128,1536]{1,0:T(8,128)(2,1)} collective-permute-done((bf16[128,1536]{1,0:T(8,128)(2,1)}, bf16[128,1536]{1,0:T(8,128)(2,1)}, u32[]{:S(2)}, u32[]{:S(2)}) %collective-permute-start.61) | collective-permute-done | bytes 393248 | tf_op jit(solution)/shard_map/ppermute | solution.py:311
  415.2 3.7 all-to-all-start.4
  420.9 2.5 fusion.1
  423.4 8.9 %all-to-all-done.4.sums = bf16[8,112,448]{2,1,0:T(8,128)(2,1)S(1)} async-done(((bf16[8,112,448]{2,1,0:T(8,128)(2,1)}), bf16[8,112,448]{2,1,0:T(8,128)(2,1)S(1)}, u32[]{:S(2)}, u32[]{:S(2)}) %all-to-all-start.4) | async-done | bytes 802848 | tf_op jit(solution)/shard_map/all_to_all | solution.py:61
  (404 shorter events, 124.5 us)
Async XLA Ops:
  7.2 289.4 %reduce-scatter.5.cloned.1.call-start = ((), (), s32[]{:S(2)}) async-start(), calls=%async_computation.9 | async-start | bytes 2949120 | tf_op jit(solution)/shard_map/reduce_scatter | solution.py:65
  8.1 14.2 %collective-permute-start = (bf16[96,128]{1,0:T(8,128)(2,1)S(1)}, bf16[96,128]{1,0:T(8,128)(2,1)S(1)}, u32[]{:S(2)}, u32[]{:S(2)}) collective-permute-start(bf16[96,128]{1,0:T(8,128)(2,1)S(1)} %pad.9), channel_id=1, source_target_pairs={{0,24},{8,0},{16,8},{24,16},{1,25},{9,1},{17,9},{25,17},{2,26},{10... | collective-permute-start | bytes 73736 | tf_op jit(solution)/shard_map/ppermute | solution.py:317
  21.1 30.2 %collective-permute-start.13 = (bf16[96,1792]{1,0:T(8,128)(2,1)}, bf16[96,1792]{1,0:T(8,128)(2,1)}, u32[]{:S(2)}, u32[]{:S(2)}) collective-permute-start(bf16[96,1792]{1,0:T(8,128)(2,1)} %pad_maximum_fusion.3), channel_id=1, source_target_pairs={{0,16},{8,24},{16,0},{24,8},{1,17},{9,25},{17,1},{25,9},{2,18},{10... | collective-permute-start | bytes 1032200 | tf_op jit(solution)/shard_map/ppermute | solution.py:317
  22.3 29.9 %collective-permute-start.12 = (bf16[96,1792]{1,0:T(8,128)(2,1)}, bf16[96,1792]{1,0:T(8,128)(2,1)}, u32[]{:S(2)}, u32[]{:S(2)}) collective-permute-start(bf16[96,1792]{1,0:T(8,128)(2,1)} %pad_maximum_fusion.3), channel_id=1, source_target_pairs={{0,8},{8,16},{16,24},{24,0},{1,9},{9,17},{17,25},{25,1},{2,10},{10... | collective-permute-start | bytes 1032200 | tf_op jit(solution)/shard_map/ppermute | solution.py:317
  30.5 26.5 %collective-permute-start.8 = (bf16[256,1536]{1,0:T(8,128)(2,1)}, bf16[256,1536]{1,0:T(8,128)(2,1)S(1)}, u32[]{:S(2)}, u32[]{:S(2)}) collective-permute-start(bf16[256,1536]{1,0:T(8,128)(2,1)} %cot.1), channel_id=1, source_target_pairs={{0,4},{4,0},{1,5},{5,1},{2,6},{6,2},{3,7},{7,3},{8,12},{12,8},{9,1... | collective-permute-start | bytes 2359304 | tf_op jit(solution)/shard_map/ppermute | solution.py:311
  31.1 25.9 %collective-permute-start.9 = (bf16[256,1536]{1,0:T(8,128)(2,1)}, bf16[256,1536]{1,0:T(8,128)(2,1)S(1)}, u32[]{:S(2)}, u32[]{:S(2)}) collective-permute-start(bf16[256,1536]{1,0:T(8,128)(2,1)} %cot.1), channel_id=1, source_target_pairs={{0,1},{1,0},{2,3},{3,2},{4,5},{5,4},{6,7},{7,6},{8,9},{9,8},{10,11... | collective-permute-start | bytes 2359304 | tf_op jit(solution)/shard_map/ppermute | solution.py:311
  57.0 19.7 %collective-permute-start.15 = (bf16[4,96,1024]{2,1,0:T(8,128)(2,1)S(1)}, bf16[4,96,1024]{2,1,0:T(8,128)(2,1)}, u32[]{:S(2)}, u32[]{:S(2)}) collective-permute-start(bf16[4,96,1024]{2,1,0:T(8,128)(2,1)S(1)} %pad_maximum_fusion.refs_0_), channel_id=1, source_target_pairs={{0,1},{1,0},{2,3},{3,2},{4,5},{5,4},{6,7},{7,6},{8,9},{9,8},{10,11... | collective-permute-start | bytes 2359304 | tf_op jit(solution)/shard_map/ppermute | solution.py:311
  58.4 17.3 %collective-permute-start.16 = (bf16[4,96,1024]{2,1,0:T(8,128)(2,1)S(1)}, bf16[4,96,1024]{2,1,0:T(8,128)(2,1)}, u32[]{:S(2)}, u32[]{:S(2)}) collective-permute-start(bf16[4,96,1024]{2,1,0:T(8,128)(2,1)S(1)} %pad_maximum_fusion.refs_0_), channel_id=1, source_target_pairs={{0,4},{4,0},{1,5},{5,1},{2,6},{6,2},{3,7},{7,3},{8,12},{12,8},{9,1... | collective-permute-start | bytes 2359304 | tf_op jit(solution)/shard_map/ppermute | solution.py:311
  89.7 19.0 %collective-permute-start.23 = (bf16[4,96,768]{2,1,0:T(8,128)(2,1)}, bf16[4,96,768]{2,1,0:T(8,128)(2,1)S(1)}, u32[]{:S(2)}, u32[]{:S(2)}) collective-permute-start(bf16[4,96,768]{2,1,0:T(8,128)(2,1)} %pad_maximum_fusion.1.refs_0_), channel_id=1, source_target_pairs={{0,1},{1,0},{2,3},{3,2},{4,5},{5,4},{6,7},{7,6},{8,9},{9,8},{10,11... | collective-permute-start | bytes 1769480 | tf_op jit(solution)/shard_map/ppermute | solution.py:311
  91.3 17.4 %collective-permute-start.24 = (bf16[4,96,768]{2,1,0:T(8,128)(2,1)}, bf16[4,96,768]{2,1,0:T(8,128)(2,1)S(1)}, u32[]{:S(2)}, u32[]{:S(2)}) collective-permute-start(bf16[4,96,768]{2,1,0:T(8,128)(2,1)} %pad_maximum_fusion.1.refs_0_), channel_id=1, source_target_pairs={{0,4},{4,0},{1,5},{5,1},{2,6},{6,2},{3,7},{7,3},{8,12},{12,8},{9,1... | collective-permute-start | bytes 1769480 | tf_op jit(solution)/shard_map/ppermute | solution.py:311
  110.4 15.7 %collective-permute-start.10 = (bf16[128,1536]{1,0:T(8,128)(2,1)S(1)}, bf16[128,1536]{1,0:T(8,128)(2,1)S(1)}, u32[]{:S(2)}, u32[]{:S(2)}) collective-permute-start(bf16[128,1536]{1,0:T(8,128)(2,1)S(1)} %slice.159), channel_id=1, source_target_pairs={{0,1},{1,0},{2,3},{3,2},{4,5},{5,4},{6,7},{7,6},{8,9},{9,8},{10,11... | collective-permute-start | bytes 1179656 | tf_op jit(solution)/shard_map/ppermute | solution.py:311
  111.6 14.9 %collective-permute-start.11 = (bf16[128,1536]{1,0:T(8,128)(2,1)S(1)}, bf16[128,1536]{1,0:T(8,128)(2,1)S(1)}, u32[]{:S(2)}, u32[]{:S(2)}) collective-permute-start(bf16[128,1536]{1,0:T(8,128)(2,1)S(1)} %slice.160), channel_id=1, source_target_pairs={{0,4},{4,0},{1,5},{5,1},{2,6},{6,2},{3,7},{7,3},{8,12},{12,8},{9,1... | collective-permute-start | bytes 1179656 | tf_op jit(solution)/shard_map/ppermute | solution.py:311
  113.1 15.2 %collective-permute-start.27 = (bf16[4,96,768]{2,1,0:T(8,128)(2,1)S(1)}, bf16[4,96,768]{2,1,0:T(8,128)(2,1)S(1)}, u32[]{:S(2)}, u32[]{:S(2)}) collective-permute-start(bf16[4,96,768]{2,1,0:T(8,128)(2,1)S(1)} %copy-done.19), channel_id=1, source_target_pairs={{0,2},{2,0},{1,3},{3,1},{4,6},{6,4},{5,7},{7,5},{8,10},{10,8},{9,1... | collective-permute-start | bytes 1769480 | tf_op jit(solution)/shard_map/ppermute | solution.py:311
  133.9 19.9 %collective-permute-start.31 = (bf16[256,1536]{1,0:T(8,128)(2,1)}, bf16[256,1536]{1,0:T(8,128)(2,1)S(1)}, u32[]{:S(2)}, u32[]{:S(2)}) collective-permute-start(bf16[256,1536]{1,0:T(8,128)(2,1)} %get-tuple-element.145.refs_0_.second), channel_id=1, source_target_pairs={{0,1},{1,0},{2,3},{3,2},{4,5},{5,4},{6,7},{7,6},{8,9},{9,8},{10,11... | collective-permute-start | bytes 2359304 | tf_op jit(solution)/shard_map/ppermute | solution.py:311
  135.4 19.4 %collective-permute-start.32 = (bf16[256,1536]{1,0:T(8,128)(2,1)}, bf16[256,1536]{1,0:T(8,128)(2,1)S(1)}, u32[]{:S(2)}, u32[]{:S(2)}) collective-permute-start(bf16[256,1536]{1,0:T(8,128)(2,1)} %get-tuple-element.145.refs_0_.second), channel_id=1, source_target_pairs={{0,4},{4,0},{1,5},{5,1},{2,6},{6,2},{3,7},{7,3},{8,12},{12,8},{9,1... | collective-permute-start | bytes 2359304 | tf_op jit(solution)/shard_map/ppermute | solution.py:311
  135.9 19.5 %collective-permute-start.37 = (bf16[256,1536]{1,0:T(8,128)(2,1)S(1)}, bf16[256,1536]{1,0:T(8,128)(2,1)S(1)}, u32[]{:S(2)}, u32[]{:S(2)}) collective-permute-start(bf16[256,1536]{1,0:T(8,128)(2,1)S(1)} %copy-done.31), channel_id=1, source_target_pairs={{0,2},{2,0},{1,3},{3,1},{4,6},{6,4},{5,7},{7,5},{8,10},{10,8},{9,1... | collective-permute-start | bytes 2359304 | tf_op jit(solution)/shard_map/ppermute | solution.py:311
  135.9 20.3 %collective-permute-start.38 = (bf16[256,1536]{1,0:T(8,128)(2,1)S(1)}, bf16[256,1536]{1,0:T(8,128)(2,1)S(1)}, u32[]{:S(2)}, u32[]{:S(2)}) collective-permute-start(bf16[256,1536]{1,0:T(8,128)(2,1)S(1)} %copy-done.28), channel_id=1, source_target_pairs={{0,2},{2,0},{1,3},{3,1},{4,6},{6,4},{5,7},{7,5},{8,10},{10,8},{9,1... | collective-permute-start | bytes 2359304 | tf_op jit(solution)/shard_map/ppermute | solution.py:311
  155.3 25.2 %collective-permute-start.43 = (bf16[256,1536]{1,0:T(8,128)(2,1)}, bf16[256,1536]{1,0:T(8,128)(2,1)S(1)}, u32[]{:S(2)}, u32[]{:S(2)}) collective-permute-start(bf16[256,1536]{1,0:T(8,128)(2,1)} %constant_dynamic-update-slice_fusion.8.refs_2_), channel_id=1, source_target_pairs={{0,2},{2,0},{1,3},{3,1},{4,6},{6,4},{5,7},{7,5},{8,10},{10,8},{9,1... | collective-permute-start | bytes 2359304 | tf_op jit(solution)/shard_map/ppermute | solution.py:311
  155.3 24.5 %collective-permute-start.40 = (bf16[128,1536]{1,0:T(8,128)(2,1)S(1)}, bf16[128,1536]{1,0:T(8,128)(2,1)S(1)}, u32[]{:S(2)}, u32[]{:S(2)}) collective-permute-start(bf16[128,1536]{1,0:T(8,128)(2,1)S(1)} %slice.135), channel_id=1, source_target_pairs={{0,1},{1,0},{2,3},{3,2},{4,5},{5,4},{6,7},{7,6},{8,9},{9,8},{10,11... | collective-permute-start | bytes 1179656 | tf_op jit(solution)/shard_map/ppermute | solution.py:311
  156.2 23.6 %collective-permute-start.41 = (bf16[128,1536]{1,0:T(8,128)(2,1)S(1)}, bf16[128,1536]{1,0:T(8,128)(2,1)S(1)}, u32[]{:S(2)}, u32[]{:S(2)}) collective-permute-start(bf16[128,1536]{1,0:T(8,128)(2,1)S(1)} %slice.136), channel_id=1, source_target_pairs={{0,4},{4,0},{1,5},{5,1},{2,6},{6,2},{3,7},{7,3},{8,12},{12,8},{9,1... | collective-permute-start | bytes 1179656 | tf_op jit(solution)/shard_map/ppermute | solution.py:311
  180.1 22.0 %collective-permute-start.47 = (bf16[256,1664]{1,0:T(8,128)(2,1)}, bf16[256,1664]{1,0:T(8,128)(2,1)}, u32[]{:S(2)}, u32[]{:S(2)}) collective-permute-start(bf16[256,1664]{1,0:T(8,128)(2,1)} %get-tuple-element.163), channel_id=1, source_target_pairs={{0,2},{2,0},{1,3},{3,1},{4,6},{6,4},{5,7},{7,5},{8,10},{10,8},{9,1... | collective-permute-start | bytes 2555912 | tf_op jit(solution)/shard_map/ppermute | solution.py:311
  201.4 25.0 %collective-permute-start.58 = (bf16[256,1664]{1,0:T(8,128)(2,1)}, bf16[256,1664]{1,0:T(8,128)(2,1)}, u32[]{:S(2)}, u32[]{:S(2)}) collective-permute-start(bf16[256,1664]{1,0:T(8,128)(2,1)} %get-tuple-element.184), channel_id=1, source_target_pairs={{0,2},{2,0},{1,3},{3,1},{4,6},{6,4},{5,7},{7,5},{8,10},{10,8},{9,1... | collective-permute-start | bytes 2555912 | tf_op jit(solution)/shard_map/ppermute | solution.py:311
  201.9 168.4 %reduce-scatter.9.cloned.1.call-start = ((), (), s32[]{:S(2)}) async-start(), calls=%async_computation.11 | async-start | bytes 2949120 | tf_op jit(solution)/shard_map/reduce_scatter | solution.py:65
  203.9 22.5 %collective-permute-start.59 = (bf16[128,1664]{1,0:T(8,128)(2,1)S(1)}, bf16[128,1664]{1,0:T(8,128)(2,1)S(1)}, u32[]{:S(2)}, u32[]{:S(2)}) collective-permute-start(bf16[128,1664]{1,0:T(8,128)(2,1)S(1)} %slice.178), channel_id=1, source_target_pairs={{0,1},{1,0},{2,3},{3,2},{4,5},{5,4},{6,7},{7,6},{8,9},{9,8},{10,11... | collective-permute-start | bytes 1277960 | tf_op jit(solution)/shard_map/ppermute | solution.py:311
  207.1 19.9 %collective-permute-start.60 = (bf16[128,1664]{1,0:T(8,128)(2,1)S(1)}, bf16[128,1664]{1,0:T(8,128)(2,1)S(1)}, u32[]{:S(2)}, u32[]{:S(2)}) collective-permute-start(bf16[128,1664]{1,0:T(8,128)(2,1)S(1)} %slice.179), channel_id=1, source_target_pairs={{0,4},{4,0},{1,5},{5,1},{2,6},{6,2},{3,7},{7,3},{8,12},{12,8},{9,1... | collective-permute-start | bytes 1277960 | tf_op jit(solution)/shard_map/ppermute | solution.py:311
  208.7 17.0 %collective-permute-start.45 = (bf16[128,1664]{1,0:T(8,128)(2,1)S(1)}, bf16[128,1664]{1,0:T(8,128)(2,1)S(1)}, u32[]{:S(2)}, u32[]{:S(2)}) collective-permute-start(bf16[128,1664]{1,0:T(8,128)(2,1)S(1)} %get-tuple-element.233), channel_id=1, source_target_pairs={{0,1},{1,0},{2,3},{3,2},{4,5},{5,4},{6,7},{7,6},{8,9},{9,8},{10,11... | collective-permute-start | bytes 1277960 | tf_op jit(solution)/shard_map/ppermute | solution.py:311
  219.2 14.9 %collective-permute-start.49 = (bf16[128,1664]{1,0:T(8,128)(2,1)S(1)}, bf16[128,1664]{1,0:T(8,128)(2,1)S(1)}, u32[]{:S(2)}, u32[]{:S(2)}) collective-permute-start(bf16[128,1664]{1,0:T(8,128)(2,1)S(1)} %reduce-precision_convert_fusion.7), channel_id=1, source_target_pairs={{0,1},{1,0},{2,3},{3,2},{4,5},{5,4},{6,7},{7,6},{8,9},{9,8},{10,11... | collective-permute-start | bytes 1277960 | tf_op jit(solution)/shard_map/ppermute | solution.py:311
  261.1 34.2 %collective-permute-start.50 = (bf16[512,1536]{1,0:T(8,128)(2,1)}, bf16[512,1536]{1,0:T(8,128)(2,1)S(1)}, u32[]{:S(2)}, u32[]{:S(2)}) collective-permute-start(bf16[512,1536]{1,0:T(8,128)(2,1)} %constant_dynamic-update-slice_fusion.16.refs_0_), channel_id=1, source_target_pairs={{0,1},{1,0},{2,3},{3,2},{4,5},{5,4},{6,7},{7,6},{8,9},{9,8},{10,11... | collective-permute-start | bytes 4718600 | tf_op jit(solution)/shard_map/ppermute | solution.py:311
  262.3 34.4 %collective-permute-start.51 = (bf16[512,1536]{1,0:T(8,128)(2,1)}, bf16[512,1536]{1,0:T(8,128)(2,1)S(1)}, u32[]{:S(2)}, u32[]{:S(2)}) collective-permute-start(bf16[512,1536]{1,0:T(8,128)(2,1)} %constant_dynamic-update-slice_fusion.16.refs_0_), channel_id=1, source_target_pairs={{0,4},{4,0},{1,5},{5,1},{2,6},{6,2},{3,7},{7,3},{8,12},{12,8},{9,1... | collective-permute-start | bytes 4718600 | tf_op jit(solution)/shard_map/ppermute | solution.py:311
  297.8 31.1 %all-to-all-start.2 = ((bf16[8,272,448]{2,1,0:T(8,128)(2,1)}), bf16[8,272,448]{2,1,0:T(8,128)(2,1)S(1)}, u32[]{:S(2)}, u32[]{:S(2)}) async-start(bf16[8,272,448]{2,1,0:T(8,128)(2,1)} %constant_dynamic-update-slice_fusion.20), calls=%async_computation.4 | async-start | bytes 4456448 | tf_op jit(solution)/shard_map/all_to_all | solution.py:61
  301.4 71.3 %reduce-scatter.7.cloned.1.call-start = ((), (), s32[]{:S(2)}) async-start(), calls=%async_computation.10 | async-start | bytes 2949120 | tf_op jit(solution)/shard_map/reduce_scatter | solution.py:65
  328.9 19.4 %collective-permute-start.63 = (bf16[256,1536]{1,0:T(8,128)(2,1)}, bf16[256,1536]{1,0:T(8,128)(2,1)S(1)}, u32[]{:S(2)}, u32[]{:S(2)}) collective-permute-start(bf16[256,1536]{1,0:T(8,128)(2,1)} %slice.148), channel_id=1, source_target_pairs={{0,1},{1,0},{2,3},{3,2},{4,5},{5,4},{6,7},{7,6},{8,9},{9,8},{10,11... | collective-permute-start | bytes 2359304 | tf_op jit(solution)/shard_map/ppermute | solution.py:311
  329.9 18.9 %collective-permute-start.64 = (bf16[256,1536]{1,0:T(8,128)(2,1)S(1)}, bf16[256,1536]{1,0:T(8,128)(2,1)S(1)}, u32[]{:S(2)}, u32[]{:S(2)}) collective-permute-start(bf16[256,1536]{1,0:T(8,128)(2,1)S(1)} %slice.149), channel_id=1, source_target_pairs={{0,4},{4,0},{1,5},{5,1},{2,6},{6,2},{3,7},{7,3},{8,12},{12,8},{9,1... | collective-permute-start | bytes 2359304 | tf_op jit(solution)/shard_map/ppermute | solution.py:311
  330.4 25.6 %collective-permute-start.65 = (bf16[512,1536]{1,0:T(8,128)(2,1)}, bf16[512,1536]{1,0:T(8,128)(2,1)}, u32[]{:S(2)}, u32[]{:S(2)}) collective-permute-start(bf16[512,1536]{1,0:T(8,128)(2,1)} %constant_dynamic-update-slice_fusion.16.refs_0_), channel_id=1, source_target_pairs={{0,2},{2,0},{1,3},{3,1},{4,6},{6,4},{5,7},{7,5},{8,10},{10,8},{9,1... | collective-permute-start | bytes 4718600 | tf_op jit(solution)/shard_map/ppermute | solution.py:311
  330.4 20.3 %collective-permute-start.55 = (bf16[256,1536]{1,0:T(8,128)(2,1)}, bf16[256,1536]{1,0:T(8,128)(2,1)S(1)}, u32[]{:S(2)}, u32[]{:S(2)}) collective-permute-start(bf16[256,1536]{1,0:T(8,128)(2,1)} %get-tuple-element.181), channel_id=1, source_target_pairs={{0,2},{2,0},{1,3},{3,1},{4,6},{6,4},{5,7},{7,5},{8,10},{10,8},{9,1... | collective-permute-start | bytes 2359304 | tf_op jit(solution)/shard_map/ppermute | solution.py:311
  331.0 25.5 %collective-permute-start.66 = (bf16[512,1536]{1,0:T(8,128)(2,1)}, bf16[512,1536]{1,0:T(8,128)(2,1)}, u32[]{:S(2)}, u32[]{:S(2)}) collective-permute-start(bf16[512,1536]{1,0:T(8,128)(2,1)} %copy-done.20), channel_id=1, source_target_pairs={{0,2},{2,0},{1,3},{3,1},{4,6},{6,4},{5,7},{7,5},{8,10},{10,8},{9,1... | collective-permute-start | bytes 4718600 | tf_op jit(solution)/shard_map/ppermute | solution.py:311
  350.7 19.6 %collective-permute-start.52 = (bf16[256,1536]{1,0:T(8,128)(2,1)}, bf16[256,1536]{1,0:T(8,128)(2,1)}, u32[]{:S(2)}, u32[]{:S(2)}) collective-permute-start(bf16[256,1536]{1,0:T(8,128)(2,1)} %get-tuple-element.177), channel_id=1, source_target_pairs={{0,2},{2,0},{1,3},{3,1},{4,6},{6,4},{5,7},{7,5},{8,10},{10,8},{9,1... | collective-permute-start | bytes 2359304 | tf_op jit(solution)/shard_map/ppermute | solution.py:311
  352.2 20.5 %all-to-all-start = ((bf16[4,96,768]{2,1,0:T(8,128)(2,1)}), bf16[4,96,768]{2,1,0:T(8,128)(2,1)S(1)}, u32[]{:S(2)}, u32[]{:S(2)}) async-start(bf16[4,96,768]{2,1,0:T(8,128)(2,1)} %bitcast.88), calls=%async_computation.1 | async-start | bytes 1179648 | tf_op jit(solution)/shard_map/all_to_all | solution.py:61
  355.7 57.1 %reduce-scatter.11.cloned.1.call-start = ((), (), s32[]{:S(2)}) async-start(), calls=%async_computation.12 | async-start | bytes 2048000 | tf_op jit(solution)/shard_map/reduce_scatter | solution.py:65
  356.0 20.2 %collective-permute-start.54 = (bf16[256,1536]{1,0:T(8,128)(2,1)}, bf16[256,1536]{1,0:T(8,128)(2,1)}, u32[]{:S(2)}, u32[]{:S(2)}) collective-permute-start(bf16[256,1536]{1,0:T(8,128)(2,1)} %get-tuple-element.179), channel_id=1, source_target_pairs={{0,2},{2,0},{1,3},{3,1},{4,6},{6,4},{5,7},{7,5},{8,10},{10,8},{9,1... | collective-permute-start | bytes 2359304 | tf_op jit(solution)/shard_map/ppermute | solution.py:311
  356.5 30.4 %collective-permute-start.56 = (bf16[128,1536]{1,0:T(8,128)(2,1)}, bf16[128,1536]{1,0:T(8,128)(2,1)}, u32[]{:S(2)}, u32[]{:S(2)}) collective-permute-start(bf16[128,1536]{1,0:T(8,128)(2,1)} %get-tuple-element.235), channel_id=1, source_target_pairs={{0,1},{1,0},{2,3},{3,2},{4,5},{5,4},{6,7},{7,6},{8,9},{9,8},{10,11... | collective-permute-start | bytes 1179656 | tf_op jit(solution)/shard_map/ppermute | solution.py:311
  357.6 29.3 %collective-permute-start.57 = (bf16[128,1536]{1,0:T(8,128)(2,1)S(1)}, bf16[128,1536]{1,0:T(8,128)(2,1)}, u32[]{:S(2)}, u32[]{:S(2)}) collective-permute-start(bf16[128,1536]{1,0:T(8,128)(2,1)S(1)} %get-tuple-element.234), channel_id=1, source_target_pairs={{0,4},{4,0},{1,5},{5,1},{2,6},{6,2},{3,7},{7,3},{8,12},{12,8},{9,1... | collective-permute-start | bytes 1179656 | tf_op jit(solution)/shard_map/ppermute | solution.py:311
  388.7 15.6 %collective-permute-start.62 = (bf16[128,1536]{1,0:T(8,128)(2,1)}, bf16[128,1536]{1,0:T(8,128)(2,1)S(1)}, u32[]{:S(2)}, u32[]{:S(2)}) collective-permute-start(bf16[128,1536]{1,0:T(8,128)(2,1)} %reduce-precision_convert_fusion.9), channel_id=1, source_target_pairs={{0,1},{1,0},{2,3},{3,2},{4,5},{5,4},{6,7},{7,6},{8,9},{9,8},{10,11... | collective-permute-start | bytes 1179656 | tf_op jit(solution)/shard_map/ppermute | solution.py:311
  395.0 16.7 %collective-permute-start.61 = (bf16[128,1536]{1,0:T(8,128)(2,1)}, bf16[128,1536]{1,0:T(8,128)(2,1)}, u32[]{:S(2)}, u32[]{:S(2)}) collective-permute-start(bf16[128,1536]{1,0:T(8,128)(2,1)} %reduce-precision_convert_fusion.10), channel_id=1, source_target_pairs={{0,4},{4,0},{1,5},{5,1},{2,6},{6,2},{3,7},{7,3},{8,12},{12,8},{9,1... | collective-permute-start | bytes 1179656 | tf_op jit(solution)/shard_map/ppermute | solution.py:311
  397.0 14.7 %collective-permute-start.53 = (bf16[128,1536]{1,0:T(8,128)(2,1)S(1)}, bf16[128,1536]{1,0:T(8,128)(2,1)S(1)}, u32[]{:S(2)}, u32[]{:S(2)}) collective-permute-start(bf16[128,1536]{1,0:T(8,128)(2,1)S(1)} %slice.174), channel_id=1, source_target_pairs={{0,1},{1,0},{2,3},{3,2},{4,5},{5,4},{6,7},{7,6},{8,9},{9,8},{10,11... | collective-permute-start | bytes 1179656 | tf_op jit(solution)/shard_map/ppermute | solution.py:311
  398.2 22.6 %collective-permute-start.70 = (bf16[256,1536]{1,0:T(8,128)(2,1)}, bf16[256,1536]{1,0:T(8,128)(2,1)}, u32[]{:S(2)}, u32[]{:S(2)}) collective-permute-start(bf16[256,1536]{1,0:T(8,128)(2,1)} %get-tuple-element.222), channel_id=1, source_target_pairs={{0,2},{2,0},{1,3},{3,1},{4,6},{6,4},{5,7},{7,5},{8,10},{10,8},{9,1... | collective-permute-start | bytes 2359304 | tf_op jit(solution)/shard_map/ppermute | solution.py:311
  399.0 20.6 %collective-permute-start.69 = (bf16[128,1536]{1,0:T(8,128)(2,1)}, bf16[128,1536]{1,0:T(8,128)(2,1)}, u32[]{:S(2)}, u32[]{:S(2)}) collective-permute-start(bf16[128,1536]{1,0:T(8,128)(2,1)} %slice.182), channel_id=1, source_target_pairs={{0,4},{4,0},{1,5},{5,1},{2,6},{6,2},{3,7},{7,3},{8,12},{12,8},{9,1... | collective-permute-start | bytes 1179656 | tf_op jit(solution)/shard_map/ppermute | solution.py:311
  415.2 17.1 %all-to-all-start.4 = ((bf16[8,112,448]{2,1,0:T(8,128)(2,1)}), bf16[8,112,448]{2,1,0:T(8,128)(2,1)S(1)}, u32[]{:S(2)}, u32[]{:S(2)}) async-start(bf16[8,112,448]{2,1,0:T(8,128)(2,1)} %maximum_maximum_fusion), calls=%async_computation.8 | async-start | bytes 1835008 | tf_op jit(solution)/shard_map/all_to_all | solution.py:61
  (114 other events, 1184.3 us)
Sparse Core Ops, SparseCore 0:
  202.0 47.9 reduce-scatter.4
  258.2 48.2 reduce-scatter.8
  308.8 47.5 reduce-scatter.6
  370.4 36.3 reduce-scatter.10

commit v5 on v4

--- a/solution.py
+++ b/solution.py
@@ -974,19 +974,20 @@
         [((plane, length + 16, dense_cols), bf16)],
         56,
     )
+    both = jnp.concatenate(
+        lax.optimization_barrier((attended, first_in, last_y, last_x))[:2], axis=0
+    )
+    both_sides = plane_sides(both)
+    *both_sides, tokens_late = lax.optimization_barrier((*both_sides, tokens))
     tokens_grad, gain_one_grad = run_kernel(
         first_back_kernel,
         5,
         at,
-        (back_cols, qkv_w, tokens, gain_one, resid_grad),
+        (back_cols, qkv_w, tokens_late, gain_one, resid_grad),
         [((length, model_width), bf16), ((1, model_width), f32)],
         24,
     )
 
-    both = jnp.concatenate(
-        lax.optimization_barrier((attended, first_in, last_y, last_x))[:2], axis=0
-    )
-    both_sides = plane_sides(both)
     narrow_part = jnp.concatenate(
         [router_acc[:, :experts_all], gain_one_grad.T, gain_two_grad.T], axis=1
     )
@@ -1038,9 +1039,9 @@
         cost_estimate=cost(8),
         compiler_params=pltpu.CompilerParams(vmem_limit_bytes=32 * 2**20),
     )(at, back_cols, *both_pieces)
-    dense_part, up_sum = lax.optimization_barrier((dense_part, up_sum))
+    mixed = [over_core(near, far) for near, far in zip(shares[:4], shares[4:])]
+    dense_part, up_sum, mixed = lax.optimization_barrier((dense_part, up_sum, mixed))
     dense_sum = scatter_sum(dense_part.reshape(-1, dense_cols), "z")
-    mixed = [over_core(near, far) for near, far in zip(shares[:4], shares[4:])]
     early = early_sums(mixed[1], mixed[2])
     first, down_grad, gate_grad = lax.optimization_barrier(
         (corner_first(mixed[3]), down_grad, gate_grad)

time: 451 us -> 465 us (1.031)
  waiting for transfers between devices: 157 us -> 177 us
  local copies, waits for them, and re-layouts: 72.2 us -> 64.4 us
    ppermute x65, waiting for transfers between devices: 102 us -> 130 us  [swap(): return lax.ppermute(block, axis, [(0, 1), (1, 0)])]
    unnamed x178, local copies, waits for them, and re-layouts: 40.9 us -> 33.3 us
    all_to_all x5, waiting for transfers between devices: 35.3 us -> 28.4 us  [exchange(): return lax.all_to_all(block, axes, split_axis=0, concat_axis=0, tiled=True)]
    convert_element_type x10 -> x11, other arithmetic: 10.1 us -> 9.8 us  [rounded(): return lax.reduce_precision(values, 8, 7).astype(jnp.bfloat16)]
  transfers between devices with their start and end apart: 80 -> 80, of which waited for: 31 -> 32; matrix products, arithmetic and copies ran while one was open for 13% -> 12% of each run, Pallas kernels for 23% -> 23%
where the time goes in v5:
time: 465 us; the launch traced here: 456 us
  waiting for transfers between devices  177 us (38%)
  Pallas kernels  105 us (23%)
  starting transfers between devices  69.8 us (15%)
  local copies, waits for them, and re-layouts  64.4 us (14%)
  other arithmetic  23.2 us (5%)
  between operations  16.1 us (3%)
    ppermute x65, waiting for transfers between devices, swap(): return lax.ppermute(block, axis, [(0, 1), (1, 0)])  130 us
    pallas_call x11, Pallas kernels, run_kernel(): pl.pallas_call(kernel, out_shape=[jax.ShapeDtypeStruct(shape, dtype) for...  98.3 us
    ppermute x65, starting transfers between devices, swap(): return lax.ppermute(block, axis, [(0, 1), (1, 0)])  40.5 us
    unnamed x178, local copies, waits for them, and re-layouts  33.3 us
    all_to_all x5, waiting for transfers between devices, exchange(): return lax.all_to_all(block, axes, split_axis=0, concat_axis=0, tiled=True)  28.4 us
    all_to_all x5, starting transfers between devices, exchange(): return lax.all_to_all(block, axes, split_axis=0, concat_axis=0, tiled=True)  18.6 us
    ppermute x6, waiting for transfers between devices, shifts(): lax.ppermute(block, 'z', [(i, (i + k) % depth) for i in range(depth)])  18.3 us
    ppermute x6, starting transfers between devices, shifts(): lax.ppermute(block, 'z', [(i, (i + k) % depth) for i in range(depth)])  10.2 us
  transfers between devices with their start and end apart: 80, of which 32 were waited for; matrix products, arithmetic and copies ran while one was open for 12% of the time, Pallas kernels for 23%

profile of v5, /device:TPU:0, one launch (start us, length us, event | category | flops | bytes accessed | tf_op | source)
XLA Modules:
  0.0 456.1 jit_solution(16692727533419571598)
XLA Ops:
  8.1 5.1 %collective-permute-start = (bf16[96,128]{1,0:T(8,128)(2,1)S(1)}, bf16[96,128]{1,0:T(8,128)(2,1)S(1)}, u32[]{:S(2)}, u32[]{:S(2)}) collective-permute-start(bf16[96,128]{1,0:T(8,128)(2,1)S(1)} %pad.9), channel_id=1, source_target_pairs={{0,24},{8,0},{16,8},{24,16},{1,25},{9,1},{17,9},{25,17},{2,26},{10... | collective-permute-start | bytes 73736 | tf_op jit(solution)/shard_map/ppermute | solution.py:317
  18.2 2.8 collective-permute-start.14
  26.1 2.7 collective-permute-done.3
  33.0 18.3 %collective-permute-done.13 = bf16[96,1792]{1,0:T(8,128)(2,1)} collective-permute-done((bf16[96,1792]{1,0:T(8,128)(2,1)}, bf16[96,1792]{1,0:T(8,128)(2,1)}, u32[]{:S(2)}, u32[]{:S(2)}) %collective-permute-start.13) | collective-permute-done | bytes 344096 | tf_op jit(solution)/shard_map/ppermute | solution.py:317
  59.1 3.2 dynamic-slice_bitcast_fusion.2.refs_4_.refs_8_
  62.4 3.2 dynamic-slice_bitcast_fusion.1.refs_5_.refs_9_
  65.6 1.8 dynamic-slice_bitcast_fusion.refs_6_.refs_10_.refs_3_
  67.4 7.3 %collective-permute-done.16.refs_2_ = bf16[4,96,1024]{2,1,0:T(8,128)(2,1)} collective-permute-done((bf16[4,96,1024]{2,1,0:T(8,128)(2,1)S(1)}, bf16[4,96,1024]{2,1,0:T(8,128)(2,1)}, u32[]{:S(2)}, u32[]{:S(2)}) %collective-permute-start.16) | collective-permute-done | bytes 786464 | tf_op jit(solution)/shard_map/ppermute | solution.py:311
  80.3 4.2 collective-permute-done.17
  94.7 9.0 %shard_map.229 = (bf16[256,1536]{1,0:T(8,128)(2,1)S(1)}, bf16[256,1536]{1,0:T(8,128)(2,1)S(1)}, bf16[256,256]{1,0:T(8,128)(2,1)S(1)}, bf16[256,256]{1,0:T(8,128)...) custom-call(s32[7]{0:T(128)S(1)} %copy-done.38, ...), custom_call_target="tpu_custom_call" | custom-call | flops 11000000512 | bytes 11000000 | tf_op jit(solution)/shard_map/pallas_call | solution.py:400
  103.8 2.7 copy-done.45
  112.1 5.7 %collective-permute-done.25 = bf16[2,96,768]{2,1,0:T(8,128)(2,1)S(1)} collective-permute-done((bf16[2,96,768]{2,1,0:T(8,128)(2,1)S(1)}, bf16[2,96,768]{2,1,0:T(8,128)(2,1)S(1)}, u32[]{:S(2)}, u32[]{:S(2)}) %collective-permute-start.25) | collective-permute-done | bytes 294944 | tf_op jit(solution)/shard_map/ppermute | solution.py:311
  119.4 5.7 %collective-permute-done.10 = bf16[128,1536]{1,0:T(8,128)(2,1)S(1)} collective-permute-done((bf16[128,1536]{1,0:T(8,128)(2,1)S(1)}, bf16[128,1536]{1,0:T(8,128)(2,1)S(1)}, u32[]{:S(2)}, u32[]{:S(2)}) %collective-permute-start.10) | collective-permute-done | bytes 393248 | tf_op jit(solution)/shard_map/ppermute | solution.py:311
  128.0 4.1 shard_map.230
  136.0 10.4 %shard_map.231 = (bf16[384,1536]{1,0:T(8,128)(2,1)S(1)}, bf16[384,1536]{1,0:T(8,128)(2,1)S(1)}, bf16[384,768]{1,0:T(8,128)(2,1)S(1)}, bf16[384,768]{1,0:T(8,128)...) custom-call(s32[7]{0:T(128)S(1)} %copy-done.39, ...), custom_call_target="tpu_custom_call" | custom-call | flops 8000000000 | bytes 8000000 | tf_op jit(solution)/shard_map/pallas_call | solution.py:400
  148.1 5.4 %collective-permute-done.34.refs_0_ = bf16[256,1536]{1,0:T(8,128)(2,1)S(1)} collective-permute-done((bf16[256,1536]{1,0:T(8,128)(2,1)}, bf16[256,1536]{1,0:T(8,128)(2,1)S(1)}, u32[]{:S(2)}, u32[]{:S(2)}) %collective-permute-start.34) | collective-permute-done | bytes 786464 | tf_op jit(solution)/shard_map/ppermute | solution.py:311
  156.4 2.1 collective-permute-done.37.refs_3_
  158.6 17.2 %shard_map.232 = (bf16[768,1536]{1,0:T(8,128)(2,1)S(1)}, bf16[768,1536]{1,0:T(8,128)(2,1)S(1)}, bf16[768,768]{1,0:T(8,128)(2,1)S(1)}, bf16[768,768]{1,0:T(8,128)...) custom-call(s32[7]{0:T(128)S(1)} %copy-done.39, ...), custom_call_target="tpu_custom_call" | custom-call | flops 16000000000 | bytes 16000000 | tf_op jit(solution)/shard_map/pallas_call | solution.py:400
  179.8 1.8 collective-permute-done.46.refs_1_
  181.6 13.1 %shard_map.233 = (bf16[384,1536]{1,0:T(8,128)(2,1)S(1)}, bf16[384,1536]{1,0:T(8,128)(2,1)}, bf16[384,768]{1,0:T(8,128)(2,1)S(1)}, bf16[384,768]{1,0:T(8,128)(2,1...) custom-call(s32[7]{0:T(128)S(1)} %copy-done.39, ...), custom_call_target="tpu_custom_call" | custom-call | flops 8000000000 | bytes 8000000 | tf_op jit(solution)/shard_map/pallas_call | solution.py:400
  209.3 15.0 %collective-permute-done.49 = bf16[128,1664]{1,0:T(8,128)(2,1)S(1)} collective-permute-done((bf16[128,1664]{1,0:T(8,128)(2,1)S(1)}, bf16[128,1664]{1,0:T(8,128)(2,1)S(1)}, u32[]{:S(2)}, u32[]{:S(2)}) %collective-permute-start.49) | collective-permute-done | bytes 426016 | tf_op jit(solution)/shard_map/ppermute | solution.py:311
  225.0 3.8 collective-permute-done.51
  230.2 6.6 %collective-permute-done.50.last_y = bf16[128,1664]{1,0:T(8,128)(2,1)S(1)} collective-permute-done((bf16[128,1664]{1,0:T(8,128)(2,1)S(1)}, bf16[128,1664]{1,0:T(8,128)(2,1)S(1)}, u32[]{:S(2)}, u32[]{:S(2)}) %collective-permute-start.50) | collective-permute-done | bytes 426016 | tf_op jit(solution)/shard_map/ppermute | solution.py:311
  239.1 8.4 %shard_map.234 = (f32[256,1536]{1,0:T(8,128)}, bf16[256,1536]{1,0:T(8,128)(2,1)}, bf16[256,1536]{1,0:T(8,128)(2,1)}, f32[1536,128]{1,0:T(8,128)}, f32[1,1536]{1,0:T(1,128)}) custom-call(s32[7]{0:T(128)} %stack.76.at, bf16[256,1664]{1,0:T(8,128)(2,1)} %copy-done.48, bf16[256,1664]{1,0:T(8,128)(2,1)} %collective-permute-done.33.far, ...), custom_call_target="tpu_custom_call" | custom-call | flops 6000000000 | bytes 6000000 | tf_op jit(solution)/shard_map/pallas_call | solution.py:400
  247.5 12.8 %shard_map.235 = (bf16[1536,768]{1,0:T(8,128)(2,1)}, bf16[1536,768]{1,0:T(8,128)(2,1)}) custom-call(s32[7]{0:T(128)} %stack.76.at, bf16[384,1536]{1,0:T(8,128)(2,1)} %copy-done.53, bf16[768,1536]{1,0:T(8,128)(2,1)} %copy-done.52, bf16[384,1536]{1,0:T(8,128)(2,1)} %copy-done.51, bf16[384,768]{1,0:T(8,128)(2,1)} %copy-done.61, bf16[768,768]{1,0:T(8,128)(2,1)} %copy-done.59, ...), custom_call_target="tpu_custom_call" | custom-call | flops 8000000000 | bytes 8000000 | tf_op jit(solution)/shard_map/pallas_call | solution.py:400
  263.6 8.5 %shard_map.236.back = bf16[8,272,448]{2,1,0:T(8,128)(2,1)} custom-call(s32[7]{0:T(128)} %stack.76.at, bf16[256,1536]{1,0:T(8,128)(2,1)} %get-tuple-element.185.attended, bf16[12,256,256]{2,1,0:T(8,128)(2,1)} %copy-done.49, bf16[256,1536]{1,0:T(8,128)(2,1)} %copy-done.54, bf16[256,256]{1,0:T(8,128)(2,1)} %copy-done.64, bf16[256,256]{1,0:T(8,128)(2,1)} %copy-done.65, ...), custom_call_target="tpu_custom_call" | custom-call | flops 6000000000 | bytes 6000000 | tf_op jit(solution)/shard_map/pallas_call | solution.py:400
  272.1 23.6 %collective-permute-done.53.refs_1_ = bf16[512,1536]{1,0:T(8,128)(2,1)} collective-permute-done((bf16[512,1536]{1,0:T(8,128)(2,1)S(1)}, bf16[512,1536]{1,0:T(8,128)(2,1)}, u32[]{:S(2)}, u32[]{:S(2)}) %collective-permute-start.53) | collective-permute-done | bytes 1572896 | tf_op jit(solution)/shard_map/ppermute | solution.py:311
  298.3 2.8 copy-done.46
  301.1 3.7 shard_map.237
  307.2 3.6 all-to-all-start
  311.6 9.3 %shard_map.238 = (bf16[256,1536]{1,0:T(8,128)(2,1)}, bf16[256,1536]{1,0:T(8,128)(2,1)}, bf16[256,1536]{1,0:T(8,128)(2,1)}, bf16[256,1536]{1,0:T(8,128)(2,1)}, bf...) custom-call(s32[7]{0:T(128)} %stack.76.at, ...), custom_call_target="tpu_custom_call" | custom-call | flops 10000000000 | bytes 10000000 | tf_op jit(solution)/shard_map/pallas_call | solution.py:400
  321.3 2.2 slice.143
  324.7 13.7 %all-to-all-done.back = bf16[8,272,448]{2,1,0:T(8,128)(2,1)S(1)} async-done(((bf16[8,272,448]{2,1,0:T(8,128)(2,1)}), bf16[8,272,448]{2,1,0:T(8,128)(2,1)S(1)}, u32[]{:S(2)}, u32[]{:S(2)}) %all-to-all-start) | async-done | bytes 1949728 | tf_op jit(solution)/shard_map/all_to_all | solution.py:61
  340.4 2.5 reduce-precision_convert_fusion.6
  342.9 14.9 %collective-permute-done.55 = bf16[256,1536]{1,0:T(8,128)(2,1)S(1)} collective-permute-done((bf16[256,1536]{1,0:T(8,128)(2,1)}, bf16[256,1536]{1,0:T(8,128)(2,1)S(1)}, u32[]{:S(2)}, u32[]{:S(2)}) %collective-permute-start.55) | collective-permute-done | bytes 786464 | tf_op jit(solution)/shard_map/ppermute | solution.py:311
  363.0 2.7 collective-permute-done.64
  365.9 4.2 all-to-all-start.1
  371.8 6.9 %shard_map.239 = bf16[4,400,448]{2,1,0:T(8,128)(2,1)S(1)} custom-call(s32[7]{0:T(128)S(1)} %copy-done.41, bf16[8,272,448]{2,1,0:T(8,128)(2,1)S(1)} %all-to-all-done.back, bf16[512,1536]{1,0:T(8,128)(2,1)S(1)} %copy-done.21, bf16[512,1536]{1,0:T(8,128)(2,1)} %collective-permute-done.53.refs_1_, bf16[512,1536]{1,0:T(8,128)(2,1)} %collective-permute-done.54.refs_2_, ...), custom_call_target="tpu_custom_call" | custom-call | flops 8000000000 | bytes 8000000 | tf_op jit(solution)/shard_map/pallas_call | solution.py:1030
  380.0 3.5 all-to-all-start.2
  385.4 2.0 collective-permute-start.67
  387.4 2.2 convert_element_type.212
  389.5 3.9 all-to-all-done.2
  394.6 3.6 all-to-all-start.3
  398.2 3.2 collective-permute-done.67
  409.3 7.3 %collective-permute-done.68 = bf16[128,1536]{1,0:T(8,128)(2,1)S(1)} collective-permute-done((bf16[128,1536]{1,0:T(8,128)(2,1)}, bf16[128,1536]{1,0:T(8,128)(2,1)S(1)}, u32[]{:S(2)}, u32[]{:S(2)}) %collective-permute-start.68) | collective-permute-done | bytes 393248 | tf_op jit(solution)/shard_map/ppermute | solution.py:311
  417.3 7.2 %collective-permute-done.70 = bf16[128,1536]{1,0:T(8,128)(2,1)S(1)} collective-permute-done((bf16[128,1536]{1,0:T(8,128)(2,1)S(1)}, bf16[128,1536]{1,0:T(8,128)(2,1)S(1)}, u32[]{:S(2)}, u32[]{:S(2)}) %collective-permute-start.70) | collective-permute-done | bytes 393248 | tf_op jit(solution)/shard_map/ppermute | solution.py:311
  428.8 3.7 all-to-all-start.4
  435.1 10.8 %all-to-all-done.4.sums = bf16[8,112,448]{2,1,0:T(8,128)(2,1)S(1)} async-done(((bf16[8,112,448]{2,1,0:T(8,128)(2,1)}), bf16[8,112,448]{2,1,0:T(8,128)(2,1)S(1)}, u32[]{:S(2)}, u32[]{:S(2)}) %all-to-all-start.4) | async-done | bytes 802848 | tf_op jit(solution)/shard_map/all_to_all | solution.py:61
  (404 shorter events, 121.4 us)
Async XLA Ops:
  7.2 300.1 %reduce-scatter.5.cloned.1.call-start = ((), (), s32[]{:S(2)}) async-start(), calls=%async_computation.9 | async-start | bytes 2949120 | tf_op jit(solution)/shard_map/reduce_scatter | solution.py:65
  8.1 14.2 %collective-permute-start = (bf16[96,128]{1,0:T(8,128)(2,1)S(1)}, bf16[96,128]{1,0:T(8,128)(2,1)S(1)}, u32[]{:S(2)}, u32[]{:S(2)}) collective-permute-start(bf16[96,128]{1,0:T(8,128)(2,1)S(1)} %pad.9), channel_id=1, source_target_pairs={{0,24},{8,0},{16,8},{24,16},{1,25},{9,1},{17,9},{25,17},{2,26},{10... | collective-permute-start | bytes 73736 | tf_op jit(solution)/shard_map/ppermute | solution.py:317
  18.2 13.8 %collective-permute-start.14 = (bf16[96,1792]{1,0:T(8,128)(2,1)}, bf16[96,1792]{1,0:T(8,128)(2,1)}, u32[]{:S(2)}, u32[]{:S(2)}) collective-permute-start(bf16[96,1792]{1,0:T(8,128)(2,1)} %pad_maximum_fusion.3), channel_id=1, source_target_pairs={{0,24},{8,0},{16,8},{24,16},{1,25},{9,1},{17,9},{25,17},{2,26},{10... | collective-permute-start | bytes 1032200 | tf_op jit(solution)/shard_map/ppermute | solution.py:317
  21.1 30.2 %collective-permute-start.13 = (bf16[96,1792]{1,0:T(8,128)(2,1)}, bf16[96,1792]{1,0:T(8,128)(2,1)}, u32[]{:S(2)}, u32[]{:S(2)}) collective-permute-start(bf16[96,1792]{1,0:T(8,128)(2,1)} %pad_maximum_fusion.3), channel_id=1, source_target_pairs={{0,16},{8,24},{16,0},{24,8},{1,17},{9,25},{17,1},{25,9},{2,18},{10... | collective-permute-start | bytes 1032200 | tf_op jit(solution)/shard_map/ppermute | solution.py:317
  22.3 29.9 %collective-permute-start.12 = (bf16[96,1792]{1,0:T(8,128)(2,1)}, bf16[96,1792]{1,0:T(8,128)(2,1)}, u32[]{:S(2)}, u32[]{:S(2)}) collective-permute-start(bf16[96,1792]{1,0:T(8,128)(2,1)} %pad_maximum_fusion.3), channel_id=1, source_target_pairs={{0,8},{8,16},{16,24},{24,0},{1,9},{9,17},{17,25},{25,1},{2,10},{10... | collective-permute-start | bytes 1032200 | tf_op jit(solution)/shard_map/ppermute | solution.py:317
  30.7 26.3 %collective-permute-start.8 = (bf16[256,1536]{1,0:T(8,128)(2,1)}, bf16[256,1536]{1,0:T(8,128)(2,1)S(1)}, u32[]{:S(2)}, u32[]{:S(2)}) collective-permute-start(bf16[256,1536]{1,0:T(8,128)(2,1)} %cot.1), channel_id=1, source_target_pairs={{0,4},{4,0},{1,5},{5,1},{2,6},{6,2},{3,7},{7,3},{8,12},{12,8},{9,1... | collective-permute-start | bytes 2359304 | tf_op jit(solution)/shard_map/ppermute | solution.py:311
  31.2 25.8 %collective-permute-start.9 = (bf16[256,1536]{1,0:T(8,128)(2,1)}, bf16[256,1536]{1,0:T(8,128)(2,1)S(1)}, u32[]{:S(2)}, u32[]{:S(2)}) collective-permute-start(bf16[256,1536]{1,0:T(8,128)(2,1)} %cot.1), channel_id=1, source_target_pairs={{0,1},{1,0},{2,3},{3,2},{4,5},{5,4},{6,7},{7,6},{8,9},{9,8},{10,11... | collective-permute-start | bytes 2359304 | tf_op jit(solution)/shard_map/ppermute | solution.py:311
  57.0 18.7 %collective-permute-start.15 = (bf16[4,96,1024]{2,1,0:T(8,128)(2,1)S(1)}, bf16[4,96,1024]{2,1,0:T(8,128)(2,1)}, u32[]{:S(2)}, u32[]{:S(2)}) collective-permute-start(bf16[4,96,1024]{2,1,0:T(8,128)(2,1)S(1)} %pad_maximum_fusion.refs_0_), channel_id=1, source_target_pairs={{0,1},{1,0},{2,3},{3,2},{4,5},{5,4},{6,7},{7,6},{8,9},{9,8},{10,11... | collective-permute-start | bytes 2359304 | tf_op jit(solution)/shard_map/ppermute | solution.py:311
  57.6 17.1 %collective-permute-start.16 = (bf16[4,96,1024]{2,1,0:T(8,128)(2,1)S(1)}, bf16[4,96,1024]{2,1,0:T(8,128)(2,1)}, u32[]{:S(2)}, u32[]{:S(2)}) collective-permute-start(bf16[4,96,1024]{2,1,0:T(8,128)(2,1)S(1)} %pad_maximum_fusion.refs_0_), channel_id=1, source_target_pairs={{0,4},{4,0},{1,5},{5,1},{2,6},{6,2},{3,7},{7,3},{8,12},{12,8},{9,1... | collective-permute-start | bytes 2359304 | tf_op jit(solution)/shard_map/ppermute | solution.py:311
  89.7 18.0 %collective-permute-start.23 = (bf16[4,96,768]{2,1,0:T(8,128)(2,1)}, bf16[4,96,768]{2,1,0:T(8,128)(2,1)S(1)}, u32[]{:S(2)}, u32[]{:S(2)}) collective-permute-start(bf16[4,96,768]{2,1,0:T(8,128)(2,1)} %pad_maximum_fusion.1.refs_0_), channel_id=1, source_target_pairs={{0,1},{1,0},{2,3},{3,2},{4,5},{5,4},{6,7},{7,6},{8,9},{9,8},{10,11... | collective-permute-start | bytes 1769480 | tf_op jit(solution)/shard_map/ppermute | solution.py:311
  90.3 17.4 %collective-permute-start.24 = (bf16[4,96,768]{2,1,0:T(8,128)(2,1)}, bf16[4,96,768]{2,1,0:T(8,128)(2,1)S(1)}, u32[]{:S(2)}, u32[]{:S(2)}) collective-permute-start(bf16[4,96,768]{2,1,0:T(8,128)(2,1)} %pad_maximum_fusion.1.refs_0_), channel_id=1, source_target_pairs={{0,4},{4,0},{1,5},{5,1},{2,6},{6,2},{3,7},{7,3},{8,12},{12,8},{9,1... | collective-permute-start | bytes 1769480 | tf_op jit(solution)/shard_map/ppermute | solution.py:311
  109.9 15.2 %collective-permute-start.10 = (bf16[128,1536]{1,0:T(8,128)(2,1)S(1)}, bf16[128,1536]{1,0:T(8,128)(2,1)S(1)}, u32[]{:S(2)}, u32[]{:S(2)}) collective-permute-start(bf16[128,1536]{1,0:T(8,128)(2,1)S(1)} %slice.159), channel_id=1, source_target_pairs={{0,1},{1,0},{2,3},{3,2},{4,5},{5,4},{6,7},{7,6},{8,9},{9,8},{10,11... | collective-permute-start | bytes 1179656 | tf_op jit(solution)/shard_map/ppermute | solution.py:311
  111.0 15.4 %collective-permute-start.11 = (bf16[128,1536]{1,0:T(8,128)(2,1)S(1)}, bf16[128,1536]{1,0:T(8,128)(2,1)S(1)}, u32[]{:S(2)}, u32[]{:S(2)}) collective-permute-start(bf16[128,1536]{1,0:T(8,128)(2,1)S(1)} %slice.160), channel_id=1, source_target_pairs={{0,4},{4,0},{1,5},{5,1},{2,6},{6,2},{3,7},{7,3},{8,12},{12,8},{9,1... | collective-permute-start | bytes 1179656 | tf_op jit(solution)/shard_map/ppermute | solution.py:311
  112.1 15.9 %collective-permute-start.27 = (bf16[4,96,768]{2,1,0:T(8,128)(2,1)S(1)}, bf16[4,96,768]{2,1,0:T(8,128)(2,1)S(1)}, u32[]{:S(2)}, u32[]{:S(2)}) collective-permute-start(bf16[4,96,768]{2,1,0:T(8,128)(2,1)S(1)} %copy-done.19), channel_id=1, source_target_pairs={{0,2},{2,0},{1,3},{3,1},{4,6},{6,4},{5,7},{7,5},{8,10},{10,8},{9,1... | collective-permute-start | bytes 1769480 | tf_op jit(solution)/shard_map/ppermute | solution.py:311
  133.8 19.7 %collective-permute-start.34 = (bf16[256,1536]{1,0:T(8,128)(2,1)}, bf16[256,1536]{1,0:T(8,128)(2,1)S(1)}, u32[]{:S(2)}, u32[]{:S(2)}) collective-permute-start(bf16[256,1536]{1,0:T(8,128)(2,1)} %get-tuple-element.151.refs_0_.second), channel_id=1, source_target_pairs={{0,1},{1,0},{2,3},{3,2},{4,5},{5,4},{6,7},{7,6},{8,9},{9,8},{10,11... | collective-permute-start | bytes 2359304 | tf_op jit(solution)/shard_map/ppermute | solution.py:311
  134.4 19.6 %collective-permute-start.35 = (bf16[256,1536]{1,0:T(8,128)(2,1)}, bf16[256,1536]{1,0:T(8,128)(2,1)S(1)}, u32[]{:S(2)}, u32[]{:S(2)}) collective-permute-start(bf16[256,1536]{1,0:T(8,128)(2,1)} %get-tuple-element.151.refs_0_.second), channel_id=1, source_target_pairs={{0,4},{4,0},{1,5},{5,1},{2,6},{6,2},{3,7},{7,3},{8,12},{12,8},{9,1... | collective-permute-start | bytes 2359304 | tf_op jit(solution)/shard_map/ppermute | solution.py:311
  134.9 19.7 %collective-permute-start.38 = (bf16[256,1536]{1,0:T(8,128)(2,1)S(1)}, bf16[256,1536]{1,0:T(8,128)(2,1)S(1)}, u32[]{:S(2)}, u32[]{:S(2)}) collective-permute-start(bf16[256,1536]{1,0:T(8,128)(2,1)S(1)} %copy-done.27), channel_id=1, source_target_pairs={{0,2},{2,0},{1,3},{3,1},{4,6},{6,4},{5,7},{7,5},{8,10},{10,8},{9,1... | collective-permute-start | bytes 2359304 | tf_op jit(solution)/shard_map/ppermute | solution.py:311
  134.9 21.0 %collective-permute-start.39 = (bf16[256,1536]{1,0:T(8,128)(2,1)S(1)}, bf16[256,1536]{1,0:T(8,128)(2,1)S(1)}, u32[]{:S(2)}, u32[]{:S(2)}) collective-permute-start(bf16[256,1536]{1,0:T(8,128)(2,1)S(1)} %copy-done.24), channel_id=1, source_target_pairs={{0,2},{2,0},{1,3},{3,1},{4,6},{6,4},{5,7},{7,5},{8,10},{10,8},{9,1... | collective-permute-start | bytes 2359304 | tf_op jit(solution)/shard_map/ppermute | solution.py:311
  154.5 25.2 %collective-permute-start.47 = (bf16[256,1536]{1,0:T(8,128)(2,1)}, bf16[256,1536]{1,0:T(8,128)(2,1)S(1)}, u32[]{:S(2)}, u32[]{:S(2)}) collective-permute-start(bf16[256,1536]{1,0:T(8,128)(2,1)} %constant_dynamic-update-slice_fusion.8.refs_2_), channel_id=1, source_target_pairs={{0,2},{2,0},{1,3},{3,1},{4,6},{6,4},{5,7},{7,5},{8,10},{10,8},{9,1... | collective-permute-start | bytes 2359304 | tf_op jit(solution)/shard_map/ppermute | solution.py:311
  154.6 24.5 %collective-permute-start.44 = (bf16[128,1536]{1,0:T(8,128)(2,1)S(1)}, bf16[128,1536]{1,0:T(8,128)(2,1)S(1)}, u32[]{:S(2)}, u32[]{:S(2)}) collective-permute-start(bf16[128,1536]{1,0:T(8,128)(2,1)S(1)} %slice.137), channel_id=1, source_target_pairs={{0,1},{1,0},{2,3},{3,2},{4,5},{5,4},{6,7},{7,6},{8,9},{9,8},{10,11... | collective-permute-start | bytes 1179656 | tf_op jit(solution)/shard_map/ppermute | solution.py:311
  155.9 23.2 %collective-permute-start.45 = (bf16[128,1536]{1,0:T(8,128)(2,1)S(1)}, bf16[128,1536]{1,0:T(8,128)(2,1)S(1)}, u32[]{:S(2)}, u32[]{:S(2)}) collective-permute-start(bf16[128,1536]{1,0:T(8,128)(2,1)S(1)} %slice.138), channel_id=1, source_target_pairs={{0,4},{4,0},{1,5},{5,1},{2,6},{6,2},{3,7},{7,3},{8,12},{12,8},{9,1... | collective-permute-start | bytes 1179656 | tf_op jit(solution)/shard_map/ppermute | solution.py:311
  179.4 22.1 %collective-permute-start.40 = (bf16[256,1664]{1,0:T(8,128)(2,1)}, bf16[256,1664]{1,0:T(8,128)(2,1)}, u32[]{:S(2)}, u32[]{:S(2)}) collective-permute-start(bf16[256,1664]{1,0:T(8,128)(2,1)} %get-tuple-element.158), channel_id=1, source_target_pairs={{0,2},{2,0},{1,3},{3,1},{4,6},{6,4},{5,7},{7,5},{8,10},{10,8},{9,1... | collective-permute-start | bytes 2555912 | tf_op jit(solution)/shard_map/ppermute | solution.py:311
  200.7 29.5 %collective-permute-start.33 = (bf16[256,1664]{1,0:T(8,128)(2,1)}, bf16[256,1664]{1,0:T(8,128)(2,1)}, u32[]{:S(2)}, u32[]{:S(2)}) collective-permute-start(bf16[256,1664]{1,0:T(8,128)(2,1)} %get-tuple-element.153), channel_id=1, source_target_pairs={{0,2},{2,0},{1,3},{3,1},{4,6},{6,4},{5,7},{7,5},{8,10},{10,8},{9,1... | collective-permute-start | bytes 2555912 | tf_op jit(solution)/shard_map/ppermute | solution.py:311
  201.2 178.7 %reduce-scatter.7.cloned.1.call-start = ((), (), s32[]{:S(2)}) async-start(), calls=%async_computation.10 | async-start | bytes 2949120 | tf_op jit(solution)/shard_map/reduce_scatter | solution.py:65
  203.2 27.0 %collective-permute-start.41 = (bf16[128,1664]{1,0:T(8,128)(2,1)S(1)}, bf16[128,1664]{1,0:T(8,128)(2,1)S(1)}, u32[]{:S(2)}, u32[]{:S(2)}) collective-permute-start(bf16[128,1664]{1,0:T(8,128)(2,1)S(1)} %slice.170), channel_id=1, source_target_pairs={{0,1},{1,0},{2,3},{3,2},{4,5},{5,4},{6,7},{7,6},{8,9},{9,8},{10,11... | collective-permute-start | bytes 1277960 | tf_op jit(solution)/shard_map/ppermute | solution.py:311
  206.0 18.2 %collective-permute-start.49 = (bf16[128,1664]{1,0:T(8,128)(2,1)S(1)}, bf16[128,1664]{1,0:T(8,128)(2,1)S(1)}, u32[]{:S(2)}, u32[]{:S(2)}) collective-permute-start(bf16[128,1664]{1,0:T(8,128)(2,1)S(1)} %get-tuple-element.247), channel_id=1, source_target_pairs={{0,1},{1,0},{2,3},{3,2},{4,5},{5,4},{6,7},{7,6},{8,9},{9,8},{10,11... | collective-permute-start | bytes 1277960 | tf_op jit(solution)/shard_map/ppermute | solution.py:311
  207.2 23.1 %collective-permute-start.43 = (bf16[128,1664]{1,0:T(8,128)(2,1)S(1)}, bf16[128,1664]{1,0:T(8,128)(2,1)S(1)}, u32[]{:S(2)}, u32[]{:S(2)}) collective-permute-start(bf16[128,1664]{1,0:T(8,128)(2,1)S(1)} %slice.171), channel_id=1, source_target_pairs={{0,4},{4,0},{1,5},{5,1},{2,6},{6,2},{3,7},{7,3},{8,12},{12,8},{9,1... | collective-permute-start | bytes 1277960 | tf_op jit(solution)/shard_map/ppermute | solution.py:311
  207.7 21.1 %collective-permute-start.51 = (bf16[128,1664]{1,0:T(8,128)(2,1)S(1)}, bf16[128,1664]{1,0:T(8,128)(2,1)S(1)}, u32[]{:S(2)}, u32[]{:S(2)}) collective-permute-start(bf16[128,1664]{1,0:T(8,128)(2,1)S(1)} %get-tuple-element.246), channel_id=1, source_target_pairs={{0,4},{4,0},{1,5},{5,1},{2,6},{6,2},{3,7},{7,3},{8,12},{12,8},{9,1... | collective-permute-start | bytes 1277960 | tf_op jit(solution)/shard_map/ppermute | solution.py:311
  261.6 34.1 %collective-permute-start.53 = (bf16[512,1536]{1,0:T(8,128)(2,1)S(1)}, bf16[512,1536]{1,0:T(8,128)(2,1)}, u32[]{:S(2)}, u32[]{:S(2)}) collective-permute-start(bf16[512,1536]{1,0:T(8,128)(2,1)S(1)} %constant_dynamic-update-slice_fusion.16.refs_0_), channel_id=1, source_target_pairs={{0,1},{1,0},{2,3},{3,2},{4,5},{5,4},{6,7},{7,6},{8,9},{9,8},{10,11... | collective-permute-start | bytes 4718600 | tf_op jit(solution)/shard_map/ppermute | solution.py:311
  262.9 33.8 %collective-permute-start.54 = (bf16[512,1536]{1,0:T(8,128)(2,1)S(1)}, bf16[512,1536]{1,0:T(8,128)(2,1)}, u32[]{:S(2)}, u32[]{:S(2)}) collective-permute-start(bf16[512,1536]{1,0:T(8,128)(2,1)S(1)} %constant_dynamic-update-slice_fusion.16.refs_0_), channel_id=1, source_target_pairs={{0,4},{4,0},{1,5},{5,1},{2,6},{6,2},{3,7},{7,3},{8,12},{12,8},{9,1... | collective-permute-start | bytes 4718600 | tf_op jit(solution)/shard_map/ppermute | solution.py:311
  307.2 31.1 %all-to-all-start = ((bf16[8,272,448]{2,1,0:T(8,128)(2,1)}), bf16[8,272,448]{2,1,0:T(8,128)(2,1)S(1)}, u32[]{:S(2)}, u32[]{:S(2)}) async-start(bf16[8,272,448]{2,1,0:T(8,128)(2,1)} %constant_dynamic-update-slice_fusion.20), calls=%async_computation.1 | async-start | bytes 4456448 | tf_op jit(solution)/shard_map/all_to_all | solution.py:61
  310.9 69.1 %reduce-scatter.9.cloned.1.call-start = ((), (), s32[]{:S(2)}) async-start(), calls=%async_computation.11 | async-start | bytes 2949120 | tf_op jit(solution)/shard_map/reduce_scatter | solution.py:65
  320.9 19.5 %collective-permute-start.61 = (bf16[256,1536]{1,0:T(8,128)(2,1)}, bf16[256,1536]{1,0:T(8,128)(2,1)}, u32[]{:S(2)}, u32[]{:S(2)}) collective-permute-start(bf16[256,1536]{1,0:T(8,128)(2,1)} %get-tuple-element.221), channel_id=1, source_target_pairs={{0,2},{2,0},{1,3},{3,1},{4,6},{6,4},{5,7},{7,5},{8,10},{10,8},{9,1... | collective-permute-start | bytes 2359304 | tf_op jit(solution)/shard_map/ppermute | solution.py:311
  338.4 19.4 %collective-permute-start.55 = (bf16[256,1536]{1,0:T(8,128)(2,1)}, bf16[256,1536]{1,0:T(8,128)(2,1)S(1)}, u32[]{:S(2)}, u32[]{:S(2)}) collective-permute-start(bf16[256,1536]{1,0:T(8,128)(2,1)} %slice.143), channel_id=1, source_target_pairs={{0,1},{1,0},{2,3},{3,2},{4,5},{5,4},{6,7},{7,6},{8,9},{9,8},{10,11... | collective-permute-start | bytes 2359304 | tf_op jit(solution)/shard_map/ppermute | solution.py:311
  339.4 18.9 %collective-permute-start.56 = (bf16[256,1536]{1,0:T(8,128)(2,1)S(1)}, bf16[256,1536]{1,0:T(8,128)(2,1)S(1)}, u32[]{:S(2)}, u32[]{:S(2)}) collective-permute-start(bf16[256,1536]{1,0:T(8,128)(2,1)S(1)} %slice.144), channel_id=1, source_target_pairs={{0,4},{4,0},{1,5},{5,1},{2,6},{6,2},{3,7},{7,3},{8,12},{12,8},{9,1... | collective-permute-start | bytes 2359304 | tf_op jit(solution)/shard_map/ppermute | solution.py:311
  339.9 30.5 %collective-permute-start.57 = (bf16[512,1536]{1,0:T(8,128)(2,1)}, bf16[512,1536]{1,0:T(8,128)(2,1)}, u32[]{:S(2)}, u32[]{:S(2)}) collective-permute-start(bf16[512,1536]{1,0:T(8,128)(2,1)} %copy-done.20), channel_id=1, source_target_pairs={{0,2},{2,0},{1,3},{3,1},{4,6},{6,4},{5,7},{7,5},{8,10},{10,8},{9,1... | collective-permute-start | bytes 4718600 | tf_op jit(solution)/shard_map/ppermute | solution.py:311
  339.9 20.4 %collective-permute-start.62 = (bf16[256,1536]{1,0:T(8,128)(2,1)}, bf16[256,1536]{1,0:T(8,128)(2,1)S(1)}, u32[]{:S(2)}, u32[]{:S(2)}) collective-permute-start(bf16[256,1536]{1,0:T(8,128)(2,1)} %get-tuple-element.223), channel_id=1, source_target_pairs={{0,2},{2,0},{1,3},{3,1},{4,6},{6,4},{5,7},{7,5},{8,10},{10,8},{9,1... | collective-permute-start | bytes 2359304 | tf_op jit(solution)/shard_map/ppermute | solution.py:311
  340.4 20.3 %collective-permute-start.63 = (bf16[256,1536]{1,0:T(8,128)(2,1)}, bf16[256,1536]{1,0:T(8,128)(2,1)S(1)}, u32[]{:S(2)}, u32[]{:S(2)}) collective-permute-start(bf16[256,1536]{1,0:T(8,128)(2,1)} %get-tuple-element.225), channel_id=1, source_target_pairs={{0,2},{2,0},{1,3},{3,1},{4,6},{6,4},{5,7},{7,5},{8,10},{10,8},{9,1... | collective-permute-start | bytes 2359304 | tf_op jit(solution)/shard_map/ppermute | solution.py:311
  365.9 14.1 %all-to-all-start.1 = ((bf16[4,96,768]{2,1,0:T(8,128)(2,1)}), bf16[4,96,768]{2,1,0:T(8,128)(2,1)}, u32[]{:S(2)}, u32[]{:S(2)}) async-start(bf16[4,96,768]{2,1,0:T(8,128)(2,1)} %bitcast.88), calls=%async_computation.3 | async-start | bytes 1179648 | tf_op jit(solution)/shard_map/all_to_all | solution.py:61
  370.1 55.6 %reduce-scatter.11.cloned.1.call-start = ((), (), s32[]{:S(2)}) async-start(), calls=%async_computation.12 | async-start | bytes 2048000 | tf_op jit(solution)/shard_map/reduce_scatter | solution.py:65
  380.0 13.5 %all-to-all-start.2 = ((bf16[4,96,768]{2,1,0:T(8,128)(2,1)}), bf16[4,96,768]{2,1,0:T(8,128)(2,1)S(1)}, u32[]{:S(2)}, u32[]{:S(2)}) async-start(bf16[4,96,768]{2,1,0:T(8,128)(2,1)} %bitcast.89), calls=%async_computation.5 | async-start | bytes 1179648 | tf_op jit(solution)/shard_map/all_to_all | solution.py:61
  384.4 13.8 %collective-permute-start.66 = (bf16[128,1536]{1,0:T(8,128)(2,1)}, bf16[128,1536]{1,0:T(8,128)(2,1)S(1)}, u32[]{:S(2)}, u32[]{:S(2)}) collective-permute-start(bf16[128,1536]{1,0:T(8,128)(2,1)} %get-tuple-element.249), channel_id=1, source_target_pairs={{0,1},{1,0},{2,3},{3,2},{4,5},{5,4},{6,7},{7,6},{8,9},{9,8},{10,11... | collective-permute-start | bytes 1179656 | tf_op jit(solution)/shard_map/ppermute | solution.py:311
  385.4 16.0 %collective-permute-start.67 = (bf16[128,1536]{1,0:T(8,128)(2,1)}, bf16[128,1536]{1,0:T(8,128)(2,1)S(1)}, u32[]{:S(2)}, u32[]{:S(2)}) collective-permute-start(bf16[128,1536]{1,0:T(8,128)(2,1)} %get-tuple-element.248), channel_id=1, source_target_pairs={{0,4},{4,0},{1,5},{5,1},{2,6},{6,2},{3,7},{7,3},{8,12},{12,8},{9,1... | collective-permute-start | bytes 1179656 | tf_op jit(solution)/shard_map/ppermute | solution.py:311
  394.6 13.6 %all-to-all-start.3 = ((bf16[4,96,768]{2,1,0:T(8,128)(2,1)}), bf16[4,96,768]{2,1,0:T(8,128)(2,1)S(1)}, u32[]{:S(2)}, u32[]{:S(2)}) async-start(bf16[4,96,768]{2,1,0:T(8,128)(2,1)} %bitcast.36), calls=%async_computation.6 | async-start | bytes 1179648 | tf_op jit(solution)/shard_map/all_to_all | solution.py:61
  402.3 14.3 %collective-permute-start.68 = (bf16[128,1536]{1,0:T(8,128)(2,1)}, bf16[128,1536]{1,0:T(8,128)(2,1)S(1)}, u32[]{:S(2)}, u32[]{:S(2)}) collective-permute-start(bf16[128,1536]{1,0:T(8,128)(2,1)} %reduce-precision_convert_fusion.10), channel_id=1, source_target_pairs={{0,4},{4,0},{1,5},{5,1},{2,6},{6,2},{3,7},{7,3},{8,12},{12,8},{9,1... | collective-permute-start | bytes 1179656 | tf_op jit(solution)/shard_map/ppermute | solution.py:311
  404.5 20.1 %collective-permute-start.70 = (bf16[128,1536]{1,0:T(8,128)(2,1)S(1)}, bf16[128,1536]{1,0:T(8,128)(2,1)S(1)}, u32[]{:S(2)}, u32[]{:S(2)}) collective-permute-start(bf16[128,1536]{1,0:T(8,128)(2,1)S(1)} %slice.150), channel_id=1, source_target_pairs={{0,4},{4,0},{1,5},{5,1},{2,6},{6,2},{3,7},{7,3},{8,12},{12,8},{9,1... | collective-permute-start | bytes 1179656 | tf_op jit(solution)/shard_map/ppermute | solution.py:311
  407.0 25.4 %collective-permute-start.65 = (bf16[128,1536]{1,0:T(8,128)(2,1)}, bf16[128,1536]{1,0:T(8,128)(2,1)}, u32[]{:S(2)}, u32[]{:S(2)}) collective-permute-start(bf16[128,1536]{1,0:T(8,128)(2,1)} %slice.145), channel_id=1, source_target_pairs={{0,1},{1,0},{2,3},{3,2},{4,5},{5,4},{6,7},{7,6},{8,9},{9,8},{10,11... | collective-permute-start | bytes 1179656 | tf_op jit(solution)/shard_map/ppermute | solution.py:311
  428.8 17.1 %all-to-all-start.4 = ((bf16[8,112,448]{2,1,0:T(8,128)(2,1)}), bf16[8,112,448]{2,1,0:T(8,128)(2,1)S(1)}, u32[]{:S(2)}, u32[]{:S(2)}) async-start(bf16[8,112,448]{2,1,0:T(8,128)(2,1)} %maximum_maximum_fusion), calls=%async_computation.8 | async-start | bytes 1835008 | tf_op jit(solution)/shard_map/all_to_all | solution.py:61
  (113 other events, 1269.1 us)
Sparse Core Ops, SparseCore 0:
  201.4 48.0 reduce-scatter.4
  260.5 47.9 reduce-scatter.6
  314.0 49.7 reduce-scatter.8
  380.1 37.4 reduce-scatter.10

commit v6 on v4

--- a/solution.py
+++ b/solution.py
@@ -1006,7 +1006,7 @@
         narrow_part.astype(bf16), ((0, 0), (0, 16 - depth * each_rows), (0, 0))
     )
     back_cols = lax.dynamic_update_slice(back_cols, narrow_part, (0, length, 0))
-    back_cols = exchange(after(back_cols, down_sum, *both_sides), PLANE)
+    back_cols = exchange(after(back_cols, down_sum), PLANE)
     shares = run_kernel(
         functools.partial(mixture_kernel, capacity, groups),
         10,
@@ -1022,7 +1022,6 @@
         total = exchange(total, ("y", "c"))
         return total.reshape(local_count, shard_rows, hidden_width).astype(f32)
 
-    down_grad, gate_grad = placed(down_sum), placed(gate_sum)
     kept_rows = -(-narrow_rows // 16) * 16
     wide_rows = local_count * shard_rows
     dense_shape = (depth, wide_rows + kept_rows, dense_cols)
@@ -1038,7 +1037,10 @@
         cost_estimate=cost(8),
         compiler_params=pltpu.CompilerParams(vmem_limit_bytes=32 * 2**20),
     )(at, back_cols, *both_pieces)
-    dense_part, up_sum = lax.optimization_barrier((dense_part, up_sum))
+    dense_part, down_sum, gate_sum, up_sum = lax.optimization_barrier(
+        (dense_part, down_sum, gate_sum, up_sum)
+    )
+    down_grad, gate_grad = placed(down_sum), placed(gate_sum)
     dense_sum = scatter_sum(dense_part.reshape(-1, dense_cols), "z")
     mixed = [over_core(near, far) for near, far in zip(shares[:4], shares[4:])]
     early = early_sums(mixed[1], mixed[2])

time: 451 us -> 454 us (level)
  waiting for transfers between devices: 157 us -> 167 us
  local copies, waits for them, and re-layouts: 72.2 us -> 63.7 us
    ppermute x65, waiting for transfers between devices: 102 us -> 114 us  [swap(): return lax.ppermute(block, axis, [(0, 1), (1, 0)])]
    unnamed x178 -> x172, local copies, waits for them, and re-layouts: 40.9 us -> 31.1 us
  transfers between devices with their start and end apart: 80 -> 80, of which waited for: 31 -> 34; matrix products, arithmetic and copies ran while one was open for 13% -> 13% of each run, Pallas kernels for 23% -> 23%
where the time goes in v6:
time: 454 us; the launch traced here: 445 us
  waiting for transfers between devices  167 us (37%)
  Pallas kernels  105 us (23%)
  starting transfers between devices  67.9 us (15%)
  local copies, waits for them, and re-layouts  63.7 us (14%)
  other arithmetic  25.9 us (6%)
  between operations  15.8 us (3%)
    ppermute x65, waiting for transfers between devices, swap(): return lax.ppermute(block, axis, [(0, 1), (1, 0)])  114 us
    pallas_call x11, Pallas kernels, run_kernel(): pl.pallas_call(kernel, out_shape=[jax.ShapeDtypeStruct(shape, dtype) for...  97.9 us
    ppermute x65, starting transfers between devices, swap(): return lax.ppermute(block, axis, [(0, 1), (1, 0)])  39 us
    all_to_all x5, waiting for transfers between devices, exchange(): return lax.all_to_all(block, axes, split_axis=0, concat_axis=0, tiled=True)  33.8 us
    unnamed x172, local copies, waits for them, and re-layouts  31.1 us
    all_to_all x5, starting transfers between devices, exchange(): return lax.all_to_all(block, axes, split_axis=0, concat_axis=0, tiled=True)  18.3 us
    ppermute x6, waiting for transfers between devices, shifts(): lax.ppermute(block, 'z', [(i, (i + k) % depth) for i in range(depth)])  16.3 us
    ppermute x6, starting transfers between devices, shifts(): lax.ppermute(block, 'z', [(i, (i + k) % depth) for i in range(depth)])  10.1 us
  transfers between devices with their start and end apart: 80, of which 34 were waited for; matrix products, arithmetic and copies ran while one was open for 13% of the time, Pallas kernels for 23%

profile of v6, /device:TPU:0, one launch (start us, length us, event | category | flops | bytes accessed | tf_op | source)
XLA Modules:
  0.0 445.3 jit_solution(9539348847284443934)
XLA Ops:
  8.1 5.1 %collective-permute-start = (bf16[96,128]{1,0:T(8,128)(2,1)S(1)}, bf16[96,128]{1,0:T(8,128)(2,1)S(1)}, u32[]{:S(2)}, u32[]{:S(2)}) collective-permute-start(bf16[96,128]{1,0:T(8,128)(2,1)S(1)} %pad.9), channel_id=1, source_target_pairs={{0,24},{8,0},{16,8},{24,16},{1,25},{9,1},{17,9},{25,17},{2,26},{10... | collective-permute-start | bytes 73736 | tf_op jit(solution)/shard_map/ppermute | solution.py:317
  19.8 2.8 collective-permute-start.14
  28.3 2.7 collective-permute-done.3
  36.5 16.3 %collective-permute-done.13 = bf16[96,1792]{1,0:T(8,128)(2,1)} collective-permute-done((bf16[96,1792]{1,0:T(8,128)(2,1)}, bf16[96,1792]{1,0:T(8,128)(2,1)}, u32[]{:S(2)}, u32[]{:S(2)}) %collective-permute-start.13) | collective-permute-done | bytes 344096 | tf_op jit(solution)/shard_map/ppermute | solution.py:317
  65.1 4.1 dynamic-slice_bitcast_fusion.1.refs_5_.refs_9_
  69.2 3.2 dynamic-slice_bitcast_fusion.2.refs_4_.refs_8_
  72.5 6.6 %collective-permute-done.16.refs_2_ = bf16[4,96,1024]{2,1,0:T(8,128)(2,1)} collective-permute-done((bf16[4,96,1024]{2,1,0:T(8,128)(2,1)S(1)}, bf16[4,96,1024]{2,1,0:T(8,128)(2,1)}, u32[]{:S(2)}, u32[]{:S(2)}) %collective-permute-start.16) | collective-permute-done | bytes 786464 | tf_op jit(solution)/shard_map/ppermute | solution.py:311
  83.8 5.3 %collective-permute-done.17 = bf16[2,96,1024]{2,1,0:T(8,128)(2,1)S(1)} collective-permute-done((bf16[2,96,1024]{2,1,0:T(8,128)(2,1)S(1)}, bf16[2,96,1024]{2,1,0:T(8,128)(2,1)S(1)}, u32[]{:S(2)}, u32[]{:S(2)}) %collective-permute-start.17) | collective-permute-done | bytes 393248 | tf_op jit(solution)/shard_map/ppermute | solution.py:311
  99.0 9.1 %shard_map.229 = (bf16[256,1536]{1,0:T(8,128)(2,1)S(1)}, bf16[256,1536]{1,0:T(8,128)(2,1)S(1)}, bf16[256,256]{1,0:T(8,128)(2,1)S(1)}, bf16[256,256]{1,0:T(8,128)...) custom-call(s32[7]{0:T(128)S(1)} %copy-done.36, ...), custom_call_target="tpu_custom_call" | custom-call | flops 11000000512 | bytes 11000000 | tf_op jit(solution)/shard_map/pallas_call | solution.py:400
  108.1 2.7 copy-done.45
  116.4 5.7 %collective-permute-done.25 = bf16[2,96,768]{2,1,0:T(8,128)(2,1)S(1)} collective-permute-done((bf16[2,96,768]{2,1,0:T(8,128)(2,1)S(1)}, bf16[2,96,768]{2,1,0:T(8,128)(2,1)S(1)}, u32[]{:S(2)}, u32[]{:S(2)}) %collective-permute-start.25) | collective-permute-done | bytes 294944 | tf_op jit(solution)/shard_map/ppermute | solution.py:311
  122.8 6.7 %collective-permute-done.10 = bf16[128,1536]{1,0:T(8,128)(2,1)S(1)} collective-permute-done((bf16[128,1536]{1,0:T(8,128)(2,1)S(1)}, bf16[128,1536]{1,0:T(8,128)(2,1)S(1)}, u32[]{:S(2)}, u32[]{:S(2)}) %collective-permute-start.10) | collective-permute-done | bytes 393248 | tf_op jit(solution)/shard_map/ppermute | solution.py:311
  131.6 4.1 shard_map.230
  139.7 10.2 %shard_map.231 = (bf16[384,1536]{1,0:T(8,128)(2,1)S(1)}, bf16[384,1536]{1,0:T(8,128)(2,1)S(1)}, bf16[384,768]{1,0:T(8,128)(2,1)S(1)}, bf16[384,768]{1,0:T(8,128)...) custom-call(s32[7]{0:T(128)S(1)} %copy-done.37, ...), custom_call_target="tpu_custom_call" | custom-call | flops 8000000000 | bytes 8000000 | tf_op jit(solution)/shard_map/pallas_call | solution.py:400
  151.6 5.5 %collective-permute-done.31.refs_0_ = bf16[256,1536]{1,0:T(8,128)(2,1)S(1)} collective-permute-done((bf16[256,1536]{1,0:T(8,128)(2,1)}, bf16[256,1536]{1,0:T(8,128)(2,1)S(1)}, u32[]{:S(2)}, u32[]{:S(2)}) %collective-permute-start.31) | collective-permute-done | bytes 786464 | tf_op jit(solution)/shard_map/ppermute | solution.py:311
  160.3 2.2 collective-permute-done.36.refs_3_
  162.6 17.4 %shard_map.232 = (bf16[768,1536]{1,0:T(8,128)(2,1)S(1)}, bf16[768,1536]{1,0:T(8,128)(2,1)S(1)}, bf16[768,768]{1,0:T(8,128)(2,1)S(1)}, bf16[768,768]{1,0:T(8,128)...) custom-call(s32[7]{0:T(128)S(1)} %copy-done.37, ...), custom_call_target="tpu_custom_call" | custom-call | flops 16000000000 | bytes 16000000 | tf_op jit(solution)/shard_map/pallas_call | solution.py:400
  185.8 12.9 %shard_map.233 = (bf16[384,1536]{1,0:T(8,128)(2,1)S(1)}, bf16[384,1536]{1,0:T(8,128)(2,1)}, bf16[384,768]{1,0:T(8,128)(2,1)S(1)}, bf16[384,768]{1,0:T(8,128)(2,1...) custom-call(s32[7]{0:T(128)S(1)} %copy-done.37, ...), custom_call_target="tpu_custom_call" | custom-call | flops 8000000000 | bytes 8000000 | tf_op jit(solution)/shard_map/pallas_call | solution.py:400
  213.2 9.1 %collective-permute-done.48 = bf16[128,1664]{1,0:T(8,128)(2,1)S(1)} collective-permute-done((bf16[128,1664]{1,0:T(8,128)(2,1)S(1)}, bf16[128,1664]{1,0:T(8,128)(2,1)S(1)}, u32[]{:S(2)}, u32[]{:S(2)}) %collective-permute-start.48) | collective-permute-done | bytes 426016 | tf_op jit(solution)/shard_map/ppermute | solution.py:311
  223.7 5.3 %collective-permute-done.45 = bf16[128,1664]{1,0:T(8,128)(2,1)S(1)} collective-permute-done((bf16[128,1664]{1,0:T(8,128)(2,1)S(1)}, bf16[128,1664]{1,0:T(8,128)(2,1)S(1)}, u32[]{:S(2)}, u32[]{:S(2)}) %collective-permute-start.45) | collective-permute-done | bytes 426016 | tf_op jit(solution)/shard_map/ppermute | solution.py:311
  230.6 7.0 %collective-permute-done.49.last_x = bf16[128,1664]{1,0:T(8,128)(2,1)S(1)} collective-permute-done((bf16[128,1664]{1,0:T(8,128)(2,1)S(1)}, bf16[128,1664]{1,0:T(8,128)(2,1)S(1)}, u32[]{:S(2)}, u32[]{:S(2)}) %collective-permute-start.49) | collective-permute-done | bytes 426016 | tf_op jit(solution)/shard_map/ppermute | solution.py:311
  237.6 2.4 collective-permute-done.46.last_y
  240.8 8.3 %shard_map.235 = (f32[256,1536]{1,0:T(8,128)}, bf16[256,1536]{1,0:T(8,128)(2,1)}, bf16[256,1536]{1,0:T(8,128)(2,1)}, f32[1536,128]{1,0:T(8,128)}, f32[1,1536]{1,0:T(1,128)}) custom-call(s32[7]{0:T(128)} %stack.76.at, bf16[256,1664]{1,0:T(8,128)(2,1)} %copy-done.47, bf16[256,1664]{1,0:T(8,128)(2,1)} %collective-permute-done.58.far, ...), custom_call_target="tpu_custom_call" | custom-call | flops 6000000000 | bytes 6000000 | tf_op jit(solution)/shard_map/pallas_call | solution.py:400
  249.0 12.7 %shard_map.236 = (bf16[1536,768]{1,0:T(8,128)(2,1)}, bf16[1536,768]{1,0:T(8,128)(2,1)}) custom-call(s32[7]{0:T(128)} %stack.76.at, bf16[384,1536]{1,0:T(8,128)(2,1)} %copy-done.52, bf16[768,1536]{1,0:T(8,128)(2,1)} %copy-done.51, bf16[384,1536]{1,0:T(8,128)(2,1)} %copy-done.50, bf16[384,768]{1,0:T(8,128)(2,1)} %copy-done.60, bf16[768,768]{1,0:T(8,128)(2,1)} %copy-done.58, ...), custom_call_target="tpu_custom_call" | custom-call | flops 8000000000 | bytes 8000000 | tf_op jit(solution)/shard_map/pallas_call | solution.py:400
  266.3 8.5 %shard_map.237.back = bf16[8,272,448]{2,1,0:T(8,128)(2,1)} custom-call(s32[7]{0:T(128)} %stack.76.at, bf16[256,1536]{1,0:T(8,128)(2,1)} %get-tuple-element.199.attended, bf16[12,256,256]{2,1,0:T(8,128)(2,1)} %copy-done.48, bf16[256,1536]{1,0:T(8,128)(2,1)} %copy-done.53, bf16[256,256]{1,0:T(8,128)(2,1)} %copy-done.63, bf16[256,256]{1,0:T(8,128)(2,1)} %copy-done.64, ...), custom_call_target="tpu_custom_call" | custom-call | flops 6000000000 | bytes 6000000 | tf_op jit(solution)/shard_map/pallas_call | solution.py:400
  277.8 3.7 shard_map.238
  284.2 3.6 all-to-all-start
  288.7 13.8 %collective-permute-done.50.refs_1_ = bf16[512,1536]{1,0:T(8,128)(2,1)} collective-permute-done((bf16[512,1536]{1,0:T(8,128)(2,1)}, bf16[512,1536]{1,0:T(8,128)(2,1)}, u32[]{:S(2)}, u32[]{:S(2)}) %collective-permute-start.50) | collective-permute-done | bytes 1572896 | tf_op jit(solution)/shard_map/ppermute | solution.py:311
  303.7 9.4 %shard_map.234 = (bf16[256,1536]{1,0:T(8,128)(2,1)}, bf16[256,1536]{1,0:T(8,128)(2,1)}, bf16[256,1536]{1,0:T(8,128)(2,1)}, bf16[256,1536]{1,0:T(8,128)(2,1)}, bf...) custom-call(s32[7]{0:T(128)} %stack.76.at, ...), custom_call_target="tpu_custom_call" | custom-call | flops 10000000000 | bytes 10000000 | tf_op jit(solution)/shard_map/pallas_call | solution.py:400
  313.0 2.1 slice.147
  316.3 8.0 %all-to-all-done.back = bf16[8,272,448]{2,1,0:T(8,128)(2,1)S(1)} async-done(((bf16[8,272,448]{2,1,0:T(8,128)(2,1)}), bf16[8,272,448]{2,1,0:T(8,128)(2,1)S(1)}, u32[]{:S(2)}, u32[]{:S(2)}) %all-to-all-start) | async-done | bytes 1949728 | tf_op jit(solution)/shard_map/all_to_all | solution.py:61
  326.3 17.1 %collective-permute-done.61 = bf16[256,1536]{1,0:T(8,128)(2,1)S(1)} collective-permute-done((bf16[256,1536]{1,0:T(8,128)(2,1)}, bf16[256,1536]{1,0:T(8,128)(2,1)S(1)}, u32[]{:S(2)}, u32[]{:S(2)}) %collective-permute-start.61) | collective-permute-done | bytes 786464 | tf_op jit(solution)/shard_map/ppermute | solution.py:311
  347.8 3.5 collective-permute-done.66.refs_7_
  351.3 7.3 %shard_map.239 = bf16[4,400,448]{2,1,0:T(8,128)(2,1)S(1)} custom-call(s32[7]{0:T(128)S(1)} %copy-done.39, bf16[8,272,448]{2,1,0:T(8,128)(2,1)S(1)} %all-to-all-done.back, bf16[512,1536]{1,0:T(8,128)(2,1)} %constant_dynamic-update-slice_fusion.16.refs_0_, bf16[512,1536]{1,0:T(8,128)(2,1)} %collective-permute-done.50.refs_1_, ...), custom_call_target="tpu_custom_call" | custom-call | flops 8000000000 | bytes 8000000 | tf_op jit(solution)/shard_map/pallas_call | solution.py:1028
  361.6 3.5 all-to-all-start.1
  365.3 9.3 %all-to-all-done.1 = bf16[4,96,768]{2,1,0:T(8,128)(2,1)S(1)} async-done(((bf16[4,96,768]{2,1,0:T(8,128)(2,1)}), bf16[4,96,768]{2,1,0:T(8,128)(2,1)S(1)}, u32[]{:S(2)}, u32[]{:S(2)}) %all-to-all-start.1) | async-done | bytes 589856 | tf_op jit(solution)/shard_map/all_to_all | solution.py:61
  374.6 3.5 all-to-all-start.2
  380.7 6.8 %all-to-all-done.2 = bf16[4,96,768]{2,1,0:T(8,128)(2,1)S(1)} async-done(((bf16[4,96,768]{2,1,0:T(8,128)(2,1)}), bf16[4,96,768]{2,1,0:T(8,128)(2,1)S(1)}, u32[]{:S(2)}, u32[]{:S(2)}) %all-to-all-start.2) | async-done | bytes 589856 | tf_op jit(solution)/shard_map/all_to_all | solution.py:61
  387.6 3.7 all-to-all-start.3
  392.4 1.8 reduce-precision_convert_fusion.9
  395.7 1.8 reduce-precision_convert_fusion.10
  397.5 2.0 collective-permute-start.67
  402.2 4.2 collective-permute-done.68
  406.4 3.5 collective-permute-done.67
  409.8 4.5 %collective-permute-done.53 = bf16[128,1536]{1,0:T(8,128)(2,1)S(1)} collective-permute-done((bf16[128,1536]{1,0:T(8,128)(2,1)S(1)}, bf16[128,1536]{1,0:T(8,128)(2,1)S(1)}, u32[]{:S(2)}, u32[]{:S(2)}) %collective-permute-start.53) | collective-permute-done | bytes 393248 | tf_op jit(solution)/shard_map/ppermute | solution.py:311
  417.9 4.0 all-to-all-start.4
  423.2 2.5 fusion.1
  425.7 9.6 %all-to-all-done.4.sums = bf16[8,112,448]{2,1,0:T(8,128)(2,1)S(1)} async-done(((bf16[8,112,448]{2,1,0:T(8,128)(2,1)}), bf16[8,112,448]{2,1,0:T(8,128)(2,1)S(1)}, u32[]{:S(2)}, u32[]{:S(2)}) %all-to-all-start.4) | async-done | bytes 802848 | tf_op jit(solution)/shard_map/all_to_all | solution.py:61
  (399 shorter events, 124.4 us)
Async XLA Ops:
  7.2 277.1 %reduce-scatter.5.cloned.1.call-start = ((), (), s32[]{:S(2)}) async-start(), calls=%async_computation.9 | async-start | bytes 2949120 | tf_op jit(solution)/shard_map/reduce_scatter | solution.py:65
  8.1 16.3 %collective-permute-start = (bf16[96,128]{1,0:T(8,128)(2,1)S(1)}, bf16[96,128]{1,0:T(8,128)(2,1)S(1)}, u32[]{:S(2)}, u32[]{:S(2)}) collective-permute-start(bf16[96,128]{1,0:T(8,128)(2,1)S(1)} %pad.9), channel_id=1, source_target_pairs={{0,24},{8,0},{16,8},{24,16},{1,25},{9,1},{17,9},{25,17},{2,26},{10... | collective-permute-start | bytes 73736 | tf_op jit(solution)/shard_map/ppermute | solution.py:317
  19.8 15.8 %collective-permute-start.14 = (bf16[96,1792]{1,0:T(8,128)(2,1)}, bf16[96,1792]{1,0:T(8,128)(2,1)}, u32[]{:S(2)}, u32[]{:S(2)}) collective-permute-start(bf16[96,1792]{1,0:T(8,128)(2,1)} %pad_maximum_fusion.3), channel_id=1, source_target_pairs={{0,24},{8,0},{16,8},{24,16},{1,25},{9,1},{17,9},{25,17},{2,26},{10... | collective-permute-start | bytes 1032200 | tf_op jit(solution)/shard_map/ppermute | solution.py:317
  23.3 29.5 %collective-permute-start.13 = (bf16[96,1792]{1,0:T(8,128)(2,1)}, bf16[96,1792]{1,0:T(8,128)(2,1)}, u32[]{:S(2)}, u32[]{:S(2)}) collective-permute-start(bf16[96,1792]{1,0:T(8,128)(2,1)} %pad_maximum_fusion.3), channel_id=1, source_target_pairs={{0,16},{8,24},{16,0},{24,8},{1,17},{9,25},{17,1},{25,9},{2,18},{10... | collective-permute-start | bytes 1032200 | tf_op jit(solution)/shard_map/ppermute | solution.py:317
  24.4 29.3 %collective-permute-start.12 = (bf16[96,1792]{1,0:T(8,128)(2,1)}, bf16[96,1792]{1,0:T(8,128)(2,1)}, u32[]{:S(2)}, u32[]{:S(2)}) collective-permute-start(bf16[96,1792]{1,0:T(8,128)(2,1)} %pad_maximum_fusion.3), channel_id=1, source_target_pairs={{0,8},{8,16},{16,24},{24,0},{1,9},{9,17},{17,25},{25,1},{2,10},{10... | collective-permute-start | bytes 1032200 | tf_op jit(solution)/shard_map/ppermute | solution.py:317
  32.6 27.7 %collective-permute-start.8 = (bf16[256,1536]{1,0:T(8,128)(2,1)S(1)}, bf16[256,1536]{1,0:T(8,128)(2,1)S(1)}, u32[]{:S(2)}, u32[]{:S(2)}) collective-permute-start(bf16[256,1536]{1,0:T(8,128)(2,1)S(1)} %copy-done.40), channel_id=1, source_target_pairs={{0,4},{4,0},{1,5},{5,1},{2,6},{6,2},{3,7},{7,3},{8,12},{12,8},{9,1... | collective-permute-start | bytes 2359304 | tf_op jit(solution)/shard_map/ppermute | solution.py:311
  33.2 27.2 %collective-permute-start.9 = (bf16[256,1536]{1,0:T(8,128)(2,1)S(1)}, bf16[256,1536]{1,0:T(8,128)(2,1)S(1)}, u32[]{:S(2)}, u32[]{:S(2)}) collective-permute-start(bf16[256,1536]{1,0:T(8,128)(2,1)S(1)} %copy-done.40), channel_id=1, source_target_pairs={{0,1},{1,0},{2,3},{3,2},{4,5},{5,4},{6,7},{7,6},{8,9},{9,8},{10,11... | collective-permute-start | bytes 2359304 | tf_op jit(solution)/shard_map/ppermute | solution.py:311
  60.4 19.7 %collective-permute-start.15 = (bf16[4,96,1024]{2,1,0:T(8,128)(2,1)S(1)}, bf16[4,96,1024]{2,1,0:T(8,128)(2,1)}, u32[]{:S(2)}, u32[]{:S(2)}) collective-permute-start(bf16[4,96,1024]{2,1,0:T(8,128)(2,1)S(1)} %pad_maximum_fusion.refs_0_), channel_id=1, source_target_pairs={{0,1},{1,0},{2,3},{3,2},{4,5},{5,4},{6,7},{7,6},{8,9},{9,8},{10,11... | collective-permute-start | bytes 2359304 | tf_op jit(solution)/shard_map/ppermute | solution.py:311
  61.7 17.3 %collective-permute-start.16 = (bf16[4,96,1024]{2,1,0:T(8,128)(2,1)S(1)}, bf16[4,96,1024]{2,1,0:T(8,128)(2,1)}, u32[]{:S(2)}, u32[]{:S(2)}) collective-permute-start(bf16[4,96,1024]{2,1,0:T(8,128)(2,1)S(1)} %pad_maximum_fusion.refs_0_), channel_id=1, source_target_pairs={{0,4},{4,0},{1,5},{5,1},{2,6},{6,2},{3,7},{7,3},{8,12},{12,8},{9,1... | collective-permute-start | bytes 2359304 | tf_op jit(solution)/shard_map/ppermute | solution.py:311
  93.1 18.9 %collective-permute-start.23 = (bf16[4,96,768]{2,1,0:T(8,128)(2,1)}, bf16[4,96,768]{2,1,0:T(8,128)(2,1)S(1)}, u32[]{:S(2)}, u32[]{:S(2)}) collective-permute-start(bf16[4,96,768]{2,1,0:T(8,128)(2,1)} %pad_maximum_fusion.1.refs_0_), channel_id=1, source_target_pairs={{0,1},{1,0},{2,3},{3,2},{4,5},{5,4},{6,7},{7,6},{8,9},{9,8},{10,11... | collective-permute-start | bytes 1769480 | tf_op jit(solution)/shard_map/ppermute | solution.py:311
  94.6 17.4 %collective-permute-start.24 = (bf16[4,96,768]{2,1,0:T(8,128)(2,1)}, bf16[4,96,768]{2,1,0:T(8,128)(2,1)S(1)}, u32[]{:S(2)}, u32[]{:S(2)}) collective-permute-start(bf16[4,96,768]{2,1,0:T(8,128)(2,1)} %pad_maximum_fusion.1.refs_0_), channel_id=1, source_target_pairs={{0,4},{4,0},{1,5},{5,1},{2,6},{6,2},{3,7},{7,3},{8,12},{12,8},{9,1... | collective-permute-start | bytes 1769480 | tf_op jit(solution)/shard_map/ppermute | solution.py:311
  113.7 15.7 %collective-permute-start.10 = (bf16[128,1536]{1,0:T(8,128)(2,1)S(1)}, bf16[128,1536]{1,0:T(8,128)(2,1)S(1)}, u32[]{:S(2)}, u32[]{:S(2)}) collective-permute-start(bf16[128,1536]{1,0:T(8,128)(2,1)S(1)} %slice.159), channel_id=1, source_target_pairs={{0,1},{1,0},{2,3},{3,2},{4,5},{5,4},{6,7},{7,6},{8,9},{9,8},{10,11... | collective-permute-start | bytes 1179656 | tf_op jit(solution)/shard_map/ppermute | solution.py:311
  114.9 14.9 %collective-permute-start.11 = (bf16[128,1536]{1,0:T(8,128)(2,1)S(1)}, bf16[128,1536]{1,0:T(8,128)(2,1)S(1)}, u32[]{:S(2)}, u32[]{:S(2)}) collective-permute-start(bf16[128,1536]{1,0:T(8,128)(2,1)S(1)} %slice.160), channel_id=1, source_target_pairs={{0,4},{4,0},{1,5},{5,1},{2,6},{6,2},{3,7},{7,3},{8,12},{12,8},{9,1... | collective-permute-start | bytes 1179656 | tf_op jit(solution)/shard_map/ppermute | solution.py:311
  116.4 15.2 %collective-permute-start.27 = (bf16[4,96,768]{2,1,0:T(8,128)(2,1)S(1)}, bf16[4,96,768]{2,1,0:T(8,128)(2,1)S(1)}, u32[]{:S(2)}, u32[]{:S(2)}) collective-permute-start(bf16[4,96,768]{2,1,0:T(8,128)(2,1)S(1)} %copy-done.19), channel_id=1, source_target_pairs={{0,2},{2,0},{1,3},{3,1},{4,6},{6,4},{5,7},{7,5},{8,10},{10,8},{9,1... | collective-permute-start | bytes 1769480 | tf_op jit(solution)/shard_map/ppermute | solution.py:311
  137.2 19.9 %collective-permute-start.31 = (bf16[256,1536]{1,0:T(8,128)(2,1)}, bf16[256,1536]{1,0:T(8,128)(2,1)S(1)}, u32[]{:S(2)}, u32[]{:S(2)}) collective-permute-start(bf16[256,1536]{1,0:T(8,128)(2,1)} %get-tuple-element.147.refs_0_.second), channel_id=1, source_target_pairs={{0,1},{1,0},{2,3},{3,2},{4,5},{5,4},{6,7},{7,6},{8,9},{9,8},{10,11... | collective-permute-start | bytes 2359304 | tf_op jit(solution)/shard_map/ppermute | solution.py:311
  138.7 19.4 %collective-permute-start.32 = (bf16[256,1536]{1,0:T(8,128)(2,1)}, bf16[256,1536]{1,0:T(8,128)(2,1)S(1)}, u32[]{:S(2)}, u32[]{:S(2)}) collective-permute-start(bf16[256,1536]{1,0:T(8,128)(2,1)} %get-tuple-element.147.refs_0_.second), channel_id=1, source_target_pairs={{0,4},{4,0},{1,5},{5,1},{2,6},{6,2},{3,7},{7,3},{8,12},{12,8},{9,1... | collective-permute-start | bytes 2359304 | tf_op jit(solution)/shard_map/ppermute | solution.py:311
  139.2 19.5 %collective-permute-start.37 = (bf16[256,1536]{1,0:T(8,128)(2,1)S(1)}, bf16[256,1536]{1,0:T(8,128)(2,1)S(1)}, u32[]{:S(2)}, u32[]{:S(2)}) collective-permute-start(bf16[256,1536]{1,0:T(8,128)(2,1)S(1)} %copy-done.25), channel_id=1, source_target_pairs={{0,2},{2,0},{1,3},{3,1},{4,6},{6,4},{5,7},{7,5},{8,10},{10,8},{9,1... | collective-permute-start | bytes 2359304 | tf_op jit(solution)/shard_map/ppermute | solution.py:311
  139.2 20.3 %collective-permute-start.38 = (bf16[256,1536]{1,0:T(8,128)(2,1)S(1)}, bf16[256,1536]{1,0:T(8,128)(2,1)S(1)}, u32[]{:S(2)}, u32[]{:S(2)}) collective-permute-start(bf16[256,1536]{1,0:T(8,128)(2,1)S(1)} %copy-done.22), channel_id=1, source_target_pairs={{0,2},{2,0},{1,3},{3,1},{4,6},{6,4},{5,7},{7,5},{8,10},{10,8},{9,1... | collective-permute-start | bytes 2359304 | tf_op jit(solution)/shard_map/ppermute | solution.py:311
  158.6 25.4 %collective-permute-start.43 = (bf16[256,1536]{1,0:T(8,128)(2,1)}, bf16[256,1536]{1,0:T(8,128)(2,1)S(1)}, u32[]{:S(2)}, u32[]{:S(2)}) collective-permute-start(bf16[256,1536]{1,0:T(8,128)(2,1)} %constant_dynamic-update-slice_fusion.8.refs_2_), channel_id=1, source_target_pairs={{0,2},{2,0},{1,3},{3,1},{4,6},{6,4},{5,7},{7,5},{8,10},{10,8},{9,1... | collective-permute-start | bytes 2359304 | tf_op jit(solution)/shard_map/ppermute | solution.py:311
  158.6 24.7 %collective-permute-start.40 = (bf16[128,1536]{1,0:T(8,128)(2,1)S(1)}, bf16[128,1536]{1,0:T(8,128)(2,1)S(1)}, u32[]{:S(2)}, u32[]{:S(2)}) collective-permute-start(bf16[128,1536]{1,0:T(8,128)(2,1)S(1)} %slice.135), channel_id=1, source_target_pairs={{0,1},{1,0},{2,3},{3,2},{4,5},{5,4},{6,7},{7,6},{8,9},{9,8},{10,11... | collective-permute-start | bytes 1179656 | tf_op jit(solution)/shard_map/ppermute | solution.py:311
  159.5 23.8 %collective-permute-start.41 = (bf16[128,1536]{1,0:T(8,128)(2,1)S(1)}, bf16[128,1536]{1,0:T(8,128)(2,1)S(1)}, u32[]{:S(2)}, u32[]{:S(2)}) collective-permute-start(bf16[128,1536]{1,0:T(8,128)(2,1)S(1)} %slice.136), channel_id=1, source_target_pairs={{0,4},{4,0},{1,5},{5,1},{2,6},{6,2},{3,7},{7,3},{8,12},{12,8},{9,1... | collective-permute-start | bytes 1179656 | tf_op jit(solution)/shard_map/ppermute | solution.py:311
  183.6 22.0 %collective-permute-start.47 = (bf16[256,1664]{1,0:T(8,128)(2,1)}, bf16[256,1664]{1,0:T(8,128)(2,1)}, u32[]{:S(2)}, u32[]{:S(2)}) collective-permute-start(bf16[256,1664]{1,0:T(8,128)(2,1)} %get-tuple-element.165), channel_id=1, source_target_pairs={{0,2},{2,0},{1,3},{3,1},{4,6},{6,4},{5,7},{7,5},{8,10},{10,8},{9,1... | collective-permute-start | bytes 2555912 | tf_op jit(solution)/shard_map/ppermute | solution.py:311
  204.6 25.0 %collective-permute-start.58 = (bf16[256,1664]{1,0:T(8,128)(2,1)}, bf16[256,1664]{1,0:T(8,128)(2,1)}, u32[]{:S(2)}, u32[]{:S(2)}) collective-permute-start(bf16[256,1664]{1,0:T(8,128)(2,1)} %get-tuple-element.185), channel_id=1, source_target_pairs={{0,2},{2,0},{1,3},{3,1},{4,6},{6,4},{5,7},{7,5},{8,10},{10,8},{9,1... | collective-permute-start | bytes 2555912 | tf_op jit(solution)/shard_map/ppermute | solution.py:311
  205.2 154.6 %reduce-scatter.7.cloned.1.call-start = ((), (), s32[]{:S(2)}) async-start(), calls=%async_computation.10 | async-start | bytes 2949120 | tf_op jit(solution)/shard_map/reduce_scatter | solution.py:65
  207.1 22.5 %collective-permute-start.59 = (bf16[128,1664]{1,0:T(8,128)(2,1)S(1)}, bf16[128,1664]{1,0:T(8,128)(2,1)S(1)}, u32[]{:S(2)}, u32[]{:S(2)}) collective-permute-start(bf16[128,1664]{1,0:T(8,128)(2,1)S(1)} %slice.178), channel_id=1, source_target_pairs={{0,1},{1,0},{2,3},{3,2},{4,5},{5,4},{6,7},{7,6},{8,9},{9,8},{10,11... | collective-permute-start | bytes 1277960 | tf_op jit(solution)/shard_map/ppermute | solution.py:311
  210.4 20.2 %collective-permute-start.60 = (bf16[128,1664]{1,0:T(8,128)(2,1)S(1)}, bf16[128,1664]{1,0:T(8,128)(2,1)S(1)}, u32[]{:S(2)}, u32[]{:S(2)}) collective-permute-start(bf16[128,1664]{1,0:T(8,128)(2,1)S(1)} %slice.179), channel_id=1, source_target_pairs={{0,4},{4,0},{1,5},{5,1},{2,6},{6,2},{3,7},{7,3},{8,12},{12,8},{9,1... | collective-permute-start | bytes 1277960 | tf_op jit(solution)/shard_map/ppermute | solution.py:311
  212.0 17.0 %collective-permute-start.45 = (bf16[128,1664]{1,0:T(8,128)(2,1)S(1)}, bf16[128,1664]{1,0:T(8,128)(2,1)S(1)}, u32[]{:S(2)}, u32[]{:S(2)}) collective-permute-start(bf16[128,1664]{1,0:T(8,128)(2,1)S(1)} %get-tuple-element.237), channel_id=1, source_target_pairs={{0,1},{1,0},{2,3},{3,2},{4,5},{5,4},{6,7},{7,6},{8,9},{9,8},{10,11... | collective-permute-start | bytes 1277960 | tf_op jit(solution)/shard_map/ppermute | solution.py:311
  222.4 15.1 %collective-permute-start.49 = (bf16[128,1664]{1,0:T(8,128)(2,1)S(1)}, bf16[128,1664]{1,0:T(8,128)(2,1)S(1)}, u32[]{:S(2)}, u32[]{:S(2)}) collective-permute-start(bf16[128,1664]{1,0:T(8,128)(2,1)S(1)} %reduce-precision_convert_fusion.7), channel_id=1, source_target_pairs={{0,1},{1,0},{2,3},{3,2},{4,5},{5,4},{6,7},{7,6},{8,9},{9,8},{10,11... | collective-permute-start | bytes 1277960 | tf_op jit(solution)/shard_map/ppermute | solution.py:311
  264.8 37.6 %collective-permute-start.50 = (bf16[512,1536]{1,0:T(8,128)(2,1)}, bf16[512,1536]{1,0:T(8,128)(2,1)}, u32[]{:S(2)}, u32[]{:S(2)}) collective-permute-start(bf16[512,1536]{1,0:T(8,128)(2,1)} %constant_dynamic-update-slice_fusion.16.refs_0_), channel_id=1, source_target_pairs={{0,1},{1,0},{2,3},{3,2},{4,5},{5,4},{6,7},{7,6},{8,9},{9,8},{10,11... | collective-permute-start | bytes 4718600 | tf_op jit(solution)/shard_map/ppermute | solution.py:311
  265.7 38.0 %collective-permute-start.51 = (bf16[512,1536]{1,0:T(8,128)(2,1)}, bf16[512,1536]{1,0:T(8,128)(2,1)}, u32[]{:S(2)}, u32[]{:S(2)}) collective-permute-start(bf16[512,1536]{1,0:T(8,128)(2,1)} %constant_dynamic-update-slice_fusion.16.refs_0_), channel_id=1, source_target_pairs={{0,4},{4,0},{1,5},{5,1},{2,6},{6,2},{3,7},{7,3},{8,12},{12,8},{9,1... | collective-permute-start | bytes 4718600 | tf_op jit(solution)/shard_map/ppermute | solution.py:311
  284.2 40.1 %all-to-all-start = ((bf16[8,272,448]{2,1,0:T(8,128)(2,1)}), bf16[8,272,448]{2,1,0:T(8,128)(2,1)S(1)}, u32[]{:S(2)}, u32[]{:S(2)}) async-start(bf16[8,272,448]{2,1,0:T(8,128)(2,1)} %constant_dynamic-update-slice_fusion.20), calls=%async_computation.1 | async-start | bytes 4456448 | tf_op jit(solution)/shard_map/all_to_all | solution.py:61
  287.9 73.7 %reduce-scatter.9.cloned.1.call-start = ((), (), s32[]{:S(2)}) async-start(), calls=%async_computation.11 | async-start | bytes 2949120 | tf_op jit(solution)/shard_map/reduce_scatter | solution.py:65
  288.6 126.9 %reduce-scatter.11.cloned.1.call-start = ((), (), s32[]{:S(2)}) async-start(), calls=%async_computation.12 | async-start | bytes 2048000 | tf_op jit(solution)/shard_map/reduce_scatter | solution.py:65
  324.3 19.1 %collective-permute-start.61 = (bf16[256,1536]{1,0:T(8,128)(2,1)}, bf16[256,1536]{1,0:T(8,128)(2,1)S(1)}, u32[]{:S(2)}, u32[]{:S(2)}) collective-permute-start(bf16[256,1536]{1,0:T(8,128)(2,1)} %slice.147), channel_id=1, source_target_pairs={{0,1},{1,0},{2,3},{3,2},{4,5},{5,4},{6,7},{7,6},{8,9},{9,8},{10,11... | collective-permute-start | bytes 2359304 | tf_op jit(solution)/shard_map/ppermute | solution.py:311
  325.3 18.1 %collective-permute-start.62 = (bf16[256,1536]{1,0:T(8,128)(2,1)S(1)}, bf16[256,1536]{1,0:T(8,128)(2,1)S(1)}, u32[]{:S(2)}, u32[]{:S(2)}) collective-permute-start(bf16[256,1536]{1,0:T(8,128)(2,1)S(1)} %slice.148), channel_id=1, source_target_pairs={{0,4},{4,0},{1,5},{5,1},{2,6},{6,2},{3,7},{7,3},{8,12},{12,8},{9,1... | collective-permute-start | bytes 2359304 | tf_op jit(solution)/shard_map/ppermute | solution.py:311
  325.8 19.5 %collective-permute-start.63 = (bf16[512,1536]{1,0:T(8,128)(2,1)}, bf16[512,1536]{1,0:T(8,128)(2,1)S(1)}, u32[]{:S(2)}, u32[]{:S(2)}) collective-permute-start(bf16[512,1536]{1,0:T(8,128)(2,1)} %constant_dynamic-update-slice_fusion.16.refs_0_), channel_id=1, source_target_pairs={{0,2},{2,0},{1,3},{3,1},{4,6},{6,4},{5,7},{7,5},{8,10},{10,8},{9,1... | collective-permute-start | bytes 4718600 | tf_op jit(solution)/shard_map/ppermute | solution.py:311
  325.8 18.3 %collective-permute-start.55 = (bf16[256,1536]{1,0:T(8,128)(2,1)}, bf16[256,1536]{1,0:T(8,128)(2,1)S(1)}, u32[]{:S(2)}, u32[]{:S(2)}) collective-permute-start(bf16[256,1536]{1,0:T(8,128)(2,1)} %get-tuple-element.183), channel_id=1, source_target_pairs={{0,2},{2,0},{1,3},{3,1},{4,6},{6,4},{5,7},{7,5},{8,10},{10,8},{9,1... | collective-permute-start | bytes 2359304 | tf_op jit(solution)/shard_map/ppermute | solution.py:311
  326.3 19.4 %collective-permute-start.64 = (bf16[512,1536]{1,0:T(8,128)(2,1)}, bf16[512,1536]{1,0:T(8,128)(2,1)S(1)}, u32[]{:S(2)}, u32[]{:S(2)}) collective-permute-start(bf16[512,1536]{1,0:T(8,128)(2,1)} %collective-permute-done.50.refs_1_), channel_id=1, source_target_pairs={{0,2},{2,0},{1,3},{3,1},{4,6},{6,4},{5,7},{7,5},{8,10},{10,8},{9,1... | collective-permute-start | bytes 4718600 | tf_op jit(solution)/shard_map/ppermute | solution.py:311
  344.1 21.0 %collective-permute-start.52 = (bf16[256,1536]{1,0:T(8,128)(2,1)}, bf16[256,1536]{1,0:T(8,128)(2,1)S(1)}, u32[]{:S(2)}, u32[]{:S(2)}) collective-permute-start(bf16[256,1536]{1,0:T(8,128)(2,1)} %get-tuple-element.179), channel_id=1, source_target_pairs={{0,2},{2,0},{1,3},{3,1},{4,6},{6,4},{5,7},{7,5},{8,10},{10,8},{9,1... | collective-permute-start | bytes 2359304 | tf_op jit(solution)/shard_map/ppermute | solution.py:311
  345.3 32.8 %collective-permute-start.54 = (bf16[256,1536]{1,0:T(8,128)(2,1)}, bf16[256,1536]{1,0:T(8,128)(2,1)}, u32[]{:S(2)}, u32[]{:S(2)}) collective-permute-start(bf16[256,1536]{1,0:T(8,128)(2,1)} %get-tuple-element.181), channel_id=1, source_target_pairs={{0,2},{2,0},{1,3},{3,1},{4,6},{6,4},{5,7},{7,5},{8,10},{10,8},{9,1... | collective-permute-start | bytes 2359304 | tf_op jit(solution)/shard_map/ppermute | solution.py:311
  345.7 46.6 %collective-permute-start.56 = (bf16[128,1536]{1,0:T(8,128)(2,1)}, bf16[128,1536]{1,0:T(8,128)(2,1)}, u32[]{:S(2)}, u32[]{:S(2)}) collective-permute-start(bf16[128,1536]{1,0:T(8,128)(2,1)} %get-tuple-element.239), channel_id=1, source_target_pairs={{0,1},{1,0},{2,3},{3,2},{4,5},{5,4},{6,7},{7,6},{8,9},{9,8},{10,11... | collective-permute-start | bytes 1179656 | tf_op jit(solution)/shard_map/ppermute | solution.py:311
  347.2 45.1 %collective-permute-start.57 = (bf16[128,1536]{1,0:T(8,128)(2,1)}, bf16[128,1536]{1,0:T(8,128)(2,1)}, u32[]{:S(2)}, u32[]{:S(2)}) collective-permute-start(bf16[128,1536]{1,0:T(8,128)(2,1)} %get-tuple-element.238), channel_id=1, source_target_pairs={{0,4},{4,0},{1,5},{5,1},{2,6},{6,2},{3,7},{7,3},{8,12},{12,8},{9,1... | collective-permute-start | bytes 1179656 | tf_op jit(solution)/shard_map/ppermute | solution.py:311
  361.6 13.0 %all-to-all-start.1 = ((bf16[4,96,768]{2,1,0:T(8,128)(2,1)}), bf16[4,96,768]{2,1,0:T(8,128)(2,1)S(1)}, u32[]{:S(2)}, u32[]{:S(2)}) async-start(bf16[4,96,768]{2,1,0:T(8,128)(2,1)} %bitcast.34), calls=%async_computation.4 | async-start | bytes 1179648 | tf_op jit(solution)/shard_map/all_to_all | solution.py:61
  387.6 13.5 %all-to-all-start.3 = ((bf16[4,96,768]{2,1,0:T(8,128)(2,1)}), bf16[4,96,768]{2,1,0:T(8,128)(2,1)S(1)}, u32[]{:S(2)}, u32[]{:S(2)}) async-start(bf16[4,96,768]{2,1,0:T(8,128)(2,1)} %bitcast.90), calls=%async_computation.6 | async-start | bytes 1179648 | tf_op jit(solution)/shard_map/all_to_all | solution.py:61
  399.6 14.8 %collective-permute-start.53 = (bf16[128,1536]{1,0:T(8,128)(2,1)S(1)}, bf16[128,1536]{1,0:T(8,128)(2,1)S(1)}, u32[]{:S(2)}, u32[]{:S(2)}) collective-permute-start(bf16[128,1536]{1,0:T(8,128)(2,1)S(1)} %slice.174), channel_id=1, source_target_pairs={{0,1},{1,0},{2,3},{3,2},{4,5},{5,4},{6,7},{7,6},{8,9},{9,8},{10,11... | collective-permute-start | bytes 1179656 | tf_op jit(solution)/shard_map/ppermute | solution.py:311
  400.2 22.9 %collective-permute-start.70 = (bf16[256,1536]{1,0:T(8,128)(2,1)}, bf16[256,1536]{1,0:T(8,128)(2,1)}, u32[]{:S(2)}, u32[]{:S(2)}) collective-permute-start(bf16[256,1536]{1,0:T(8,128)(2,1)} %get-tuple-element.226), channel_id=1, source_target_pairs={{0,2},{2,0},{1,3},{3,1},{4,6},{6,4},{5,7},{7,5},{8,10},{10,8},{9,1... | collective-permute-start | bytes 2359304 | tf_op jit(solution)/shard_map/ppermute | solution.py:311
  401.0 20.8 %collective-permute-start.69 = (bf16[128,1536]{1,0:T(8,128)(2,1)}, bf16[128,1536]{1,0:T(8,128)(2,1)}, u32[]{:S(2)}, u32[]{:S(2)}) collective-permute-start(bf16[128,1536]{1,0:T(8,128)(2,1)} %slice.182), channel_id=1, source_target_pairs={{0,4},{4,0},{1,5},{5,1},{2,6},{6,2},{3,7},{7,3},{8,12},{12,8},{9,1... | collective-permute-start | bytes 1179656 | tf_op jit(solution)/shard_map/ppermute | solution.py:311
  417.9 17.5 %all-to-all-start.4 = ((bf16[8,112,448]{2,1,0:T(8,128)(2,1)}), bf16[8,112,448]{2,1,0:T(8,128)(2,1)S(1)}, u32[]{:S(2)}, u32[]{:S(2)}) async-start(bf16[8,112,448]{2,1,0:T(8,128)(2,1)} %maximum_maximum_fusion), calls=%async_computation.8 | async-start | bytes 1835008 | tf_op jit(solution)/shard_map/all_to_all | solution.py:61
  (111 other events, 1200.5 us)
Sparse Core Ops, SparseCore 0:
  205.3 49.6 reduce-scatter.4
  261.9 49.7 reduce-scatter.6
  314.0 47.5 reduce-scatter.8
  363.7 35.7 reduce-scatter.10

commit v7 on v6

--- a/solution.py
+++ b/solution.py
@@ -375,10 +375,13 @@
     return swap(corner[:half], "x"), swap(corner[half:], "y")
 
 
-def corner_last(over_x, over_y, first):
+def corner_sums(over_x, over_y, first):
     half = over_x.shape[0] // 2
-    over_y, over_x = add(over_y[:half], first[0]), add(over_x[half:], first[1])
-    return swap(over_y, "y"), swap(over_x, "x"), over_y, over_x
+    return add(over_y[:half], first[0]), add(over_x[half:], first[1])
+
+
+def corner_last(sums):
+    return swap(sums[0], "y"), swap(sums[1], "x")
 
 
 def cost(micros):
@@ -919,7 +922,7 @@
     stages = (stage_own, stage_sides, stage_corner)
     rows_in, rows_cot, gated, gate_back, up_back = ([stage[n] for stage in stages] for n in range(5))
     gates = stage_own[5]
-    last_y, last_x = corner_last(back_x, back_y, passed)[:2]
+    last_y, last_x = corner_last(corner_sums(back_x, back_y, passed))
     down_sum = scatter_sum(down_part, "z")
 
     resid_grad, branch_grad, attended_grad, router_acc, gain_two_grad = run_kernel(
@@ -1047,9 +1050,10 @@
     first, down_grad, gate_grad = lax.optimization_barrier(
         (corner_first(mixed[3]), down_grad, gate_grad)
     )
-    last, up_grad = lax.optimization_barrier(
-        (corner_last(mixed[1], mixed[2], first)[:2], placed(up_sum))
-    )
+    sums, up_grad, dense_sum = lax.optimization_barrier(
+        (corner_sums(mixed[1], mixed[2], first), placed(up_sum), dense_sum)
+    )
+    last = corner_last(sums)
     mixture = jnp.concatenate(
         [left.astype(f32) + right.astype(f32) for left, right in zip(early, last)], axis=0
     )

time: 454 us -> 454 us (level)
    all_to_all x5, waiting for transfers between devices: 33.8 us -> 26.6 us  [exchange(): return lax.all_to_all(block, axes, split_axis=0, concat_axis=0, tiled=True)]
    ppermute x65, waiting for transfers between devices: 114 us -> 120 us  [swap(): return lax.ppermute(block, axis, [(0, 1), (1, 0)])]
  transfers between devices with their start and end apart: 80 -> 80, of which waited for: 34 -> 33; matrix products, arithmetic and copies ran while one was open for 13% -> 13% of each run, Pallas kernels for 23% -> 23%
where the time goes in v7:
time: 454 us; the launch traced here: 446 us
  waiting for transfers between devices  168 us (37%)
  Pallas kernels  105 us (23%)
  starting transfers between devices  70.7 us (16%)
  local copies, waits for them, and re-layouts  62.1 us (14%)
  other arithmetic  23.5 us (5%)
  between operations  15.9 us (4%)
    ppermute x65, waiting for transfers between devices, swap(): return lax.ppermute(block, axis, [(0, 1), (1, 0)])  120 us
    pallas_call x11, Pallas kernels, run_kernel(): pl.pallas_call(kernel, out_shape=[jax.ShapeDtypeStruct(shape, dtype) for...  97.9 us
    ppermute x65, starting transfers between devices, swap(): return lax.ppermute(block, axis, [(0, 1), (1, 0)])  42.2 us
    unnamed x172, local copies, waits for them, and re-layouts  31.1 us
    all_to_all x5, waiting for transfers between devices, exchange(): return lax.all_to_all(block, axes, split_axis=0, concat_axis=0, tiled=True)  26.6 us
    all_to_all x5, starting transfers between devices, exchange(): return lax.all_to_all(block, axes, split_axis=0, concat_axis=0, tiled=True)  17.8 us
    ppermute x6, waiting for transfers between devices, shifts(): lax.ppermute(block, 'z', [(i, (i + k) % depth) for i in range(depth)])  16.3 us
    ppermute x6, starting transfers between devices, shifts(): lax.ppermute(block, 'z', [(i, (i + k) % depth) for i in range(depth)])  10.1 us
  transfers between devices with their start and end apart: 80, of which 33 were waited for; matrix products, arithmetic and copies ran while one was open for 13% of the time, Pallas kernels for 23%

profile of v7, /device:TPU:0, one launch (start us, length us, event | category | flops | bytes accessed | tf_op | source)
XLA Modules:
  0.0 445.8 jit_solution(14132530904976596844)
XLA Ops:
  8.1 5.1 %collective-permute-start = (bf16[96,128]{1,0:T(8,128)(2,1)S(1)}, bf16[96,128]{1,0:T(8,128)(2,1)S(1)}, u32[]{:S(2)}, u32[]{:S(2)}) collective-permute-start(bf16[96,128]{1,0:T(8,128)(2,1)S(1)} %pad.9), channel_id=1, source_target_pairs={{0,24},{8,0},{16,8},{24,16},{1,25},{9,1},{17,9},{25,17},{2,26},{10... | collective-permute-start | bytes 73736 | tf_op jit(solution)/shard_map/ppermute | solution.py:317
  18.3 2.8 collective-permute-start.14
  26.8 2.7 collective-permute-done.3
  35.0 16.3 %collective-permute-done.13 = bf16[96,1792]{1,0:T(8,128)(2,1)} collective-permute-done((bf16[96,1792]{1,0:T(8,128)(2,1)}, bf16[96,1792]{1,0:T(8,128)(2,1)}, u32[]{:S(2)}, u32[]{:S(2)}) %collective-permute-start.13) | collective-permute-done | bytes 344096 | tf_op jit(solution)/shard_map/ppermute | solution.py:317
  61.8 1.8 dynamic-slice_bitcast_fusion.refs_6_.refs_10_.refs_3_
  63.6 4.2 dynamic-slice_bitcast_fusion.1.refs_5_.refs_9_
  67.8 3.2 dynamic-slice_bitcast_fusion.2.refs_4_.refs_8_
  71.0 6.6 %collective-permute-done.16.refs_2_ = bf16[4,96,1024]{2,1,0:T(8,128)(2,1)} collective-permute-done((bf16[4,96,1024]{2,1,0:T(8,128)(2,1)S(1)}, bf16[4,96,1024]{2,1,0:T(8,128)(2,1)}, u32[]{:S(2)}, u32[]{:S(2)}) %collective-permute-start.16) | collective-permute-done | bytes 786464 | tf_op jit(solution)/shard_map/ppermute | solution.py:311
  82.3 5.3 %collective-permute-done.17 = bf16[2,96,1024]{2,1,0:T(8,128)(2,1)S(1)} collective-permute-done((bf16[2,96,1024]{2,1,0:T(8,128)(2,1)S(1)}, bf16[2,96,1024]{2,1,0:T(8,128)(2,1)S(1)}, u32[]{:S(2)}, u32[]{:S(2)}) %collective-permute-start.17) | collective-permute-done | bytes 393248 | tf_op jit(solution)/shard_map/ppermute | solution.py:311
  97.6 9.1 %shard_map.229 = (bf16[256,1536]{1,0:T(8,128)(2,1)S(1)}, bf16[256,1536]{1,0:T(8,128)(2,1)S(1)}, bf16[256,256]{1,0:T(8,128)(2,1)S(1)}, bf16[256,256]{1,0:T(8,128)...) custom-call(s32[7]{0:T(128)S(1)} %copy-done.36, ...), custom_call_target="tpu_custom_call" | custom-call | flops 11000000512 | bytes 11000000 | tf_op jit(solution)/shard_map/pallas_call | solution.py:403
  106.7 2.7 copy-done.45
  114.9 5.7 %collective-permute-done.25 = bf16[2,96,768]{2,1,0:T(8,128)(2,1)S(1)} collective-permute-done((bf16[2,96,768]{2,1,0:T(8,128)(2,1)S(1)}, bf16[2,96,768]{2,1,0:T(8,128)(2,1)S(1)}, u32[]{:S(2)}, u32[]{:S(2)}) %collective-permute-start.25) | collective-permute-done | bytes 294944 | tf_op jit(solution)/shard_map/ppermute | solution.py:311
  121.3 6.7 %collective-permute-done.10 = bf16[128,1536]{1,0:T(8,128)(2,1)S(1)} collective-permute-done((bf16[128,1536]{1,0:T(8,128)(2,1)S(1)}, bf16[128,1536]{1,0:T(8,128)(2,1)S(1)}, u32[]{:S(2)}, u32[]{:S(2)}) %collective-permute-start.10) | collective-permute-done | bytes 393248 | tf_op jit(solution)/shard_map/ppermute | solution.py:311
  130.2 4.1 shard_map.230
  138.3 10.2 %shard_map.231 = (bf16[384,1536]{1,0:T(8,128)(2,1)S(1)}, bf16[384,1536]{1,0:T(8,128)(2,1)S(1)}, bf16[384,768]{1,0:T(8,128)(2,1)S(1)}, bf16[384,768]{1,0:T(8,128)...) custom-call(s32[7]{0:T(128)S(1)} %copy-done.37, ...), custom_call_target="tpu_custom_call" | custom-call | flops 8000000000 | bytes 8000000 | tf_op jit(solution)/shard_map/pallas_call | solution.py:403
  150.1 5.5 %collective-permute-done.31.refs_0_ = bf16[256,1536]{1,0:T(8,128)(2,1)S(1)} collective-permute-done((bf16[256,1536]{1,0:T(8,128)(2,1)}, bf16[256,1536]{1,0:T(8,128)(2,1)S(1)}, u32[]{:S(2)}, u32[]{:S(2)}) %collective-permute-start.31) | collective-permute-done | bytes 786464 | tf_op jit(solution)/shard_map/ppermute | solution.py:311
  158.9 2.2 collective-permute-done.36.refs_3_
  161.1 17.4 %shard_map.232 = (bf16[768,1536]{1,0:T(8,128)(2,1)S(1)}, bf16[768,1536]{1,0:T(8,128)(2,1)S(1)}, bf16[768,768]{1,0:T(8,128)(2,1)S(1)}, bf16[768,768]{1,0:T(8,128)...) custom-call(s32[7]{0:T(128)S(1)} %copy-done.37, ...), custom_call_target="tpu_custom_call" | custom-call | flops 16000000000 | bytes 16000000 | tf_op jit(solution)/shard_map/pallas_call | solution.py:403
  184.3 12.9 %shard_map.233 = (bf16[384,1536]{1,0:T(8,128)(2,1)S(1)}, bf16[384,1536]{1,0:T(8,128)(2,1)}, bf16[384,768]{1,0:T(8,128)(2,1)S(1)}, bf16[384,768]{1,0:T(8,128)(2,1...) custom-call(s32[7]{0:T(128)S(1)} %copy-done.37, ...), custom_call_target="tpu_custom_call" | custom-call | flops 8000000000 | bytes 8000000 | tf_op jit(solution)/shard_map/pallas_call | solution.py:403
  211.7 9.1 %collective-permute-done.48 = bf16[128,1664]{1,0:T(8,128)(2,1)S(1)} collective-permute-done((bf16[128,1664]{1,0:T(8,128)(2,1)S(1)}, bf16[128,1664]{1,0:T(8,128)(2,1)S(1)}, u32[]{:S(2)}, u32[]{:S(2)}) %collective-permute-start.48) | collective-permute-done | bytes 426016 | tf_op jit(solution)/shard_map/ppermute | solution.py:311
  222.2 5.3 %collective-permute-done.45 = bf16[128,1664]{1,0:T(8,128)(2,1)S(1)} collective-permute-done((bf16[128,1664]{1,0:T(8,128)(2,1)S(1)}, bf16[128,1664]{1,0:T(8,128)(2,1)S(1)}, u32[]{:S(2)}, u32[]{:S(2)}) %collective-permute-start.45) | collective-permute-done | bytes 426016 | tf_op jit(solution)/shard_map/ppermute | solution.py:311
  229.1 7.0 %collective-permute-done.49.last_x = bf16[128,1664]{1,0:T(8,128)(2,1)S(1)} collective-permute-done((bf16[128,1664]{1,0:T(8,128)(2,1)S(1)}, bf16[128,1664]{1,0:T(8,128)(2,1)S(1)}, u32[]{:S(2)}, u32[]{:S(2)}) %collective-permute-start.49) | collective-permute-done | bytes 426016 | tf_op jit(solution)/shard_map/ppermute | solution.py:311
  236.1 2.4 collective-permute-done.46.last_y
  239.3 8.3 %shard_map.235 = (f32[256,1536]{1,0:T(8,128)}, bf16[256,1536]{1,0:T(8,128)(2,1)}, bf16[256,1536]{1,0:T(8,128)(2,1)}, f32[1536,128]{1,0:T(8,128)}, f32[1,1536]{1,0:T(1,128)}) custom-call(s32[7]{0:T(128)} %stack.76.at, bf16[256,1664]{1,0:T(8,128)(2,1)} %copy-done.47, bf16[256,1664]{1,0:T(8,128)(2,1)} %collective-permute-done.58.far, ...), custom_call_target="tpu_custom_call" | custom-call | flops 6000000000 | bytes 6000000 | tf_op jit(solution)/shard_map/pallas_call | solution.py:403
  247.5 12.8 %shard_map.236 = (bf16[1536,768]{1,0:T(8,128)(2,1)}, bf16[1536,768]{1,0:T(8,128)(2,1)}) custom-call(s32[7]{0:T(128)} %stack.76.at, bf16[384,1536]{1,0:T(8,128)(2,1)} %copy-done.52, bf16[768,1536]{1,0:T(8,128)(2,1)} %copy-done.51, bf16[384,1536]{1,0:T(8,128)(2,1)} %copy-done.50, bf16[384,768]{1,0:T(8,128)(2,1)} %copy-done.60, bf16[768,768]{1,0:T(8,128)(2,1)} %copy-done.58, ...), custom_call_target="tpu_custom_call" | custom-call | flops 8000000000 | bytes 8000000 | tf_op jit(solution)/shard_map/pallas_call | solution.py:403
  264.9 8.5 %shard_map.237.back = bf16[8,272,448]{2,1,0:T(8,128)(2,1)} custom-call(s32[7]{0:T(128)} %stack.76.at, bf16[256,1536]{1,0:T(8,128)(2,1)} %get-tuple-element.200.attended, bf16[12,256,256]{2,1,0:T(8,128)(2,1)} %copy-done.48, bf16[256,1536]{1,0:T(8,128)(2,1)} %copy-done.53, bf16[256,256]{1,0:T(8,128)(2,1)} %copy-done.63, bf16[256,256]{1,0:T(8,128)(2,1)} %copy-done.64, ...), custom_call_target="tpu_custom_call" | custom-call | flops 6000000000 | bytes 6000000 | tf_op jit(solution)/shard_map/pallas_call | solution.py:403
  276.5 3.7 shard_map.238
  282.9 3.6 all-to-all-start
  287.3 13.8 %collective-permute-done.50.refs_1_ = bf16[512,1536]{1,0:T(8,128)(2,1)} collective-permute-done((bf16[512,1536]{1,0:T(8,128)(2,1)}, bf16[512,1536]{1,0:T(8,128)(2,1)}, u32[]{:S(2)}, u32[]{:S(2)}) %collective-permute-start.50) | collective-permute-done | bytes 1572896 | tf_op jit(solution)/shard_map/ppermute | solution.py:311
  302.3 9.3 %shard_map.234 = (bf16[256,1536]{1,0:T(8,128)(2,1)}, bf16[256,1536]{1,0:T(8,128)(2,1)}, bf16[256,1536]{1,0:T(8,128)(2,1)}, bf16[256,1536]{1,0:T(8,128)(2,1)}, bf...) custom-call(s32[7]{0:T(128)} %stack.76.at, ...), custom_call_target="tpu_custom_call" | custom-call | flops 10000000000 | bytes 10000000 | tf_op jit(solution)/shard_map/pallas_call | solution.py:403
  311.6 2.1 slice.147
  314.9 8.1 %all-to-all-done.back = bf16[8,272,448]{2,1,0:T(8,128)(2,1)S(1)} async-done(((bf16[8,272,448]{2,1,0:T(8,128)(2,1)}), bf16[8,272,448]{2,1,0:T(8,128)(2,1)S(1)}, u32[]{:S(2)}, u32[]{:S(2)}) %all-to-all-start) | async-done | bytes 1949728 | tf_op jit(solution)/shard_map/all_to_all | solution.py:61
  324.9 17.1 %collective-permute-done.61 = bf16[256,1536]{1,0:T(8,128)(2,1)S(1)} collective-permute-done((bf16[256,1536]{1,0:T(8,128)(2,1)}, bf16[256,1536]{1,0:T(8,128)(2,1)S(1)}, u32[]{:S(2)}, u32[]{:S(2)}) %collective-permute-start.61) | collective-permute-done | bytes 786464 | tf_op jit(solution)/shard_map/ppermute | solution.py:311
  343.2 3.8 collective-permute-done.66.refs_7_
  347.1 7.3 %shard_map.239 = bf16[4,400,448]{2,1,0:T(8,128)(2,1)S(1)} custom-call(s32[7]{0:T(128)S(1)} %copy-done.39, bf16[8,272,448]{2,1,0:T(8,128)(2,1)S(1)} %all-to-all-done.back, bf16[512,1536]{1,0:T(8,128)(2,1)} %constant_dynamic-update-slice_fusion.16.refs_0_, bf16[512,1536]{1,0:T(8,128)(2,1)} %collective-permute-done.50.refs_1_, ...), custom_call_target="tpu_custom_call" | custom-call | flops 8000000000 | bytes 8000000 | tf_op jit(solution)/shard_map/pallas_call | solution.py:1031
  355.5 4.6 %reduce-scatter.9.cloned.1.call-done = bf16[384,768]{1,0:T(8,128)(2,1)} async-done(((bf16[1536,768]{1,0:T(8,128)(2,1)}), bf16[384,768]{1,0:T(8,128)(2,1)}) %reduce-scatter.9.cloned.1.call-update) | async-done | bytes 589840 | tf_op jit(solution)/shard_map/reduce_scatter | solution.py:65
  360.4 3.5 all-to-all-start.1
  366.3 2.0 collective-permute-start.57
  368.3 5.6 %all-to-all-done.1 = bf16[4,96,768]{2,1,0:T(8,128)(2,1)S(1)} async-done(((bf16[4,96,768]{2,1,0:T(8,128)(2,1)}), bf16[4,96,768]{2,1,0:T(8,128)(2,1)S(1)}, u32[]{:S(2)}, u32[]{:S(2)}) %all-to-all-start.1) | async-done | bytes 589856 | tf_op jit(solution)/shard_map/all_to_all | solution.py:61
  373.9 3.5 all-to-all-start.2
  381.0 7.2 %all-to-all-done.2 = bf16[4,96,768]{2,1,0:T(8,128)(2,1)S(1)} async-done(((bf16[4,96,768]{2,1,0:T(8,128)(2,1)}), bf16[4,96,768]{2,1,0:T(8,128)(2,1)S(1)}, u32[]{:S(2)}, u32[]{:S(2)}) %all-to-all-start.2) | async-done | bytes 589856 | tf_op jit(solution)/shard_map/all_to_all | solution.py:61
  388.2 3.7 all-to-all-start.3
  395.6 5.7 %all-to-all-done.3 = bf16[4,96,768]{2,1,0:T(8,128)(2,1)S(1)} async-done(((bf16[4,96,768]{2,1,0:T(8,128)(2,1)}), bf16[4,96,768]{2,1,0:T(8,128)(2,1)S(1)}, u32[]{:S(2)}, u32[]{:S(2)}) %all-to-all-start.3) | async-done | bytes 589856 | tf_op jit(solution)/shard_map/all_to_all | solution.py:61
  408.4 3.6 all-to-all-start.4
  411.9 1.9 collective-permute-start.69
  413.8 3.0 collective-permute-done.67
  418.1 12.1 %collective-permute-done.68 = bf16[128,1536]{1,0:T(8,128)(2,1)} collective-permute-done((bf16[128,1536]{1,0:T(8,128)(2,1)S(1)}, bf16[128,1536]{1,0:T(8,128)(2,1)}, u32[]{:S(2)}, u32[]{:S(2)}) %collective-permute-start.68) | collective-permute-done | bytes 393248 | tf_op jit(solution)/shard_map/ppermute | solution.py:311
  430.2 3.1 collective-permute-done.69
  (400 shorter events, 123.8 us)
Async XLA Ops:
  7.2 275.7 %reduce-scatter.5.cloned.1.call-start = ((), (), s32[]{:S(2)}) async-start(), calls=%async_computation.9 | async-start | bytes 2949120 | tf_op jit(solution)/shard_map/reduce_scatter | solution.py:65
  8.1 14.9 %collective-permute-start = (bf16[96,128]{1,0:T(8,128)(2,1)S(1)}, bf16[96,128]{1,0:T(8,128)(2,1)S(1)}, u32[]{:S(2)}, u32[]{:S(2)}) collective-permute-start(bf16[96,128]{1,0:T(8,128)(2,1)S(1)} %pad.9), channel_id=1, source_target_pairs={{0,24},{8,0},{16,8},{24,16},{1,25},{9,1},{17,9},{25,17},{2,26},{10... | collective-permute-start | bytes 73736 | tf_op jit(solution)/shard_map/ppermute | solution.py:317
  18.3 15.8 %collective-permute-start.14 = (bf16[96,1792]{1,0:T(8,128)(2,1)}, bf16[96,1792]{1,0:T(8,128)(2,1)}, u32[]{:S(2)}, u32[]{:S(2)}) collective-permute-start(bf16[96,1792]{1,0:T(8,128)(2,1)} %pad_maximum_fusion.3), channel_id=1, source_target_pairs={{0,24},{8,0},{16,8},{24,16},{1,25},{9,1},{17,9},{25,17},{2,26},{10... | collective-permute-start | bytes 1032200 | tf_op jit(solution)/shard_map/ppermute | solution.py:317
  21.8 29.5 %collective-permute-start.13 = (bf16[96,1792]{1,0:T(8,128)(2,1)}, bf16[96,1792]{1,0:T(8,128)(2,1)}, u32[]{:S(2)}, u32[]{:S(2)}) collective-permute-start(bf16[96,1792]{1,0:T(8,128)(2,1)} %pad_maximum_fusion.3), channel_id=1, source_target_pairs={{0,16},{8,24},{16,0},{24,8},{1,17},{9,25},{17,1},{25,9},{2,18},{10... | collective-permute-start | bytes 1032200 | tf_op jit(solution)/shard_map/ppermute | solution.py:317
  23.0 29.3 %collective-permute-start.12 = (bf16[96,1792]{1,0:T(8,128)(2,1)}, bf16[96,1792]{1,0:T(8,128)(2,1)}, u32[]{:S(2)}, u32[]{:S(2)}) collective-permute-start(bf16[96,1792]{1,0:T(8,128)(2,1)} %pad_maximum_fusion.3), channel_id=1, source_target_pairs={{0,8},{8,16},{16,24},{24,0},{1,9},{9,17},{17,25},{25,1},{2,10},{10... | collective-permute-start | bytes 1032200 | tf_op jit(solution)/shard_map/ppermute | solution.py:317
  31.1 27.7 %collective-permute-start.8 = (bf16[256,1536]{1,0:T(8,128)(2,1)S(1)}, bf16[256,1536]{1,0:T(8,128)(2,1)S(1)}, u32[]{:S(2)}, u32[]{:S(2)}) collective-permute-start(bf16[256,1536]{1,0:T(8,128)(2,1)S(1)} %copy-done.40), channel_id=1, source_target_pairs={{0,4},{4,0},{1,5},{5,1},{2,6},{6,2},{3,7},{7,3},{8,12},{12,8},{9,1... | collective-permute-start | bytes 2359304 | tf_op jit(solution)/shard_map/ppermute | solution.py:311
  31.7 27.2 %collective-permute-start.9 = (bf16[256,1536]{1,0:T(8,128)(2,1)S(1)}, bf16[256,1536]{1,0:T(8,128)(2,1)S(1)}, u32[]{:S(2)}, u32[]{:S(2)}) collective-permute-start(bf16[256,1536]{1,0:T(8,128)(2,1)S(1)} %copy-done.40), channel_id=1, source_target_pairs={{0,1},{1,0},{2,3},{3,2},{4,5},{5,4},{6,7},{7,6},{8,9},{9,8},{10,11... | collective-permute-start | bytes 2359304 | tf_op jit(solution)/shard_map/ppermute | solution.py:311
  58.9 19.7 %collective-permute-start.15 = (bf16[4,96,1024]{2,1,0:T(8,128)(2,1)S(1)}, bf16[4,96,1024]{2,1,0:T(8,128)(2,1)}, u32[]{:S(2)}, u32[]{:S(2)}) collective-permute-start(bf16[4,96,1024]{2,1,0:T(8,128)(2,1)S(1)} %pad_maximum_fusion.refs_0_), channel_id=1, source_target_pairs={{0,1},{1,0},{2,3},{3,2},{4,5},{5,4},{6,7},{7,6},{8,9},{9,8},{10,11... | collective-permute-start | bytes 2359304 | tf_op jit(solution)/shard_map/ppermute | solution.py:311
  60.3 17.3 %collective-permute-start.16 = (bf16[4,96,1024]{2,1,0:T(8,128)(2,1)S(1)}, bf16[4,96,1024]{2,1,0:T(8,128)(2,1)}, u32[]{:S(2)}, u32[]{:S(2)}) collective-permute-start(bf16[4,96,1024]{2,1,0:T(8,128)(2,1)S(1)} %pad_maximum_fusion.refs_0_), channel_id=1, source_target_pairs={{0,4},{4,0},{1,5},{5,1},{2,6},{6,2},{3,7},{7,3},{8,12},{12,8},{9,1... | collective-permute-start | bytes 2359304 | tf_op jit(solution)/shard_map/ppermute | solution.py:311
  91.6 19.0 %collective-permute-start.23 = (bf16[4,96,768]{2,1,0:T(8,128)(2,1)}, bf16[4,96,768]{2,1,0:T(8,128)(2,1)S(1)}, u32[]{:S(2)}, u32[]{:S(2)}) collective-permute-start(bf16[4,96,768]{2,1,0:T(8,128)(2,1)} %pad_maximum_fusion.1.refs_0_), channel_id=1, source_target_pairs={{0,1},{1,0},{2,3},{3,2},{4,5},{5,4},{6,7},{7,6},{8,9},{9,8},{10,11... | collective-permute-start | bytes 1769480 | tf_op jit(solution)/shard_map/ppermute | solution.py:311
  93.1 17.4 %collective-permute-start.24 = (bf16[4,96,768]{2,1,0:T(8,128)(2,1)}, bf16[4,96,768]{2,1,0:T(8,128)(2,1)S(1)}, u32[]{:S(2)}, u32[]{:S(2)}) collective-permute-start(bf16[4,96,768]{2,1,0:T(8,128)(2,1)} %pad_maximum_fusion.1.refs_0_), channel_id=1, source_target_pairs={{0,4},{4,0},{1,5},{5,1},{2,6},{6,2},{3,7},{7,3},{8,12},{12,8},{9,1... | collective-permute-start | bytes 1769480 | tf_op jit(solution)/shard_map/ppermute | solution.py:311
  112.3 15.7 %collective-permute-start.10 = (bf16[128,1536]{1,0:T(8,128)(2,1)S(1)}, bf16[128,1536]{1,0:T(8,128)(2,1)S(1)}, u32[]{:S(2)}, u32[]{:S(2)}) collective-permute-start(bf16[128,1536]{1,0:T(8,128)(2,1)S(1)} %slice.159), channel_id=1, source_target_pairs={{0,1},{1,0},{2,3},{3,2},{4,5},{5,4},{6,7},{7,6},{8,9},{9,8},{10,11... | collective-permute-start | bytes 1179656 | tf_op jit(solution)/shard_map/ppermute | solution.py:311
  113.4 14.9 %collective-permute-start.11 = (bf16[128,1536]{1,0:T(8,128)(2,1)S(1)}, bf16[128,1536]{1,0:T(8,128)(2,1)S(1)}, u32[]{:S(2)}, u32[]{:S(2)}) collective-permute-start(bf16[128,1536]{1,0:T(8,128)(2,1)S(1)} %slice.160), channel_id=1, source_target_pairs={{0,4},{4,0},{1,5},{5,1},{2,6},{6,2},{3,7},{7,3},{8,12},{12,8},{9,1... | collective-permute-start | bytes 1179656 | tf_op jit(solution)/shard_map/ppermute | solution.py:311
  114.9 15.2 %collective-permute-start.27 = (bf16[4,96,768]{2,1,0:T(8,128)(2,1)S(1)}, bf16[4,96,768]{2,1,0:T(8,128)(2,1)S(1)}, u32[]{:S(2)}, u32[]{:S(2)}) collective-permute-start(bf16[4,96,768]{2,1,0:T(8,128)(2,1)S(1)} %copy-done.19), channel_id=1, source_target_pairs={{0,2},{2,0},{1,3},{3,1},{4,6},{6,4},{5,7},{7,5},{8,10},{10,8},{9,1... | collective-permute-start | bytes 1769480 | tf_op jit(solution)/shard_map/ppermute | solution.py:311
  135.7 19.9 %collective-permute-start.31 = (bf16[256,1536]{1,0:T(8,128)(2,1)}, bf16[256,1536]{1,0:T(8,128)(2,1)S(1)}, u32[]{:S(2)}, u32[]{:S(2)}) collective-permute-start(bf16[256,1536]{1,0:T(8,128)(2,1)} %get-tuple-element.148.refs_0_.second), channel_id=1, source_target_pairs={{0,1},{1,0},{2,3},{3,2},{4,5},{5,4},{6,7},{7,6},{8,9},{9,8},{10,11... | collective-permute-start | bytes 2359304 | tf_op jit(solution)/shard_map/ppermute | solution.py:311
  137.2 19.4 %collective-permute-start.32 = (bf16[256,1536]{1,0:T(8,128)(2,1)}, bf16[256,1536]{1,0:T(8,128)(2,1)S(1)}, u32[]{:S(2)}, u32[]{:S(2)}) collective-permute-start(bf16[256,1536]{1,0:T(8,128)(2,1)} %get-tuple-element.148.refs_0_.second), channel_id=1, source_target_pairs={{0,4},{4,0},{1,5},{5,1},{2,6},{6,2},{3,7},{7,3},{8,12},{12,8},{9,1... | collective-permute-start | bytes 2359304 | tf_op jit(solution)/shard_map/ppermute | solution.py:311
  137.7 19.5 %collective-permute-start.37 = (bf16[256,1536]{1,0:T(8,128)(2,1)S(1)}, bf16[256,1536]{1,0:T(8,128)(2,1)S(1)}, u32[]{:S(2)}, u32[]{:S(2)}) collective-permute-start(bf16[256,1536]{1,0:T(8,128)(2,1)S(1)} %copy-done.25), channel_id=1, source_target_pairs={{0,2},{2,0},{1,3},{3,1},{4,6},{6,4},{5,7},{7,5},{8,10},{10,8},{9,1... | collective-permute-start | bytes 2359304 | tf_op jit(solution)/shard_map/ppermute | solution.py:311
  137.7 20.3 %collective-permute-start.38 = (bf16[256,1536]{1,0:T(8,128)(2,1)S(1)}, bf16[256,1536]{1,0:T(8,128)(2,1)S(1)}, u32[]{:S(2)}, u32[]{:S(2)}) collective-permute-start(bf16[256,1536]{1,0:T(8,128)(2,1)S(1)} %copy-done.22), channel_id=1, source_target_pairs={{0,2},{2,0},{1,3},{3,1},{4,6},{6,4},{5,7},{7,5},{8,10},{10,8},{9,1... | collective-permute-start | bytes 2359304 | tf_op jit(solution)/shard_map/ppermute | solution.py:311
  157.1 25.4 %collective-permute-start.43 = (bf16[256,1536]{1,0:T(8,128)(2,1)}, bf16[256,1536]{1,0:T(8,128)(2,1)S(1)}, u32[]{:S(2)}, u32[]{:S(2)}) collective-permute-start(bf16[256,1536]{1,0:T(8,128)(2,1)} %constant_dynamic-update-slice_fusion.8.refs_2_), channel_id=1, source_target_pairs={{0,2},{2,0},{1,3},{3,1},{4,6},{6,4},{5,7},{7,5},{8,10},{10,8},{9,1... | collective-permute-start | bytes 2359304 | tf_op jit(solution)/shard_map/ppermute | solution.py:311
  157.2 24.7 %collective-permute-start.40 = (bf16[128,1536]{1,0:T(8,128)(2,1)S(1)}, bf16[128,1536]{1,0:T(8,128)(2,1)S(1)}, u32[]{:S(2)}, u32[]{:S(2)}) collective-permute-start(bf16[128,1536]{1,0:T(8,128)(2,1)S(1)} %slice.135), channel_id=1, source_target_pairs={{0,1},{1,0},{2,3},{3,2},{4,5},{5,4},{6,7},{7,6},{8,9},{9,8},{10,11... | collective-permute-start | bytes 1179656 | tf_op jit(solution)/shard_map/ppermute | solution.py:311
  158.0 23.8 %collective-permute-start.41 = (bf16[128,1536]{1,0:T(8,128)(2,1)S(1)}, bf16[128,1536]{1,0:T(8,128)(2,1)S(1)}, u32[]{:S(2)}, u32[]{:S(2)}) collective-permute-start(bf16[128,1536]{1,0:T(8,128)(2,1)S(1)} %slice.136), channel_id=1, source_target_pairs={{0,4},{4,0},{1,5},{5,1},{2,6},{6,2},{3,7},{7,3},{8,12},{12,8},{9,1... | collective-permute-start | bytes 1179656 | tf_op jit(solution)/shard_map/ppermute | solution.py:311
  182.1 22.0 %collective-permute-start.47 = (bf16[256,1664]{1,0:T(8,128)(2,1)}, bf16[256,1664]{1,0:T(8,128)(2,1)}, u32[]{:S(2)}, u32[]{:S(2)}) collective-permute-start(bf16[256,1664]{1,0:T(8,128)(2,1)} %get-tuple-element.166), channel_id=1, source_target_pairs={{0,2},{2,0},{1,3},{3,1},{4,6},{6,4},{5,7},{7,5},{8,10},{10,8},{9,1... | collective-permute-start | bytes 2555912 | tf_op jit(solution)/shard_map/ppermute | solution.py:311
  203.1 25.0 %collective-permute-start.58 = (bf16[256,1664]{1,0:T(8,128)(2,1)}, bf16[256,1664]{1,0:T(8,128)(2,1)}, u32[]{:S(2)}, u32[]{:S(2)}) collective-permute-start(bf16[256,1664]{1,0:T(8,128)(2,1)} %get-tuple-element.186), channel_id=1, source_target_pairs={{0,2},{2,0},{1,3},{3,1},{4,6},{6,4},{5,7},{7,5},{8,10},{10,8},{9,1... | collective-permute-start | bytes 2555912 | tf_op jit(solution)/shard_map/ppermute | solution.py:311
  203.7 151.9 %reduce-scatter.7.cloned.1.call-start = ((), (), s32[]{:S(2)}) async-start(), calls=%async_computation.10 | async-start | bytes 2949120 | tf_op jit(solution)/shard_map/reduce_scatter | solution.py:65
  205.6 22.5 %collective-permute-start.59 = (bf16[128,1664]{1,0:T(8,128)(2,1)S(1)}, bf16[128,1664]{1,0:T(8,128)(2,1)S(1)}, u32[]{:S(2)}, u32[]{:S(2)}) collective-permute-start(bf16[128,1664]{1,0:T(8,128)(2,1)S(1)} %slice.178), channel_id=1, source_target_pairs={{0,1},{1,0},{2,3},{3,2},{4,5},{5,4},{6,7},{7,6},{8,9},{9,8},{10,11... | collective-permute-start | bytes 1277960 | tf_op jit(solution)/shard_map/ppermute | solution.py:311
  208.9 20.2 %collective-permute-start.60 = (bf16[128,1664]{1,0:T(8,128)(2,1)S(1)}, bf16[128,1664]{1,0:T(8,128)(2,1)S(1)}, u32[]{:S(2)}, u32[]{:S(2)}) collective-permute-start(bf16[128,1664]{1,0:T(8,128)(2,1)S(1)} %slice.179), channel_id=1, source_target_pairs={{0,4},{4,0},{1,5},{5,1},{2,6},{6,2},{3,7},{7,3},{8,12},{12,8},{9,1... | collective-permute-start | bytes 1277960 | tf_op jit(solution)/shard_map/ppermute | solution.py:311
  210.5 17.0 %collective-permute-start.45 = (bf16[128,1664]{1,0:T(8,128)(2,1)S(1)}, bf16[128,1664]{1,0:T(8,128)(2,1)S(1)}, u32[]{:S(2)}, u32[]{:S(2)}) collective-permute-start(bf16[128,1664]{1,0:T(8,128)(2,1)S(1)} %get-tuple-element.239), channel_id=1, source_target_pairs={{0,1},{1,0},{2,3},{3,2},{4,5},{5,4},{6,7},{7,6},{8,9},{9,8},{10,11... | collective-permute-start | bytes 1277960 | tf_op jit(solution)/shard_map/ppermute | solution.py:311
  220.9 15.1 %collective-permute-start.49 = (bf16[128,1664]{1,0:T(8,128)(2,1)S(1)}, bf16[128,1664]{1,0:T(8,128)(2,1)S(1)}, u32[]{:S(2)}, u32[]{:S(2)}) collective-permute-start(bf16[128,1664]{1,0:T(8,128)(2,1)S(1)} %reduce-precision_convert_fusion.7), channel_id=1, source_target_pairs={{0,1},{1,0},{2,3},{3,2},{4,5},{5,4},{6,7},{7,6},{8,9},{9,8},{10,11... | collective-permute-start | bytes 1277960 | tf_op jit(solution)/shard_map/ppermute | solution.py:311
  263.4 37.6 %collective-permute-start.50 = (bf16[512,1536]{1,0:T(8,128)(2,1)}, bf16[512,1536]{1,0:T(8,128)(2,1)}, u32[]{:S(2)}, u32[]{:S(2)}) collective-permute-start(bf16[512,1536]{1,0:T(8,128)(2,1)} %constant_dynamic-update-slice_fusion.16.refs_0_), channel_id=1, source_target_pairs={{0,1},{1,0},{2,3},{3,2},{4,5},{5,4},{6,7},{7,6},{8,9},{9,8},{10,11... | collective-permute-start | bytes 4718600 | tf_op jit(solution)/shard_map/ppermute | solution.py:311
  264.3 37.9 %collective-permute-start.51 = (bf16[512,1536]{1,0:T(8,128)(2,1)}, bf16[512,1536]{1,0:T(8,128)(2,1)}, u32[]{:S(2)}, u32[]{:S(2)}) collective-permute-start(bf16[512,1536]{1,0:T(8,128)(2,1)} %constant_dynamic-update-slice_fusion.16.refs_0_), channel_id=1, source_target_pairs={{0,4},{4,0},{1,5},{5,1},{2,6},{6,2},{3,7},{7,3},{8,12},{12,8},{9,1... | collective-permute-start | bytes 4718600 | tf_op jit(solution)/shard_map/ppermute | solution.py:311
  282.9 40.1 %all-to-all-start = ((bf16[8,272,448]{2,1,0:T(8,128)(2,1)}), bf16[8,272,448]{2,1,0:T(8,128)(2,1)S(1)}, u32[]{:S(2)}, u32[]{:S(2)}) async-start(bf16[8,272,448]{2,1,0:T(8,128)(2,1)} %constant_dynamic-update-slice_fusion.20), calls=%async_computation.1 | async-start | bytes 4456448 | tf_op jit(solution)/shard_map/all_to_all | solution.py:61
  286.5 73.7 %reduce-scatter.9.cloned.1.call-start = ((), (), s32[]{:S(2)}) async-start(), calls=%async_computation.11 | async-start | bytes 2949120 | tf_op jit(solution)/shard_map/reduce_scatter | solution.py:65
  287.2 117.4 %reduce-scatter.11.cloned.1.call-start = ((), (), s32[]{:S(2)}) async-start(), calls=%async_computation.12 | async-start | bytes 2048000 | tf_op jit(solution)/shard_map/reduce_scatter | solution.py:65
  322.9 19.1 %collective-permute-start.61 = (bf16[256,1536]{1,0:T(8,128)(2,1)}, bf16[256,1536]{1,0:T(8,128)(2,1)S(1)}, u32[]{:S(2)}, u32[]{:S(2)}) collective-permute-start(bf16[256,1536]{1,0:T(8,128)(2,1)} %slice.147), channel_id=1, source_target_pairs={{0,1},{1,0},{2,3},{3,2},{4,5},{5,4},{6,7},{7,6},{8,9},{9,8},{10,11... | collective-permute-start | bytes 2359304 | tf_op jit(solution)/shard_map/ppermute | solution.py:311
  323.9 18.1 %collective-permute-start.62 = (bf16[256,1536]{1,0:T(8,128)(2,1)S(1)}, bf16[256,1536]{1,0:T(8,128)(2,1)S(1)}, u32[]{:S(2)}, u32[]{:S(2)}) collective-permute-start(bf16[256,1536]{1,0:T(8,128)(2,1)S(1)} %slice.148), channel_id=1, source_target_pairs={{0,4},{4,0},{1,5},{5,1},{2,6},{6,2},{3,7},{7,3},{8,12},{12,8},{9,1... | collective-permute-start | bytes 2359304 | tf_op jit(solution)/shard_map/ppermute | solution.py:311
  324.4 18.3 %collective-permute-start.63 = (bf16[512,1536]{1,0:T(8,128)(2,1)}, bf16[512,1536]{1,0:T(8,128)(2,1)S(1)}, u32[]{:S(2)}, u32[]{:S(2)}) collective-permute-start(bf16[512,1536]{1,0:T(8,128)(2,1)} %constant_dynamic-update-slice_fusion.16.refs_0_), channel_id=1, source_target_pairs={{0,2},{2,0},{1,3},{3,1},{4,6},{6,4},{5,7},{7,5},{8,10},{10,8},{9,1... | collective-permute-start | bytes 4718600 | tf_op jit(solution)/shard_map/ppermute | solution.py:311
  324.4 18.4 %collective-permute-start.64 = (bf16[512,1536]{1,0:T(8,128)(2,1)}, bf16[512,1536]{1,0:T(8,128)(2,1)S(1)}, u32[]{:S(2)}, u32[]{:S(2)}) collective-permute-start(bf16[512,1536]{1,0:T(8,128)(2,1)} %collective-permute-done.50.refs_1_), channel_id=1, source_target_pairs={{0,2},{2,0},{1,3},{3,1},{4,6},{6,4},{5,7},{7,5},{8,10},{10,8},{9,1... | collective-permute-start | bytes 4718600 | tf_op jit(solution)/shard_map/ppermute | solution.py:311
  324.9 18.3 %collective-permute-start.65 = (bf16[512,1536]{1,0:T(8,128)(2,1)}, bf16[512,1536]{1,0:T(8,128)(2,1)S(1)}, u32[]{:S(2)}, u32[]{:S(2)}) collective-permute-start(bf16[512,1536]{1,0:T(8,128)(2,1)} %collective-permute-done.51.refs_2_), channel_id=1, source_target_pairs={{0,2},{2,0},{1,3},{3,1},{4,6},{6,4},{5,7},{7,5},{8,10},{10,8},{9,1... | collective-permute-start | bytes 4718600 | tf_op jit(solution)/shard_map/ppermute | solution.py:311
  342.2 18.0 %collective-permute-start.55 = (bf16[256,1536]{1,0:T(8,128)(2,1)}, bf16[256,1536]{1,0:T(8,128)(2,1)S(1)}, u32[]{:S(2)}, u32[]{:S(2)}) collective-permute-start(bf16[256,1536]{1,0:T(8,128)(2,1)} %get-tuple-element.184), channel_id=1, source_target_pairs={{0,2},{2,0},{1,3},{3,1},{4,6},{6,4},{5,7},{7,5},{8,10},{10,8},{9,1... | collective-permute-start | bytes 2359304 | tf_op jit(solution)/shard_map/ppermute | solution.py:311
  342.7 34.7 %collective-permute-start.52 = (bf16[256,1536]{1,0:T(8,128)(2,1)}, bf16[256,1536]{1,0:T(8,128)(2,1)}, u32[]{:S(2)}, u32[]{:S(2)}) collective-permute-start(bf16[256,1536]{1,0:T(8,128)(2,1)} %get-tuple-element.180), channel_id=1, source_target_pairs={{0,2},{2,0},{1,3},{3,1},{4,6},{6,4},{5,7},{7,5},{8,10},{10,8},{9,1... | collective-permute-start | bytes 2359304 | tf_op jit(solution)/shard_map/ppermute | solution.py:311
  342.8 49.1 %collective-permute-start.54 = (bf16[256,1536]{1,0:T(8,128)(2,1)}, bf16[256,1536]{1,0:T(8,128)(2,1)}, u32[]{:S(2)}, u32[]{:S(2)}) collective-permute-start(bf16[256,1536]{1,0:T(8,128)(2,1)} %get-tuple-element.182), channel_id=1, source_target_pairs={{0,2},{2,0},{1,3},{3,1},{4,6},{6,4},{5,7},{7,5},{8,10},{10,8},{9,1... | collective-permute-start | bytes 2359304 | tf_op jit(solution)/shard_map/ppermute | solution.py:311
  364.8 30.8 %collective-permute-start.56 = (bf16[128,1536]{1,0:T(8,128)(2,1)}, bf16[128,1536]{1,0:T(8,128)(2,1)}, u32[]{:S(2)}, u32[]{:S(2)}) collective-permute-start(bf16[128,1536]{1,0:T(8,128)(2,1)} %get-tuple-element.241), channel_id=1, source_target_pairs={{0,1},{1,0},{2,3},{3,2},{4,5},{5,4},{6,7},{7,6},{8,9},{9,8},{10,11... | collective-permute-start | bytes 1179656 | tf_op jit(solution)/shard_map/ppermute | solution.py:311
  366.3 29.3 %collective-permute-start.57 = (bf16[128,1536]{1,0:T(8,128)(2,1)}, bf16[128,1536]{1,0:T(8,128)(2,1)}, u32[]{:S(2)}, u32[]{:S(2)}) collective-permute-start(bf16[128,1536]{1,0:T(8,128)(2,1)} %get-tuple-element.240), channel_id=1, source_target_pairs={{0,4},{4,0},{1,5},{5,1},{2,6},{6,2},{3,7},{7,3},{8,12},{12,8},{9,1... | collective-permute-start | bytes 1179656 | tf_op jit(solution)/shard_map/ppermute | solution.py:311
  379.5 34.3 %collective-permute-start.53 = (bf16[128,1536]{1,0:T(8,128)(2,1)}, bf16[128,1536]{1,0:T(8,128)(2,1)}, u32[]{:S(2)}, u32[]{:S(2)}) collective-permute-start(bf16[128,1536]{1,0:T(8,128)(2,1)} %slice.174), channel_id=1, source_target_pairs={{0,1},{1,0},{2,3},{3,2},{4,5},{5,4},{6,7},{7,6},{8,9},{9,8},{10,11... | collective-permute-start | bytes 1179656 | tf_op jit(solution)/shard_map/ppermute | solution.py:311
  405.2 29.2 %collective-permute-start.70 = (bf16[256,1536]{1,0:T(8,128)(2,1)}, bf16[256,1536]{1,0:T(8,128)(2,1)S(1)}, u32[]{:S(2)}, u32[]{:S(2)}) collective-permute-start(bf16[256,1536]{1,0:T(8,128)(2,1)} %get-tuple-element.228), channel_id=1, source_target_pairs={{0,2},{2,0},{1,3},{3,1},{4,6},{6,4},{5,7},{7,5},{8,10},{10,8},{9,1... | collective-permute-start | bytes 2359304 | tf_op jit(solution)/shard_map/ppermute | solution.py:311
  405.2 25.0 %collective-permute-start.68 = (bf16[128,1536]{1,0:T(8,128)(2,1)S(1)}, bf16[128,1536]{1,0:T(8,128)(2,1)}, u32[]{:S(2)}, u32[]{:S(2)}) collective-permute-start(bf16[128,1536]{1,0:T(8,128)(2,1)S(1)} %slice.182), channel_id=1, source_target_pairs={{0,4},{4,0},{1,5},{5,1},{2,6},{6,2},{3,7},{7,3},{8,12},{12,8},{9,1... | collective-permute-start | bytes 1179656 | tf_op jit(solution)/shard_map/ppermute | solution.py:311
  408.4 27.5 %all-to-all-start.4 = ((bf16[8,112,448]{2,1,0:T(8,128)(2,1)}), bf16[8,112,448]{2,1,0:T(8,128)(2,1)S(1)}, u32[]{:S(2)}, u32[]{:S(2)}) async-start(bf16[8,112,448]{2,1,0:T(8,128)(2,1)} %maximum_maximum_fusion), calls=%async_computation.8 | async-start | bytes 1835008 | tf_op jit(solution)/shard_map/all_to_all | solution.py:61
  411.9 21.4 %collective-permute-start.69 = (bf16[128,1536]{1,0:T(8,128)(2,1)S(1)}, bf16[128,1536]{1,0:T(8,128)(2,1)S(1)}, u32[]{:S(2)}, u32[]{:S(2)}) collective-permute-start(bf16[128,1536]{1,0:T(8,128)(2,1)S(1)} %reduce-precision_convert_fusion.9), channel_id=1, source_target_pairs={{0,1},{1,0},{2,3},{3,2},{4,5},{5,4},{6,7},{7,6},{8,9},{9,8},{10,11... | collective-permute-start | bytes 1179656 | tf_op jit(solution)/shard_map/ppermute | solution.py:311
  (112 other events, 1259.6 us)
Sparse Core Ops, SparseCore 0:
  203.8 49.6 reduce-scatter.4
  260.5 49.7 reduce-scatter.6
  312.6 47.5 reduce-scatter.8
  362.3 35.7 reduce-scatter.10

commit v8 on v6

--- a/solution.py
+++ b/solution.py
@@ -1050,11 +1050,6 @@
     last, up_grad = lax.optimization_barrier(
         (corner_last(mixed[1], mixed[2], first)[:2], placed(up_sum))
     )
-    mixture = jnp.concatenate(
-        [left.astype(f32) + right.astype(f32) for left, right in zip(early, last)], axis=0
-    )
-    block_out = (resid + (mixture + mixed[0].astype(f32))).astype(bf16)
-
     wide_sum = dense_sum[: local_count * shard_rows].reshape(2, 2, 1, shard_rows, dense_cols)
     wide_sum = jnp.broadcast_to(wide_sum, (2, 2, owners, shard_rows, dense_cols)).reshape(
         plane, shard_rows, dense_cols
@@ -1064,6 +1059,12 @@
     pad_rows = -(shard_rows + narrow_rows) % 16
     padding = jnp.zeros((plane, pad_rows, dense_cols), bf16)
     dense_sum = exchange(jnp.concatenate([wide_sum, narrow_sum, padding], axis=1), PLANE)
+    dense_sum, early, last = lax.optimization_barrier((dense_sum, early, last))
+    mixture = jnp.concatenate(
+        [left.astype(f32) + right.astype(f32) for left, right in zip(early, last)], axis=0
+    )
+    block_out = (resid + (mixture + mixed[0].astype(f32))).astype(bf16)
+
     query_grad, key_grad, value_grad, output_grad = run_kernel(
         finish_kernel,
         2,

time: 454 us -> 466 us (1.026)
  waiting for transfers between devices: 167 us -> 177 us
    ppermute x65, waiting for transfers between devices: 114 us -> 129 us  [swap(): return lax.ppermute(block, axis, [(0, 1), (1, 0)])]
    all_to_all x5, waiting for transfers between devices: 33.8 us -> 27.9 us  [exchange(): return lax.all_to_all(block, axes, split_axis=0, concat_axis=0, tiled=True)]
    unnamed x172 -> x176, local copies, waits for them, and re-layouts: 31.1 us -> 32.4 us
  transfers between devices with their start and end apart: 80 -> 80, of which waited for: 34 -> 31; matrix products, arithmetic and copies ran while one was open for 13% -> 12% of each run, Pallas kernels for 23% -> 23%
where the time goes in v8:
time: 466 us; the launch traced here: 457 us
  waiting for transfers between devices  177 us (38%)
  Pallas kernels  106 us (23%)
  starting transfers between devices  70.3 us (15%)
  local copies, waits for them, and re-layouts  63.4 us (14%)
  other arithmetic  25 us (5%)
  between operations  15.9 us (3%)
    ppermute x65, waiting for transfers between devices, swap(): return lax.ppermute(block, axis, [(0, 1), (1, 0)])  129 us
    pallas_call x11, Pallas kernels, run_kernel(): pl.pallas_call(kernel, out_shape=[jax.ShapeDtypeStruct(shape, dtype) for...  98.4 us
    ppermute x65, starting transfers between devices, swap(): return lax.ppermute(block, axis, [(0, 1), (1, 0)])  42.1 us
    unnamed x176, local copies, waits for them, and re-layouts  32.4 us
    all_to_all x5, waiting for transfers between devices, exchange(): return lax.all_to_all(block, axes, split_axis=0, concat_axis=0, tiled=True)  27.9 us
    all_to_all x5, starting transfers between devices, exchange(): return lax.all_to_all(block, axes, split_axis=0, concat_axis=0, tiled=True)  17.6 us
    ppermute x6, waiting for transfers between devices, shifts(): lax.ppermute(block, 'z', [(i, (i + k) % depth) for i in range(depth)])  15.4 us
    ppermute x6, starting transfers between devices, shifts(): lax.ppermute(block, 'z', [(i, (i + k) % depth) for i in range(depth)])  10.1 us
  transfers between devices with their start and end apart: 80, of which 31 were waited for; matrix products, arithmetic and copies ran while one was open for 12% of the time, Pallas kernels for 23%

profile of v8, /device:TPU:0, one launch (start us, length us, event | category | flops | bytes accessed | tf_op | source)
XLA Modules:
  0.0 457.4 jit_solution(4695983085025087149)
XLA Ops:
  8.1 5.1 %collective-permute-start = (bf16[96,128]{1,0:T(8,128)(2,1)S(1)}, bf16[96,128]{1,0:T(8,128)(2,1)S(1)}, u32[]{:S(2)}, u32[]{:S(2)}) collective-permute-start(bf16[96,128]{1,0:T(8,128)(2,1)S(1)} %pad.9), channel_id=1, source_target_pairs={{0,24},{8,0},{16,8},{24,16},{1,25},{9,1},{17,9},{25,17},{2,26},{10... | collective-permute-start | bytes 73736 | tf_op jit(solution)/shard_map/ppermute | solution.py:317
  18.3 2.8 collective-permute-start.14
  26.8 2.7 collective-permute-done.3
  36.0 15.4 %collective-permute-done.13 = bf16[96,1792]{1,0:T(8,128)(2,1)} collective-permute-done((bf16[96,1792]{1,0:T(8,128)(2,1)}, bf16[96,1792]{1,0:T(8,128)(2,1)}, u32[]{:S(2)}, u32[]{:S(2)}) %collective-permute-start.13) | collective-permute-done | bytes 344096 | tf_op jit(solution)/shard_map/ppermute | solution.py:317
  61.0 3.2 dynamic-slice_bitcast_fusion.2.refs_4_.refs_8_
  64.3 3.2 dynamic-slice_bitcast_fusion.1.refs_5_.refs_9_
  69.3 7.3 %collective-permute-done.16.refs_2_ = bf16[4,96,1024]{2,1,0:T(8,128)(2,1)} collective-permute-done((bf16[4,96,1024]{2,1,0:T(8,128)(2,1)S(1)}, bf16[4,96,1024]{2,1,0:T(8,128)(2,1)}, u32[]{:S(2)}, u32[]{:S(2)}) %collective-permute-start.16) | collective-permute-done | bytes 786464 | tf_op jit(solution)/shard_map/ppermute | solution.py:311
  82.2 4.2 collective-permute-done.17
  96.6 9.1 %shard_map.229 = (bf16[256,1536]{1,0:T(8,128)(2,1)S(1)}, bf16[256,1536]{1,0:T(8,128)(2,1)S(1)}, bf16[256,256]{1,0:T(8,128)(2,1)S(1)}, bf16[256,256]{1,0:T(8,128)...) custom-call(s32[7]{0:T(128)S(1)} %copy-done.36, ...), custom_call_target="tpu_custom_call" | custom-call | flops 11000000512 | bytes 11000000 | tf_op jit(solution)/shard_map/pallas_call | solution.py:400
  105.8 2.7 copy-done.45
  114.0 5.7 %collective-permute-done.25 = bf16[2,96,768]{2,1,0:T(8,128)(2,1)S(1)} collective-permute-done((bf16[2,96,768]{2,1,0:T(8,128)(2,1)S(1)}, bf16[2,96,768]{2,1,0:T(8,128)(2,1)S(1)}, u32[]{:S(2)}, u32[]{:S(2)}) %collective-permute-start.25) | collective-permute-done | bytes 294944 | tf_op jit(solution)/shard_map/ppermute | solution.py:311
  121.4 5.7 %collective-permute-done.10 = bf16[128,1536]{1,0:T(8,128)(2,1)S(1)} collective-permute-done((bf16[128,1536]{1,0:T(8,128)(2,1)S(1)}, bf16[128,1536]{1,0:T(8,128)(2,1)S(1)}, u32[]{:S(2)}, u32[]{:S(2)}) %collective-permute-start.10) | collective-permute-done | bytes 393248 | tf_op jit(solution)/shard_map/ppermute | solution.py:311
  130.0 4.1 shard_map.230
  138.0 10.2 %shard_map.231 = (bf16[384,1536]{1,0:T(8,128)(2,1)S(1)}, bf16[384,1536]{1,0:T(8,128)(2,1)S(1)}, bf16[384,768]{1,0:T(8,128)(2,1)S(1)}, bf16[384,768]{1,0:T(8,128)...) custom-call(s32[7]{0:T(128)S(1)} %copy-done.37, ...), custom_call_target="tpu_custom_call" | custom-call | flops 8000000000 | bytes 8000000 | tf_op jit(solution)/shard_map/pallas_call | solution.py:400
  149.9 5.6 %collective-permute-done.34.refs_0_ = bf16[256,1536]{1,0:T(8,128)(2,1)S(1)} collective-permute-done((bf16[256,1536]{1,0:T(8,128)(2,1)}, bf16[256,1536]{1,0:T(8,128)(2,1)S(1)}, u32[]{:S(2)}, u32[]{:S(2)}) %collective-permute-start.34) | collective-permute-done | bytes 786464 | tf_op jit(solution)/shard_map/ppermute | solution.py:311
  158.4 2.1 collective-permute-done.37.refs_3_
  160.5 17.5 %shard_map.232 = (bf16[768,1536]{1,0:T(8,128)(2,1)S(1)}, bf16[768,1536]{1,0:T(8,128)(2,1)S(1)}, bf16[768,768]{1,0:T(8,128)(2,1)S(1)}, bf16[768,768]{1,0:T(8,128)...) custom-call(s32[7]{0:T(128)S(1)} %copy-done.37, ...), custom_call_target="tpu_custom_call" | custom-call | flops 16000000000 | bytes 16000000 | tf_op jit(solution)/shard_map/pallas_call | solution.py:400
  183.8 13.0 %shard_map.233 = (bf16[384,1536]{1,0:T(8,128)(2,1)S(1)}, bf16[384,1536]{1,0:T(8,128)(2,1)}, bf16[384,768]{1,0:T(8,128)(2,1)S(1)}, bf16[384,768]{1,0:T(8,128)(2,1...) custom-call(s32[7]{0:T(128)S(1)} %copy-done.37, ...), custom_call_target="tpu_custom_call" | custom-call | flops 8000000000 | bytes 8000000 | tf_op jit(solution)/shard_map/pallas_call | solution.py:400
  210.2 16.4 %collective-permute-done.49 = bf16[128,1664]{1,0:T(8,128)(2,1)S(1)} collective-permute-done((bf16[128,1664]{1,0:T(8,128)(2,1)S(1)}, bf16[128,1664]{1,0:T(8,128)(2,1)S(1)}, u32[]{:S(2)}, u32[]{:S(2)}) %collective-permute-start.49) | collective-permute-done | bytes 426016 | tf_op jit(solution)/shard_map/ppermute | solution.py:311
  230.5 7.8 %collective-permute-done.50.last_y = bf16[128,1664]{1,0:T(8,128)(2,1)S(1)} collective-permute-done((bf16[128,1664]{1,0:T(8,128)(2,1)S(1)}, bf16[128,1664]{1,0:T(8,128)(2,1)S(1)}, u32[]{:S(2)}, u32[]{:S(2)}) %collective-permute-start.50) | collective-permute-done | bytes 426016 | tf_op jit(solution)/shard_map/ppermute | solution.py:311
  238.2 2.1 collective-permute-done.52.last_x
  241.1 8.3 %shard_map.234 = (f32[256,1536]{1,0:T(8,128)}, bf16[256,1536]{1,0:T(8,128)(2,1)}, bf16[256,1536]{1,0:T(8,128)(2,1)}, f32[1536,128]{1,0:T(8,128)}, f32[1,1536]{1,0:T(1,128)}) custom-call(s32[7]{0:T(128)} %stack.76.at, bf16[256,1664]{1,0:T(8,128)(2,1)} %copy-done.48, bf16[256,1664]{1,0:T(8,128)(2,1)} %collective-permute-done.33.far, ...), custom_call_target="tpu_custom_call" | custom-call | flops 6000000000 | bytes 6000000 | tf_op jit(solution)/shard_map/pallas_call | solution.py:400
  249.4 12.8 %shard_map.235 = (bf16[1536,768]{1,0:T(8,128)(2,1)}, bf16[1536,768]{1,0:T(8,128)(2,1)}) custom-call(s32[7]{0:T(128)} %stack.76.at, bf16[384,1536]{1,0:T(8,128)(2,1)} %copy-done.53, bf16[768,1536]{1,0:T(8,128)(2,1)} %copy-done.52, bf16[384,1536]{1,0:T(8,128)(2,1)} %copy-done.51, bf16[384,768]{1,0:T(8,128)(2,1)} %copy-done.61, bf16[768,768]{1,0:T(8,128)(2,1)} %copy-done.59, ...), custom_call_target="tpu_custom_call" | custom-call | flops 8000000000 | bytes 8000000 | tf_op jit(solution)/shard_map/pallas_call | solution.py:400
  266.9 8.5 %shard_map.236.back = bf16[8,272,448]{2,1,0:T(8,128)(2,1)} custom-call(s32[7]{0:T(128)} %stack.76.at, bf16[256,1536]{1,0:T(8,128)(2,1)} %get-tuple-element.185.attended, bf16[12,256,256]{2,1,0:T(8,128)(2,1)} %copy-done.49, bf16[256,1536]{1,0:T(8,128)(2,1)} %copy-done.54, bf16[256,256]{1,0:T(8,128)(2,1)} %copy-done.64, bf16[256,256]{1,0:T(8,128)(2,1)} %copy-done.65, ...), custom_call_target="tpu_custom_call" | custom-call | flops 6000000000 | bytes 6000000 | tf_op jit(solution)/shard_map/pallas_call | solution.py:400
  277.0 2.8 copy-done.46
  279.8 3.8 shard_map.237
  286.2 3.6 all-to-all-start
  290.6 12.3 %collective-permute-done.53.refs_1_ = bf16[512,1536]{1,0:T(8,128)(2,1)} collective-permute-done((bf16[512,1536]{1,0:T(8,128)(2,1)}, bf16[512,1536]{1,0:T(8,128)(2,1)}, u32[]{:S(2)}, u32[]{:S(2)}) %collective-permute-start.53) | collective-permute-done | bytes 1572896 | tf_op jit(solution)/shard_map/ppermute | solution.py:311
  304.4 9.4 %shard_map.238 = (bf16[256,1536]{1,0:T(8,128)(2,1)}, bf16[256,1536]{1,0:T(8,128)(2,1)}, bf16[256,1536]{1,0:T(8,128)(2,1)}, bf16[256,1536]{1,0:T(8,128)(2,1)}, bf...) custom-call(s32[7]{0:T(128)} %stack.76.at, ...), custom_call_target="tpu_custom_call" | custom-call | flops 10000000000 | bytes 10000000 | tf_op jit(solution)/shard_map/pallas_call | solution.py:400
  313.8 2.1 slice.143
  317.0 7.9 %all-to-all-done.back = bf16[8,272,448]{2,1,0:T(8,128)(2,1)S(1)} async-done(((bf16[8,272,448]{2,1,0:T(8,128)(2,1)}), bf16[8,272,448]{2,1,0:T(8,128)(2,1)S(1)}, u32[]{:S(2)}, u32[]{:S(2)}) %all-to-all-start) | async-done | bytes 1949728 | tf_op jit(solution)/shard_map/all_to_all | solution.py:61
  326.9 17.2 %collective-permute-done.55 = bf16[256,1536]{1,0:T(8,128)(2,1)S(1)} collective-permute-done((bf16[256,1536]{1,0:T(8,128)(2,1)}, bf16[256,1536]{1,0:T(8,128)(2,1)S(1)}, u32[]{:S(2)}, u32[]{:S(2)}) %collective-permute-start.55) | collective-permute-done | bytes 786464 | tf_op jit(solution)/shard_map/ppermute | solution.py:311
  344.8 4.0 collective-permute-done.60.refs_7_
  348.8 7.3 %shard_map.239 = bf16[4,400,448]{2,1,0:T(8,128)(2,1)S(1)} custom-call(s32[7]{0:T(128)S(1)} %copy-done.39, bf16[8,272,448]{2,1,0:T(8,128)(2,1)S(1)} %all-to-all-done.back, bf16[512,1536]{1,0:T(8,128)(2,1)} %constant_dynamic-update-slice_fusion.16.refs_0_, bf16[512,1536]{1,0:T(8,128)(2,1)} %collective-permute-done.53.refs_1_, ...), custom_call_target="tpu_custom_call" | custom-call | flops 8000000000 | bytes 8000000 | tf_op jit(solution)/shard_map/pallas_call | solution.py:1028
  357.3 4.6 reduce-scatter.9.cloned.1.call-done
  366.6 3.5 all-to-all-start.2
  371.5 10.9 %all-to-all-done.2 = bf16[4,96,768]{2,1,0:T(8,128)(2,1)S(1)} async-done(((bf16[4,96,768]{2,1,0:T(8,128)(2,1)}), bf16[4,96,768]{2,1,0:T(8,128)(2,1)S(1)}, u32[]{:S(2)}, u32[]{:S(2)}) %all-to-all-start.2) | async-done | bytes 589856 | tf_op jit(solution)/shard_map/all_to_all | solution.py:61
  382.5 3.5 all-to-all-start.3
  388.4 7.0 %all-to-all-done.3 = bf16[4,96,768]{2,1,0:T(8,128)(2,1)S(1)} async-done(((bf16[4,96,768]{2,1,0:T(8,128)(2,1)}), bf16[4,96,768]{2,1,0:T(8,128)(2,1)S(1)}, u32[]{:S(2)}, u32[]{:S(2)}) %all-to-all-start.3) | async-done | bytes 589856 | tf_op jit(solution)/shard_map/all_to_all | solution.py:61
  395.5 3.5 all-to-all-start.4
  401.9 2.0 collective-permute-start.68
  406.9 2.0 all-to-all-done.4
  408.9 3.6 all-to-all-start.1
  414.3 1.9 collective-permute-start.69
  416.5 1.9 collective-permute-start.64
  419.5 15.0 %collective-permute-done.69 = bf16[128,1536]{1,0:T(8,128)(2,1)} collective-permute-done((bf16[128,1536]{1,0:T(8,128)(2,1)}, bf16[128,1536]{1,0:T(8,128)(2,1)}, u32[]{:S(2)}, u32[]{:S(2)}) %collective-permute-start.69) | collective-permute-done | bytes 393248 | tf_op jit(solution)/shard_map/ppermute | solution.py:311
  434.5 7.8 %collective-permute-done.62 = bf16[128,1536]{1,0:T(8,128)(2,1)S(1)} collective-permute-done((bf16[128,1536]{1,0:T(8,128)(2,1)S(1)}, bf16[128,1536]{1,0:T(8,128)(2,1)S(1)}, u32[]{:S(2)}, u32[]{:S(2)}) %collective-permute-start.62) | collective-permute-done | bytes 393248 | tf_op jit(solution)/shard_map/ppermute | solution.py:311
  448.2 2.5 fusion.1
  (401 shorter events, 126.0 us)
Async XLA Ops:
  7.2 279.0 %reduce-scatter.5.cloned.1.call-start = ((), (), s32[]{:S(2)}) async-start(), calls=%async_computation.9 | async-start | bytes 2949120 | tf_op jit(solution)/shard_map/reduce_scatter | solution.py:65
  18.3 16.7 %collective-permute-start.14 = (bf16[96,1792]{1,0:T(8,128)(2,1)}, bf16[96,1792]{1,0:T(8,128)(2,1)}, u32[]{:S(2)}, u32[]{:S(2)}) collective-permute-start(bf16[96,1792]{1,0:T(8,128)(2,1)} %pad_maximum_fusion.3), channel_id=1, source_target_pairs={{0,24},{8,0},{16,8},{24,16},{1,25},{9,1},{17,9},{25,17},{2,26},{10... | collective-permute-start | bytes 1032200 | tf_op jit(solution)/shard_map/ppermute | solution.py:317
  21.8 29.5 %collective-permute-start.13 = (bf16[96,1792]{1,0:T(8,128)(2,1)}, bf16[96,1792]{1,0:T(8,128)(2,1)}, u32[]{:S(2)}, u32[]{:S(2)}) collective-permute-start(bf16[96,1792]{1,0:T(8,128)(2,1)} %pad_maximum_fusion.3), channel_id=1, source_target_pairs={{0,16},{8,24},{16,0},{24,8},{1,17},{9,25},{17,1},{25,9},{2,18},{10... | collective-permute-start | bytes 1032200 | tf_op jit(solution)/shard_map/ppermute | solution.py:317
  23.0 29.3 %collective-permute-start.12 = (bf16[96,1792]{1,0:T(8,128)(2,1)}, bf16[96,1792]{1,0:T(8,128)(2,1)}, u32[]{:S(2)}, u32[]{:S(2)}) collective-permute-start(bf16[96,1792]{1,0:T(8,128)(2,1)} %pad_maximum_fusion.3), channel_id=1, source_target_pairs={{0,8},{8,16},{16,24},{24,0},{1,9},{9,17},{17,25},{25,1},{2,10},{10... | collective-permute-start | bytes 1032200 | tf_op jit(solution)/shard_map/ppermute | solution.py:317
  32.3 26.6 %collective-permute-start.8 = (bf16[256,1536]{1,0:T(8,128)(2,1)S(1)}, bf16[256,1536]{1,0:T(8,128)(2,1)S(1)}, u32[]{:S(2)}, u32[]{:S(2)}) collective-permute-start(bf16[256,1536]{1,0:T(8,128)(2,1)S(1)} %copy-done.40), channel_id=1, source_target_pairs={{0,4},{4,0},{1,5},{5,1},{2,6},{6,2},{3,7},{7,3},{8,12},{12,8},{9,1... | collective-permute-start | bytes 2359304 | tf_op jit(solution)/shard_map/ppermute | solution.py:311
  32.8 26.1 %collective-permute-start.9 = (bf16[256,1536]{1,0:T(8,128)(2,1)S(1)}, bf16[256,1536]{1,0:T(8,128)(2,1)S(1)}, u32[]{:S(2)}, u32[]{:S(2)}) collective-permute-start(bf16[256,1536]{1,0:T(8,128)(2,1)S(1)} %copy-done.40), channel_id=1, source_target_pairs={{0,1},{1,0},{2,3},{3,2},{4,5},{5,4},{6,7},{7,6},{8,9},{9,8},{10,11... | collective-permute-start | bytes 2359304 | tf_op jit(solution)/shard_map/ppermute | solution.py:311
  58.9 18.7 %collective-permute-start.15 = (bf16[4,96,1024]{2,1,0:T(8,128)(2,1)S(1)}, bf16[4,96,1024]{2,1,0:T(8,128)(2,1)}, u32[]{:S(2)}, u32[]{:S(2)}) collective-permute-start(bf16[4,96,1024]{2,1,0:T(8,128)(2,1)S(1)} %pad_maximum_fusion.refs_0_), channel_id=1, source_target_pairs={{0,1},{1,0},{2,3},{3,2},{4,5},{5,4},{6,7},{7,6},{8,9},{9,8},{10,11... | collective-permute-start | bytes 2359304 | tf_op jit(solution)/shard_map/ppermute | solution.py:311
  59.5 17.1 %collective-permute-start.16 = (bf16[4,96,1024]{2,1,0:T(8,128)(2,1)S(1)}, bf16[4,96,1024]{2,1,0:T(8,128)(2,1)}, u32[]{:S(2)}, u32[]{:S(2)}) collective-permute-start(bf16[4,96,1024]{2,1,0:T(8,128)(2,1)S(1)} %pad_maximum_fusion.refs_0_), channel_id=1, source_target_pairs={{0,4},{4,0},{1,5},{5,1},{2,6},{6,2},{3,7},{7,3},{8,12},{12,8},{9,1... | collective-permute-start | bytes 2359304 | tf_op jit(solution)/shard_map/ppermute | solution.py:311
  91.6 18.1 %collective-permute-start.23 = (bf16[4,96,768]{2,1,0:T(8,128)(2,1)}, bf16[4,96,768]{2,1,0:T(8,128)(2,1)S(1)}, u32[]{:S(2)}, u32[]{:S(2)}) collective-permute-start(bf16[4,96,768]{2,1,0:T(8,128)(2,1)} %pad_maximum_fusion.1.refs_0_), channel_id=1, source_target_pairs={{0,1},{1,0},{2,3},{3,2},{4,5},{5,4},{6,7},{7,6},{8,9},{9,8},{10,11... | collective-permute-start | bytes 1769480 | tf_op jit(solution)/shard_map/ppermute | solution.py:311
  92.2 17.5 %collective-permute-start.24 = (bf16[4,96,768]{2,1,0:T(8,128)(2,1)}, bf16[4,96,768]{2,1,0:T(8,128)(2,1)S(1)}, u32[]{:S(2)}, u32[]{:S(2)}) collective-permute-start(bf16[4,96,768]{2,1,0:T(8,128)(2,1)} %pad_maximum_fusion.1.refs_0_), channel_id=1, source_target_pairs={{0,4},{4,0},{1,5},{5,1},{2,6},{6,2},{3,7},{7,3},{8,12},{12,8},{9,1... | collective-permute-start | bytes 1769480 | tf_op jit(solution)/shard_map/ppermute | solution.py:311
  111.9 15.2 %collective-permute-start.10 = (bf16[128,1536]{1,0:T(8,128)(2,1)S(1)}, bf16[128,1536]{1,0:T(8,128)(2,1)S(1)}, u32[]{:S(2)}, u32[]{:S(2)}) collective-permute-start(bf16[128,1536]{1,0:T(8,128)(2,1)S(1)} %slice.159), channel_id=1, source_target_pairs={{0,1},{1,0},{2,3},{3,2},{4,5},{5,4},{6,7},{7,6},{8,9},{9,8},{10,11... | collective-permute-start | bytes 1179656 | tf_op jit(solution)/shard_map/ppermute | solution.py:311
  112.9 15.4 %collective-permute-start.11 = (bf16[128,1536]{1,0:T(8,128)(2,1)S(1)}, bf16[128,1536]{1,0:T(8,128)(2,1)S(1)}, u32[]{:S(2)}, u32[]{:S(2)}) collective-permute-start(bf16[128,1536]{1,0:T(8,128)(2,1)S(1)} %slice.160), channel_id=1, source_target_pairs={{0,4},{4,0},{1,5},{5,1},{2,6},{6,2},{3,7},{7,3},{8,12},{12,8},{9,1... | collective-permute-start | bytes 1179656 | tf_op jit(solution)/shard_map/ppermute | solution.py:311
  114.0 15.9 %collective-permute-start.27 = (bf16[4,96,768]{2,1,0:T(8,128)(2,1)S(1)}, bf16[4,96,768]{2,1,0:T(8,128)(2,1)S(1)}, u32[]{:S(2)}, u32[]{:S(2)}) collective-permute-start(bf16[4,96,768]{2,1,0:T(8,128)(2,1)S(1)} %copy-done.19), channel_id=1, source_target_pairs={{0,2},{2,0},{1,3},{3,1},{4,6},{6,4},{5,7},{7,5},{8,10},{10,8},{9,1... | collective-permute-start | bytes 1769480 | tf_op jit(solution)/shard_map/ppermute | solution.py:311
  135.8 19.7 %collective-permute-start.34 = (bf16[256,1536]{1,0:T(8,128)(2,1)}, bf16[256,1536]{1,0:T(8,128)(2,1)S(1)}, u32[]{:S(2)}, u32[]{:S(2)}) collective-permute-start(bf16[256,1536]{1,0:T(8,128)(2,1)} %get-tuple-element.151.refs_0_.second), channel_id=1, source_target_pairs={{0,1},{1,0},{2,3},{3,2},{4,5},{5,4},{6,7},{7,6},{8,9},{9,8},{10,11... | collective-permute-start | bytes 2359304 | tf_op jit(solution)/shard_map/ppermute | solution.py:311
  136.4 19.6 %collective-permute-start.35 = (bf16[256,1536]{1,0:T(8,128)(2,1)}, bf16[256,1536]{1,0:T(8,128)(2,1)S(1)}, u32[]{:S(2)}, u32[]{:S(2)}) collective-permute-start(bf16[256,1536]{1,0:T(8,128)(2,1)} %get-tuple-element.151.refs_0_.second), channel_id=1, source_target_pairs={{0,4},{4,0},{1,5},{5,1},{2,6},{6,2},{3,7},{7,3},{8,12},{12,8},{9,1... | collective-permute-start | bytes 2359304 | tf_op jit(solution)/shard_map/ppermute | solution.py:311
  136.9 19.7 %collective-permute-start.38 = (bf16[256,1536]{1,0:T(8,128)(2,1)S(1)}, bf16[256,1536]{1,0:T(8,128)(2,1)S(1)}, u32[]{:S(2)}, u32[]{:S(2)}) collective-permute-start(bf16[256,1536]{1,0:T(8,128)(2,1)S(1)} %copy-done.25), channel_id=1, source_target_pairs={{0,2},{2,0},{1,3},{3,1},{4,6},{6,4},{5,7},{7,5},{8,10},{10,8},{9,1... | collective-permute-start | bytes 2359304 | tf_op jit(solution)/shard_map/ppermute | solution.py:311
  136.9 21.0 %collective-permute-start.39 = (bf16[256,1536]{1,0:T(8,128)(2,1)S(1)}, bf16[256,1536]{1,0:T(8,128)(2,1)S(1)}, u32[]{:S(2)}, u32[]{:S(2)}) collective-permute-start(bf16[256,1536]{1,0:T(8,128)(2,1)S(1)} %copy-done.22), channel_id=1, source_target_pairs={{0,2},{2,0},{1,3},{3,1},{4,6},{6,4},{5,7},{7,5},{8,10},{10,8},{9,1... | collective-permute-start | bytes 2359304 | tf_op jit(solution)/shard_map/ppermute | solution.py:311
  156.5 25.5 %collective-permute-start.47 = (bf16[256,1536]{1,0:T(8,128)(2,1)}, bf16[256,1536]{1,0:T(8,128)(2,1)S(1)}, u32[]{:S(2)}, u32[]{:S(2)}) collective-permute-start(bf16[256,1536]{1,0:T(8,128)(2,1)} %constant_dynamic-update-slice_fusion.8.refs_2_), channel_id=1, source_target_pairs={{0,2},{2,0},{1,3},{3,1},{4,6},{6,4},{5,7},{7,5},{8,10},{10,8},{9,1... | collective-permute-start | bytes 2359304 | tf_op jit(solution)/shard_map/ppermute | solution.py:311
  156.6 24.8 %collective-permute-start.44 = (bf16[128,1536]{1,0:T(8,128)(2,1)S(1)}, bf16[128,1536]{1,0:T(8,128)(2,1)S(1)}, u32[]{:S(2)}, u32[]{:S(2)}) collective-permute-start(bf16[128,1536]{1,0:T(8,128)(2,1)S(1)} %slice.137), channel_id=1, source_target_pairs={{0,1},{1,0},{2,3},{3,2},{4,5},{5,4},{6,7},{7,6},{8,9},{9,8},{10,11... | collective-permute-start | bytes 1179656 | tf_op jit(solution)/shard_map/ppermute | solution.py:311
  157.9 23.5 %collective-permute-start.45 = (bf16[128,1536]{1,0:T(8,128)(2,1)S(1)}, bf16[128,1536]{1,0:T(8,128)(2,1)S(1)}, u32[]{:S(2)}, u32[]{:S(2)}) collective-permute-start(bf16[128,1536]{1,0:T(8,128)(2,1)S(1)} %slice.138), channel_id=1, source_target_pairs={{0,4},{4,0},{1,5},{5,1},{2,6},{6,2},{3,7},{7,3},{8,12},{12,8},{9,1... | collective-permute-start | bytes 1179656 | tf_op jit(solution)/shard_map/ppermute | solution.py:311
  181.7 22.1 %collective-permute-start.40 = (bf16[256,1664]{1,0:T(8,128)(2,1)}, bf16[256,1664]{1,0:T(8,128)(2,1)}, u32[]{:S(2)}, u32[]{:S(2)}) collective-permute-start(bf16[256,1664]{1,0:T(8,128)(2,1)} %get-tuple-element.158), channel_id=1, source_target_pairs={{0,2},{2,0},{1,3},{3,1},{4,6},{6,4},{5,7},{7,5},{8,10},{10,8},{9,1... | collective-permute-start | bytes 2555912 | tf_op jit(solution)/shard_map/ppermute | solution.py:311
  202.8 27.6 %collective-permute-start.33 = (bf16[256,1664]{1,0:T(8,128)(2,1)}, bf16[256,1664]{1,0:T(8,128)(2,1)}, u32[]{:S(2)}, u32[]{:S(2)}) collective-permute-start(bf16[256,1664]{1,0:T(8,128)(2,1)} %get-tuple-element.153), channel_id=1, source_target_pairs={{0,2},{2,0},{1,3},{3,1},{4,6},{6,4},{5,7},{7,5},{8,10},{10,8},{9,1... | collective-permute-start | bytes 2555912 | tf_op jit(solution)/shard_map/ppermute | solution.py:311
  203.3 154.0 %reduce-scatter.7.cloned.1.call-start = ((), (), s32[]{:S(2)}) async-start(), calls=%async_computation.10 | async-start | bytes 2949120 | tf_op jit(solution)/shard_map/reduce_scatter | solution.py:65
  205.3 25.1 %collective-permute-start.41 = (bf16[128,1664]{1,0:T(8,128)(2,1)S(1)}, bf16[128,1664]{1,0:T(8,128)(2,1)S(1)}, u32[]{:S(2)}, u32[]{:S(2)}) collective-permute-start(bf16[128,1664]{1,0:T(8,128)(2,1)S(1)} %slice.170), channel_id=1, source_target_pairs={{0,1},{1,0},{2,3},{3,2},{4,5},{5,4},{6,7},{7,6},{8,9},{9,8},{10,11... | collective-permute-start | bytes 1277960 | tf_op jit(solution)/shard_map/ppermute | solution.py:311
  207.0 19.7 %collective-permute-start.49 = (bf16[128,1664]{1,0:T(8,128)(2,1)S(1)}, bf16[128,1664]{1,0:T(8,128)(2,1)S(1)}, u32[]{:S(2)}, u32[]{:S(2)}) collective-permute-start(bf16[128,1664]{1,0:T(8,128)(2,1)S(1)} %get-tuple-element.247), channel_id=1, source_target_pairs={{0,1},{1,0},{2,3},{3,2},{4,5},{5,4},{6,7},{7,6},{8,9},{9,8},{10,11... | collective-permute-start | bytes 1277960 | tf_op jit(solution)/shard_map/ppermute | solution.py:311
  208.1 22.3 %collective-permute-start.43 = (bf16[128,1664]{1,0:T(8,128)(2,1)S(1)}, bf16[128,1664]{1,0:T(8,128)(2,1)S(1)}, u32[]{:S(2)}, u32[]{:S(2)}) collective-permute-start(bf16[128,1664]{1,0:T(8,128)(2,1)S(1)} %slice.171), channel_id=1, source_target_pairs={{0,4},{4,0},{1,5},{5,1},{2,6},{6,2},{3,7},{7,3},{8,12},{12,8},{9,1... | collective-permute-start | bytes 1277960 | tf_op jit(solution)/shard_map/ppermute | solution.py:311
  208.7 20.4 %collective-permute-start.51 = (bf16[128,1664]{1,0:T(8,128)(2,1)S(1)}, bf16[128,1664]{1,0:T(8,128)(2,1)S(1)}, u32[]{:S(2)}, u32[]{:S(2)}) collective-permute-start(bf16[128,1664]{1,0:T(8,128)(2,1)S(1)} %get-tuple-element.246), channel_id=1, source_target_pairs={{0,4},{4,0},{1,5},{5,1},{2,6},{6,2},{3,7},{7,3},{8,12},{12,8},{9,1... | collective-permute-start | bytes 1277960 | tf_op jit(solution)/shard_map/ppermute | solution.py:311
  265.3 37.6 %collective-permute-start.53 = (bf16[512,1536]{1,0:T(8,128)(2,1)}, bf16[512,1536]{1,0:T(8,128)(2,1)}, u32[]{:S(2)}, u32[]{:S(2)}) collective-permute-start(bf16[512,1536]{1,0:T(8,128)(2,1)} %constant_dynamic-update-slice_fusion.16.refs_0_), channel_id=1, source_target_pairs={{0,1},{1,0},{2,3},{3,2},{4,5},{5,4},{6,7},{7,6},{8,9},{9,8},{10,11... | collective-permute-start | bytes 4718600 | tf_op jit(solution)/shard_map/ppermute | solution.py:311
  266.4 38.0 %collective-permute-start.54 = (bf16[512,1536]{1,0:T(8,128)(2,1)}, bf16[512,1536]{1,0:T(8,128)(2,1)}, u32[]{:S(2)}, u32[]{:S(2)}) collective-permute-start(bf16[512,1536]{1,0:T(8,128)(2,1)} %constant_dynamic-update-slice_fusion.16.refs_0_), channel_id=1, source_target_pairs={{0,4},{4,0},{1,5},{5,1},{2,6},{6,2},{3,7},{7,3},{8,12},{12,8},{9,1... | collective-permute-start | bytes 4718600 | tf_op jit(solution)/shard_map/ppermute | solution.py:311
  286.2 38.7 %all-to-all-start = ((bf16[8,272,448]{2,1,0:T(8,128)(2,1)}), bf16[8,272,448]{2,1,0:T(8,128)(2,1)S(1)}, u32[]{:S(2)}, u32[]{:S(2)}) async-start(bf16[8,272,448]{2,1,0:T(8,128)(2,1)} %constant_dynamic-update-slice_fusion.20), calls=%async_computation.1 | async-start | bytes 4456448 | tf_op jit(solution)/shard_map/all_to_all | solution.py:61
  289.8 72.0 %reduce-scatter.9.cloned.1.call-start = ((), (), s32[]{:S(2)}) async-start(), calls=%async_computation.11 | async-start | bytes 2949120 | tf_op jit(solution)/shard_map/reduce_scatter | solution.py:65
  290.6 113.3 %reduce-scatter.11.cloned.1.call-start = ((), (), s32[]{:S(2)}) async-start(), calls=%async_computation.12 | async-start | bytes 2048000 | tf_op jit(solution)/shard_map/reduce_scatter | solution.py:65
  324.9 19.2 %collective-permute-start.55 = (bf16[256,1536]{1,0:T(8,128)(2,1)}, bf16[256,1536]{1,0:T(8,128)(2,1)S(1)}, u32[]{:S(2)}, u32[]{:S(2)}) collective-permute-start(bf16[256,1536]{1,0:T(8,128)(2,1)} %slice.143), channel_id=1, source_target_pairs={{0,1},{1,0},{2,3},{3,2},{4,5},{5,4},{6,7},{7,6},{8,9},{9,8},{10,11... | collective-permute-start | bytes 2359304 | tf_op jit(solution)/shard_map/ppermute | solution.py:311
  325.9 18.2 %collective-permute-start.56 = (bf16[256,1536]{1,0:T(8,128)(2,1)S(1)}, bf16[256,1536]{1,0:T(8,128)(2,1)S(1)}, u32[]{:S(2)}, u32[]{:S(2)}) collective-permute-start(bf16[256,1536]{1,0:T(8,128)(2,1)S(1)} %slice.144), channel_id=1, source_target_pairs={{0,4},{4,0},{1,5},{5,1},{2,6},{6,2},{3,7},{7,3},{8,12},{12,8},{9,1... | collective-permute-start | bytes 2359304 | tf_op jit(solution)/shard_map/ppermute | solution.py:311
  326.4 18.4 %collective-permute-start.57 = (bf16[512,1536]{1,0:T(8,128)(2,1)}, bf16[512,1536]{1,0:T(8,128)(2,1)S(1)}, u32[]{:S(2)}, u32[]{:S(2)}) collective-permute-start(bf16[512,1536]{1,0:T(8,128)(2,1)} %constant_dynamic-update-slice_fusion.16.refs_0_), channel_id=1, source_target_pairs={{0,2},{2,0},{1,3},{3,1},{4,6},{6,4},{5,7},{7,5},{8,10},{10,8},{9,1... | collective-permute-start | bytes 4718600 | tf_op jit(solution)/shard_map/ppermute | solution.py:311
  326.4 18.4 %collective-permute-start.58 = (bf16[512,1536]{1,0:T(8,128)(2,1)}, bf16[512,1536]{1,0:T(8,128)(2,1)S(1)}, u32[]{:S(2)}, u32[]{:S(2)}) collective-permute-start(bf16[512,1536]{1,0:T(8,128)(2,1)} %collective-permute-done.53.refs_1_), channel_id=1, source_target_pairs={{0,2},{2,0},{1,3},{3,1},{4,6},{6,4},{5,7},{7,5},{8,10},{10,8},{9,1... | collective-permute-start | bytes 4718600 | tf_op jit(solution)/shard_map/ppermute | solution.py:311
  326.9 17.9 %collective-permute-start.59 = (bf16[512,1536]{1,0:T(8,128)(2,1)}, bf16[512,1536]{1,0:T(8,128)(2,1)S(1)}, u32[]{:S(2)}, u32[]{:S(2)}) collective-permute-start(bf16[512,1536]{1,0:T(8,128)(2,1)} %collective-permute-done.54.refs_2_), channel_id=1, source_target_pairs={{0,2},{2,0},{1,3},{3,1},{4,6},{6,4},{5,7},{7,5},{8,10},{10,8},{9,1... | collective-permute-start | bytes 4718600 | tf_op jit(solution)/shard_map/ppermute | solution.py:311
  344.3 18.2 %collective-permute-start.65 = (bf16[256,1536]{1,0:T(8,128)(2,1)}, bf16[256,1536]{1,0:T(8,128)(2,1)S(1)}, u32[]{:S(2)}, u32[]{:S(2)}) collective-permute-start(bf16[256,1536]{1,0:T(8,128)(2,1)} %get-tuple-element.223), channel_id=1, source_target_pairs={{0,2},{2,0},{1,3},{3,1},{4,6},{6,4},{5,7},{7,5},{8,10},{10,8},{9,1... | collective-permute-start | bytes 2359304 | tf_op jit(solution)/shard_map/ppermute | solution.py:311
  362.0 23.9 %collective-permute-start.63 = (bf16[256,1536]{1,0:T(8,128)(2,1)}, bf16[256,1536]{1,0:T(8,128)(2,1)}, u32[]{:S(2)}, u32[]{:S(2)}) collective-permute-start(bf16[256,1536]{1,0:T(8,128)(2,1)} %get-tuple-element.221), channel_id=1, source_target_pairs={{0,2},{2,0},{1,3},{3,1},{4,6},{6,4},{5,7},{7,5},{8,10},{10,8},{9,1... | collective-permute-start | bytes 2359304 | tf_op jit(solution)/shard_map/ppermute | solution.py:311
  363.7 36.4 %collective-permute-start.66 = (bf16[128,1536]{1,0:T(8,128)(2,1)}, bf16[128,1536]{1,0:T(8,128)(2,1)}, u32[]{:S(2)}, u32[]{:S(2)}) collective-permute-start(bf16[128,1536]{1,0:T(8,128)(2,1)} %get-tuple-element.249), channel_id=1, source_target_pairs={{0,1},{1,0},{2,3},{3,2},{4,5},{5,4},{6,7},{7,6},{8,9},{9,8},{10,11... | collective-permute-start | bytes 1179656 | tf_op jit(solution)/shard_map/ppermute | solution.py:311
  365.1 35.0 %collective-permute-start.67 = (bf16[128,1536]{1,0:T(8,128)(2,1)}, bf16[128,1536]{1,0:T(8,128)(2,1)}, u32[]{:S(2)}, u32[]{:S(2)}) collective-permute-start(bf16[128,1536]{1,0:T(8,128)(2,1)} %get-tuple-element.248), channel_id=1, source_target_pairs={{0,4},{4,0},{1,5},{5,1},{2,6},{6,2},{3,7},{7,3},{8,12},{12,8},{9,1... | collective-permute-start | bytes 1179656 | tf_op jit(solution)/shard_map/ppermute | solution.py:311
  366.6 15.9 %all-to-all-start.2 = ((bf16[4,96,768]{2,1,0:T(8,128)(2,1)}), bf16[4,96,768]{2,1,0:T(8,128)(2,1)S(1)}, u32[]{:S(2)}, u32[]{:S(2)}) async-start(bf16[4,96,768]{2,1,0:T(8,128)(2,1)} %bitcast.88), calls=%async_computation.6 | async-start | bytes 1179648 | tf_op jit(solution)/shard_map/all_to_all | solution.py:61
  401.9 17.6 %collective-permute-start.68 = (bf16[128,1536]{1,0:T(8,128)(2,1)}, bf16[128,1536]{1,0:T(8,128)(2,1)}, u32[]{:S(2)}, u32[]{:S(2)}) collective-permute-start(bf16[128,1536]{1,0:T(8,128)(2,1)} %reduce-precision_convert_fusion.10), channel_id=1, source_target_pairs={{0,4},{4,0},{1,5},{5,1},{2,6},{6,2},{3,7},{7,3},{8,12},{12,8},{9,1... | collective-permute-start | bytes 1179656 | tf_op jit(solution)/shard_map/ppermute | solution.py:311
  408.9 33.4 %all-to-all-start.1 = ((bf16[8,112,448]{2,1,0:T(8,128)(2,1)}), bf16[8,112,448]{2,1,0:T(8,128)(2,1)S(1)}, u32[]{:S(2)}, u32[]{:S(2)}) async-start(bf16[8,112,448]{2,1,0:T(8,128)(2,1)} %maximum_maximum_fusion), calls=%async_computation.5 | async-start | bytes 1835008 | tf_op jit(solution)/shard_map/all_to_all | solution.py:61
  414.3 20.2 %collective-permute-start.69 = (bf16[128,1536]{1,0:T(8,128)(2,1)}, bf16[128,1536]{1,0:T(8,128)(2,1)}, u32[]{:S(2)}, u32[]{:S(2)}) collective-permute-start(bf16[128,1536]{1,0:T(8,128)(2,1)} %reduce-precision_convert_fusion.9), channel_id=1, source_target_pairs={{0,1},{1,0},{2,3},{3,2},{4,5},{5,4},{6,7},{7,6},{8,9},{9,8},{10,11... | collective-permute-start | bytes 1179656 | tf_op jit(solution)/shard_map/ppermute | solution.py:311
  416.3 26.0 %collective-permute-start.62 = (bf16[128,1536]{1,0:T(8,128)(2,1)S(1)}, bf16[128,1536]{1,0:T(8,128)(2,1)S(1)}, u32[]{:S(2)}, u32[]{:S(2)}) collective-permute-start(bf16[128,1536]{1,0:T(8,128)(2,1)S(1)} %slice.179), channel_id=1, source_target_pairs={{0,1},{1,0},{2,3},{3,2},{4,5},{5,4},{6,7},{7,6},{8,9},{9,8},{10,11... | collective-permute-start | bytes 1179656 | tf_op jit(solution)/shard_map/ppermute | solution.py:311
  416.5 25.9 %collective-permute-start.64 = (bf16[128,1536]{1,0:T(8,128)(2,1)S(1)}, bf16[128,1536]{1,0:T(8,128)(2,1)S(1)}, u32[]{:S(2)}, u32[]{:S(2)}) collective-permute-start(bf16[128,1536]{1,0:T(8,128)(2,1)S(1)} %slice.180), channel_id=1, source_target_pairs={{0,4},{4,0},{1,5},{5,1},{2,6},{6,2},{3,7},{7,3},{8,12},{12,8},{9,1... | collective-permute-start | bytes 1179656 | tf_op jit(solution)/shard_map/ppermute | solution.py:311
  418.4 29.8 %collective-permute-start.70 = (bf16[256,1536]{1,0:T(8,128)(2,1)}, bf16[256,1536]{1,0:T(8,128)(2,1)}, u32[]{:S(2)}, u32[]{:S(2)}) collective-permute-start(bf16[256,1536]{1,0:T(8,128)(2,1)} %get-tuple-element.236), channel_id=1, source_target_pairs={{0,2},{2,0},{1,3},{3,1},{4,6},{6,4},{5,7},{7,5},{8,10},{10,8},{9,1... | collective-permute-start | bytes 2359304 | tf_op jit(solution)/shard_map/ppermute | solution.py:311
  (112 other events, 1212.4 us)
Sparse Core Ops, SparseCore 0:
  203.4 49.7 reduce-scatter.4
  262.4 49.5 reduce-scatter.6
  314.3 47.5 reduce-scatter.8
  364.0 35.7 reduce-scatter.10
